TPU v7x, 32 devices: a whole 2x2x4 slice. The times are simulated.
32 devices in a mesh: rows: 8 (over z, x), cols: 4 (over y, core).
Axes of the slice: x: 2, y: 2, z: 4, core: 2. Of those that a mesh axis runs over, the one named last changes fastest.
Arguments:
- states: bfloat16 [8, 96, 176, 768], P(None, 'rows', 'cols'), may hold values from -6 to 6
- heights: int32 [8], replicated, may hold values from 32 to 90, as said below
- widths: int32 [8], replicated, may hold values from 64 to 176, as said below
- first_gain: float32 [768], replicated, may hold values from 0.5 to 1.5
- first_shift: float32 [768], replicated, may hold values from -3 to 3
- filter_inner: bfloat16 [2, 8, 96, 96], P(None, 'cols'), may hold values from -0.4375 to 0.4375
- inner_bias: float32 [2, 8, 96], P(None, 'cols'), may hold values from -0.75 to 0.75
- filter_outer: bfloat16 [2, 8, 96, 96], P(None, 'cols'), may hold values from -0.4375 to 0.4375
- outer_bias: float32 [2, 8, 96], P(None, 'cols'), may hold values from -0.3125 to 0.3125
- later_gain: float32 [768], replicated, may hold values from 0.5 to 1.5
- later_shift: float32 [768], replicated, may hold values from -3 to 3
- expand_weight: bfloat16 [768, 3072], replicated, may hold values from -0.21875 to 0.21875
- expand_bias: float32 [3072], replicated, may hold values from -1.5 to 1.5
- reduce_weight: bfloat16 [3072, 768], replicated, may hold values from -0.109375 to 0.109375
- reduce_bias: float32 [768], replicated, may hold values from -1.5 to 1.5
- cotangent: bfloat16 [8, 96, 176, 768], P(None, 'rows', 'cols'), may hold values from -6 to 6
Outputs:
- result: bfloat16 [8, 96, 176, 768], P(None, 'rows', 'cols')
- states_grad: bfloat16 [8, 96, 176, 768], P(None, 'rows', 'cols')
- first_gain_grad: float32 [768], replicated
- first_shift_grad: float32 [768], replicated
- filter_inner_grad: float32 [2, 8, 96, 96], P(None, 'cols')
- inner_bias_grad: float32 [2, 8, 96], P(None, 'cols')
- filter_outer_grad: float32 [2, 8, 96, 96], P(None, 'cols')
- outer_bias_grad: float32 [2, 8, 96], P(None, 'cols')
- later_gain_grad: float32 [768], replicated
- later_shift_grad: float32 [768], replicated
- expand_weight_grad: float32 [768, 3072], replicated
- expand_bias_grad: float32 [3072], replicated
- reduce_weight_grad: float32 [3072, 768], replicated
- reduce_bias_grad: float32 [768], replicated
Inputs may be any that keep to these rules, and one draw needn't show every extreme that they name: `heights`: some frame has exactly 90 rows. `widths`: some frame spans all 176 columns.
All inputs are finite; a program needn't handle non-finite values.
Results may differ from a plain program's by a relative error of at most 0.012.
The roundings to bfloat16 on the way count: a program that leaves them out, or rounds other values in their place, can miss the bound.
Values sent between devices are 32-bit elements; how exact they have to be, the bound alone decides.
A program may use at most 576 MiB of HBM per device.

v0:
```python
import math

import jax
import jax.numpy as jnp
from jax import lax
from jax.sharding import PartitionSpec as P

BS = 96
BINS = 96


norm_eps = 1e-06
shrink_width = 0.01
highest = lax.Precision.HIGHEST


def gelu_exact(v):
    return jax.nn.gelu(v, approximate=False)


def standardize(values):
    centre = jnp.mean(values, axis=-1, keepdims=True)
    centred = values - centre
    spread = jnp.mean(centred * centred, axis=-1, keepdims=True)
    scale = lax.rsqrt(spread + norm_eps)
    return (centred * scale, scale)


def standardize_back(grad_norm, normal, scale):
    first = jnp.mean(grad_norm, axis=-1, keepdims=True)
    second = jnp.mean(grad_norm * normal, axis=-1, keepdims=True)
    return scale * (grad_norm - first - normal * second)


def wide_tables(width, bins):
    freq = jnp.arange(bins, dtype=jnp.int32)
    place = jnp.arange(width, dtype=jnp.int32)
    phase = place[:, None] * freq[None, :] % width
    angle = phase.astype(jnp.float32) * (2.0 * math.pi / width)
    live = (2 * freq <= width).astype(jnp.float32)
    edge = (freq == 0) | (2 * freq == width)
    weight_k = jnp.where(edge, 1.0, 2.0).astype(jnp.float32) * live
    factor = 1.0 / math.sqrt(width)
    cosine = jnp.cos(angle)
    sine = jnp.sin(angle)
    ahead = jnp.stack([cosine * live[None, :], -sine * live[None, :]], axis=-1) * factor
    behind = jnp.stack([weight_k[:, None] * cosine.T, -weight_k[:, None] * sine.T], axis=1) * factor
    return (ahead, behind)


def tall_table(height, sign):
    place = jnp.arange(height, dtype=jnp.int32)
    phase = place[:, None] * place[None, :] % height
    angle = phase.astype(jnp.float32) * (2.0 * math.pi / height)
    cosine = jnp.cos(angle)
    sine = jnp.sin(angle)
    upper = jnp.stack([cosine, sign * sine], axis=-1)
    lower_part = jnp.stack([-sign * sine, cosine], axis=-1)
    return jnp.stack([upper, lower_part], axis=1) / math.sqrt(height)


def tall_apply(values, table):
    return jnp.einsum("gshr,fhbrc->fgbsc", table, values, precision=highest)


def to_spectral(field, wide, table):
    moved = lax.all_to_all(field, "cols", split_axis=3, concat_axis=2, tiled=True)
    half = jnp.einsum("fhwc,wbr->fhbrc", moved, wide, precision=highest)
    half = lax.all_to_all(half, "rows", split_axis=2, concat_axis=1, tiled=True)
    return tall_apply(half, table)


def to_spatial(spectral, narrow, table):
    whole = tall_apply(spectral, table)
    back = lax.all_to_all(whole, "rows", split_axis=1, concat_axis=2, tiled=True)
    plane = jnp.einsum("fhbrc,brw->fhwc", back, narrow, precision=highest)
    return lax.all_to_all(plane, "cols", split_axis=2, concat_axis=3, tiled=True)


def mixing_matrix(weight):
    real = weight[0]
    imag = weight[1]
    upper = jnp.stack([real, imag], axis=2)
    lower_part = jnp.stack([-imag, real], axis=2)
    return jnp.stack([upper, lower_part], axis=1)


def unmix(grad_matrix):
    real = grad_matrix[:, 0, :, 0, :] + grad_matrix[:, 1, :, 1, :]
    imag = grad_matrix[:, 0, :, 1, :] - grad_matrix[:, 1, :, 0, :]
    return jnp.stack([real, imag], axis=0)


def filter_forward(spectral, inner_mix, inner_bias, outer_mix, outer_bias):
    count = spectral.shape[0] * spectral.shape[1] * spectral.shape[2]
    groups = inner_mix.shape[0]
    entries = spectral.reshape(count, 2, groups, BS).astype(jnp.bfloat16)
    first = (
        jnp.einsum("nrpi,priso->nspo", entries, inner_mix, preferred_element_type=jnp.float32)
        + inner_bias
    )
    active = gelu_exact(first).astype(jnp.bfloat16)
    second = (
        jnp.einsum("nrpi,priso->nspo", active, outer_mix, preferred_element_type=jnp.float32)
        + outer_bias
    )
    return (entries, first, active, second)


def body(
    states,
    heights,
    widths,
    first_gain,
    first_shift,
    filter_inner,
    inner_bias,
    filter_outer,
    outer_bias,
    later_gain,
    later_shift,
    expand_weight,
    expand_bias,
    reduce_weight,
    reduce_bias,
    cotangent,
):
    frames, rows_here, cols_here, chans = states.shape
    height = rows_here * lax.axis_size("rows")
    width = cols_here * lax.axis_size("cols")
    row_ids = lax.axis_index("rows") * rows_here + jnp.arange(rows_here, dtype=jnp.int32)
    col_ids = lax.axis_index("cols") * cols_here + jnp.arange(cols_here, dtype=jnp.int32)
    inside = (row_ids[None, :, None] < heights[:, None, None]) & (
        col_ids[None, None, :] < widths[:, None, None]
    )
    mask = inside.astype(jnp.float32)[..., None]
    ahead_wide, behind_wide = wide_tables(width, BINS)
    ahead_tall = tall_table(height, 1.0)
    behind_tall = tall_table(height, -1.0)
    inner_mix = mixing_matrix(filter_inner)
    outer_mix = mixing_matrix(filter_outer)
    lower = mask * states.astype(jnp.float32)
    first_norm, first_scale = standardize(lower)
    filter_in = mask * (first_norm * first_gain + first_shift)
    spectral = to_spectral(filter_in, ahead_wide, ahead_tall)
    entries, first, active, second = filter_forward(
        spectral, inner_mix, inner_bias, outer_mix, outer_bias
    )
    shrunk = second - shrink_width * jnp.tanh(second / shrink_width)
    spatial = to_spatial(shrunk.reshape(spectral.shape), behind_wide, behind_tall)
    mixed = lower + mask * (spatial + filter_in)
    tokens = frames * rows_here * cols_here
    flat = mixed.reshape(tokens, chans)
    flat_mask = mask.reshape(tokens, 1)
    later_norm, later_scale = standardize(flat)
    normed = (later_norm * later_gain + later_shift).astype(jnp.bfloat16)
    pre = jnp.dot(normed, expand_weight, preferred_element_type=jnp.float32) + expand_bias
    hidden = gelu_exact(pre).astype(jnp.bfloat16)
    branch = jnp.dot(hidden, reduce_weight, preferred_element_type=jnp.float32) + reduce_bias
    result = (flat_mask * (flat + branch)).astype(jnp.bfloat16).reshape(states.shape)
    contract_rows = (((0,), (0,)), ((), ()))
    contract_cols = (((1,), (1,)), ((), ()))
    grad_out = flat_mask * cotangent.reshape(tokens, chans).astype(jnp.float32)
    grad_branch = grad_out.astype(jnp.bfloat16)
    reduce_bias_grad = jnp.sum(grad_out, axis=0)
    reduce_weight_grad = lax.dot_general(
        hidden, grad_branch, contract_rows, preferred_element_type=jnp.float32
    )
    grad_hidden = lax.dot_general(
        grad_branch, reduce_weight, contract_cols, preferred_element_type=jnp.float32
    )
    grad_pre = jax.vjp(gelu_exact, pre)[1](grad_hidden)[0]
    expand_bias_grad = jnp.sum(grad_pre, axis=0)
    grad_pre_low = grad_pre.astype(jnp.bfloat16)
    expand_weight_grad = lax.dot_general(
        normed, grad_pre_low, contract_rows, preferred_element_type=jnp.float32
    )
    grad_normed = lax.dot_general(
        grad_pre_low, expand_weight, contract_cols, preferred_element_type=jnp.float32
    )
    later_gain_grad = jnp.sum(grad_normed * later_norm, axis=0)
    later_shift_grad = jnp.sum(grad_normed, axis=0)
    grad_mixed = grad_out + standardize_back(grad_normed * later_gain, later_norm, later_scale)
    grad_mixed = grad_mixed.reshape(states.shape)
    entries, first, active, second = filter_forward(
        to_spectral(filter_in, ahead_wide, ahead_tall), inner_mix, inner_bias, outer_mix, outer_bias
    )
    grad_shrunk = to_spectral(mask * grad_mixed, jnp.transpose(behind_wide, (2, 0, 1)), ahead_tall)
    grad_outer = grad_shrunk.reshape(second.shape) * jnp.square(jnp.tanh(second / shrink_width))
    outer_bias_grad = jnp.sum(grad_outer, axis=0)
    grad_outer_low = grad_outer.astype(jnp.bfloat16)
    outer_mix_grad = jnp.einsum(
        "nrpi,nspo->priso", active, grad_outer_low, preferred_element_type=jnp.float32
    )
    grad_active = jnp.einsum(
        "nspo,priso->nrpi", grad_outer_low, outer_mix, preferred_element_type=jnp.float32
    )
    grad_inner = jax.vjp(gelu_exact, first)[1](grad_active)[0]
    inner_bias_grad = jnp.sum(grad_inner, axis=0)
    grad_inner_low = grad_inner.astype(jnp.bfloat16)
    inner_mix_grad = jnp.einsum(
        "nrpi,nspo->priso", entries, grad_inner_low, preferred_element_type=jnp.float32
    )
    grad_entries = jnp.einsum(
        "nspo,priso->nrpi", grad_inner_low, inner_mix, preferred_element_type=jnp.float32
    )
    grad_spectral = grad_entries.reshape(grad_shrunk.shape)
    grad_filter_in = mask * grad_mixed + to_spatial(
        grad_spectral, jnp.transpose(ahead_wide, (1, 2, 0)), behind_tall
    )
    grad_first_norm = mask * grad_filter_in
    first_gain_grad = jnp.sum((grad_first_norm * first_norm).reshape(tokens, chans), axis=0)
    first_shift_grad = jnp.sum(grad_first_norm.reshape(tokens, chans), axis=0)
    grad_lower = grad_mixed + standardize_back(
        grad_first_norm * first_gain, first_norm, first_scale
    )
    states_grad = (mask * grad_lower).astype(jnp.bfloat16)
    inner_sum, inner_bias_sum, outer_sum, outer_bias_sum = lax.psum(
        (unmix(inner_mix_grad), inner_bias_grad, unmix(outer_mix_grad), outer_bias_grad), "rows"
    )
    dense = lax.psum(
        (
            first_gain_grad,
            first_shift_grad,
            later_gain_grad,
            later_shift_grad,
            expand_weight_grad,
            expand_bias_grad,
            reduce_weight_grad,
            reduce_bias_grad,
        ),
        ("rows", "cols"),
    )
    return (
        result,
        states_grad,
        dense[0],
        dense[1],
        inner_sum,
        inner_bias_sum,
        outer_sum,
        outer_bias_sum,
        dense[2],
        dense[3],
        dense[4],
        dense[5],
        dense[6],
        dense[7],
    )


def solution(mesh):
    in_specs = (
        P(None, "rows", "cols", None),
        P(),
        P(),
        P(),
        P(),
        P(None, "cols", None, None),
        P(None, "cols", None),
        P(None, "cols", None, None),
        P(None, "cols", None),
        P(),
        P(),
        P(),
        P(),
        P(),
        P(),
        P(None, "rows", "cols", None),
    )
    out_specs = (
        P(None, "rows", "cols", None),
        P(None, "rows", "cols", None),
        P(),
        P(),
        P(None, "cols", None, None),
        P(None, "cols", None),
        P(None, "cols", None, None),
        P(None, "cols", None),
        P(),
        P(),
        P(),
        P(),
        P(),
        P(),
    )
    return jax.shard_map(body, mesh=mesh, in_specs=in_specs, out_specs=out_specs, check_vma=False)
```

profile of v0, /device:TPU:15, one launch (start us, length us, event | category | flops | bytes accessed | tf_op | source)
XLA Modules:
  0.0 4620.8 jit_solution(16914792397599365503)
XLA Ops:
  29.1 31.4 copy.237
  60.6 87.5 %reshape.632 = f32[4,1,811008]{2,1,0:T(1,128)} reshape(f32[768,12,8,44]{3,2,1,0:T(8,128)} %bitcast.268) | data formatting | bytes 25952256
  155.6 140.0 %all-to-all-done = f32[4,1,811008]{2,1,0:T(1,128)} async-done(((f32[4,1,811008]{2,1,0:T(1,128)}), f32[4,1,811008]{2,1,0:T(1,128)}, u32[]{:S(2)}, u32[]{:S(2)}) %all-to-all-start) | async-done | bytes 12976160 | tf_op jit(solution)/shard_map/all_to_all | solution.py:67
  296.2 141.6 %reduce.5 = f32[4,811008]{1,0:T(4,128)} reduce(f32[4,1,811008]{2,1,0:T(1,128)} %all-to-all-done, f32[]{:T(128)} %broadcast.955), dimensions={1}, to_apply=%all_to_all.116.reduce_sub_computation | reduce | bytes 25952260 | tf_op jit(solution)/shard_map/all_to_all | solution.py:67
  437.8 85.0 %reshape.633 = f32[768,12,8,44]{3,2,1,0:T(8,128)} reshape(f32[4,811008]{1,0:T(4,128)} %reduce.5) | data formatting | bytes 25952256
  522.8 35.5 copy.324
  572.8 26.1 fusion.73
  598.9 21.9 copy.241
  628.9 403.2 %all-to-all-done.1 = f32[8,12,96,2,192]{4,0,3,1,2:T(8,128)} async-done(((f32[8,12,96,2,192]{4,0,3,1,2:T(8,128)}), f32[8,12,96,2,192]{4,0,3,1,2:T(8,128)}, u32[]{:S(2)}, u32[]{:S(2)}) %all-to-all-start.1) | async-done | bytes 14155808 | tf_op jit(solution)/shard_map/all_to_all | solution.py:69
  1039.6 43.5 fusion.47
  1104.8 26.7 convert_element_type.153
  1131.6 38.8 multiply_convert_fusion.1
  1181.8 24.4 copy.249
  1206.3 28.4 reshape.596
  1234.7 44.7 fusion.54
  1279.3 26.8 copy.251
  1314.9 404.8 %all-to-all-done.2 = f32[8,96,12,2,192]{4,3,2,0,1:T(2,128)} async-done(((f32[8,96,12,2,192]{4,3,2,0,1:T(2,128)}), f32[8,96,12,2,192]{4,3,2,0,1:T(2,128)}, u32[]{:S(2)}, u32[]{:S(2)}) %all-to-all-start.2) | async-done | bytes 14155808 | tf_op jit(solution)/shard_map/all_to_all | solution.py:75
  1739.9 30.4 fusion.60
  1770.3 22.7 copy.255
  1825.7 162.5 %all-to-all-done.3 = f32[8,12,176,192]{3,0,1,2:T(8,128)} async-done(((f32[8,12,176,192]{3,0,1,2:T(8,128)}), f32[8,12,176,192]{3,0,1,2:T(8,128)}, u32[]{:S(2)}, u32[]{:S(2)}) %all-to-all-start.3) | async-done | bytes 12976160 | tf_op jit(solution)/shard_map/all_to_all | solution.py:77
  2076.6 136.1 %multiply_convert_fusion = (bf16[4224,3072]{1,0:T(8,128)(2,1)}, f32[4224,3072]{1,0:T(8,128)}, f32[4224,3072]{1,0:T(8,128)}) fusion(f32[3072]{0:T(1024)S(1)} %copy-done.60, bf16[768,3072]{1,0:T(8,128)(2,1)} %param.27, f32[4224,768]{1,0:T(8,128)} %reshape.597, f32[768]{0:T(1024)S(1)} %copy-done.61, f32[768]{0:T(1024)S(1)} %copy-done.53, f32[4224]{0:T(1024)S(1)} %rsqrt.21, ...), kind=kOutput, calls=%fused_computation.3 | convolution fusion | flops 20803977216 | bytes 147508224 | tf_op jit(solution)/shard_map/dot_general | solution.py:157
  2212.6 56.8 %fusion.158 = (f32[3072]{0:T(1024)}, bf16[4224,3072]{1,0:T(8,128)(2,1)}) fusion(f32[4224,3072]{1,0:T(8,128)} %get-tuple-element.105, bf16[3072,768]{1,0:T(8,128)(2,1)} %param.29, f32[4224,768]{1,0:T(8,128)} %reshape.604, f32[4224]{0:T(1024)S(1)} %copy-done.37, f32[4224,3072]{1,0:T(8,128)} %get-tuple-element.131, f32[3072]{0:T(1024)S(1)} %copy-done.60), kind=kOutput, calls=%fused_computation.239 | convolution fusion | flops 20145434624 | bytes 147497472 | tf_op jit(solution)/shard_map/dot_general | solution.py:169
  2269.4 32.6 multiply_reduce_fusion.1
  2350.8 31.4 copy.263
  2382.2 75.2 %reshape.634 = f32[4,1,811008]{2,1,0:T(1,128)} reshape(f32[768,12,8,44]{3,2,1,0:T(8,128)} %bitcast.270) | data formatting | bytes 25952256
  2457.4 151.9 %all_to_all.157 = f32[4,1,811008]{2,1,0:T(1,128)} all-to-all(f32[4,1,811008]{2,1,0:T(1,128)} %reshape.634), channel_id=1, replica_groups=mesh['rows'=8,'cols'=4] {'cols'}, dimensions={0} | all-to-all | bytes 25952256 | tf_op jit(solution)/shard_map/all_to_all | solution.py:67
  2609.3 141.6 %reduce.6 = f32[4,811008]{1,0:T(4,128)} reduce(f32[4,1,811008]{2,1,0:T(1,128)} %all_to_all.157, f32[]{:T(128)} %broadcast.955), dimensions={1}, to_apply=%all_to_all.132.reduce_sub_computation | reduce | bytes 25952260 | tf_op jit(solution)/shard_map/all_to_all | solution.py:67
  2750.9 85.0 %reshape.635 = f32[768,12,8,44]{3,2,1,0:T(8,128)} reshape(f32[4,811008]{1,0:T(4,128)} %reduce.6) | data formatting | bytes 25952256
  2835.9 35.5 copy.335
  2885.9 25.9 fusion.76
  2933.6 415.9 %all_to_all.158 = f32[8,12,96,2,192]{4,0,3,1,2:T(8,128)} all-to-all(f32[8,12,96,2,192]{4,0,3,1,2:T(8,128)} %copy.267), channel_id=1, replica_groups=mesh['rows'=8,'cols'=4] {'rows'}, dimensions={2} | all-to-all | bytes 28311552 | tf_op jit(solution)/shard_map/all_to_all | solution.py:69
  3357.0 45.0 fusion.51
  3402.1 26.9 copy.271
  3429.0 28.9 reshape.600
  3457.9 24.4 copy.272
  3523.8 24.4 copy.275
  3548.2 28.4 reshape.601
  3576.6 44.5 fusion.57
  3621.1 26.8 copy.277
  3656.5 30.4 fusion.151
  3686.9 374.7 %all-to-all-done.6 = f32[8,96,12,2,192]{4,3,2,0,1:T(2,128)} async-done(((f32[8,96,12,2,192]{4,3,2,0,1:T(2,128)}), f32[8,96,12,2,192]{4,3,2,0,1:T(2,128)}, u32[]{:S(2)}, u32[]{:S(2)}) %all-to-all-start.6) | async-done | bytes 14155808 | tf_op jit(solution)/shard_map/all_to_all | solution.py:75
  4081.9 30.2 fusion.63
  4112.1 22.6 copy.281
  4143.4 33.0 fusion.40
  4197.3 29.0 multiply_convert_fusion.3
  4284.3 110.2 %all-to-all-done.7 = f32[8,12,176,192]{3,0,1,2:T(8,128)} async-done(((f32[8,12,176,192]{3,0,1,2:T(8,128)}), f32[8,12,176,192]{3,0,1,2:T(8,128)}, u32[]{:S(2)}, u32[]{:S(2)}) %all-to-all-start.7) | async-done | bytes 12976160 | tf_op jit(solution)/shard_map/all_to_all | solution.py:77
  4416.1 21.9 copy.283
  4552.2 45.6 all-reduce
  (261 shorter events, 644.3 us)
Async XLA Ops:
  7.2 15.8 slice-start
  7.2 15.8 copy-start.39
  8.9 20.2 copy-start.27
  9.1 20.0 copy-start
  148.1 147.6 %all-to-all-start = ((f32[4,1,811008]{2,1,0:T(1,128)}), f32[4,1,811008]{2,1,0:T(1,128)}, u32[]{:S(2)}, u32[]{:S(2)}) async-start(f32[4,1,811008]{2,1,0:T(1,128)} %reshape.632), calls=%async_computation | async-start | bytes 25952256 | tf_op jit(solution)/shard_map/all_to_all | solution.py:67
  155.6 417.1 %copy-start.19 = (f32[176,96,1]{1,0,2:T(8,128)}, f32[176,96,1]{1,0,2:T(8,128)S(1)}, u32[]{:S(2)}) copy-start(f32[176,96,1]{1,0,2:T(8,128)S(1)} %get-tuple-element.126) | copy-start | bytes 202756
  155.6 417.1 %copy-start.21 = (f32[176,96,1]{1,0,2:T(8,128)}, f32[176,96,1]{1,0,2:T(8,128)S(1)}, u32[]{:S(2)}) copy-start(f32[176,96,1]{1,0,2:T(8,128)S(1)} %get-tuple-element.127) | copy-start | bytes 202756
  620.8 411.3 %all-to-all-start.1 = ((f32[8,12,96,2,192]{4,0,3,1,2:T(8,128)}), f32[8,12,96,2,192]{4,0,3,1,2:T(8,128)}, u32[]{:S(2)}, u32[]{:S(2)}) async-start(f32[8,12,96,2,192]{4,0,3,1,2:T(8,128)} %copy.241), calls=%async_computation.1 | async-start | bytes 37748736 | tf_op jit(solution)/shard_map/all_to_all | solution.py:69
  628.1 503.5 %copy-start.29 = (bf16[2,1,96,2,96]{2,4,1,3,0:T(8,128)(2,1)}, bf16[2,1,96,2,96]{2,4,1,3,0:T(8,128)(2,1)S(1)}, u32[]{:S(2)}) copy-start(bf16[2,1,96,2,96]{2,4,1,3,0:T(8,128)(2,1)S(1)} %get-tuple-element.124) | copy-start | bytes 221188
  628.1 503.5 %copy-start.31 = (bf16[2,1,96,2,96]{2,4,1,3,0:T(8,128)(2,1)}, bf16[2,1,96,2,96]{2,4,1,3,0:T(8,128)(2,1)S(1)}, u32[]{:S(2)}) copy-start(bf16[2,1,96,2,96]{2,4,1,3,0:T(8,128)(2,1)S(1)} %get-tuple-element.125) | copy-start | bytes 221188
  628.2 542.2 %copy-start.33 = (bf16[2,1,96,2,96]{2,4,1,3,0:T(8,128)(2,1)}, bf16[2,1,96,2,96]{2,4,1,3,0:T(8,128)(2,1)S(1)}, u32[]{:S(2)}) copy-start(bf16[2,1,96,2,96]{2,4,1,3,0:T(8,128)(2,1)S(1)} %get-tuple-element.122) | copy-start | bytes 221188
  628.2 542.2 %copy-start.35 = (bf16[2,1,96,2,96]{2,4,1,3,0:T(8,128)(2,1)}, bf16[2,1,96,2,96]{2,4,1,3,0:T(8,128)(2,1)S(1)}, u32[]{:S(2)}) copy-start(bf16[2,1,96,2,96]{2,4,1,3,0:T(8,128)(2,1)S(1)} %get-tuple-element.123) | copy-start | bytes 221188
  628.9 410.7 %copy-start.15 = (f32[96,1,96,2]{2,0,3,1:T(8,128)}, f32[96,1,96,2]{2,0,3,1:T(8,128)S(1)}, u32[]{:S(2)}) copy-start(f32[96,1,96,2]{2,0,3,1:T(8,128)S(1)} %get-tuple-element.113) | copy-start | bytes 221188
  628.9 410.7 %copy-start.17 = (f32[96,1,96,2]{2,0,3,1:T(8,128)}, f32[96,1,96,2]{2,0,3,1:T(8,128)S(1)}, u32[]{:S(2)}) copy-start(f32[96,1,96,2]{2,0,3,1:T(8,128)S(1)} %get-tuple-element.120) | copy-start | bytes 221188
  1206.2 28.4 copy-start.11
  1206.2 28.4 copy-start.13
  1306.2 413.5 %all-to-all-start.2 = ((f32[8,96,12,2,192]{4,3,2,0,1:T(2,128)}), f32[8,96,12,2,192]{4,3,2,0,1:T(2,128)}, u32[]{:S(2)}, u32[]{:S(2)}) async-start(f32[8,96,12,2,192]{4,3,2,0,1:T(2,128)} %copy.251), calls=%async_computation.2 | async-start | bytes 37748736 | tf_op jit(solution)/shard_map/all_to_all | solution.py:75
  1314.9 425.0 %copy-start.23 = (f32[96,1,176]{0,2,1:T(8,128)}, f32[96,1,176]{0,2,1:T(8,128)S(1)}, u32[]{:S(2)}) copy-start(f32[96,1,176]{0,2,1:T(8,128)S(1)} %get-tuple-element.139) | copy-start | bytes 202756
  1314.9 425.0 %copy-start.25 = (f32[96,1,176]{0,2,1:T(8,128)}, f32[96,1,176]{0,2,1:T(8,128)S(1)}, u32[]{:S(2)}) copy-start(f32[96,1,176]{0,2,1:T(8,128)S(1)} %get-tuple-element.140) | copy-start | bytes 202756
  1793.0 195.2 %all-to-all-start.3 = ((f32[8,12,176,192]{3,0,1,2:T(8,128)}), f32[8,12,176,192]{3,0,1,2:T(8,128)}, u32[]{:S(2)}, u32[]{:S(2)}) async-start(f32[8,12,176,192]{3,0,1,2:T(8,128)} %copy.255), calls=%async_computation.3 | async-start | bytes 34603008 | tf_op jit(solution)/shard_map/all_to_all | solution.py:77
  2009.7 18.9 copy-start.1
  2009.7 18.9 copy-start.5
  2009.7 18.9 copy-start.8
  2009.7 18.9 copy-start.40
  2009.7 18.9 copy-start.50
  2062.5 239.5 %copy-start.44 = (f32[4224]{0:T(1024)}, f32[4224]{0:T(1024)S(1)}, u32[]{:S(2)}) copy-start(f32[4224]{0:T(1024)S(1)} %rsqrt.21) | copy-start | bytes 50692
  2076.5 225.5 %copy-start.46 = (f32[4224]{0:T(1024)}, f32[4224]{0:T(1024)S(1)}, u32[]{:S(2)}) copy-start(f32[4224]{0:T(1024)S(1)} %div.42) | copy-start | bytes 50692
  2076.6 136.1 %copy-start.37 = (f32[4224]{0:T(1024)S(1)}, f32[4224]{0:T(1024)}, u32[]{:S(2)}) copy-start(f32[4224]{0:T(1024)} %reshape.603) | copy-start | bytes 50692
  3496.1 17.6 copy-start.30
  3496.1 17.6 copy-start.32
  3548.2 28.4 copy-start.12
  3548.2 28.4 copy-start.14
  3648.0 413.7 %all-to-all-start.6 = ((f32[8,96,12,2,192]{4,3,2,0,1:T(2,128)}), f32[8,96,12,2,192]{4,3,2,0,1:T(2,128)}, u32[]{:S(2)}, u32[]{:S(2)}) async-start(f32[8,96,12,2,192]{4,3,2,0,1:T(2,128)} %copy.277), calls=%async_computation.6 | async-start | bytes 37748736 | tf_op jit(solution)/shard_map/all_to_all | solution.py:75
  4134.8 259.7 %all-to-all-start.7 = ((f32[8,12,176,192]{3,0,1,2:T(8,128)}), f32[8,12,176,192]{3,0,1,2:T(8,128)}, u32[]{:S(2)}, u32[]{:S(2)}) async-start(f32[8,12,176,192]{3,0,1,2:T(8,128)} %copy.281), calls=%async_computation.7 | async-start | bytes 34603008 | tf_op jit(solution)/shard_map/all_to_all | solution.py:77
  4143.4 454.5 %all-reduce.7.cloned.1.call-start = ((), (), s32[]{:S(2)}) async-start(), calls=%async_computation.8 | async-start | bytes 37748736 | tf_op jit(solution)/shard_map/psum | solution.py:221
  4176.5 421.4 %all-reduce.9.cloned.1.call-start = ((), (), s32[]{:S(2)}) async-start(), calls=%async_computation.9 | async-start | bytes 786432 | tf_op jit(solution)/shard_map/psum | solution.py:218
  4177.2 20.1 copy-start.63
  4226.3 19.5 copy-start.52
  4226.3 19.5 copy-start.59
  4456.9 19.3 copy-start.3
  4456.9 19.3 copy-start.6
  4456.9 19.3 copy-start.9
  4494.0 33.0 slice-start.2
  4494.0 33.0 slice-start.4
  4494.0 33.0 slice-start.5
  4508.0 19.0 slice-start.3
  4508.0 19.0 slice-start.6
  4508.0 19.0 slice-start.7
  (35 other events, 336.7 us)
Sparse Core Ops, SparseCore 0:
  4176.6 341.2 all-reduce.6
  4521.8 70.0 all-reduce.8
where the time goes:
time: 4640 us; the launch traced here: 4620 us
  waiting for transfers between devices  1600 us (34%)
  local copies, waits for them, and re-layouts  1190 us (26%)
  matrix products  706 us (15%)
  blocking collectives  629 us (14%)
  other arithmetic  437 us (9%)
  starting transfers between devices  47.2 us (1%)
    all_to_all x2, waiting for transfers between devices, to_spatial(): lax.all_to_all(whole, 'rows', split_axis=1, concat_axis=2, tiled=True)  780 us
    all_to_all x1, blocking collectives, to_spectral(): half = lax.all_to_all(half, 'rows', split_axis=2, concat_axis=1, tiled=True)  416 us
    all_to_all x1, waiting for transfers between devices, to_spectral(): half = lax.all_to_all(half, 'rows', split_axis=2, concat_axis=1, tiled=True)  403 us
    unnamed x167, local copies, waits for them, and re-layouts  361 us
    all_to_all x2, other arithmetic, to_spectral(): lax.all_to_all(field, 'cols', split_axis=3, concat_axis=2, tiled=True)  283 us
    all_to_all x2, waiting for transfers between devices, to_spatial(): lax.all_to_all(plane, 'cols', split_axis=2, concat_axis=3, tiled=True)  273 us
    dot_general x4, matrix products, tall_apply(): return jnp.einsum('gshr,fhbrc->fgbsc', table, values, precision=highest)  178 us
    all_to_all x1, blocking collectives, to_spectral(): lax.all_to_all(field, 'cols', split_axis=3, concat_axis=2, tiled=True)  152 us
  transfers between devices with their start and end apart: 8, of which 6 were waited for; matrix products, arithmetic and copies ran while one was open for 7% of the time, Pallas kernels for 0%

commit v1 on v0

v1 whole, which is shorter than its diff:
```python
import functools
import math

import jax
import jax.numpy as jnp
import numpy as np
from jax import lax
from jax.experimental import pallas as pl
from jax.experimental.pallas import tpu as pltpu
from jax.sharding import PartitionSpec as P

BS = 96
BINS = 96
PAIR = 2
GROUP = 8
norm_eps = 1e-06
shrink_width = 0.01
VMEM = 60 * 1024 * 1024
f32 = jnp.float32
bf16 = jnp.bfloat16


def phi_parts(v):
    cdf = 0.5 * (1.0 + lax.erf(v * math.sqrt(0.5)))
    slope = cdf + v * (jnp.exp(v * v * -0.5) * (1.0 / math.sqrt(2.0 * math.pi)))
    return cdf, slope


def dot(a, b):
    return lax.dot_general(a, b, (((1,), (0,)), ((), ())), preferred_element_type=f32)


def dot_tn(a, b):
    return lax.dot_general(a, b, (((0,), (0,)), ((), ())), preferred_element_type=f32)


def dot_nt(a, b):
    return lax.dot_general(a, b, (((1,), (1,)), ((), ())), preferred_element_type=f32)


def row_mask(meta, heights, widths, frame, row, cols_here):
    cols = meta[1] + lax.broadcasted_iota(jnp.int32, (cols_here, 1), 0)
    tall = (meta[0] + row < heights[frame]).astype(jnp.int32)
    return (cols < widths[frame] * tall).astype(f32)


def standardize(v):
    centre = jnp.mean(v, axis=-1, keepdims=True)
    centred = v - centre
    spread = jnp.mean(centred * centred, axis=-1, keepdims=True)
    scale = lax.rsqrt(spread + norm_eps)
    return centred * scale, scale


def standardize_back(grad, normal, scale):
    first = jnp.mean(grad, axis=-1, keepdims=True)
    second = jnp.mean(grad * normal, axis=-1, keepdims=True)
    return scale * (grad - first - normal * second)


def unpack_row(ref, i, cols_here, groups, width, pairs):
    half, j = divmod(i, pairs)
    parts = [
        ref[c, j * cols_here : (j + 1) * cols_here, half * width : (half + 1) * width]
        for c in range(groups)
    ]
    return jnp.concatenate(parts, axis=1) if groups > 1 else parts[0]


def first_kernel(meta, heights, widths, states, gain, shift, out):
    frame = pl.program_id(0)
    rows_here, cols_here, _ = states.shape[1:]
    groups, _, lanes = out.shape
    width = lanes // PAIR
    pairs = rows_here // PAIR
    for j in range(pairs):
        sides = []
        for half in range(PAIR):
            row = half * pairs + j
            mask = row_mask(meta, heights, widths, frame, row, cols_here)
            normal, _ = standardize(states[0, row].astype(f32) * mask)
            sides.append(mask * (normal * gain[...] + shift[...]))
        for c in range(groups):
            part = jnp.concatenate([s[:, c * width : (c + 1) * width] for s in sides], axis=1)
            out[c, j * cols_here : (j + 1) * cols_here, :] = part


def table_dot(table, x):
    rows = table.shape[0] // 2
    high = x.astype(bf16)
    both = dot(table[...], high)
    rest = dot(table[:rows, :], (x - high.astype(f32)).astype(bf16))
    return both[:rows] + both[rows:] + rest


def take_rows(step, block, table, wide, held, pairs, cols_here, fine):
    groups = block.shape[0]
    for j in range(pairs):
        for c in range(groups):
            wide[c * cols_here : (c + 1) * cols_here, :] = block[
                c, j * cols_here : (j + 1) * cols_here, :
            ]
        x = wide[...]
        held[step * pairs + j] = table_dot(table, x) if fine else dot(table[...], x.astype(bf16))


def give_rows(step, block, table, held, pairs, cols_here, factor):
    groups = block.shape[0]
    for j in range(pairs):
        plane = dot(table[...], held[step * pairs + j].astype(bf16)) * factor
        for c in range(groups):
            block[c, j * cols_here : (j + 1) * cols_here, :] = plane[
                c * cols_here : (c + 1) * cols_here, :
            ]


def bins_in(held, group, table, width, fine):
    kind = f32 if fine else bf16
    start = pl.multiple_of(group * GROUP, GROUP)
    real = jnp.swapaxes(held[:, pl.ds(start, GROUP), :], 0, 1).astype(kind)
    imag = jnp.swapaxes(held[:, pl.ds(BINS + start, GROUP), :], 0, 1).astype(kind)
    outs = []
    for k in range(GROUP):
        x = jnp.concatenate(
            [part[k][:, h * width : (h + 1) * width] for part in (real, imag) for h in range(PAIR)],
            axis=0,
        )
        outs.append(table_dot(table, x) if fine else dot(table[...], x))
    return outs


def bins_out(held, group, table, width, values):
    start = pl.multiple_of(group * GROUP, GROUP)
    short = held.shape[0]
    real, imag = [], []
    for value in values:
        z = dot(table[...], value)
        pieces = [z[i * short : (i + 1) * short, :] for i in range(2 * PAIR)]
        real.append(jnp.concatenate(pieces[:PAIR], axis=1))
        imag.append(jnp.concatenate(pieces[PAIR:], axis=1))
    held[:, pl.ds(start, GROUP), :] = jnp.swapaxes(jnp.stack(real, axis=0), 0, 1)
    held[:, pl.ds(BINS + start, GROUP), :] = jnp.swapaxes(jnp.stack(imag, axis=0), 0, 1)


def halves(v, count, tall):
    return [
        (v[k * 2 * tall : k * 2 * tall + tall], v[k * 2 * tall + tall : (k + 1) * 2 * tall])
        for k in range(count)
    ]


def complex_product(x, first, second, count, tall, conj):
    a = dot(x, first)
    b = dot(x, second)
    parts = []
    for (a_re, a_im), (b_re, b_im) in zip(halves(a, count, tall), halves(b, count, tall)):
        if conj:
            parts += [a_re + b_im, a_im - b_re]
        else:
            parts += [a_re - b_im, a_im + b_re]
    return parts


def spectral_forward_kernel(
    steps, pairs, cols_here, factor,
    block, table_in, table_down, table_up, table_out, inner, inner_bias, outer, outer_bias,
    out, entries, active, slope, damp,
    wide, held,
):
    i = pl.program_id(0)
    bin_steps = BINS // GROUP
    width = block.shape[2] // PAIR
    tall = held.shape[0] * PAIR

    @pl.when(i < steps)
    def _():
        take_rows(i, block, table_in, wide, held, pairs, cols_here, True)

    @pl.when((i >= steps) & (i < steps + bin_steps))
    def _():
        group = i - steps
        spec = bins_in(held, group, table_down, width, True)
        low = jnp.concatenate([(s * factor).astype(bf16) for s in spec], axis=0)
        entries[...] = low
        parts = complex_product(low, inner[0], inner[1], GROUP, tall, False)
        acts = []
        for n, part in enumerate(parts):
            v = part + inner_bias[n % 2 : n % 2 + 1, :]
            cdf, der = phi_parts(v)
            acts.append((v * cdf).astype(bf16))
            slope[n * tall : (n + 1) * tall, :] = der.astype(bf16)
        act = jnp.concatenate(acts, axis=0)
        active[...] = act
        parts = complex_product(act, outer[0], outer[1], GROUP, tall, False)
        shrunk = []
        for n, part in enumerate(parts):
            v = part + outer_bias[n % 2 : n % 2 + 1, :]
            t = jnp.tanh(v * (1.0 / shrink_width))
            shrunk.append((v - shrink_width * t).astype(bf16))
            damp[n * tall : (n + 1) * tall, :] = (t * t).astype(bf16)
        values = [jnp.concatenate(shrunk[2 * k : 2 * k + 2], axis=0) for k in range(GROUP)]
        bins_out(held, group, table_up, width, values)

    @pl.when(i >= steps + bin_steps)
    def _():
        give_rows(i - steps - bin_steps, out, table_out, held, pairs, cols_here, factor)


def spectral_backward_kernel(
    steps, pairs, cols_here, factor,
    block, table_in, table_down, table_up, table_out, inner_t, outer_t, entries, active, slope, damp,
    out, inner_grad, inner_bias_grad, outer_grad, outer_bias_grad,
    wide, held,
):
    i = pl.program_id(0)
    bin_steps = BINS // GROUP
    width = block.shape[2] // PAIR
    tall = held.shape[0] * PAIR

    @pl.when(i == 0)
    def _():
        for ref in (inner_grad, inner_bias_grad, outer_grad, outer_bias_grad):
            ref[...] = jnp.zeros_like(ref)

    @pl.when(i < steps)
    def _():
        take_rows(i, block, table_in, wide, held, pairs, cols_here, False)

    def weight_grads(ref, before, grads):
        plain = jnp.concatenate(grads, axis=0)
        turned = []
        for k in range(GROUP):
            turned += [grads[2 * k + 1], -grads[2 * k]]
        ref[0] += dot_tn(before, plain)
        ref[1] += dot_tn(before, jnp.concatenate(turned, axis=0))
        return plain

    @pl.when((i >= steps) & (i < steps + bin_steps))
    def _():
        group = i - steps
        spec = bins_in(held, group, table_down, width, False)
        grads = []
        sums = [0.0, 0.0]
        for k in range(GROUP):
            for side in range(2):
                at = (2 * k + side) * tall
                g = spec[k][side * tall : (side + 1) * tall] * factor
                g = g * damp[at : at + tall, :].astype(f32)
                sums[side] = sums[side] + jnp.sum(g, axis=0, keepdims=True)
                grads.append(g.astype(bf16))
        outer_bias_grad[...] += jnp.concatenate(sums, axis=0)
        low = weight_grads(outer_grad, active[...], grads)
        parts = complex_product(low, outer_t[0], outer_t[1], GROUP, tall, True)
        grads = []
        sums = [0.0, 0.0]
        for n, part in enumerate(parts):
            g = part * slope[n * tall : (n + 1) * tall, :].astype(f32)
            sums[n % 2] = sums[n % 2] + jnp.sum(g, axis=0, keepdims=True)
            grads.append(g.astype(bf16))
        inner_bias_grad[...] += jnp.concatenate(sums, axis=0)
        low = weight_grads(inner_grad, entries[...], grads)
        parts = complex_product(low, inner_t[0], inner_t[1], GROUP, tall, True)
        values = [
            jnp.concatenate([parts[2 * k], parts[2 * k + 1]], axis=0).astype(bf16)
            for k in range(GROUP)
        ]
        bins_out(held, group, table_up, width, values)

    @pl.when(i >= steps + bin_steps)
    def _():
        give_rows(i - steps - bin_steps, out, table_out, held, pairs, cols_here, factor)


def dense_kernel(
    meta, heights, widths,
    states, cot, spat, first_gain, first_shift, later_gain, later_shift,
    expand_bias, reduce_bias, expand_hbm, reduce_hbm,
    result, back, sums, expand_bias_grad, expand_grad_hbm, reduce_grad_hbm,
    expand, reduce, expand_grad, reduce_grad, mixed, normed, normal, low_out, branch, grad_n, copy_sem,
):
    frame = pl.program_id(0)
    hc = pl.program_id(1)
    last_hc = hc == pl.num_programs(1) - 1
    rows_here, cols_here, chans = states.shape[1:]
    groups, _, lanes = spat.shape
    width = lanes // PAIR
    pairs = rows_here // PAIR
    tokens = rows_here * cols_here
    chunk = tokens
    for size in (48, 32, 16):
        if tokens % size == 0:
            chunk = size
            break
    chunks = tokens // chunk
    slabs, _, slab = expand.shape

    @pl.when((frame == 0) & (hc == 0))
    def _():
        copies = [
            pltpu.make_async_copy(
                expand_hbm.at[:, pl.ds(s * slab, slab)], expand.at[s], copy_sem.at[s]
            )
            for s in range(slabs)
        ]
        copies.append(pltpu.make_async_copy(reduce_hbm, reduce, copy_sem.at[slabs]))
        for c in copies:
            c.start()
        expand_grad[...] = jnp.zeros_like(expand_grad)
        reduce_grad[...] = jnp.zeros_like(reduce_grad)
        sums[...] = jnp.zeros_like(sums)
        expand_bias_grad[...] = jnp.zeros_like(expand_bias_grad)
        for c in copies:
            c.wait()

    @pl.when(hc == 0)
    def _():
        for row in range(rows_here):
            mask = row_mask(meta, heights, widths, frame, row, cols_here)
            lower = mask * states[0, row].astype(f32)
            first, _ = standardize(lower)
            filter_in = first * first_gain[...] + first_shift[...]
            spatial = unpack_row(spat, row, cols_here, groups, width, pairs)
            at = slice(row * cols_here, (row + 1) * cols_here)
            mixed[at, :] = lower + mask * (spatial + filter_in)
            grad_n[at, :] = mask * cot[0, row].astype(f32)

        def token_chunk(n, carry):
            at = pl.ds(pl.multiple_of(n * chunk, chunk), chunk)
            later, _ = standardize(mixed[at, :])
            normal[at, :] = later
            normed[at, :] = (later * later_gain[...] + later_shift[...]).astype(bf16)
            go = grad_n[at, :]
            low_out[at, :] = go.astype(bf16)
            sums[0:1, :] += jnp.sum(go, axis=0, keepdims=True)
            return carry

        lax.fori_loop(0, chunks, token_chunk, 0)
        branch[...] = jnp.zeros_like(branch)
        grad_n[...] = jnp.zeros_like(grad_n)

    at = pl.ds(pl.multiple_of(hc * slab, slab), slab)
    weight_up = expand[hc]
    weight_down = reduce[at, :]
    x = normed[...]
    go = low_out[...]
    pre = dot(x, weight_up) + expand_bias[...]
    cdf, der = phi_parts(pre)
    hidden = (pre * cdf).astype(bf16)
    branch[...] += dot(hidden, weight_down)
    grad_pre = dot_nt(go, weight_down) * der
    expand_bias_grad[pl.ds(hc, 1), :] += jnp.sum(grad_pre, axis=0, keepdims=True)
    grad_low = grad_pre.astype(bf16)
    grad_n[...] += dot_nt(grad_low, weight_up)
    reduce_grad[at, :] += dot_tn(hidden, go)
    expand_grad[hc] += dot_tn(x, grad_low)

    @pl.when(last_hc)
    def _():
        def token_chunk(n, carry):
            at = pl.ds(pl.multiple_of(n * chunk, chunk), chunk)
            later, scale = standardize(mixed[at, :])
            g = grad_n[at, :]
            sums[1:2, :] += jnp.sum(g * later, axis=0, keepdims=True)
            sums[2:3, :] += jnp.sum(g, axis=0, keepdims=True)
            grad_n[at, :] = low_out[at, :].astype(f32) + standardize_back(
                g * later_gain[...], later, scale
            )
            return carry

        lax.fori_loop(0, chunks, token_chunk, 0)
        for j in range(pairs):
            sides = []
            for half in range(PAIR):
                row = half * pairs + j
                mask = row_mask(meta, heights, widths, frame, row, cols_here)
                at = slice(row * cols_here, (row + 1) * cols_here)
                out = mask * (mixed[at, :] + branch[at, :] + reduce_bias[...])
                result[0, row] = out.astype(bf16)
                sides.append(mask * grad_n[at, :])
            for c in range(groups):
                part = jnp.concatenate([s[:, c * width : (c + 1) * width] for s in sides], axis=1)
                back[c, j * cols_here : (j + 1) * cols_here, :] = part

    @pl.when(last_hc & (frame == pl.num_programs(0) - 1))
    def _():
        copies = [
            pltpu.make_async_copy(
                expand_grad.at[s], expand_grad_hbm.at[:, pl.ds(s * slab, slab)], copy_sem.at[s]
            )
            for s in range(slabs)
        ]
        copies.append(pltpu.make_async_copy(reduce_grad, reduce_grad_hbm, copy_sem.at[slabs]))
        for c in copies:
            c.start()
        for c in copies:
            c.wait()


def last_kernel(meta, heights, widths, states, back, spat, gain, out, sums):
    frame = pl.program_id(0)
    rows_here, cols_here, _ = states.shape[1:]
    groups, _, lanes = spat.shape
    width = lanes // PAIR
    pairs = rows_here // PAIR

    @pl.when(frame == 0)
    def _():
        sums[...] = jnp.zeros_like(sums)

    for row in range(rows_here):
        mask = row_mask(meta, heights, widths, frame, row, cols_here)
        normal, scale = standardize(mask * states[0, row].astype(f32))
        grad_mixed = unpack_row(back, row, cols_here, groups, width, pairs)
        spatial = unpack_row(spat, row, cols_here, groups, width, pairs)
        grad = mask * (grad_mixed + spatial)
        sums[0:1, :] += jnp.sum(grad * normal, axis=0, keepdims=True)
        sums[1:2, :] += jnp.sum(grad, axis=0, keepdims=True)
        grad = grad_mixed + standardize_back(grad * gain[...], normal, scale)
        out[0, row] = (mask * grad).astype(bf16)


def wide_tables(width):
    freq = np.arange(BINS)
    place = np.arange(width)
    angle = (freq[:, None] * place[None, :] % width) * (2.0 * math.pi / width)
    live = (2 * freq <= width).astype(np.float64)[:, None]
    edge = (freq == 0) | (2 * freq == width)
    weight = np.where(edge, 1.0, 2.0)[:, None] * live
    cosine, sine = np.cos(angle), np.sin(angle)
    plain = np.concatenate([live * cosine, -live * sine], axis=0)
    doubled = np.concatenate([weight * cosine, -weight * sine], axis=0)
    return plain, doubled


def tall_tables(height, rows_here):
    pairs = rows_here // PAIR
    order = np.array(
        [
            r * rows_here + h * pairs + j
            for h in range(PAIR)
            for r in range(height // rows_here)
            for j in range(pairs)
        ]
    )
    freq = np.arange(height)
    angle = (freq[:, None] * order[None, :] % height) * (2.0 * math.pi / height)
    cosine, sine = np.cos(angle), np.sin(angle)
    down = np.block([[cosine, sine], [-sine, cosine]])
    up = np.block([[cosine.T, -sine.T], [sine.T, cosine.T]])
    return down, up


def spread(weight):
    count = weight.shape[1]
    eye = jnp.eye(count, dtype=weight.dtype)
    full = jnp.einsum("rbio,bd->rbido", weight, eye)
    return full.reshape(2, count * BS, count * BS)


def gather_blocks(full):
    count = full.shape[1] // BS
    return jnp.stack(
        [full[:, b * BS : (b + 1) * BS, b * BS : (b + 1) * BS] for b in range(count)], axis=1
    )


def bias_rows(bias):
    return bias.reshape(2, -1)


def whole(shape):
    return pl.BlockSpec(shape, lambda *_: (0,) * len(shape))


def params(count):
    return pltpu.CompilerParams(
        dimension_semantics=("arbitrary",) * count, vmem_limit_bytes=VMEM
    )


def body(
    states,
    heights,
    widths,
    first_gain,
    first_shift,
    filter_inner,
    inner_bias,
    filter_outer,
    outer_bias,
    later_gain,
    later_shift,
    expand_weight,
    expand_bias,
    reduce_weight,
    reduce_bias,
    cotangent,
):
    frames, rows_here, cols_here, chans = states.shape
    ranks, groups = lax.axis_size("rows"), lax.axis_size("cols")
    assert frames == ranks and rows_here % PAIR == 0
    height, breadth = rows_here * ranks, cols_here * groups
    devices = ranks * groups
    pairs = rows_here // PAIR
    pixels = pairs * cols_here
    width = chans // groups
    lanes = width * PAIR
    tokens = rows_here * cols_here
    hidden = expand_weight.shape[1]
    factor = 1.0 / math.sqrt(height * breadth)

    meta = jnp.stack([lax.axis_index("rows") * rows_here, lax.axis_index("cols") * cols_here])
    meta = meta.astype(jnp.int32)
    row = lambda v: v.reshape(1, -1)

    tile = pl.BlockSpec((1, rows_here, cols_here, chans), lambda f, *_: (f, 0, 0, 0))
    packed = pl.BlockSpec((groups, pixels, lanes), lambda f, *_: (f, 0, 0))
    packed_shape = jax.ShapeDtypeStruct((devices, pixels, lanes), f32)
    chan_row = whole((1, chans))

    def exchange(v):
        return lax.all_to_all(v, ("rows", "cols"), 0, 0, tiled=True)

    sent = pl.pallas_call(
        first_kernel,
        grid_spec=pltpu.PrefetchScalarGridSpec(
            num_scalar_prefetch=3,
            grid=(frames,),
            in_specs=[tile, chan_row, chan_row],
            out_specs=packed,
        ),
        out_shape=packed_shape,
        compiler_params=params(1),
        name="first_norm",
    )(meta, heights, widths, states, row(first_gain), row(first_shift))

    plain, doubled = wide_tables(breadth)
    down, up = tall_tables(height, rows_here)
    as_table = lambda t: jnp.asarray(t, dtype=bf16)

    def fine_table(t):
        high = t.astype(jnp.bfloat16)
        return jnp.asarray(np.concatenate([high, (t - high.astype(np.float64)).astype(jnp.bfloat16)]))

    inner_full, outer_full = spread(filter_inner), spread(filter_outer)
    turn = lambda t: jnp.swapaxes(t, 1, 2)

    bin_steps = BINS // GROUP
    steps = ranks
    total = 2 * steps + bin_steps
    short = ranks * pairs
    group_rows = GROUP * 2 * height
    field_in = pl.BlockSpec((groups, pixels, lanes), lambda i: (jnp.minimum(i, steps - 1), 0, 0))
    field_out = pl.BlockSpec(
        (groups, pixels, lanes), lambda i: (jnp.maximum(i - steps - bin_steps, 0), 0, 0)
    )
    kept = pl.BlockSpec(
        (group_rows, width), lambda i: (jnp.clip(i - steps, 0, bin_steps - 1), 0)
    )
    kept_shape = jax.ShapeDtypeStruct((bin_steps * group_rows, width), bf16)
    def table_specs(parts):
        return [
            whole((parts * 2 * BINS, breadth)),
            whole((parts * 2 * height, 2 * height)),
            whole((2 * height, 2 * height)),
            whole((breadth, 2 * BINS)),
        ]

    mix_spec = whole((2, width, width))
    bias_spec = whole((2, width))
    scratch = [
        pltpu.VMEM((breadth, lanes), f32),
        pltpu.VMEM((short, 2 * BINS, lanes), f32),
    ]

    spatial, entries, active, slope, damp = pl.pallas_call(
        functools.partial(spectral_forward_kernel, steps, pairs, cols_here, factor),
        grid=(total,),
        in_specs=[field_in] + table_specs(2) + [mix_spec, bias_spec, mix_spec, bias_spec],
        out_specs=[field_out] + [kept] * 4,
        out_shape=[packed_shape] + [kept_shape] * 4,
        scratch_shapes=scratch,
        compiler_params=params(1),
        name="spectral_forward",
    )(
        exchange(sent),
        fine_table(plain),
        fine_table(down),
        as_table(up),
        as_table(doubled.T),
        inner_full,
        bias_rows(inner_bias),
        outer_full,
        bias_rows(outer_bias),
    )

    slabs = 6
    slab = hidden // slabs
    tile2 = pl.BlockSpec((1, rows_here, cols_here, chans), lambda f, h, *_: (f, 0, 0, 0))
    packed2 = pl.BlockSpec((groups, pixels, lanes), lambda f, h, *_: (f, 0, 0))
    anywhere = pl.BlockSpec(memory_space=pl.ANY)
    result, back, sums, expand_bias_grad, expand_grad, reduce_grad = pl.pallas_call(
        dense_kernel,
        grid_spec=pltpu.PrefetchScalarGridSpec(
            num_scalar_prefetch=3,
            grid=(frames, slabs),
            in_specs=[tile2, tile2, packed2]
            + [chan_row] * 4
            + [pl.BlockSpec((1, slab), lambda f, h, *_: (0, h)), chan_row, anywhere, anywhere],
            out_specs=[
                tile2,
                packed2,
                whole((8, chans)),
                whole((slabs, slab)),
                anywhere,
                anywhere,
            ],
            scratch_shapes=[
                pltpu.VMEM((slabs, chans, slab), bf16),
                pltpu.VMEM((hidden, chans), bf16),
                pltpu.VMEM((slabs, chans, slab), f32),
                pltpu.VMEM((hidden, chans), f32),
                pltpu.VMEM((tokens, chans), f32),
                pltpu.VMEM((tokens, chans), bf16),
                pltpu.VMEM((tokens, chans), f32),
                pltpu.VMEM((tokens, chans), bf16),
                pltpu.VMEM((tokens, chans), f32),
                pltpu.VMEM((tokens, chans), f32),
                pltpu.SemaphoreType.DMA((slabs + 1,)),
            ],
        ),
        out_shape=[
            jax.ShapeDtypeStruct(states.shape, bf16),
            packed_shape,
            jax.ShapeDtypeStruct((8, chans), f32),
            jax.ShapeDtypeStruct((slabs, slab), f32),
            jax.ShapeDtypeStruct((chans, hidden), f32),
            jax.ShapeDtypeStruct((hidden, chans), f32),
        ],
        compiler_params=params(2),
        name="dense_both_ways",
    )(
        meta,
        heights,
        widths,
        states,
        cotangent,
        exchange(spatial),
        row(first_gain),
        row(first_shift),
        row(later_gain),
        row(later_shift),
        row(expand_bias),
        row(reduce_bias),
        expand_weight,
        reduce_weight,
    )

    spatial_back, inner_grad, inner_bias_grad, outer_grad, outer_bias_grad = pl.pallas_call(
        functools.partial(spectral_backward_kernel, steps, pairs, cols_here, factor),
        grid=(total,),
        in_specs=[field_in] + table_specs(1) + [mix_spec, mix_spec] + [kept] * 4,
        out_specs=[field_out, mix_spec, bias_spec, mix_spec, bias_spec],
        out_shape=[
            packed_shape,
            jax.ShapeDtypeStruct((2, width, width), f32),
            jax.ShapeDtypeStruct((2, width), f32),
            jax.ShapeDtypeStruct((2, width, width), f32),
            jax.ShapeDtypeStruct((2, width), f32),
        ],
        scratch_shapes=scratch,
        compiler_params=params(1),
        name="spectral_backward",
    )(
        exchange(back),
        as_table(doubled),
        as_table(down),
        as_table(up),
        as_table(plain.T),
        turn(inner_full),
        turn(outer_full),
        entries,
        active,
        slope,
        damp,
    )

    states_grad, first_sums = pl.pallas_call(
        last_kernel,
        grid_spec=pltpu.PrefetchScalarGridSpec(
            num_scalar_prefetch=3,
            grid=(frames,),
            in_specs=[tile, packed, packed, chan_row],
            out_specs=[tile, whole((8, chans))],
        ),
        out_shape=[
            jax.ShapeDtypeStruct(states.shape, bf16),
            jax.ShapeDtypeStruct((8, chans), f32),
        ],
        compiler_params=params(1),
        name="first_norm_backward",
    )(meta, heights, widths, states, back, exchange(spatial_back), row(first_gain))

    inner_sum, inner_bias_sum, outer_sum, outer_bias_sum = lax.psum(
        (gather_blocks(inner_grad), inner_bias_grad, gather_blocks(outer_grad), outer_bias_grad),
        "rows",
    )
    expand_sum, reduce_sum = lax.psum((expand_grad, reduce_grad), ("rows", "cols"))
    small, first_small, expand_bias_sum = lax.psum(
        (sums, first_sums, expand_bias_grad), ("rows", "cols")
    )
    return (
        result,
        states_grad,
        first_small[0],
        first_small[1],
        inner_sum,
        inner_bias_sum.reshape(2, -1, BS),
        outer_sum,
        outer_bias_sum.reshape(2, -1, BS),
        small[1],
        small[2],
        expand_sum,
        expand_bias_sum.reshape(-1),
        reduce_sum,
        small[0],
    )


def solution(mesh):
    tile = P(None, "rows", "cols", None)
    mix = P(None, "cols", None, None)
    bias = P(None, "cols", None)
    in_specs = (
        tile, P(), P(), P(), P(), mix, bias, mix, bias, P(), P(), P(), P(), P(), P(), tile,
    )
    out_specs = (
        tile, tile, P(), P(), mix, bias, mix, bias, P(), P(), P(), P(), P(), P(),
    )
    return jax.shard_map(body, mesh=mesh, in_specs=in_specs, out_specs=out_specs, check_vma=False)
```

time: 4640 us -> 1900 us (0.41)
  local copies, waits for them, and re-layouts: 1190 us -> 57.5 us
  waiting for transfers between devices: 1600 us -> 679 us
  matrix products: 706 us -> 0 us
  other arithmetic: 437 us -> 2.34 us
  Pallas kernels: 0 us -> 407 us
  blocking collectives: 629 us -> 711 us
    all_to_all x6 -> x3, waiting for transfers between devices: 1600 us -> 563 us  [exchange(): return lax.all_to_all(v, ('rows', 'cols'), 0, 0, tiled=True)]
    dot_general x20 -> x0, matrix products: 706 us -> none  [the longest x4 178 us: tall_apply(): return jnp.einsum('gshr,fhbrc->fgbsc', table, values, precision=highest)]
    pallas_call x0 -> x5, Pallas kernels: none -> 407 us  [the longest x1 243 us: body(): pl.pallas_call(dense_kernel, grid_spec=pltpu.PrefetchScalarGridSpec(num_s...]
    psum x2, blocking collectives: 61.7 us -> 423 us  [the longest x1 380 us: body(): lax.psum((gather_blocks(inner_grad), inner_bias_grad, gather_blocks(outer...]
    unnamed x167 -> x42, local copies, waits for them, and re-layouts: 361 us -> 48.9 us
    all_to_all x18 -> x0, local copies, waits for them, and re-layouts: 292 us -> none  [the longest x7 136 us: to_spatial(): lax.all_to_all(plane, 'cols', split_axis=2, concat_axis=3, tiled=True)]
    all_to_all x2 -> x0, other arithmetic: 283 us -> none  [to_spectral(): lax.all_to_all(field, 'cols', split_axis=3, concat_axis=2, tiled=True)]
    all_to_all x2 -> x1, blocking collectives: 568 us -> 287 us  [exchange(): return lax.all_to_all(v, ('rows', 'cols'), 0, 0, tiled=True)]
  transfers between devices with their start and end apart: 8 -> 5, of which waited for: 6 -> 3; matrix products, arithmetic and copies ran while one was open for 7% -> 2% of each run, Pallas kernels for 0% -> 2%
where the time goes in v1:
time: 1900 us; the launch traced here: 1890 us
  blocking collectives  711 us (37%)
  waiting for transfers between devices  679 us (36%)
  Pallas kernels  407 us (21%)
  local copies, waits for them, and re-layouts  57.5 us (3%)
  starting transfers between devices  22 us (1%)
    all_to_all x3, waiting for transfers between devices, exchange(): return lax.all_to_all(v, ('rows', 'cols'), 0, 0, tiled=True)  563 us
    psum x1, blocking collectives, body(): lax.psum((gather_blocks(inner_grad), inner_bias_grad, gather_blocks(outer...  380 us
    all_to_all x1, blocking collectives, exchange(): return lax.all_to_all(v, ('rows', 'cols'), 0, 0, tiled=True)  287 us
    pallas_call x1, Pallas kernels, body(): pl.pallas_call(dense_kernel, grid_spec=pltpu.PrefetchScalarGridSpec(num_s...  243 us
    psum x1, waiting for transfers between devices, body(): lax.psum((expand_grad, reduce_grad), ('rows', 'cols'))  115 us
    pallas_call x1, Pallas kernels, body(): pl.pallas_call(functools.partial(spectral_backward_kernel, steps, pairs,...  59 us
    pallas_call x1, Pallas kernels, body(): pl.pallas_call(functools.partial(spectral_forward_kernel, steps, pairs, c...  58.4 us
    unnamed x42, local copies, waits for them, and re-layouts  48.9 us
  transfers between devices with their start and end apart: 5, of which 3 were waited for; matrix products, arithmetic and copies ran while one was open for 2% of the time, Pallas kernels for 2%

profile of v1, /device:TPU:15, one launch (start us, length us, event | category | flops | bytes accessed | tf_op | source)
XLA Modules:
  0.0 1893.1 jit_solution(12850098033157489775)
XLA Ops:
  7.2 1.3 reshape.70.gain.first_gain
  8.5 1.3 reshape.71.shift.first_shift
  9.7 7.1 copy.43.states
  16.8 0.6 pad_add_fusion.meta
  17.4 16.3 first_norm.1
  33.7 0.0 copy-start.4
  33.7 6.3 all-to-all-start
  40.0 0.7 reshape.73.inner_bias
  40.7 0.7 reshape.75.outer_bias
  41.4 0.1 copy.39
  41.5 0.1 copy.40
  41.6 0.4 multiply_bitcast_fusion
  42.0 0.1 reshape.74
  42.1 0.1 reshape.72
  42.3 0.8 copy.41.inner
  43.1 0.8 copy.42.outer
  43.9 283.5 %all-to-all-done.block = f32[32,264,384]{2,1,0:T(8,128)} async-done(((f32[32,264,384]{2,1,0:T(8,128)}), f32[32,264,384]{2,1,0:T(8,128)}, u32[]{:S(2)}, u32[]{:S(2)}) %all-to-all-start) | async-done | bytes 12976160 | tf_op jit(solution)/shard_map/all_to_all | solution.py:522
  327.5 58.4 %spectral_forward.1 = (f32[32,264,384]{2,1,0:T(8,128)}, bf16[18432,192]{1,0:T(8,128)(2,1)}, bf16[18432,192]{1,0:T(8,128)(2,1)}, bf16[18432,192]{1,0:T(8,128)(2,1)}, bf16[18432,192]{1,0:T(8,128)(2,1)}) custom-call(f32[32,264,384]{2,1,0:T(8,128)} %all-to-all-done.block, bf16[384,176]{1,0:T(8,128)(2,1)} %constant.27.clone.table_in, ...), custom_call_target="tpu_custom_call" | custom-call | tf_op jit(solution)/shard_map/spectral_forward/pallas_call | solution.py:576
  385.9 8.8 all-to-all-start.1
  394.7 0.6 reshape.76.later_gain
  395.3 0.6 reshape.77.later_shift
  395.9 0.6 reshape.79.reduce_bias
  396.5 7.2 copy.44.cot
  403.7 279.5 %all-to-all-done.1.spat = f32[32,264,384]{2,1,0:T(8,128)} async-done(((f32[32,264,384]{2,1,0:T(8,128)}), f32[32,264,384]{2,1,0:T(8,128)}, u32[]{:S(2)}, u32[]{:S(2)}) %all-to-all-start.1) | async-done | bytes 12976160 | tf_op jit(solution)/shard_map/all_to_all | solution.py:522
  683.1 243.2 %dense_both_ways.1 = (bf16[8,12,44,768]{3,2,1,0:T(8,128)(2,1)}, f32[32,264,384]{2,1,0:T(8,128)}, f32[8,768]{1,0:T(8,128)}, f32[6,512]{1,0:T(8,128)}, f32[768,3072]{1,0:T(8,128)}, /*index=5*/f32[3072,768]{1,0:T(8,128)}) custom-call(s32[2]{0:T(128)} %pad_add_fusion.meta, s32[8]{0:T(128)} %heights.5, s32[8]{0:T(128)} %widths.5, ...), custom_call_target="tpu_custom_call" | custom-call | tf_op jit(solution)/shard_map/dense_both_ways/pallas_call | solution.py:602
  926.3 287.4 %all_to_all.20.block = f32[32,264,384]{2,1,0:T(8,128)} all-to-all(f32[32,264,384]{2,1,0:T(8,128)} %get-tuple-element.34.back), channel_id=1, replica_groups=mesh['rows'=8,'cols'=4] {'rows','cols'}, dimensions={0} | all-to-all | bytes 25952256 | tf_op jit(solution)/shard_map/all_to_all | solution.py:522
  1213.7 59.0 %spectral_backward.1 = (f32[32,264,384]{2,1,0:T(8,128)}, f32[2,192,192]{2,1,0:T(8,128)}, f32[2,192]{1,0:T(2,128)}, f32[2,192,192]{2,1,0:T(8,128)}, f32[2,192]{1,0:T(2,128)}) custom-call(f32[32,264,384]{2,1,0:T(8,128)} %all_to_all.20.block, bf16[192,176]{1,0:T(8,128)(2,1)} %constant.31.clone.table_in, bf16[192,192]{1,0:T(8,128)(2,1)} %constant.32.clone.table_down, ...), custom_call_target="tpu_custom_call" | custom-call | tf_op jit(solution)/shard_map/spectral_backward/pallas_call | solution.py:659
  1272.8 6.8 all-to-all-start.3
  1279.5 0.0 all-reduce.9.cloned.1.call-start
  1279.6 0.1 slice_bitcast_fusion.1
  1279.7 0.7 pad_maximum_fusion.1
  1280.4 0.7 pad_maximum_fusion
  1281.1 0.0 all-reduce.9.cloned.1.call-update
  1281.1 0.0 all-reduce.7.cloned.1.call-start
  1281.2 0.7 all-reduce.7.cloned.1.call-update
  1281.9 9.4 copy.46
  1291.3 0.1 reshape.80
  1291.4 0.1 reshape.81
  1291.5 380.4 %all-reduce.2 = (f32[2,2,96]{2,1,0:T(2,128)}, f32[2,2,96]{2,1,0:T(2,128)}) all-reduce(f32[2,2,96]{2,1,0:T(2,128)S(1)} %reshape.80, f32[2,2,96]{2,1,0:T(2,128)S(1)} %reshape.81), channel_id=1, replica_groups=mesh['rows'=8,'cols'=4] {'rows'}, use_global_device_ids=true, to_apply=%region_2.0 | all-reduce | flops 768 | bytes 6144 | tf_op jit(solution)/shard_map/psum | solution.py:704
  1671.9 1.7 copy.48
  1673.6 1.6 copy.49
  1675.2 30.4 %first_norm_backward.1 = (bf16[8,12,44,768]{3,2,1,0:T(8,128)(2,1)}, f32[8,768]{1,0:T(8,128)}) custom-call(s32[2]{0:T(128)} %pad_add_fusion.meta, s32[8]{0:T(128)} %heights.5, s32[8]{0:T(128)} %widths.5, bf16[8,12,44,768]{3,2,1,0:T(8,128)(2,1)} %copy.43.states, f32[32,264,384]{2,1,0:T(8,128)} %get-tuple-element.34.back, f32[32,264,384]{2,1,0:T(8,128)} %all-to-all-done.3.spat, ...), custom_call_target="tpu_custom_call" | custom-call | tf_op jit(solution)/shard_map/first_norm_backward/pallas_call | solution.py:688
  1705.6 9.4 copy.47
  1715.0 43.1 %all-reduce = (f32[8,768]{1,0:T(8,128)S(1)}, f32[8,768]{1,0:T(8,128)S(1)}, f32[3072]{0:T(1024)}) all-reduce(f32[8,768]{1,0:T(8,128)S(1)} %copy-done.8, f32[8,768]{1,0:T(8,128)S(1)} %copy-done.7, f32[3072]{0:T(1024)S(1)} %reshape.82), channel_id=1, replica_groups=mesh['rows'=8,'cols'=4] {'rows','cols'}, use_global_device_ids=true, to_apply=%region_0.0 | all-reduce | flops 15360 | bytes 122880 | tf_op jit(solution)/shard_map/psum | solution.py:709
  1758.1 0.6 slice_reduce_fusion
  1758.7 115.0 %all-reduce.7.cloned.1.call-done = (f32[768,3072]{1,0:T(8,128)}, f32[3072,768]{1,0:T(8,128)}) async-done(((f32[768,3072]{1,0:T(8,128)}, f32[3072,768]{1,0:T(8,128)}), (f32[768,3072]{1,0:T(8,128)}, f32[3072,768]{1,0:T(8,128)})) %all-reduce.7.cloned.1.call-update) | async-done | bytes 18874384 | tf_op jit(solution)/shard_map/psum | solution.py:708
  1873.7 8.8 copy.54
  1882.5 3.7 copy.55
  (37 shorter events, 0.1 us)
Async XLA Ops:
  33.7 6.4 copy-start.13
  33.7 7.0 copy-start.14
  33.7 7.7 copy-start.3
  33.7 7.8 copy-start.4
  33.7 293.8 %all-to-all-start = ((f32[32,264,384]{2,1,0:T(8,128)}), f32[32,264,384]{2,1,0:T(8,128)}, u32[]{:S(2)}, u32[]{:S(2)}) async-start(f32[32,264,384]{2,1,0:T(8,128)} %first_norm.1), calls=%async_computation | async-start | bytes 25952256 | tf_op jit(solution)/shard_map/all_to_all | solution.py:522
  42.1 343.7 %copy-start.1 = (bf16[2,192,192]{1,2,0:T(8,128)(2,1)}, bf16[2,192,192]{1,2,0:T(8,128)(2,1)S(1)}, u32[]{:S(2)}) copy-start(bf16[2,192,192]{1,2,0:T(8,128)(2,1)S(1)} %reshape.74) | copy-start | bytes 442372
  42.3 343.6 %copy-start.2 = (bf16[2,192,192]{1,2,0:T(8,128)(2,1)}, bf16[2,192,192]{1,2,0:T(8,128)(2,1)S(1)}, u32[]{:S(2)}) copy-start(bf16[2,192,192]{1,2,0:T(8,128)(2,1)S(1)} %reshape.72) | copy-start | bytes 442372
  385.8 8.9 copy-start.10
  385.8 9.5 copy-start.11
  385.9 10.1 copy-start.12
  385.9 297.2 %all-to-all-start.1 = ((f32[32,264,384]{2,1,0:T(8,128)}), f32[32,264,384]{2,1,0:T(8,128)}, u32[]{:S(2)}, u32[]{:S(2)}) async-start(f32[32,264,384]{2,1,0:T(8,128)} %get-tuple-element.32), calls=%async_computation.1 | async-start | bytes 25952256 | tf_op jit(solution)/shard_map/all_to_all | solution.py:522
  1272.7 6.8 copy-start.5
  1272.7 6.8 copy-start.6
  1272.8 402.5 %all-to-all-start.3 = ((f32[32,264,384]{2,1,0:T(8,128)}), f32[32,264,384]{2,1,0:T(8,128)}, u32[]{:S(2)}, u32[]{:S(2)}) async-start(f32[32,264,384]{2,1,0:T(8,128)} %get-tuple-element.39), calls=%async_computation.3 | async-start | bytes 25952256 | tf_op jit(solution)/shard_map/all_to_all | solution.py:522
  1279.5 392.4 %all-reduce.9.cloned.1.call-start = ((), (), s32[]{:S(2)}) async-start(), calls=%async_computation.5 | async-start | bytes 786432 | tf_op jit(solution)/shard_map/psum | solution.py:704
  1281.1 592.6 %all-reduce.7.cloned.1.call-start = ((), (), s32[]{:S(2)}) async-start(), calls=%async_computation.4 | async-start | bytes 37748736 | tf_op jit(solution)/shard_map/psum | solution.py:708
  1281.9 9.4 copy-start.9
  1281.9 9.4 copy-start.16
  1281.9 9.5 copy-start.15
  1705.6 9.4 copy-start.7
  1705.6 9.4 copy-start.8
  1873.7 8.8 copy-start
Sparse Core Ops, SparseCore 0:
  1284.3 154.2 all-reduce.8
  1446.2 427.5 all-reduce.6

commit v2 on v0

v2 whole, which is shorter than its diff:
```python
import functools
import math

import jax
import jax.numpy as jnp
import numpy as np
from jax import lax
from jax.experimental import pallas as pl
from jax.experimental.pallas import tpu as pltpu
from jax.sharding import PartitionSpec as P

BS = 96
BINS = 96
PAIR = 2
GROUP = 8
PARTS = 3
norm_eps = 1e-06
shrink_width = 0.01
VMEM = 60 * 1024 * 1024
f32 = jnp.float32
bf16 = jnp.bfloat16


def phi_parts(v):
    cdf = 0.5 * (1.0 + lax.erf(v * math.sqrt(0.5)))
    slope = cdf + v * (jnp.exp(v * v * -0.5) * (1.0 / math.sqrt(2.0 * math.pi)))
    return cdf, slope


def dot(a, b):
    return lax.dot_general(a, b, (((1,), (0,)), ((), ())), preferred_element_type=f32)


def dot_tn(a, b):
    return lax.dot_general(a, b, (((0,), (0,)), ((), ())), preferred_element_type=f32)


def dot_nt(a, b):
    return lax.dot_general(a, b, (((1,), (1,)), ((), ())), preferred_element_type=f32)


def standardize(v):
    centre = jnp.mean(v, axis=-1, keepdims=True)
    centred = v - centre
    spread = jnp.mean(centred * centred, axis=-1, keepdims=True)
    scale = lax.rsqrt(spread + norm_eps)
    return centred * scale, scale


def standardize_back(grad, normal, scale):
    first = jnp.mean(grad, axis=-1, keepdims=True)
    second = jnp.mean(grad * normal, axis=-1, keepdims=True)
    return scale * (grad - first - normal * second)


def pack(sides, out, width):
    turned = [jnp.swapaxes(s, 0, 1) for s in sides]
    for c in range(out.shape[1]):
        out[:, c] = jnp.concatenate([t[:, :, c * width : (c + 1) * width] for t in turned], axis=2)


def unpack(ref, half, width):
    parts = [ref[:, c, :, half * width : (half + 1) * width] for c in range(ref.shape[1])]
    return jnp.swapaxes(jnp.concatenate(parts, axis=2) if len(parts) > 1 else parts[0], 0, 1)


def first_kernel(states, mask, gain, shift, out):
    width = out.shape[3] // PAIR
    sides = []
    for half in range(PAIR):
        inside = mask[half][..., :1]
        normal, _ = standardize(states[half].astype(f32) * inside)
        sides.append(inside * (normal * gain[...] + shift[...]))
    pack(sides, out, width)


def table_dot(table, x):
    rows = table.shape[0] // 2
    high = x.astype(bf16)
    both = dot(table[...], high)
    rest = dot(table[:rows, :], (x - high.astype(f32)).astype(bf16))
    return both[:rows] + both[rows:] + rest


def wide_in_kernel(cols_here, fine, block, table, held, wide):
    groups, rows = block.shape[1], block.shape[2] // cols_here
    for j in range(rows):
        for c in range(groups):
            wide[c * cols_here : (c + 1) * cols_here, :] = block[
                0, c, j * cols_here : (j + 1) * cols_here, :
            ]
        x = wide[...]
        y = table_dot(table, x) if fine else dot(table[...], x.astype(bf16))
        held[j, 0] = y[:BINS]
        held[j, 1] = y[BINS:]


def wide_out_kernel(cols_here, factor, held, table, block):
    groups, rows = block.shape[1], block.shape[2] // cols_here
    for j in range(rows):
        x = jnp.concatenate([held[j, 0], held[j, 1]], axis=0).astype(bf16)
        plane = dot(table[...], x) * factor
        for c in range(groups):
            block[0, c, j * cols_here : (j + 1) * cols_here, :] = plane[
                c * cols_here : (c + 1) * cols_here, :
            ]


def bins_in(held, table, width, fine):
    kind = f32 if fine else bf16
    turned = [
        [jnp.swapaxes(part[:, side], 0, 1).astype(kind) for part in held] for side in range(2)
    ]
    outs = []
    for k in range(GROUP):
        x = jnp.concatenate(
            [
                part[k][:, h * width : (h + 1) * width]
                for side in turned
                for h in range(PAIR)
                for part in side
            ],
            axis=0,
        )
        outs.append(table_dot(table, x) if fine else dot(table[...], x))
    return outs


def bins_out(held, table, width, values):
    short = held[0].shape[0]
    count = len(held)
    products = [dot(table[...], value) for value in values]
    for side in range(2):
        for q in range(count):
            rows = []
            for z in products:
                at = [((side * PAIR + h) * count + q) * short for h in range(PAIR)]
                rows.append(jnp.concatenate([z[a : a + short] for a in at], axis=1))
            held[q][:, side] = jnp.swapaxes(jnp.stack(rows, axis=0), 0, 1)


def halves(v, count, tall):
    return [
        (v[k * 2 * tall : k * 2 * tall + tall], v[k * 2 * tall + tall : (k + 1) * 2 * tall])
        for k in range(count)
    ]


def complex_product(x, first, second, count, tall, conj):
    a = dot(x, first)
    b = dot(x, second)
    parts = []
    for (a_re, a_im), (b_re, b_im) in zip(halves(a, count, tall), halves(b, count, tall)):
        if conj:
            parts += [a_re + b_im, a_im - b_re]
        else:
            parts += [a_re - b_im, a_im + b_re]
    return parts


def spectral_forward_kernel(factor, *refs):
    held, refs = refs[:PARTS], refs[PARTS:]
    table_down, table_up, inner, inner_bias, outer, outer_bias = refs[:6]
    given, (entries, active, slope, damp) = refs[6 : 6 + PARTS], refs[6 + PARTS :]
    width = inner.shape[2]
    tall = table_up.shape[0] // 2
    spec = bins_in(held, table_down, width, True)
    low = jnp.concatenate([(s * factor).astype(bf16) for s in spec], axis=0)
    entries[...] = low
    parts = complex_product(low, inner[0], inner[1], GROUP, tall, False)
    acts = []
    for n, part in enumerate(parts):
        v = part + inner_bias[n % 2 : n % 2 + 1, :]
        cdf, der = phi_parts(v)
        acts.append((v * cdf).astype(bf16))
        slope[n * tall : (n + 1) * tall, :] = der.astype(bf16)
    act = jnp.concatenate(acts, axis=0)
    active[...] = act
    parts = complex_product(act, outer[0], outer[1], GROUP, tall, False)
    shrunk = []
    for n, part in enumerate(parts):
        v = part + outer_bias[n % 2 : n % 2 + 1, :]
        t = jnp.tanh(v * (1.0 / shrink_width))
        shrunk.append((v - shrink_width * t).astype(bf16))
        damp[n * tall : (n + 1) * tall, :] = (t * t).astype(bf16)
    values = [jnp.concatenate(shrunk[2 * k : 2 * k + 2], axis=0) for k in range(GROUP)]
    bins_out(given, table_up, width, values)


def spectral_backward_kernel(factor, *refs):
    held, refs = refs[:PARTS], refs[PARTS:]
    table_down, table_up, inner_t, outer_t, entries, active, slope, damp = refs[:8]
    given, refs = refs[8 : 8 + PARTS], refs[8 + PARTS :]
    inner_grad, inner_bias_grad, outer_grad, outer_bias_grad = refs
    width = inner_t.shape[2]
    tall = table_up.shape[0] // 2

    @pl.when(pl.program_id(0) == 0)
    def _():
        for ref in (inner_grad, inner_bias_grad, outer_grad, outer_bias_grad):
            ref[...] = jnp.zeros_like(ref)

    def weight_grads(ref, before, grads):
        plain = jnp.concatenate(grads, axis=0)
        turned = []
        for k in range(GROUP):
            turned += [grads[2 * k + 1], -grads[2 * k]]
        ref[0] += dot_tn(before, plain)
        ref[1] += dot_tn(before, jnp.concatenate(turned, axis=0))
        return plain

    spec = bins_in(held, table_down, width, False)
    grads = []
    sums = [0.0, 0.0]
    for k in range(GROUP):
        for side in range(2):
            at = (2 * k + side) * tall
            g = spec[k][side * tall : (side + 1) * tall] * factor
            g = g * damp[at : at + tall, :].astype(f32)
            sums[side] = sums[side] + jnp.sum(g, axis=0, keepdims=True)
            grads.append(g.astype(bf16))
    outer_bias_grad[...] += jnp.concatenate(sums, axis=0)
    low = weight_grads(outer_grad, active[...], grads)
    parts = complex_product(low, outer_t[0], outer_t[1], GROUP, tall, True)
    grads = []
    sums = [0.0, 0.0]
    for n, part in enumerate(parts):
        g = part * slope[n * tall : (n + 1) * tall, :].astype(f32)
        sums[n % 2] = sums[n % 2] + jnp.sum(g, axis=0, keepdims=True)
        grads.append(g.astype(bf16))
    inner_bias_grad[...] += jnp.concatenate(sums, axis=0)
    low = weight_grads(inner_grad, entries[...], grads)
    parts = complex_product(low, inner_t[0], inner_t[1], GROUP, tall, True)
    values = [
        jnp.concatenate([parts[2 * k], parts[2 * k + 1]], axis=0).astype(bf16)
        for k in range(GROUP)
    ]
    bins_out(given, table_up, width, values)


def dense_kernel(steps, slabs, first_part, *refs):
    (
        states, cot, spat, mask, first_gain, first_shift, later_gain, later_shift,
        expand_bias, reduce_bias, expand_hbm, reduce_hbm,
    ) = refs[:12]
    refs = refs[12:]
    if not first_part:
        grads_before = refs[0]
        refs = refs[2:]
    result, back, sums, expand_bias_grad, grads_hbm = refs[:5]
    (
        expand, reduce, expand_grad, reduce_grad, mixed, normed, low_out, branch, grad_n,
        hidden_all, grad_all, copy_sem,
    ) = refs[5:]
    step = pl.program_id(0)
    chans = states.shape[3]
    width = spat.shape[3] // PAIR
    side_tokens = states.shape[1] * states.shape[2]
    slab = expand.shape[2]
    tokens = mixed.shape[0]
    square = states.shape[1:]

    def parts_of(grads):
        pairs = [(grads.at[pl.ds(s * chans, chans)], expand_grad.at[s]) for s in range(slabs)]
        return pairs + [(grads.at[pl.ds(slabs * chans, slabs * slab)], reduce_grad)]

    def fetches():
        copies = [
            pltpu.make_async_copy(
                expand_hbm.at[:, pl.ds(s * slab, slab)], expand.at[s], copy_sem.at[s]
            )
            for s in range(slabs)
        ]
        copies.append(pltpu.make_async_copy(reduce_hbm, reduce, copy_sem.at[slabs]))
        if not first_part:
            copies += [
                pltpu.make_async_copy(far, near, copy_sem.at[slabs + 1 + n])
                for n, (far, near) in enumerate(parts_of(grads_before))
            ]
        return copies

    @pl.when(step == 0)
    def _():
        for c in fetches():
            c.start()
        if first_part:
            expand_grad[...] = jnp.zeros_like(expand_grad)
            reduce_grad[...] = jnp.zeros_like(reduce_grad)
        sums[...] = jnp.zeros_like(sums)
        expand_bias_grad[...] = jnp.zeros_like(expand_bias_grad)

    @pl.when(step < steps)
    def _():
        start = pl.multiple_of(step * (PAIR * side_tokens), PAIR * side_tokens)
        for half in range(PAIR):
            at = pl.ds(start + half * side_tokens, side_tokens)
            inside = mask[half][..., :1]
            lower = inside * states[half].astype(f32)
            first, _ = standardize(lower)
            filter_in = first * first_gain[...] + first_shift[...]
            full = lower + inside * (unpack(spat, half, width) + filter_in)
            later, _ = standardize(full)
            full = full.reshape(side_tokens, chans)
            mixed[at, :] = full
            branch[at, :] = full + reduce_bias[...]
            normal = (later * later_gain[...] + later_shift[...]).reshape(side_tokens, chans)
            normed[at, :] = normal.astype(bf16)
            go = (inside * cot[half].astype(f32)).reshape(side_tokens, chans)
            low_out[at, :] = go.astype(bf16)
            grad_n[at, :] = jnp.zeros_like(full)
            sums[0:1, :] += jnp.sum(go, axis=0, keepdims=True)

    @pl.when(step == steps)
    def _():
        for c in fetches():
            c.wait()

    @pl.when((step >= steps) & (step < steps + slabs))
    def _():
        hc = step - steps
        at = pl.ds(pl.multiple_of(hc * slab, slab), slab)
        piece = tokens // 4 if tokens % 64 == 0 else tokens

        def some(n, carry):
            here = pl.ds(pl.multiple_of(n * piece, piece), piece)
            weight_up = expand[hc]
            weight_down = reduce[at, :]
            go = low_out[here, :]
            pre = dot(normed[here, :], weight_up) + expand_bias[...]
            cdf, der = phi_parts(pre)
            hidden = (pre * cdf).astype(bf16)
            hidden_all[here, :] = hidden
            branch[here, :] += dot(hidden, weight_down)
            grad_pre = dot_nt(go, weight_down) * der
            expand_bias_grad[pl.ds(hc, 1), :] += jnp.sum(grad_pre, axis=0, keepdims=True)
            grad_low = grad_pre.astype(bf16)
            grad_all[here, :] = grad_low
            grad_n[here, :] += dot_nt(grad_low, weight_up)
            return carry

        lax.fori_loop(0, tokens // piece, some, 0)
        reduce_grad[at, :] += dot_tn(hidden_all[...], low_out[...])
        expand_grad[hc] += dot_tn(normed[...], grad_all[...])

    @pl.when(step >= steps + slabs)
    def _():
        start = pl.multiple_of(
            (step - steps - slabs) * (PAIR * side_tokens), PAIR * side_tokens
        )
        sides = []
        for half in range(PAIR):
            at = pl.ds(start + half * side_tokens, side_tokens)
            inside = mask[half][..., :1]
            later, scale = standardize(mixed[at, :])
            g = grad_n[at, :]
            sums[1:2, :] += jnp.sum(g * later, axis=0, keepdims=True)
            sums[2:3, :] += jnp.sum(g, axis=0, keepdims=True)
            g = low_out[at, :].astype(f32) + standardize_back(g * later_gain[...], later, scale)
            sides.append(inside * g.reshape(square))
            result[half] = (inside * branch[at, :].reshape(square)).astype(bf16)
        pack(sides, back, width)

    @pl.when(step == pl.num_programs(0) - 1)
    def _():
        copies = [
            pltpu.make_async_copy(near, far, copy_sem.at[n])
            for n, (far, near) in enumerate(parts_of(grads_hbm))
        ]
        for c in copies:
            c.start()
        for c in copies:
            c.wait()


def last_kernel(states, back, spat, mask, gain, *refs):
    out, sums = refs[-2:]
    width = spat.shape[3] // PAIR
    chans = states.shape[3]

    @pl.when(pl.program_id(0) == 0)
    def _():
        sums[...] = jnp.zeros_like(sums)

    for half in range(PAIR):
        inside = mask[half][..., :1]
        normal, scale = standardize(inside * states[half].astype(f32))
        grad_mixed = unpack(back, half, width)
        grad = inside * (grad_mixed + unpack(spat, half, width))
        flat = (-1, chans)
        sums[0:1, :] += jnp.sum((grad * normal).reshape(flat), axis=0, keepdims=True)
        sums[1:2, :] += jnp.sum(grad.reshape(flat), axis=0, keepdims=True)
        grad = grad_mixed + standardize_back(grad * gain[...], normal, scale)
        out[half] = (inside * grad).astype(bf16)


def wide_tables(width):
    freq = np.arange(BINS)
    place = np.arange(width)
    angle = (freq[:, None] * place[None, :] % width) * (2.0 * math.pi / width)
    live = (2 * freq <= width).astype(np.float64)[:, None]
    edge = (freq == 0) | (2 * freq == width)
    weight = np.where(edge, 1.0, 2.0)[:, None] * live
    cosine, sine = np.cos(angle), np.sin(angle)
    plain = np.concatenate([live * cosine, -live * sine], axis=0)
    doubled = np.concatenate([weight * cosine, -weight * sine], axis=0)
    return plain, doubled


def tall_tables(height, rows_here):
    pairs = rows_here // PAIR
    rows = pairs // PARTS
    order = np.array(
        [
            r * rows_here + h * pairs + q * rows + j
            for h in range(PAIR)
            for q in range(PARTS)
            for r in range(height // rows_here)
            for j in range(rows)
        ]
    )
    freq = np.arange(height)
    angle = (freq[:, None] * order[None, :] % height) * (2.0 * math.pi / height)
    cosine, sine = np.cos(angle), np.sin(angle)
    down = np.block([[cosine, sine], [-sine, cosine]])
    up = np.block([[cosine.T, -sine.T], [sine.T, cosine.T]])
    return down, up


def spread(weight):
    count = weight.shape[1]
    eye = jnp.eye(count, dtype=weight.dtype)
    full = jnp.einsum("rbio,bd->rbido", weight, eye)
    return full.reshape(2, count * BS, count * BS)


def gather_blocks(full):
    count = full.shape[1] // BS
    return jnp.stack(
        [full[:, b * BS : (b + 1) * BS, b * BS : (b + 1) * BS] for b in range(count)], axis=1
    )


def bias_rows(bias):
    return bias.reshape(2, -1)


def whole(shape):
    return pl.BlockSpec(shape, lambda *_: (0,) * len(shape))


def call(kernel, grid, in_specs, out_specs, out_shape, name, flops=0, nbytes=0, scratch=(), **kw):
    return pl.pallas_call(
        kernel,
        grid=(grid,),
        in_specs=in_specs,
        out_specs=out_specs,
        out_shape=out_shape,
        scratch_shapes=scratch,
        compiler_params=pltpu.CompilerParams(
            dimension_semantics=("arbitrary",), vmem_limit_bytes=VMEM
        ),
        cost_estimate=pl.CostEstimate(flops=flops, bytes_accessed=nbytes, transcendentals=0),
        name=name,
        **kw,
    )


def body(
    states,
    heights,
    widths,
    first_gain,
    first_shift,
    filter_inner,
    inner_bias,
    filter_outer,
    outer_bias,
    later_gain,
    later_shift,
    expand_weight,
    expand_bias,
    reduce_weight,
    reduce_bias,
    cotangent,
):
    frames, rows_here, cols_here, chans = states.shape
    ranks, groups = lax.axis_size("rows"), lax.axis_size("cols")
    assert frames == ranks and rows_here % (PAIR * PARTS) == 0
    height, breadth = rows_here * ranks, cols_here * groups
    devices = ranks * groups
    pairs = rows_here // PAIR
    rows = pairs // PARTS
    pixels = rows * cols_here
    width = chans // groups
    lanes = width * PAIR
    hidden = expand_weight.shape[1]
    factor = 1.0 / math.sqrt(height * breadth)
    short = ranks * rows
    step_pixels = 8 if pixels % 8 == 0 else pixels
    steps = pixels // step_pixels
    tokens = PAIR * pixels * frames
    message = devices * pixels * lanes * 4
    row = lambda v: v.reshape(1, -1)
    shape = jax.ShapeDtypeStruct

    order = lambda v: jnp.transpose(v, (1, 2, 0, 3)).reshape(PAIR, pairs * cols_here, frames, chans)
    restore = lambda v: jnp.transpose(v.reshape(rows_here, cols_here, frames, chans), (2, 0, 1, 3))
    states_in, cot_in = order(states), order(cotangent)
    row_ids = lax.axis_index("rows") * rows_here + jnp.arange(rows_here, dtype=jnp.int32)
    col_ids = lax.axis_index("cols") * cols_here + jnp.arange(cols_here, dtype=jnp.int32)
    inside = (row_ids[:, None, None] < heights) & (col_ids[None, :, None] < widths)
    mask = jnp.broadcast_to(
        inside.astype(f32).reshape(PAIR, pairs * cols_here, frames, 1),
        (PAIR, pairs * cols_here, frames, 128),
    )

    buffers = {} if steps > 1 else {"pipeline_mode": pl.Buffered(1)}

    def token_spec(q, where, last=chans):
        return pl.BlockSpec(
            (PAIR, step_pixels, frames, last), lambda i: (0, q * steps + where(i), 0, 0), **buffers
        )

    def packed_spec(where):
        return pl.BlockSpec(
            (ranks, groups, step_pixels, lanes), lambda i: (0, 0, where(i), 0), **buffers
        )

    same = lambda i: i
    token_shape = shape((PAIR, pairs * cols_here, frames, chans), bf16)
    packed_shape = shape((ranks, groups, pixels, lanes), f32)
    chan_row = whole((1, chans))
    anywhere = pl.BlockSpec(memory_space=pl.ANY)

    def scatter(v, axis):
        return lax.psum_scatter(v, axis, scatter_dimension=0, tiled=True)

    def gather(v, axis):
        return lax.all_gather(v, axis, axis=0, tiled=True)

    def sum_small(v, *after):
        v = jnp.broadcast_to(behind(v, *after), (devices,) + v.shape)
        return jnp.sum(lax.all_to_all(v, ("rows", "cols"), 0, 0, tiled=True), axis=0)

    def behind(v, *after):
        return lax.optimization_barrier((v,) + after)[0] if after else v

    def exchange(v, *after):
        v = v.reshape(devices, pixels, lanes)
        v = behind(v, *after)
        v = lax.all_to_all(v, ("rows", "cols"), 0, 0, tiled=True)
        return v.reshape(ranks, groups, pixels, lanes)

    def first_norm(q):
        return call(
            first_kernel,
            steps,
            [token_spec(q, same), token_spec(q, same, 128), chan_row, chan_row],
            packed_spec(same),
            packed_shape,
            "first_norm",
            nbytes=2 * message,
        )(states_in, mask, row(first_gain), row(first_shift))

    plain, doubled = wide_tables(breadth)
    down, up = tall_tables(height, rows_here)
    as_table = lambda t: jnp.asarray(t, dtype=bf16)

    def fine_table(t):
        high = t.astype(jnp.bfloat16)
        return jnp.asarray(np.concatenate([high, (t - high.astype(np.float64)).astype(jnp.bfloat16)]))

    inner_full, outer_full = spread(filter_inner), spread(filter_outer)
    turn = lambda t: jnp.swapaxes(t, 1, 2)
    bin_steps = BINS // GROUP
    group_rows = GROUP * 2 * height
    held_shape = shape((short, 2, BINS, lanes), f32)
    held_row = pl.BlockSpec((rows, 2, BINS, lanes), lambda i: (i, 0, 0, 0))
    held_bins = pl.BlockSpec((short, 2, GROUP, lanes), lambda i: (0, 0, i, 0))
    field = pl.BlockSpec((1, groups, pixels, lanes), lambda i: (i, 0, 0, 0))
    kept = pl.BlockSpec((group_rows, width), lambda i: (i, 0))
    kept_shape = shape((bin_steps * group_rows, width), bf16)
    mix_spec = whole((2, width, width))
    bias_spec = whole((2, width))
    up_spec = whole((2 * height, 2 * height))

    def wide_in(v, table, fine):
        return call(
            functools.partial(wide_in_kernel, cols_here, fine),
            ranks,
            [field, whole(table.shape)],
            held_row,
            held_shape,
            "wide_in",
            nbytes=2 * message,
            scratch=[pltpu.VMEM((breadth, lanes), f32)],
        )(v, table)

    def wide_out(v, table):
        return call(
            functools.partial(wide_out_kernel, cols_here, factor),
            ranks,
            [held_row, whole(table.shape)],
            field,
            packed_shape,
            "wide_out",
            nbytes=2 * message,
        )(v, table)

    def spectral_forward(held):
        table = fine_table(down)
        outs = call(
            functools.partial(spectral_forward_kernel, factor),
            bin_steps,
            [held_bins] * PARTS
            + [whole(table.shape), up_spec, mix_spec, bias_spec, mix_spec, bias_spec],
            [held_bins] * PARTS + [kept] * 4,
            [held_shape] * PARTS + [kept_shape] * 4,
            "spectral_forward",
            flops=20 * 10**9,
            nbytes=8 * PARTS * message,
        )(
            *held,
            table,
            as_table(up),
            inner_full,
            bias_rows(inner_bias),
            outer_full,
            bias_rows(outer_bias),
        )
        return outs[:PARTS], outs[PARTS:]

    def spectral_backward(held, saved):
        outs = call(
            functools.partial(spectral_backward_kernel, factor),
            bin_steps,
            [held_bins] * PARTS + [up_spec, up_spec, mix_spec, mix_spec] + [kept] * 4,
            [held_bins] * PARTS + [mix_spec, bias_spec, mix_spec, bias_spec],
            [held_shape] * PARTS + [shape((2, width, width), f32), shape((2, width), f32)] * 2,
            "spectral_backward",
            flops=20 * 10**9,
            nbytes=8 * PARTS * message,
        )(*held, as_table(down), as_table(up), turn(inner_full), turn(outer_full), *saved)
        return outs[:PARTS], outs[PARTS:]

    slab = chans
    slabs = hidden // slab
    dense_steps = 2 * steps + slabs
    enter = lambda i: jnp.minimum(i, steps - 1)
    leave = lambda i: jnp.maximum(i - steps - slabs, 0)
    either = lambda i: jnp.where(i < steps + slabs, enter(i), leave(i))

    def dense(q, spatial, before):
        grads_before = () if q == 0 else before
        return call(
            functools.partial(dense_kernel, steps, slabs, q == 0),
            dense_steps,
            [token_spec(q, enter), token_spec(q, enter), packed_spec(enter)]
            + [token_spec(q, either, 128)]
            + [chan_row] * 4
            + [pl.BlockSpec((1, slab), lambda i: (0, jnp.clip(i - steps, 0, slabs - 1)))]
            + [chan_row]
            + [anywhere] * (2 + len(grads_before)),
            [
                token_spec(q, leave),
                packed_spec(leave),
                whole((8, chans)),
                whole((slabs, slab)),
                anywhere,
            ],
            [
                token_shape,
                packed_shape,
                shape((8, chans), f32),
                shape((slabs, slab), f32),
                shape((2 * hidden, chans), f32),
            ],
            "dense_both_ways",
            flops=12 * tokens * chans * hidden,
            nbytes=4 * message,
            scratch=[
                pltpu.VMEM((slabs, chans, slab), bf16),
                pltpu.VMEM((hidden, chans), bf16),
                pltpu.VMEM((slabs, chans, slab), f32),
                pltpu.VMEM((hidden, chans), f32),
                pltpu.VMEM((tokens, chans), f32),
                pltpu.VMEM((tokens, chans), bf16),
                pltpu.VMEM((tokens, chans), bf16),
                pltpu.VMEM((tokens, chans), f32),
                pltpu.VMEM((tokens, chans), f32),
                pltpu.VMEM((tokens, slab), bf16),
                pltpu.VMEM((tokens, slab), bf16),
                pltpu.SemaphoreType.DMA((2 * slabs + 2,)),
            ],
            input_output_aliases={} if q == 0 else {13: 0},
        )(
            states_in,
            cot_in,
            spatial,
            mask,
            row(first_gain),
            row(first_shift),
            row(later_gain),
            row(later_shift),
            row(expand_bias),
            row(reduce_bias),
            expand_weight,
            reduce_weight,
            *grads_before,
        )

    def last_norm(q, back, spatial, before):
        given = () if q == 0 else (before,)
        return call(
            last_kernel,
            steps,
            [token_spec(q, same), packed_spec(same), packed_spec(same), token_spec(q, same, 128)]
            + [chan_row]
            + [anywhere] * len(given),
            [token_spec(q, same), whole((8, chans))],
            [token_shape, shape((8, chans), f32)],
            "first_norm_backward",
            nbytes=4 * message,
            input_output_aliases={} if q == 0 else {5: 0},
        )(states_in, back, spatial, mask, row(first_gain), *given)

    def scatter(v, axis):
        return lax.psum_scatter(v, axis, scatter_dimension=0, tiled=True)

    def gather(v, axis):
        return lax.all_gather(v, axis, axis=0, tiled=True)

    def sum_small(v, *after):
        v = jnp.broadcast_to(behind(v, *after), (devices,) + v.shape)
        return jnp.sum(lax.all_to_all(v, ("rows", "cols"), 0, 0, tiled=True), axis=0)

    every = range(PARTS)
    got = []
    for q in every:
        got.append(exchange(first_norm(q), *got[-1:]))
    held = [wide_in(v, fine_table(plain), True) for v in got]
    given, saved = spectral_forward(held)

    made = [wide_out(v, as_table(doubled.T)) for v in given]
    spatial, backs, sums, expand_bias_grad, before = [], [], 0.0, 0.0, ()
    for q in range(PARTS + 1):
        if q < PARTS:
            spatial.append(exchange(made[q], *spatial[-1:], *backs[-1:]))
        if q > 0:
            result, back, part, bias_part, grads = dense(q - 1, spatial[q - 1], before)
            before = (grads, result)
            backs.append(back)
            sums, expand_bias_grad = sums + part, expand_bias_grad + bias_part
    got, held = spatial[-1:], []
    for q in every:
        got.append(exchange(backs[q], got[-1], backs[min(q + 1, PARTS - 1)], *held[-1:]))
        if q == 0:
            grads = scatter(behind(grads, got[-1]), "cols")
        else:
            held.append(wide_in(got[q], as_table(doubled), False))
    rows_of_sums = jnp.concatenate([sums[:3], expand_bias_grad.reshape(-1, chans)])
    rows_of_sums = jnp.pad(rows_of_sums, ((0, -rows_of_sums.shape[0] % 8), (0, 0)))
    dense_small = sum_small(rows_of_sums, got[-1], held[-1])
    held.append(wide_in(got[-1], as_table(doubled), False))
    grads = scatter(behind(grads, held[-1]), "rows")

    given, filter_grads = spectral_backward(held, saved)
    inner_grad, inner_bias_grad, outer_grad, outer_bias_grad = filter_grads
    filter_parts = (
        gather_blocks(inner_grad), inner_bias_grad, gather_blocks(outer_grad), outer_bias_grad
    )
    flat = jnp.concatenate([v.reshape(-1) for v in filter_parts])
    flat = lax.psum(jnp.pad(flat, (0, -flat.shape[0] % 1024)).reshape(-1, 128), "rows").reshape(-1)
    grads = gather(behind(grads, given[-1]), ("cols", "rows"))
    expand_sum = jnp.swapaxes(grads[:hidden].reshape(slabs, chans, slab), 0, 1)
    expand_sum = expand_sum.reshape(chans, hidden)
    reduce_sum = grads[hidden:]
    made = [wide_out(v, as_table(plain.T)) for v in given]
    got, first_sums, states_grad = [dense_small], [], None
    for q in range(PARTS + 1):
        if q < PARTS:
            got.append(exchange(made[q], got[-1], *first_sums[-1:]))
        if q > 0:
            states_grad, part = last_norm(q - 1, backs[q - 1], got[q], states_grad)
            first_sums.append(part)
    first_small = sum_small(sum(first_sums), got[-1])
    sizes = [v.size for v in filter_parts]
    ends = np.cumsum(sizes)
    filter_sums = [
        flat[e - n : e].reshape(v.shape) for e, n, v in zip(ends, sizes, filter_parts)
    ]
    inner_sum, inner_bias_sum, outer_sum, outer_bias_sum = filter_sums
    bias_rows_count = hidden // chans
    return (
        restore(result),
        restore(states_grad),
        first_small[0],
        first_small[1],
        inner_sum,
        inner_bias_sum.reshape(2, -1, BS),
        outer_sum,
        outer_bias_sum.reshape(2, -1, BS),
        dense_small[1],
        dense_small[2],
        expand_sum,
        dense_small[3 : 3 + bias_rows_count].reshape(-1),
        reduce_sum,
        dense_small[0],
    )


def solution(mesh):
    tile = P(None, "rows", "cols", None)
    mix = P(None, "cols", None, None)
    bias = P(None, "cols", None)
    in_specs = (
        tile, P(), P(), P(), P(), mix, bias, mix, bias, P(), P(), P(), P(), P(), P(), tile,
    )
    out_specs = (
        tile, tile, P(), P(), mix, bias, mix, bias, P(), P(), P(), P(), P(), P(),
    )
    return jax.shard_map(body, mesh=mesh, in_specs=in_specs, out_specs=out_specs, check_vma=False)
```

time: 4640 us -> 1600 us (0.34)
  local copies, waits for them, and re-layouts: 1190 us -> 37.6 us
  waiting for transfers between devices: 1600 us -> 850 us
  matrix products: 706 us -> 0 us
  blocking collectives: 629 us -> 102 us
  Pallas kernels: 0 us -> 490 us
  other arithmetic: 437 us -> 3.59 us
    all_to_all x6 -> x13, waiting for transfers between devices: 1600 us -> 810 us  [the longest x11 784 us: exchange(): v = lax.all_to_all(v, ('rows', 'cols'), 0, 0, tiled=True)]
    dot_general x20 -> x0, matrix products: 706 us -> none  [the longest x4 178 us: tall_apply(): return jnp.einsum('gshr,fhbrc->fgbsc', table, values, precision=highest)]
    pallas_call x0 -> x23, Pallas kernels: none -> 490 us  [the longest x3 244 us: dense(): call(functools.partial(dense_kernel, steps, slabs, q == 0), dense_steps,...]
    all_to_all x2 -> x1, blocking collectives: 568 us -> 102 us  [exchange(): v = lax.all_to_all(v, ('rows', 'cols'), 0, 0, tiled=True)]
    unnamed x167 -> x34, local copies, waits for them, and re-layouts: 361 us -> 0.07 us
    all_to_all x18 -> x0, local copies, waits for them, and re-layouts: 292 us -> none  [the longest x7 136 us: to_spatial(): lax.all_to_all(plane, 'cols', split_axis=2, concat_axis=3, tiled=True)]
    all_to_all x2 -> x0, other arithmetic: 283 us -> none  [to_spectral(): lax.all_to_all(field, 'cols', split_axis=3, concat_axis=2, tiled=True)]
    transpose x8 -> x0, local copies, waits for them, and re-layouts: 194 us -> none  [the longest x3 80.6 us: tall_apply(): return jnp.einsum('gshr,fhbrc->fgbsc', table, values, precision=highest)]
  transfers between devices with their start and end apart: 8 -> 17, of which waited for: 6 -> 14; matrix products, arithmetic and copies ran while one was open for 7% -> 1% of each run, Pallas kernels for 0% -> 27%
where the time goes in v2:
time: 1600 us; the launch traced here: 1590 us
  waiting for transfers between devices  850 us (53%)
  Pallas kernels  490 us (31%)
  blocking collectives  102 us (6%)
  starting transfers between devices  88.5 us (6%)
  local copies, waits for them, and re-layouts  37.6 us (2%)
    all_to_all x11, waiting for transfers between devices, exchange(): v = lax.all_to_all(v, ('rows', 'cols'), 0, 0, tiled=True)  784 us
    pallas_call x3, Pallas kernels, dense(): call(functools.partial(dense_kernel, steps, slabs, q == 0), dense_steps,...  244 us
    all_to_all x1, blocking collectives, exchange(): v = lax.all_to_all(v, ('rows', 'cols'), 0, 0, tiled=True)  102 us
    all_to_all x11, starting transfers between devices, exchange(): v = lax.all_to_all(v, ('rows', 'cols'), 0, 0, tiled=True)  76.6 us
    pallas_call x6, Pallas kernels, wide_in(): call(functools.partial(wide_in_kernel, cols_here, fine), ranks, [field, w...  48.6 us
    pallas_call x6, Pallas kernels, wide_out(): call(functools.partial(wide_out_kernel, cols_here, factor), ranks, [held_...  45.5 us
    pallas_call x1, Pallas kernels, spectral_backward(): call(functools.partial(spectral_backward_kernel, factor), bin_steps, [hel...  44.7 us
    pallas_call x1, Pallas kernels, spectral_forward(): call(functools.partial(spectral_forward_kernel, factor), bin_steps, [held...  40.1 us
  transfers between devices with their start and end apart: 17, of which 14 were waited for; matrix products, arithmetic and copies ran while one was open for 1% of the time, Pallas kernels for 27%

profile of v2, /device:TPU:15, one launch (start us, length us, event | category | flops | bytes accessed | tf_op | source)
XLA Modules:
  0.0 1586.5 jit_solution(17483894856391816939)
XLA Ops:
  13.6 10.0 first_norm.3
  29.9 10.0 first_norm.4
  39.9 85.6 %all-to-all-done = f32[32,88,384]{2,1,0:T(8,128)} async-done(((f32[32,88,384]{2,1,0:T(8,128)}), f32[32,88,384]{2,1,0:T(8,128)}, u32[]{:S(2)}, u32[]{:S(2)}) %all-to-all-start) | async-done | bytes 4325408 | tf_op jit(solution)/shard_map/all_to_all | solution.py:551
  125.5 6.9 all-to-all-start.1
  132.4 10.0 first_norm.5
  142.5 85.5 %all-to-all-done.1 = f32[32,88,384]{2,1,0:T(8,128)} async-done(((f32[32,88,384]{2,1,0:T(8,128)}), f32[32,88,384]{2,1,0:T(8,128)}, u32[]{:S(2)}, u32[]{:S(2)}) %all-to-all-start.1) | async-done | bytes 4325408 | tf_op jit(solution)/shard_map/all_to_all | solution.py:551
  228.0 6.9 all-to-all-start.2
  238.8 8.3 wide_in.6.refs_0_
  247.1 8.3 wide_in.7.refs_1_
  255.5 75.0 %all-to-all-done.2 = f32[32,88,384]{2,1,0:T(8,128)} async-done(((f32[32,88,384]{2,1,0:T(8,128)}), f32[32,88,384]{2,1,0:T(8,128)}, u32[]{:S(2)}, u32[]{:S(2)}) %all-to-all-start.2) | async-done | bytes 4325408 | tf_op jit(solution)/shard_map/all_to_all | solution.py:551
  330.5 8.3 wide_in.8.refs_2_
  338.8 40.1 %spectral_forward.1 = (f32[16,2,96,384]{3,2,1,0:T(8,128)}, f32[16,2,96,384]{3,2,1,0:T(8,128)}, f32[16,2,96,384]{3,2,1,0:T(8,128)}, bf16[18432,192]{1,0:T(8,128)(...) custom-call(f32[16,2,96,384]{3,2,1,0:T(8,128)} %wide_in.6.refs_0_, ...), custom_call_target="tpu_custom_call" | custom-call | flops 20000000000 | bytes 103809024 | tf_op jit(solution)/shard_map/spectral_forward/pallas_call | solution.py:612
  378.9 7.6 wide_out.8
  386.5 6.9 all-to-all-start.3
  393.4 7.6 wide_out.7
  401.0 88.0 %all-to-all-done.3 = f32[32,88,384]{2,1,0:T(8,128)} async-done(((f32[32,88,384]{2,1,0:T(8,128)}), f32[32,88,384]{2,1,0:T(8,128)}, u32[]{:S(2)}, u32[]{:S(2)}) %all-to-all-start.3) | async-done | bytes 4325408 | tf_op jit(solution)/shard_map/all_to_all | solution.py:551
  489.0 7.2 all-to-all-start.4
  498.0 7.6 wide_out.6
  505.6 77.6 %dense_both_ways.3 = (bf16[2,264,8,768]{3,2,1,0:T(8,128)(2,1)}, f32[8,4,88,384]{3,2,1,0:T(8,128)}, f32[8,768]{1,0:T(8,128)}, f32[4,768]{1,0:T(4,128)}, f32[6144,768]{1,0:T(8,128)}) custom-call(bf16[2,264,8,768]{3,2,1,0:T(8,128)(2,1)} %bitcast.73, bf16[2,264,8,768]{3,2,1,0:T(8,128)(2,1)} %bitcast.99, f32[8,4,88,384]{3,2,1,0:T(8,128)} %bitcast.18.refs_2_, ...), custom_call_target="tpu_custom_call" | custom-call | flops 39862665216 | bytes 17301504 | tf_op jit(solution)/shard_map/dense_both_ways/pallas_call | solution.py:655
  583.1 8.6 all-to-all-done.4
  591.7 7.3 all-to-all-start.5
  599.0 83.5 %dense_both_ways.4 = (bf16[2,264,8,768]{3,2,1,0:T(8,128)(2,1)}, f32[8,4,88,384]{3,2,1,0:T(8,128)}, f32[8,768]{1,0:T(8,128)}, f32[4,768]{1,0:T(4,128)}, f32[6144,768]{1,0:T(8,128)}) custom-call(bf16[2,264,8,768]{3,2,1,0:T(8,128)(2,1)} %bitcast.74, bf16[2,264,8,768]{3,2,1,0:T(8,128)(2,1)} %bitcast.100, ...), custom_call_target="tpu_custom_call", output_to_operand_aliasing={{0}: (13, {})} | custom-call | flops 39862665216 | bytes 17301504 | tf_op jit(solution)/shard_map/dense_both_ways/pallas_call | solution.py:655
  682.5 12.0 all-to-all-done.5
  694.5 6.9 all-to-all-start.6
  701.4 83.3 %dense_both_ways.5 = (bf16[2,264,8,768]{3,2,1,0:T(8,128)(2,1)}, f32[8,4,88,384]{3,2,1,0:T(8,128)}, f32[8,768]{1,0:T(8,128)}, f32[4,768]{1,0:T(4,128)}, f32[6144,768]{1,0:T(8,128)}) custom-call(bf16[2,264,8,768]{3,2,1,0:T(8,128)(2,1)} %bitcast.75, bf16[2,264,8,768]{3,2,1,0:T(8,128)(2,1)} %bitcast.101, ...), custom_call_target="tpu_custom_call", output_to_operand_aliasing={{0}: (13, {})} | custom-call | flops 39862665216 | bytes 17301504 | tf_op jit(solution)/shard_map/dense_both_ways/pallas_call | solution.py:655
  784.8 12.2 all-to-all-done.6
  797.0 6.9 all-to-all-start.7
  804.0 8.2 wide_in.9.refs_0_
  812.2 87.4 %all-to-all-done.7 = f32[32,88,384]{2,1,0:T(8,128)} async-done(((f32[32,88,384]{2,1,0:T(8,128)}), f32[32,88,384]{2,1,0:T(8,128)}, u32[]{:S(2)}, u32[]{:S(2)}) %all-to-all-start.7) | async-done | bytes 4325408 | tf_op jit(solution)/shard_map/all_to_all | solution.py:551
  899.5 102.1 %all_to_all.70 = f32[32,88,384]{2,1,0:T(8,128)} all-to-all(f32[32,88,384]{2,1,0:T(8,128)} %bitcast.87), channel_id=1, replica_groups=mesh['rows'=8,'cols'=4] {'rows','cols'}, dimensions={0} | all-to-all | bytes 8650752 | tf_op jit(solution)/shard_map/all_to_all | solution.py:551
  1001.6 7.7 wide_in.11.refs_2_
  1009.4 7.7 wide_in.10.refs_1_
  1017.1 44.7 %spectral_backward.1 = (f32[16,2,96,384]{3,2,1,0:T(8,128)}, f32[16,2,96,384]{3,2,1,0:T(8,128)}, f32[16,2,96,384]{3,2,1,0:T(8,128)}, f32[2,192,192]{2,1,0:T(8,128...) custom-call(f32[16,2,96,384]{3,2,1,0:T(8,128)} %wide_in.9.refs_0_, ...), custom_call_target="tpu_custom_call" | custom-call | flops 20000000000 | bytes 103809024 | tf_op jit(solution)/shard_map/spectral_backward/pallas_call | solution.py:634
  1065.8 39.6 %reduce-scatter.5.cloned.1.call-done = f32[192,768]{1,0:T(8,128)} async-done(((f32[1536,768]{1,0:T(8,128)}), f32[192,768]{1,0:T(8,128)}) %reduce-scatter.5.cloned.1.call-update) | async-done | bytes 589840 | tf_op jit(solution)/shard_map/reduce_scatter | solution.py:728
  1111.4 7.6 wide_out.11
  1119.0 14.1 all-to-all-done.9
  1139.3 7.6 wide_out.10
  1146.8 116.7 %all-to-all-done.10 = f32[32,88,384]{2,1,0:T(8,128)} async-done(((f32[32,88,384]{2,1,0:T(8,128)}), f32[32,88,384]{2,1,0:T(8,128)}, u32[]{:S(2)}, u32[]{:S(2)}) %all-to-all-start.10) | async-done | bytes 4325408 | tf_op jit(solution)/shard_map/all_to_all | solution.py:551
  1263.5 8.3 all-to-all-start.11
  1271.8 7.6 wide_out.9
  1279.4 12.3 first_norm_backward.3
  1291.7 129.7 %all-to-all-done.11 = f32[32,88,384]{2,1,0:T(8,128)} async-done(((f32[32,88,384]{2,1,0:T(8,128)}), f32[32,88,384]{2,1,0:T(8,128)}, u32[]{:S(2)}, u32[]{:S(2)}) %all-to-all-start.11) | async-done | bytes 4325408 | tf_op jit(solution)/shard_map/all_to_all | solution.py:551
  1421.4 6.9 all-to-all-start.12
  1428.3 12.4 first_norm_backward.4
  1440.7 83.2 %all-to-all-done.12 = f32[32,88,384]{2,1,0:T(8,128)} async-done(((f32[32,88,384]{2,1,0:T(8,128)}), f32[32,88,384]{2,1,0:T(8,128)}, u32[]{:S(2)}, u32[]{:S(2)}) %all-to-all-start.12) | async-done | bytes 4325408 | tf_op jit(solution)/shard_map/all_to_all | solution.py:551
  1523.9 12.3 first_norm_backward.5
  1550.6 12.1 all-to-all-done.13
  1563.4 11.0 fusion.1
  (101 shorter events, 54.8 us)
Async XLA Ops:
  23.6 101.9 %all-to-all-start = ((f32[32,88,384]{2,1,0:T(8,128)}), f32[32,88,384]{2,1,0:T(8,128)}, u32[]{:S(2)}, u32[]{:S(2)}) async-start(f32[32,88,384]{2,1,0:T(8,128)} %bitcast.84), calls=%async_computation | async-start | bytes 8650752 | tf_op jit(solution)/shard_map/all_to_all | solution.py:551
  125.5 102.5 %all-to-all-start.1 = ((f32[32,88,384]{2,1,0:T(8,128)}), f32[32,88,384]{2,1,0:T(8,128)}, u32[]{:S(2)}, u32[]{:S(2)}) async-start(f32[32,88,384]{2,1,0:T(8,128)} %bitcast.83), calls=%async_computation.1 | async-start | bytes 8650752 | tf_op jit(solution)/shard_map/all_to_all | solution.py:551
  142.4 92.5 %copy-start.15 = (f32[2,2,96]{2,1,0:T(2,128)S(1)}, f32[2,2,96]{2,1,0:T(2,128)}, u32[]{:S(2)}) copy-start(f32[2,2,96]{2,1,0:T(2,128)} %param.38) | copy-start | bytes 4612
  142.4 93.1 %copy-start.16 = (f32[2,2,96]{2,1,0:T(2,128)S(1)}, f32[2,2,96]{2,1,0:T(2,128)}, u32[]{:S(2)}) copy-start(f32[2,2,96]{2,1,0:T(2,128)} %param.40) | copy-start | bytes 4612
  142.4 93.8 %copy-start.2 = (bf16[2,2,96,96]{3,2,1,0:T(8,128)(2,1)S(1)}, bf16[2,2,96,96]{3,2,1,0:T(8,128)(2,1)}, u32[]{:S(2)}) copy-start(bf16[2,2,96,96]{3,2,1,0:T(8,128)(2,1)} %param.37) | copy-start | bytes 221188
  142.4 93.9 %copy-start.3 = (bf16[2,2,96,96]{3,2,1,0:T(8,128)(2,1)S(1)}, bf16[2,2,96,96]{3,2,1,0:T(8,128)(2,1)}, u32[]{:S(2)}) copy-start(bf16[2,2,96,96]{3,2,1,0:T(8,128)(2,1)} %param.39) | copy-start | bytes 221188
  228.0 102.5 %all-to-all-start.2 = ((f32[32,88,384]{2,1,0:T(8,128)}), f32[32,88,384]{2,1,0:T(8,128)}, u32[]{:S(2)}, u32[]{:S(2)}) async-start(f32[32,88,384]{2,1,0:T(8,128)} %bitcast.82), calls=%async_computation.2 | async-start | bytes 8650752 | tf_op jit(solution)/shard_map/all_to_all | solution.py:551
  237.0 10.1 copy-start
  237.1 10.0 copy-start.1
  386.5 102.5 %all-to-all-start.3 = ((f32[32,88,384]{2,1,0:T(8,128)}), f32[32,88,384]{2,1,0:T(8,128)}, u32[]{:S(2)}, u32[]{:S(2)}) async-start(f32[32,88,384]{2,1,0:T(8,128)} %bitcast.93), calls=%async_computation.3 | async-start | bytes 8650752 | tf_op jit(solution)/shard_map/all_to_all | solution.py:551
  401.0 95.2 %copy-start.12 = (f32[768]{0:T(1024)S(1)}, f32[768]{0:T(1024)}, u32[]{:S(2)}) copy-start(f32[768]{0:T(1024)} %param.41) | copy-start | bytes 9220
  401.0 95.8 %copy-start.13 = (f32[768]{0:T(1024)S(1)}, f32[768]{0:T(1024)}, u32[]{:S(2)}) copy-start(f32[768]{0:T(1024)} %param.42) | copy-start | bytes 9220
  401.0 96.4 %copy-start.14 = (f32[768]{0:T(1024)S(1)}, f32[768]{0:T(1024)}, u32[]{:S(2)}) copy-start(f32[768]{0:T(1024)} %param.46) | copy-start | bytes 9220
  489.0 102.7 %all-to-all-start.4 = ((f32[32,88,384]{2,1,0:T(8,128)}), f32[32,88,384]{2,1,0:T(8,128)}, u32[]{:S(2)}, u32[]{:S(2)}) async-start(f32[32,88,384]{2,1,0:T(8,128)} %bitcast.89), calls=%async_computation.4 | async-start | bytes 8650752 | tf_op jit(solution)/shard_map/all_to_all | solution.py:551
  591.7 102.8 %all-to-all-start.5 = ((f32[32,88,384]{2,1,0:T(8,128)}), f32[32,88,384]{2,1,0:T(8,128)}, u32[]{:S(2)}, u32[]{:S(2)}) async-start(f32[32,88,384]{2,1,0:T(8,128)} %bitcast.88), calls=%async_computation.5 | async-start | bytes 8650752 | tf_op jit(solution)/shard_map/all_to_all | solution.py:551
  694.5 102.5 %all-to-all-start.6 = ((f32[32,88,384]{2,1,0:T(8,128)}), f32[32,88,384]{2,1,0:T(8,128)}, u32[]{:S(2)}, u32[]{:S(2)}) async-start(f32[32,88,384]{2,1,0:T(8,128)} %bitcast.81), calls=%async_computation.6 | async-start | bytes 8650752 | tf_op jit(solution)/shard_map/all_to_all | solution.py:551
  701.4 307.9 %reduce-scatter.3.cloned.1.call-start = ((), (), s32[]{:S(2)}) async-start(), calls=%async_computation.17 | async-start | bytes 23592960 | tf_op jit(solution)/shard_map/reduce_scatter | solution.py:728
  797.0 102.5 %all-to-all-start.7 = ((f32[32,88,384]{2,1,0:T(8,128)}), f32[32,88,384]{2,1,0:T(8,128)}, u32[]{:S(2)}, u32[]{:S(2)}) async-start(f32[32,88,384]{2,1,0:T(8,128)} %bitcast.86), calls=%async_computation.7 | async-start | bytes 8650752 | tf_op jit(solution)/shard_map/all_to_all | solution.py:551
  803.9 301.4 %reduce-scatter.5.cloned.1.call-start = ((), (), s32[]{:S(2)}) async-start(), calls=%async_computation.18 | async-start | bytes 5308416 | tf_op jit(solution)/shard_map/reduce_scatter | solution.py:728
  1009.3 535.5 %all-reduce.4.cloned.1.call-start = ((), (), s32[]{:S(2)}) async-start(), calls=%async_computation.16 | async-start | bytes 598016 | tf_op jit(solution)/shard_map/psum | solution.py:773
  1017.1 88.3 %copy-start.6 = (f32[4,768]{1,0:T(4,128)S(1)}, f32[4,768]{1,0:T(4,128)}, u32[]{:S(2)}) copy-start(f32[4,768]{1,0:T(4,128)} %get-tuple-element.92) | copy-start | bytes 36868
  1017.1 88.3 %copy-start.7 = (f32[4,768]{1,0:T(4,128)S(1)}, f32[4,768]{1,0:T(4,128)}, u32[]{:S(2)}) copy-start(f32[4,768]{1,0:T(4,128)} %get-tuple-element.93) | copy-start | bytes 36868
  1017.1 88.3 %copy-start.8 = (f32[4,768]{1,0:T(4,128)S(1)}, f32[4,768]{1,0:T(4,128)}, u32[]{:S(2)}) copy-start(f32[4,768]{1,0:T(4,128)} %get-tuple-element.94) | copy-start | bytes 36868
  1017.1 88.4 %copy-start.9 = (f32[8,768]{1,0:T(8,128)S(1)}, f32[8,768]{1,0:T(8,128)}, u32[]{:S(2)}) copy-start(f32[8,768]{1,0:T(8,128)} %get-tuple-element.89) | copy-start | bytes 73732
  1017.1 88.4 %copy-start.10 = (f32[8,768]{1,0:T(8,128)S(1)}, f32[8,768]{1,0:T(8,128)}, u32[]{:S(2)}) copy-start(f32[8,768]{1,0:T(8,128)} %get-tuple-element.90) | copy-start | bytes 73732
  1017.1 88.4 %copy-start.11 = (f32[8,768]{1,0:T(8,128)S(1)}, f32[8,768]{1,0:T(8,128)}, u32[]{:S(2)}) copy-start(f32[8,768]{1,0:T(8,128)} %get-tuple-element.91) | copy-start | bytes 73732
  1065.7 497.7 %all-gather.2.cloned.1.call-start = ((), (), s32[]{:S(2)}) async-start(), calls=%async_computation.19 | async-start | bytes 19464192 | tf_op jit(solution)/shard_map/all_gather | solution.py:731
  1106.4 26.6 %all-to-all-start.9 = ((f32[32,8,768]{2,1,0:T(8,128)}), f32[32,8,768]{2,1,0:T(8,128)S(1)}, u32[]{:S(2)}, u32[]{:S(2)}) async-start(f32[32,8,768]{2,1,0:T(8,128)} %broadcast_in_dim.7), calls=%async_computation.9 | async-start | bytes 1572864 | tf_op jit(solution)/shard_map/all_to_all | solution.py:735
  1133.1 130.4 %all-to-all-start.10 = ((f32[32,88,384]{2,1,0:T(8,128)}), f32[32,88,384]{2,1,0:T(8,128)}, u32[]{:S(2)}, u32[]{:S(2)}) async-start(f32[32,88,384]{2,1,0:T(8,128)} %bitcast.92), calls=%async_computation.10 | async-start | bytes 8650752 | tf_op jit(solution)/shard_map/all_to_all | solution.py:551
  1263.5 157.9 %all-to-all-start.11 = ((f32[32,88,384]{2,1,0:T(8,128)}), f32[32,88,384]{2,1,0:T(8,128)}, u32[]{:S(2)}, u32[]{:S(2)}) async-start(f32[32,88,384]{2,1,0:T(8,128)} %bitcast.91), calls=%async_computation.11 | async-start | bytes 8650752 | tf_op jit(solution)/shard_map/all_to_all | solution.py:551
  1421.4 102.5 %all-to-all-start.12 = ((f32[32,88,384]{2,1,0:T(8,128)}), f32[32,88,384]{2,1,0:T(8,128)}, u32[]{:S(2)}, u32[]{:S(2)}) async-start(f32[32,88,384]{2,1,0:T(8,128)} %bitcast.90), calls=%async_computation.12 | async-start | bytes 8650752 | tf_op jit(solution)/shard_map/all_to_all | solution.py:551
  1523.9 12.3 copy-start.4
  1523.9 12.3 copy-start.5
  1537.9 24.8 %all-to-all-start.13 = ((f32[32,8,768]{2,1,0:T(8,128)}), f32[32,8,768]{2,1,0:T(8,128)S(1)}, u32[]{:S(2)}, u32[]{:S(2)}) async-start(f32[32,8,768]{2,1,0:T(8,128)} %broadcast_in_dim.8), calls=%async_computation.13 | async-start | bytes 1572864 | tf_op jit(solution)/shard_map/all_to_all | solution.py:735
Sparse Core Ops, SparseCore 0:
  797.1 208.2 reduce-scatter.2
  1009.5 95.7 reduce-scatter.4
  1109.1 94.8 all-reduce.3
  1206.8 197.7 all-gather.1

commit v3 on v2

--- a/solution.py
+++ b/solution.py
@@ -247,11 +247,11 @@
     if not first_part:
         grads_before = refs[0]
         refs = refs[2:]
-    result, back, sums, expand_bias_grad, grads_hbm = refs[:5]
+    result, back, later_grad, sums, expand_bias_grad, grads_hbm = refs[:6]
     (
         expand, reduce, expand_grad, reduce_grad, mixed, normed, low_out, branch, grad_n,
         hidden_all, grad_all, copy_sem,
-    ) = refs[5:]
+    ) = refs[6:]
     step = pl.program_id(0)
     chans = states.shape[3]
     width = spat.shape[3] // PAIR
@@ -357,6 +357,7 @@
             sums[2:3, :] += jnp.sum(g, axis=0, keepdims=True)
             g = low_out[at, :].astype(f32) + standardize_back(g * later_gain[...], later, scale)
             sides.append(inside * g.reshape(square))
+            later_grad[half] = sides[-1]
             result[half] = (inside * branch[at, :].reshape(square)).astype(bf16)
         pack(sides, back, width)
 
@@ -372,7 +373,7 @@
             c.wait()
 
 
-def last_kernel(states, back, spat, mask, gain, *refs):
+def last_kernel(states, later_grad, spat, mask, gain, *refs):
     out, sums = refs[-2:]
     width = spat.shape[3] // PAIR
     chans = states.shape[3]
@@ -384,13 +385,73 @@
     for half in range(PAIR):
         inside = mask[half][..., :1]
         normal, scale = standardize(inside * states[half].astype(f32))
-        grad_mixed = unpack(back, half, width)
+        grad_mixed = later_grad[half]
         grad = inside * (grad_mixed + unpack(spat, half, width))
         flat = (-1, chans)
         sums[0:1, :] += jnp.sum((grad * normal).reshape(flat), axis=0, keepdims=True)
         sums[1:2, :] += jnp.sum(grad.reshape(flat), axis=0, keepdims=True)
         grad = grad_mixed + standardize_back(grad * gain[...], normal, scale)
         out[half] = (inside * grad).astype(bf16)
+
+
+def sum_kernel(ranks, groups, own, out, got, send_sem, recv_sem):
+    devices = ranks * groups
+    me = lax.axis_index("rows") * groups + lax.axis_index("cols")
+
+    def place(i):
+        other = lax.rem(me + i, devices)
+        return lax.div(other, groups), lax.rem(other, groups)
+
+    def copy(i):
+        return pltpu.make_async_remote_copy(
+            src_ref=own,
+            dst_ref=got.at[i],
+            send_sem=send_sem.at[i],
+            recv_sem=recv_sem.at[i],
+            device_id=place(i),
+            device_id_type=pl.DeviceIdType.MESH,
+        )
+
+    barrier = pltpu.get_barrier_semaphore()
+
+    def greet(i, carry):
+        pl.semaphore_signal(
+            barrier, inc=1, device_id=place(i), device_id_type=pl.DeviceIdType.MESH
+        )
+        return carry
+
+    def start(i, carry):
+        copy(i).start()
+        return carry
+
+    def finish(i, carry):
+        copy(i).wait()
+        return carry
+
+    lax.fori_loop(1, devices, greet, 0)
+    pl.semaphore_wait(barrier, devices - 1)
+    lax.fori_loop(1, devices, start, 0)
+    lax.fori_loop(1, devices, finish, 0)
+    out[...] = lax.fori_loop(1, devices, lambda i, total: total + got[i], own[...])
+
+
+def split_kernel(slabs, grads, expand, reduce, copy_sem):
+    chans = reduce.shape[1]
+    copies = [
+        pltpu.make_async_copy(
+            grads.at[pl.ds(s * chans, chans)], expand.at[:, pl.ds(s * chans, chans)], copy_sem.at[s]
+        )
+        for s in range(slabs)
+    ]
+    copies.append(
+        pltpu.make_async_copy(
+            grads.at[pl.ds(slabs * chans, slabs * chans)], reduce, copy_sem.at[slabs]
+        )
+    )
+    for c in copies:
+        c.start()
+    for c in copies:
+        c.wait()
 
 
 def wide_tables(width):
@@ -538,9 +599,33 @@
     def gather(v, axis):
         return lax.all_gather(v, axis, axis=0, tiled=True)
 
-    def sum_small(v, *after):
-        v = jnp.broadcast_to(behind(v, *after), (devices,) + v.shape)
-        return jnp.sum(lax.all_to_all(v, ("rows", "cols"), 0, 0, tiled=True), axis=0)
+    def sum_small(v):
+        flat = v.reshape(-1, 128)
+        flat = jnp.pad(flat, ((0, -flat.shape[0] % 8), (0, 0)))
+        vmem = pl.BlockSpec(memory_space=pltpu.VMEM)
+        return pl.pallas_call(
+            functools.partial(sum_kernel, ranks, groups),
+            in_specs=[vmem],
+            out_specs=vmem,
+            out_shape=shape(flat.shape, f32),
+            scratch_shapes=[
+                pltpu.VMEM((devices,) + flat.shape, f32),
+                pltpu.SemaphoreType.DMA((devices,)),
+                pltpu.SemaphoreType.DMA((devices,)),
+            ],
+            compiler_params=pltpu.CompilerParams(collective_id=0, has_side_effects=True),
+            name="small_sums",
+        )(flat).reshape(-1)[: v.size].reshape(v.shape)
+
+    def split_grads(v):
+        return pl.pallas_call(
+            functools.partial(split_kernel, slabs),
+            in_specs=[anywhere],
+            out_specs=[anywhere, anywhere],
+            out_shape=[shape((chans, hidden), f32), shape((hidden, chans), f32)],
+            scratch_shapes=[pltpu.SemaphoreType.DMA((slabs + 1,))],
+            name="split_gradients",
+        )(v)
 
     def behind(v, *after):
         return lax.optimization_barrier((v,) + after)[0] if after else v
@@ -664,6 +749,7 @@
             [
                 token_spec(q, leave),
                 packed_spec(leave),
+                token_spec(0, leave),
                 whole((8, chans)),
                 whole((slabs, slab)),
                 anywhere,
@@ -671,6 +757,7 @@
             [
                 token_shape,
                 packed_shape,
+                shape((PAIR, pixels, frames, chans), f32),
                 shape((8, chans), f32),
                 shape((slabs, slab), f32),
                 shape((2 * hidden, chans), f32),
@@ -709,12 +796,12 @@
             *grads_before,
         )
 
-    def last_norm(q, back, spatial, before):
+    def last_norm(q, later_grad, spatial, before):
         given = () if q == 0 else (before,)
         return call(
             last_kernel,
             steps,
-            [token_spec(q, same), packed_spec(same), packed_spec(same), token_spec(q, same, 128)]
+            [token_spec(q, same), token_spec(0, same), packed_spec(same), token_spec(q, same, 128)]
             + [chan_row]
             + [anywhere] * len(given),
             [token_spec(q, same), whole((8, chans))],
@@ -722,17 +809,7 @@
             "first_norm_backward",
             nbytes=4 * message,
             input_output_aliases={} if q == 0 else {5: 0},
-        )(states_in, back, spatial, mask, row(first_gain), *given)
-
-    def scatter(v, axis):
-        return lax.psum_scatter(v, axis, scatter_dimension=0, tiled=True)
-
-    def gather(v, axis):
-        return lax.all_gather(v, axis, axis=0, tiled=True)
-
-    def sum_small(v, *after):
-        v = jnp.broadcast_to(behind(v, *after), (devices,) + v.shape)
-        return jnp.sum(lax.all_to_all(v, ("rows", "cols"), 0, 0, tiled=True), axis=0)
+        )(states_in, later_grad, spatial, mask, row(first_gain), *given)
 
     every = range(PARTS)
     got = []
@@ -742,14 +819,15 @@
     given, saved = spectral_forward(held)
 
     made = [wide_out(v, as_table(doubled.T)) for v in given]
-    spatial, backs, sums, expand_bias_grad, before = [], [], 0.0, 0.0, ()
+    spatial, backs, later_grads, sums, expand_bias_grad, before = [], [], [], 0.0, 0.0, ()
     for q in range(PARTS + 1):
         if q < PARTS:
             spatial.append(exchange(made[q], *spatial[-1:], *backs[-1:]))
         if q > 0:
-            result, back, part, bias_part, grads = dense(q - 1, spatial[q - 1], before)
+            result, back, kept_grad, part, bias_part, grads = dense(q - 1, spatial[q - 1], before)
             before = (grads, result)
             backs.append(back)
+            later_grads.append(kept_grad)
             sums, expand_bias_grad = sums + part, expand_bias_grad + bias_part
     got, held = spatial[-1:], []
     for q in every:
@@ -758,10 +836,7 @@
             grads = scatter(behind(grads, got[-1]), "cols")
         else:
             held.append(wide_in(got[q], as_table(doubled), False))
-    rows_of_sums = jnp.concatenate([sums[:3], expand_bias_grad.reshape(-1, chans)])
-    rows_of_sums = jnp.pad(rows_of_sums, ((0, -rows_of_sums.shape[0] % 8), (0, 0)))
-    dense_small = sum_small(rows_of_sums, got[-1], held[-1])
-    held.append(wide_in(got[-1], as_table(doubled), False))
+    held.append(wide_in(behind(got[-1], held[-1]), as_table(doubled), False))
     grads = scatter(behind(grads, held[-1]), "rows")
 
     given, filter_grads = spectral_backward(held, saved)
@@ -771,41 +846,43 @@
     )
     flat = jnp.concatenate([v.reshape(-1) for v in filter_parts])
     flat = lax.psum(jnp.pad(flat, (0, -flat.shape[0] % 1024)).reshape(-1, 128), "rows").reshape(-1)
-    grads = gather(behind(grads, given[-1]), ("cols", "rows"))
-    expand_sum = jnp.swapaxes(grads[:hidden].reshape(slabs, chans, slab), 0, 1)
-    expand_sum = expand_sum.reshape(chans, hidden)
-    reduce_sum = grads[hidden:]
     made = [wide_out(v, as_table(plain.T)) for v in given]
-    got, first_sums, states_grad = [dense_small], [], None
+    got, first_sums, states_grad = [], [], None
     for q in range(PARTS + 1):
         if q < PARTS:
-            got.append(exchange(made[q], got[-1], *first_sums[-1:]))
-        if q > 0:
-            states_grad, part = last_norm(q - 1, backs[q - 1], got[q], states_grad)
+            got.append(exchange(made[q], *got[-1:], *first_sums[-1:]))
+        if q == 0:
+            grads = gather(behind(grads, got[0], flat, *made[1:2]), ("cols", "rows"))
+            expand_sum, reduce_sum = split_grads(grads)
+        else:
+            if q == PARTS:
+                states_grad = behind(states_grad, expand_sum)
+            states_grad, part = last_norm(q - 1, later_grads[q - 1], got[q - 1], states_grad)
             first_sums.append(part)
-    first_small = sum_small(sum(first_sums), got[-1])
+    small = sum_small(
+        jnp.concatenate([sum(first_sums)[:2], sums[:3], expand_bias_grad.reshape(-1, chans)])
+    )
     sizes = [v.size for v in filter_parts]
     ends = np.cumsum(sizes)
     filter_sums = [
         flat[e - n : e].reshape(v.shape) for e, n, v in zip(ends, sizes, filter_parts)
     ]
     inner_sum, inner_bias_sum, outer_sum, outer_bias_sum = filter_sums
-    bias_rows_count = hidden // chans
     return (
         restore(result),
         restore(states_grad),
-        first_small[0],
-        first_small[1],
+        small[0],
+        small[1],
         inner_sum,
         inner_bias_sum.reshape(2, -1, BS),
         outer_sum,
         outer_bias_sum.reshape(2, -1, BS),
-        dense_small[1],
-        dense_small[2],
+        small[3],
+        small[4],
         expand_sum,
-        dense_small[3 : 3 + bias_rows_count].reshape(-1),
+        small[5:].reshape(-1),
         reduce_sum,
-        dense_small[0],
+        small[2],
     )
 
 

time: 1600 us -> 2100 us (1.31)
  Pallas kernels: 490 us -> 1100 us
  blocking collectives: 102 us -> 0 us
  waiting for transfers between devices: 850 us -> 875 us
    pallas_call x3 -> x5, Pallas kernels: 37 us -> 642 us  [the longest x1 573 us: split_grads(): pl.pallas_call(functools.partial(split_kernel, slabs), in_specs=[anywhere...]
    all_gather x1, waiting for transfers between devices: 0.01 us -> 107 us  [gather(): return lax.all_gather(v, axis, axis=0, tiled=True)]
    all_to_all x1 -> x0, blocking collectives: 102 us -> none  [exchange(): v = lax.all_to_all(v, ('rows', 'cols'), 0, 0, tiled=True)]
    reduce_scatter x2, waiting for transfers between devices: 39.6 us -> 0.01 us  [scatter(): return lax.psum_scatter(v, axis, scatter_dimension=0, tiled=True)]
    all_to_all x2 -> x0, waiting for transfers between devices: 26.2 us -> none  [sum_small(): lax.all_to_all(v, ('rows', 'cols'), 0, 0, tiled=True)]
    all_to_all x11 -> x12, waiting for transfers between devices: 784 us -> 769 us  [exchange(): v = lax.all_to_all(v, ('rows', 'cols'), 0, 0, tiled=True)]
    all_to_all x11 -> x12, starting transfers between devices: 76.6 us -> 82.4 us  [exchange(): v = lax.all_to_all(v, ('rows', 'cols'), 0, 0, tiled=True)]
  transfers between devices with their start and end apart: 17 -> 16, of which waited for: 14 -> 12; matrix products, arithmetic and copies ran while one was open for 1% -> 1% of each run, Pallas kernels for 27% -> 47%
where the time goes in v3:
time: 2100 us; the launch traced here: 2090 us
  Pallas kernels  1100 us (52%)
  waiting for transfers between devices  875 us (42%)
  starting transfers between devices  82.8 us (4%)
    all_to_all x12, waiting for transfers between devices, exchange(): v = lax.all_to_all(v, ('rows', 'cols'), 0, 0, tiled=True)  769 us
    pallas_call x1, Pallas kernels, split_grads(): pl.pallas_call(functools.partial(split_kernel, slabs), in_specs=[anywhere...  573 us
    pallas_call x3, Pallas kernels, dense(): call(functools.partial(dense_kernel, steps, slabs, q == 0), dense_steps,...  245 us
    all_gather x1, waiting for transfers between devices, gather(): return lax.all_gather(v, axis, axis=0, tiled=True)  107 us
    all_to_all x12, starting transfers between devices, exchange(): v = lax.all_to_all(v, ('rows', 'cols'), 0, 0, tiled=True)  82.4 us
    pallas_call x6, Pallas kernels, wide_in(): call(functools.partial(wide_in_kernel, cols_here, fine), ranks, [field, w...  48.7 us
    pallas_call x6, Pallas kernels, wide_out(): call(functools.partial(wide_out_kernel, cols_here, factor), ranks, [held_...  45.5 us
    pallas_call x1, Pallas kernels, spectral_backward(): call(functools.partial(spectral_backward_kernel, factor), bin_steps, [hel...  44.2 us
  transfers between devices with their start and end apart: 16, of which 12 were waited for; matrix products, arithmetic and copies ran while one was open for 1% of the time, Pallas kernels for 47%

profile of v3, /device:TPU:15, one launch (start us, length us, event | category | flops | bytes accessed | tf_op | source)
XLA Modules:
  0.0 2090.2 jit_solution(7603374279932798484)
XLA Ops:
  13.6 10.0 first_norm.3
  29.9 10.0 first_norm.4
  39.9 85.6 %all-to-all-done = f32[32,88,384]{2,1,0:T(8,128)} async-done(((f32[32,88,384]{2,1,0:T(8,128)}), f32[32,88,384]{2,1,0:T(8,128)}, u32[]{:S(2)}, u32[]{:S(2)}) %all-to-all-start) | async-done | bytes 4325408 | tf_op jit(solution)/shard_map/all_to_all | solution.py:636
  125.5 6.9 all-to-all-start.1
  132.4 10.0 first_norm.5
  142.4 85.6 %all-to-all-done.1 = f32[32,88,384]{2,1,0:T(8,128)} async-done(((f32[32,88,384]{2,1,0:T(8,128)}), f32[32,88,384]{2,1,0:T(8,128)}, u32[]{:S(2)}, u32[]{:S(2)}) %all-to-all-start.1) | async-done | bytes 4325408 | tf_op jit(solution)/shard_map/all_to_all | solution.py:636
  228.0 6.9 all-to-all-start.2
  238.7 8.3 wide_in.6.refs_0_
  247.1 8.3 wide_in.7.refs_1_
  255.4 75.0 %all-to-all-done.2 = f32[32,88,384]{2,1,0:T(8,128)} async-done(((f32[32,88,384]{2,1,0:T(8,128)}), f32[32,88,384]{2,1,0:T(8,128)}, u32[]{:S(2)}, u32[]{:S(2)}) %all-to-all-start.2) | async-done | bytes 4325408 | tf_op jit(solution)/shard_map/all_to_all | solution.py:636
  330.5 8.4 wide_in.8.refs_2_
  338.9 40.1 %spectral_forward.1 = (f32[16,2,96,384]{3,2,1,0:T(8,128)}, f32[16,2,96,384]{3,2,1,0:T(8,128)}, f32[16,2,96,384]{3,2,1,0:T(8,128)}, bf16[18432,192]{1,0:T(8,128)(...) custom-call(f32[16,2,96,384]{3,2,1,0:T(8,128)} %wide_in.6.refs_0_, ...), custom_call_target="tpu_custom_call" | custom-call | flops 20000000000 | bytes 103809024 | tf_op jit(solution)/shard_map/spectral_forward/pallas_call | solution.py:697
  378.9 7.6 wide_out.8
  386.5 6.9 all-to-all-start.3
  393.4 7.6 wide_out.7
  401.0 88.0 %all-to-all-done.3 = f32[32,88,384]{2,1,0:T(8,128)} async-done(((f32[32,88,384]{2,1,0:T(8,128)}), f32[32,88,384]{2,1,0:T(8,128)}, u32[]{:S(2)}, u32[]{:S(2)}) %all-to-all-start.3) | async-done | bytes 4325408 | tf_op jit(solution)/shard_map/all_to_all | solution.py:636
  489.0 6.9 all-to-all-start.4
  497.7 7.6 wide_out.6
  505.2 78.1 %dense_both_ways.3 = (bf16[2,264,8,768]{3,2,1,0:T(8,128)(2,1)}, f32[8,4,88,384]{3,2,1,0:T(8,128)}, f32[2,88,8,768]{3,2,1,0:T(8,128)}, f32[8,768]{1,0:T(8,128)}, f32[4,768]{1,0:T(4,128)}, /*index=5*/f32[6144,768]{1,0:T(8,128)}) custom-call(bf16[2,264,8,768]{3,2,1,0:T(8,128)(2,1)} %bitcast.80, bf16[2,264,8,768]{3,2,1,0:T(8,128)(2,1)} %bitcast.103, ...), custom_call_target="tpu_custom_call" | custom-call | flops 39862665216 | bytes 17301504 | tf_op jit(solution)/shard_map/dense_both_ways/pallas_call | solution.py:740
  583.3 8.2 all-to-all-done.4
  591.5 6.9 all-to-all-start.5
  598.4 83.7 %dense_both_ways.4 = (bf16[2,264,8,768]{3,2,1,0:T(8,128)(2,1)}, f32[8,4,88,384]{3,2,1,0:T(8,128)}, f32[2,88,8,768]{3,2,1,0:T(8,128)}, f32[8,768]{1,0:T(8,128)}, f32[4,768]{1,0:T(4,128)}, /*index=5*/f32[6144,768]{1,0:T(8,128)}) custom-call(bf16[2,264,8,768]{3,2,1,0:T(8,128)(2,1)} %bitcast.81, ...), custom_call_target="tpu_custom_call", output_to_operand_aliasing={{0}: (13, {})} | custom-call | flops 39862665216 | bytes 17301504 | tf_op jit(solution)/shard_map/dense_both_ways/pallas_call | solution.py:740
  682.1 11.9 all-to-all-done.5
  694.0 6.9 all-to-all-start.6
  700.9 83.7 %dense_both_ways.5 = (bf16[2,264,8,768]{3,2,1,0:T(8,128)(2,1)}, f32[8,4,88,384]{3,2,1,0:T(8,128)}, f32[2,88,8,768]{3,2,1,0:T(8,128)}, f32[8,768]{1,0:T(8,128)}, f32[4,768]{1,0:T(4,128)}, /*index=5*/f32[6144,768]{1,0:T(8,128)}) custom-call(bf16[2,264,8,768]{3,2,1,0:T(8,128)(2,1)} %bitcast.82, ...), custom_call_target="tpu_custom_call", output_to_operand_aliasing={{0}: (13, {})} | custom-call | flops 39862665216 | bytes 17301504 | tf_op jit(solution)/shard_map/dense_both_ways/pallas_call | solution.py:740
  784.6 11.8 all-to-all-done.6
  796.5 6.9 all-to-all-start.7
  803.4 8.1 wide_in.9.refs_0_
  811.5 87.5 %all-to-all-done.7 = f32[32,88,384]{2,1,0:T(8,128)} async-done(((f32[32,88,384]{2,1,0:T(8,128)}), f32[32,88,384]{2,1,0:T(8,128)}, u32[]{:S(2)}, u32[]{:S(2)}) %all-to-all-start.7) | async-done | bytes 4325408 | tf_op jit(solution)/shard_map/all_to_all | solution.py:636
  899.0 6.9 all-to-all-start.8
  906.2 7.7 wide_in.10.refs_1_
  913.9 87.7 %all-to-all-done.8 = f32[32,88,384]{2,1,0:T(8,128)} async-done(((f32[32,88,384]{2,1,0:T(8,128)}), f32[32,88,384]{2,1,0:T(8,128)}, u32[]{:S(2)}, u32[]{:S(2)}) %all-to-all-start.8) | async-done | bytes 4325408 | tf_op jit(solution)/shard_map/all_to_all | solution.py:636
  1001.6 7.7 wide_in.11.refs_2_
  1009.3 44.2 %spectral_backward.1 = (f32[16,2,96,384]{3,2,1,0:T(8,128)}, f32[16,2,96,384]{3,2,1,0:T(8,128)}, f32[16,2,96,384]{3,2,1,0:T(8,128)}, f32[2,192,192]{2,1,0:T(8,128...) custom-call(f32[16,2,96,384]{3,2,1,0:T(8,128)} %wide_in.9.refs_0_, ...), custom_call_target="tpu_custom_call" | custom-call | flops 20000000000 | bytes 103809024 | tf_op jit(solution)/shard_map/spectral_backward/pallas_call | solution.py:719
  1053.5 7.6 wide_out.11
  1061.1 6.9 all-to-all-start.9
  1069.6 7.6 wide_out.10
  1077.2 109.8 %all-to-all-done.9 = f32[32,88,384]{2,1,0:T(8,128)} async-done(((f32[32,88,384]{2,1,0:T(8,128)}), f32[32,88,384]{2,1,0:T(8,128)}, u32[]{:S(2)}, u32[]{:S(2)}) %all-to-all-start.9) | async-done | bytes 4325408 | tf_op jit(solution)/shard_map/all_to_all | solution.py:636
  1187.0 7.1 all-to-all-start.10
  1194.1 7.6 wide_out.9
  1201.7 11.7 first_norm_backward.3
  1213.4 117.8 %all-to-all-done.10 = f32[32,88,384]{2,1,0:T(8,128)} async-done(((f32[32,88,384]{2,1,0:T(8,128)}), f32[32,88,384]{2,1,0:T(8,128)}, u32[]{:S(2)}, u32[]{:S(2)}) %all-to-all-start.10) | async-done | bytes 4325408 | tf_op jit(solution)/shard_map/all_to_all | solution.py:636
  1331.2 7.0 all-to-all-start.11
  1342.9 11.7 first_norm_backward.4
  1354.6 106.6 %all-gather.2.cloned.1.call-done.grads = f32[6144,768]{1,0:T(8,128)} async-done(((f32[192,768]{1,0:T(8,128)}), f32[6144,768]{1,0:T(8,128)}) %all-gather.2.cloned.1.call-update) | async-done | bytes 18874384 | tf_op jit(solution)/shard_map/all_gather | solution.py:600
  1461.2 572.9 %split_gradients.1 = (f32[768,3072]{1,0:T(8,128)}, f32[3072,768]{1,0:T(8,128)}) custom-call(f32[6144,768]{1,0:T(8,128)} %all-gather.2.cloned.1.call-done.grads), custom_call_target="tpu_custom_call" | custom-call | tf_op jit(solution)/shard_map/split_gradients/pallas_call | solution.py:621
  2034.1 11.7 first_norm_backward.5
  2047.2 33.7 %small_sums.1 = f32[56,128]{1,0:T(8,128)} custom-call(f32[56,128]{1,0:T(8,128)} %pad.8.own), custom_call_target="tpu_custom_call" | custom-call | tf_op jit(solution)/shard_map/small_sums/pallas_call | solution.py:606
  (98 shorter events, 28.9 us)
Async XLA Ops:
  23.5 101.9 %all-to-all-start = ((f32[32,88,384]{2,1,0:T(8,128)}), f32[32,88,384]{2,1,0:T(8,128)}, u32[]{:S(2)}, u32[]{:S(2)}) async-start(f32[32,88,384]{2,1,0:T(8,128)} %bitcast.89), calls=%async_computation | async-start | bytes 8650752 | tf_op jit(solution)/shard_map/all_to_all | solution.py:636
  125.5 102.5 %all-to-all-start.1 = ((f32[32,88,384]{2,1,0:T(8,128)}), f32[32,88,384]{2,1,0:T(8,128)}, u32[]{:S(2)}, u32[]{:S(2)}) async-start(f32[32,88,384]{2,1,0:T(8,128)} %bitcast.88), calls=%async_computation.1 | async-start | bytes 8650752 | tf_op jit(solution)/shard_map/all_to_all | solution.py:636
  142.4 92.5 %copy-start.2 = (bf16[2,2,96,96]{3,2,1,0:T(8,128)(2,1)S(1)}, bf16[2,2,96,96]{3,2,1,0:T(8,128)(2,1)}, u32[]{:S(2)}) copy-start(bf16[2,2,96,96]{3,2,1,0:T(8,128)(2,1)} %param.37) | copy-start | bytes 221188
  142.4 92.6 %copy-start.3 = (bf16[2,2,96,96]{3,2,1,0:T(8,128)(2,1)S(1)}, bf16[2,2,96,96]{3,2,1,0:T(8,128)(2,1)}, u32[]{:S(2)}) copy-start(bf16[2,2,96,96]{3,2,1,0:T(8,128)(2,1)} %param.39) | copy-start | bytes 221188
  228.0 9.5 copy-start.15
  228.0 10.1 copy-start.16
  228.0 102.5 %all-to-all-start.2 = ((f32[32,88,384]{2,1,0:T(8,128)}), f32[32,88,384]{2,1,0:T(8,128)}, u32[]{:S(2)}, u32[]{:S(2)}) async-start(f32[32,88,384]{2,1,0:T(8,128)} %bitcast.87), calls=%async_computation.2 | async-start | bytes 8650752 | tf_op jit(solution)/shard_map/all_to_all | solution.py:636
  235.6 11.5 copy-start
  236.6 10.5 copy-start.1
  386.5 102.5 %all-to-all-start.3 = ((f32[32,88,384]{2,1,0:T(8,128)}), f32[32,88,384]{2,1,0:T(8,128)}, u32[]{:S(2)}, u32[]{:S(2)}) async-start(f32[32,88,384]{2,1,0:T(8,128)} %bitcast.95), calls=%async_computation.3 | async-start | bytes 8650752 | tf_op jit(solution)/shard_map/all_to_all | solution.py:636
  401.0 94.9 %copy-start.12 = (f32[768]{0:T(1024)S(1)}, f32[768]{0:T(1024)}, u32[]{:S(2)}) copy-start(f32[768]{0:T(1024)} %param.41) | copy-start | bytes 9220
  401.0 95.5 %copy-start.13 = (f32[768]{0:T(1024)S(1)}, f32[768]{0:T(1024)}, u32[]{:S(2)}) copy-start(f32[768]{0:T(1024)} %param.42) | copy-start | bytes 9220
  401.0 96.1 %copy-start.14 = (f32[768]{0:T(1024)S(1)}, f32[768]{0:T(1024)}, u32[]{:S(2)}) copy-start(f32[768]{0:T(1024)} %param.46) | copy-start | bytes 9220
  489.0 102.5 %all-to-all-start.4 = ((f32[32,88,384]{2,1,0:T(8,128)}), f32[32,88,384]{2,1,0:T(8,128)}, u32[]{:S(2)}, u32[]{:S(2)}) async-start(f32[32,88,384]{2,1,0:T(8,128)} %bitcast.94), calls=%async_computation.4 | async-start | bytes 8650752 | tf_op jit(solution)/shard_map/all_to_all | solution.py:636
  591.5 102.5 %all-to-all-start.5 = ((f32[32,88,384]{2,1,0:T(8,128)}), f32[32,88,384]{2,1,0:T(8,128)}, u32[]{:S(2)}, u32[]{:S(2)}) async-start(f32[32,88,384]{2,1,0:T(8,128)} %bitcast.93), calls=%async_computation.5 | async-start | bytes 8650752 | tf_op jit(solution)/shard_map/all_to_all | solution.py:636
  694.0 102.5 %all-to-all-start.6 = ((f32[32,88,384]{2,1,0:T(8,128)}), f32[32,88,384]{2,1,0:T(8,128)}, u32[]{:S(2)}, u32[]{:S(2)}) async-start(f32[32,88,384]{2,1,0:T(8,128)} %bitcast.97), calls=%async_computation.6 | async-start | bytes 8650752 | tf_op jit(solution)/shard_map/all_to_all | solution.py:636
  700.9 308.4 %reduce-scatter.3.cloned.1.call-start = ((), (), s32[]{:S(2)}) async-start(), calls=%async_computation.14 | async-start | bytes 23592960 | tf_op jit(solution)/shard_map/reduce_scatter | solution.py:597
  796.5 102.5 %all-to-all-start.7 = ((f32[32,88,384]{2,1,0:T(8,128)}), f32[32,88,384]{2,1,0:T(8,128)}, u32[]{:S(2)}, u32[]{:S(2)}) async-start(f32[32,88,384]{2,1,0:T(8,128)} %bitcast.96), calls=%async_computation.7 | async-start | bytes 8650752 | tf_op jit(solution)/shard_map/all_to_all | solution.py:636
  899.0 102.6 %all-to-all-start.8 = ((f32[32,88,384]{2,1,0:T(8,128)}), f32[32,88,384]{2,1,0:T(8,128)}, u32[]{:S(2)}, u32[]{:S(2)}) async-start(f32[32,88,384]{2,1,0:T(8,128)} %bitcast.98), calls=%async_computation.8 | async-start | bytes 8650752 | tf_op jit(solution)/shard_map/all_to_all | solution.py:636
  905.9 281.1 %reduce-scatter.5.cloned.1.call-start = ((), (), s32[]{:S(2)}) async-start(), calls=%async_computation.15 | async-start | bytes 5308416 | tf_op jit(solution)/shard_map/reduce_scatter | solution.py:597
  1061.1 7.0 copy-start.4
  1061.1 7.0 copy-start.5
  1061.1 7.5 copy-start.18
  1061.1 7.6 copy-start.17
  1061.1 125.8 %all-to-all-start.9 = ((f32[32,88,384]{2,1,0:T(8,128)}), f32[32,88,384]{2,1,0:T(8,128)}, u32[]{:S(2)}, u32[]{:S(2)}) async-start(f32[32,88,384]{2,1,0:T(8,128)} %bitcast.91), calls=%async_computation.9 | async-start | bytes 8650752 | tf_op jit(solution)/shard_map/all_to_all | solution.py:636
  1068.0 270.3 %all-reduce.4.cloned.1.call-start = ((), (), s32[]{:S(2)}) async-start(), calls=%async_computation.17 | async-start | bytes 598016 | tf_op jit(solution)/shard_map/psum | solution.py:848
  1069.5 391.7 %all-gather.2.cloned.1.call-start = ((), (), s32[]{:S(2)}) async-start(), calls=%async_computation.16 | async-start | bytes 19464192 | tf_op jit(solution)/shard_map/all_gather | solution.py:600
  1187.0 144.3 %all-to-all-start.10 = ((f32[32,88,384]{2,1,0:T(8,128)}), f32[32,88,384]{2,1,0:T(8,128)}, u32[]{:S(2)}, u32[]{:S(2)}) async-start(f32[32,88,384]{2,1,0:T(8,128)} %bitcast.92), calls=%async_computation.10 | async-start | bytes 8650752 | tf_op jit(solution)/shard_map/all_to_all | solution.py:636
  1213.4 124.9 %copy-start.6 = (f32[4,768]{1,0:T(4,128)S(1)}, f32[4,768]{1,0:T(4,128)}, u32[]{:S(2)}) copy-start(f32[4,768]{1,0:T(4,128)} %get-tuple-element.114) | copy-start | bytes 36868
  1213.4 124.9 %copy-start.7 = (f32[4,768]{1,0:T(4,128)S(1)}, f32[4,768]{1,0:T(4,128)}, u32[]{:S(2)}) copy-start(f32[4,768]{1,0:T(4,128)} %get-tuple-element.115) | copy-start | bytes 36868
  1213.4 124.9 %copy-start.8 = (f32[4,768]{1,0:T(4,128)S(1)}, f32[4,768]{1,0:T(4,128)}, u32[]{:S(2)}) copy-start(f32[4,768]{1,0:T(4,128)} %get-tuple-element.116) | copy-start | bytes 36868
  1213.4 124.9 %copy-start.9 = (f32[8,768]{1,0:T(8,128)S(1)}, f32[8,768]{1,0:T(8,128)}, u32[]{:S(2)}) copy-start(f32[8,768]{1,0:T(8,128)} %get-tuple-element.111) | copy-start | bytes 73732
  1213.4 124.9 %copy-start.10 = (f32[8,768]{1,0:T(8,128)S(1)}, f32[8,768]{1,0:T(8,128)}, u32[]{:S(2)}) copy-start(f32[8,768]{1,0:T(8,128)} %get-tuple-element.112) | copy-start | bytes 73732
  1213.4 124.9 %copy-start.11 = (f32[8,768]{1,0:T(8,128)S(1)}, f32[8,768]{1,0:T(8,128)}, u32[]{:S(2)}) copy-start(f32[8,768]{1,0:T(8,128)} %get-tuple-element.113) | copy-start | bytes 73732
  1331.2 702.9 %all-to-all-start.11 = ((f32[32,88,384]{2,1,0:T(8,128)}), f32[32,88,384]{2,1,0:T(8,128)}, u32[]{:S(2)}, u32[]{:S(2)}) async-start(f32[32,88,384]{2,1,0:T(8,128)} %bitcast.90), calls=%async_computation.11 | async-start | bytes 8650752 | tf_op jit(solution)/shard_map/all_to_all | solution.py:636
Sparse Core Ops, SparseCore 0:
  796.6 208.2 reduce-scatter.2
  1009.4 139.1 reduce-scatter.4
  1153.0 90.2 all-reduce.3
  1246.1 215.0 all-gather.1

commit v4 on v3

--- a/solution.py
+++ b/solution.py
@@ -84,24 +84,26 @@
 
 def wide_in_kernel(cols_here, fine, block, table, held, wide):
     groups, rows = block.shape[1], block.shape[2] // cols_here
-    for j in range(rows):
+    for n in range(block.shape[0] * rows):
+        r, j = divmod(n, rows)
         for c in range(groups):
-            wide[c * cols_here : (c + 1) * cols_here, :] = block[
-                0, c, j * cols_here : (j + 1) * cols_here, :
+            wide[n, c * cols_here : (c + 1) * cols_here, :] = block[
+                r, c, j * cols_here : (j + 1) * cols_here, :
             ]
-        x = wide[...]
+        x = wide[n]
         y = table_dot(table, x) if fine else dot(table[...], x.astype(bf16))
-        held[j, 0] = y[:BINS]
-        held[j, 1] = y[BINS:]
+        held[n, 0] = y[:BINS]
+        held[n, 1] = y[BINS:]
 
 
 def wide_out_kernel(cols_here, factor, held, table, block):
     groups, rows = block.shape[1], block.shape[2] // cols_here
-    for j in range(rows):
-        x = jnp.concatenate([held[j, 0], held[j, 1]], axis=0).astype(bf16)
+    for n in range(block.shape[0] * rows):
+        r, j = divmod(n, rows)
+        x = jnp.concatenate([held[n, 0], held[n, 1]], axis=0).astype(bf16)
         plane = dot(table[...], x) * factor
         for c in range(groups):
-            block[0, c, j * cols_here : (j + 1) * cols_here, :] = plane[
+            block[r, c, j * cols_here : (j + 1) * cols_here, :] = plane[
                 c * cols_here : (c + 1) * cols_here, :
             ]
 
@@ -158,56 +160,58 @@
     return parts
 
 
+def activate(low, mix, bias, tall):
+    parts = complex_product(low, mix[0], mix[1], low.shape[0] // (2 * tall), tall, False)
+    return [part + bias[n % 2 : n % 2 + 1, :] for n, part in enumerate(parts)]
+
+
+def gelu_low(v):
+    return (v * (0.5 * (1.0 + lax.erf(v * math.sqrt(0.5))))).astype(bf16)
+
+
 def spectral_forward_kernel(factor, *refs):
     held, refs = refs[:PARTS], refs[PARTS:]
     table_down, table_up, inner, inner_bias, outer, outer_bias = refs[:6]
-    given, (entries, active, slope, damp) = refs[6 : 6 + PARTS], refs[6 + PARTS :]
+    given, entries = refs[6 : 6 + PARTS], refs[6 + PARTS]
     width = inner.shape[2]
     tall = table_up.shape[0] // 2
     spec = bins_in(held, table_down, width, True)
     low = jnp.concatenate([(s * factor).astype(bf16) for s in spec], axis=0)
     entries[...] = low
-    parts = complex_product(low, inner[0], inner[1], GROUP, tall, False)
+    act = jnp.concatenate([gelu_low(v) for v in activate(low, inner, inner_bias, tall)], axis=0)
+    shrunk = [
+        (v - shrink_width * jnp.tanh(v * (1.0 / shrink_width))).astype(bf16)
+        for v in activate(act, outer, outer_bias, tall)
+    ]
+    values = [jnp.concatenate(shrunk[2 * k : 2 * k + 2], axis=0) for k in range(GROUP)]
+    bins_out(given, table_up, width, values)
+
+
+def spectral_keep_kernel(tall, entries, inner, inner_bias, outer, outer_bias, active, slope, damp):
     acts = []
-    for n, part in enumerate(parts):
-        v = part + inner_bias[n % 2 : n % 2 + 1, :]
+    for n, v in enumerate(activate(entries[...], inner, inner_bias, tall)):
         cdf, der = phi_parts(v)
         acts.append((v * cdf).astype(bf16))
         slope[n * tall : (n + 1) * tall, :] = der.astype(bf16)
     act = jnp.concatenate(acts, axis=0)
     active[...] = act
-    parts = complex_product(act, outer[0], outer[1], GROUP, tall, False)
-    shrunk = []
-    for n, part in enumerate(parts):
-        v = part + outer_bias[n % 2 : n % 2 + 1, :]
+    for n, v in enumerate(activate(act, outer, outer_bias, tall)):
         t = jnp.tanh(v * (1.0 / shrink_width))
-        shrunk.append((v - shrink_width * t).astype(bf16))
         damp[n * tall : (n + 1) * tall, :] = (t * t).astype(bf16)
-    values = [jnp.concatenate(shrunk[2 * k : 2 * k + 2], axis=0) for k in range(GROUP)]
-    bins_out(given, table_up, width, values)
 
 
 def spectral_backward_kernel(factor, *refs):
     held, refs = refs[:PARTS], refs[PARTS:]
-    table_down, table_up, inner_t, outer_t, entries, active, slope, damp = refs[:8]
-    given, refs = refs[8 : 8 + PARTS], refs[8 + PARTS :]
-    inner_grad, inner_bias_grad, outer_grad, outer_bias_grad = refs
+    table_down, table_up, inner_t, outer_t, slope, damp = refs[:6]
+    given, refs = refs[6 : 6 + PARTS], refs[6 + PARTS :]
+    inner_low, inner_bias_grad, outer_low, outer_bias_grad = refs
     width = inner_t.shape[2]
     tall = table_up.shape[0] // 2
 
     @pl.when(pl.program_id(0) == 0)
     def _():
-        for ref in (inner_grad, inner_bias_grad, outer_grad, outer_bias_grad):
+        for ref in (inner_bias_grad, outer_bias_grad):
             ref[...] = jnp.zeros_like(ref)
-
-    def weight_grads(ref, before, grads):
-        plain = jnp.concatenate(grads, axis=0)
-        turned = []
-        for k in range(GROUP):
-            turned += [grads[2 * k + 1], -grads[2 * k]]
-        ref[0] += dot_tn(before, plain)
-        ref[1] += dot_tn(before, jnp.concatenate(turned, axis=0))
-        return plain
 
     spec = bins_in(held, table_down, width, False)
     grads = []
@@ -220,7 +224,8 @@
             sums[side] = sums[side] + jnp.sum(g, axis=0, keepdims=True)
             grads.append(g.astype(bf16))
     outer_bias_grad[...] += jnp.concatenate(sums, axis=0)
-    low = weight_grads(outer_grad, active[...], grads)
+    low = jnp.concatenate(grads, axis=0)
+    outer_low[...] = low
     parts = complex_product(low, outer_t[0], outer_t[1], GROUP, tall, True)
     grads = []
     sums = [0.0, 0.0]
@@ -229,13 +234,29 @@
         sums[n % 2] = sums[n % 2] + jnp.sum(g, axis=0, keepdims=True)
         grads.append(g.astype(bf16))
     inner_bias_grad[...] += jnp.concatenate(sums, axis=0)
-    low = weight_grads(inner_grad, entries[...], grads)
+    low = jnp.concatenate(grads, axis=0)
+    inner_low[...] = low
     parts = complex_product(low, inner_t[0], inner_t[1], GROUP, tall, True)
     values = [
         jnp.concatenate([parts[2 * k], parts[2 * k + 1]], axis=0).astype(bf16)
         for k in range(GROUP)
     ]
     bins_out(given, table_up, width, values)
+
+
+def filter_grad_kernel(tall, entries, inner_low, active, outer_low, inner_grad, outer_grad):
+    @pl.when(pl.program_id(0) == 0)
+    def _():
+        inner_grad[...] = jnp.zeros_like(inner_grad)
+        outer_grad[...] = jnp.zeros_like(outer_grad)
+
+    for before, low, grad in ((entries, inner_low, inner_grad), (active, outer_low, outer_grad)):
+        turned = []
+        for k in range(GROUP):
+            top, bottom = low[2 * k * tall : (2 * k + 1) * tall], low[(2 * k + 1) * tall : (2 * k + 2) * tall]
+            turned += [bottom, -top]
+        grad[0] += dot_tn(before[...], low[...])
+        grad[1] += dot_tn(before[...], jnp.concatenate(turned, axis=0))
 
 
 def dense_kernel(steps, slabs, first_part, *refs):
@@ -435,23 +456,59 @@
     out[...] = lax.fori_loop(1, devices, lambda i, total: total + got[i], own[...])
 
 
-def split_kernel(slabs, grads, expand, reduce, copy_sem):
-    chans = reduce.shape[1]
-    copies = [
-        pltpu.make_async_copy(
-            grads.at[pl.ds(s * chans, chans)], expand.at[:, pl.ds(s * chans, chans)], copy_sem.at[s]
+def rows_sum_kernel(ranks, own, out, got, done, pick_send, pick_recv, give_send, give_recv):
+    me = lax.axis_index("rows")
+    piece = own.shape[0] // ranks
+
+    def at(ref, r):
+        return ref.at[pl.ds(pl.multiple_of(r * piece, piece), piece)]
+
+    def copy(src, dst, i, send, recv):
+        return pltpu.make_async_remote_copy(
+            src_ref=src,
+            dst_ref=dst,
+            send_sem=send.at[i],
+            recv_sem=recv.at[i],
+            device_id={"rows": lax.rem(me + i, ranks)},
+            device_id_type=pl.DeviceIdType.MESH,
         )
-        for s in range(slabs)
+
+    barrier = pltpu.get_barrier_semaphore()
+    for i in range(1, ranks):
+        pl.semaphore_signal(
+            barrier,
+            inc=1,
+            device_id={"rows": lax.rem(me + i, ranks)},
+            device_id_type=pl.DeviceIdType.MESH,
+        )
+    pl.semaphore_wait(barrier, ranks - 1)
+    picks = [
+        copy(at(own, lax.rem(me + i, ranks)), got.at[i], i, pick_send, pick_recv)
+        for i in range(1, ranks)
     ]
-    copies.append(
-        pltpu.make_async_copy(
-            grads.at[pl.ds(slabs * chans, slabs * chans)], reduce, copy_sem.at[slabs]
-        )
-    )
-    for c in copies:
+    for c in picks:
         c.start()
-    for c in copies:
+    for c in picks:
         c.wait()
+    start = pl.ds(pl.multiple_of(me * piece, piece), piece)
+    total = own[start, :]
+    for i in range(1, ranks):
+        total = total + got[i]
+    done[0] = total
+    gives = [copy(done.at[0], done.at[i], i, give_send, give_recv) for i in range(1, ranks)]
+    for c in gives:
+        c.start()
+    for c in gives:
+        c.wait()
+    out[start, :] = total
+    for i in range(1, ranks):
+        source = lax.rem(me - i + ranks, ranks)
+        out[pl.ds(pl.multiple_of(source * piece, piece), piece), :] = done[i]
+
+
+def split_kernel(expand_in, reduce_in, expand_out, reduce_out):
+    expand_out[...] = expand_in[...]
+    reduce_out[...] = reduce_in[...]
 
 
 def wide_tables(width):
@@ -617,15 +674,39 @@
             name="small_sums",
         )(flat).reshape(-1)[: v.size].reshape(v.shape)
 
+    def sum_rows(v):
+        flat = v.reshape(-1)
+        flat = jnp.pad(flat, (0, -flat.shape[0] % (ranks * 1024))).reshape(-1, 128)
+        slots = (ranks, flat.shape[0] // ranks, 128)
+        vmem = pl.BlockSpec(memory_space=pltpu.VMEM)
+        return pl.pallas_call(
+            functools.partial(rows_sum_kernel, ranks),
+            in_specs=[vmem],
+            out_specs=vmem,
+            out_shape=shape(flat.shape, f32),
+            scratch_shapes=[pltpu.VMEM(slots, f32)] * 2 + [pltpu.SemaphoreType.DMA((ranks,))] * 4,
+            compiler_params=pltpu.CompilerParams(collective_id=1, has_side_effects=True),
+            name="filter_sums",
+        )(flat).reshape(-1)[: v.size]
+
     def split_grads(v):
-        return pl.pallas_call(
-            functools.partial(split_kernel, slabs),
-            in_specs=[anywhere],
-            out_specs=[anywhere, anywhere],
-            out_shape=[shape((chans, hidden), f32), shape((hidden, chans), f32)],
-            scratch_shapes=[pltpu.SemaphoreType.DMA((slabs + 1,))],
-            name="split_gradients",
-        )(v)
+        cuts = 4
+        piece = (chans // cuts, chans)
+        return call(
+            split_kernel,
+            slabs * cuts,
+            [
+                pl.BlockSpec(piece, lambda i: (i, 0)),
+                pl.BlockSpec(piece, lambda i: (slabs * cuts + i, 0)),
+            ],
+            [
+                pl.BlockSpec(piece, lambda i: (lax.rem(i, cuts), lax.div(i, cuts))),
+                pl.BlockSpec(piece, lambda i: (i, 0)),
+            ],
+            [shape((chans, hidden), f32), shape((hidden, chans), f32)],
+            "split_gradients",
+            nbytes=16 * chans * hidden,
+        )(v, v)
 
     def behind(v, *after):
         return lax.optimization_barrier((v,) + after)[0] if after else v
@@ -660,9 +741,10 @@
     bin_steps = BINS // GROUP
     group_rows = GROUP * 2 * height
     held_shape = shape((short, 2, BINS, lanes), f32)
-    held_row = pl.BlockSpec((rows, 2, BINS, lanes), lambda i: (i, 0, 0, 0))
+    at_once = 2
+    held_row = pl.BlockSpec((at_once * rows, 2, BINS, lanes), lambda i: (i, 0, 0, 0))
     held_bins = pl.BlockSpec((short, 2, GROUP, lanes), lambda i: (0, 0, i, 0))
-    field = pl.BlockSpec((1, groups, pixels, lanes), lambda i: (i, 0, 0, 0))
+    field = pl.BlockSpec((at_once, groups, pixels, lanes), lambda i: (i, 0, 0, 0))
     kept = pl.BlockSpec((group_rows, width), lambda i: (i, 0))
     kept_shape = shape((bin_steps * group_rows, width), bf16)
     mix_spec = whole((2, width, width))
@@ -672,19 +754,19 @@
     def wide_in(v, table, fine):
         return call(
             functools.partial(wide_in_kernel, cols_here, fine),
-            ranks,
+            ranks // at_once,
             [field, whole(table.shape)],
             held_row,
             held_shape,
             "wide_in",
             nbytes=2 * message,
-            scratch=[pltpu.VMEM((breadth, lanes), f32)],
+            scratch=[pltpu.VMEM((at_once * rows, breadth, lanes), f32)],
         )(v, table)
 
     def wide_out(v, table):
         return call(
             functools.partial(wide_out_kernel, cols_here, factor),
-            ranks,
+            ranks // at_once,
             [held_row, whole(table.shape)],
             field,
             packed_shape,
@@ -692,41 +774,59 @@
             nbytes=2 * message,
         )(v, table)
 
+    forward_mix = (inner_full, bias_rows(inner_bias), outer_full, bias_rows(outer_bias))
+    forward_specs = [mix_spec, bias_spec, mix_spec, bias_spec]
+
     def spectral_forward(held):
         table = fine_table(down)
         outs = call(
             functools.partial(spectral_forward_kernel, factor),
             bin_steps,
-            [held_bins] * PARTS
-            + [whole(table.shape), up_spec, mix_spec, bias_spec, mix_spec, bias_spec],
-            [held_bins] * PARTS + [kept] * 4,
-            [held_shape] * PARTS + [kept_shape] * 4,
+            [held_bins] * PARTS + [whole(table.shape), up_spec] + forward_specs,
+            [held_bins] * PARTS + [kept],
+            [held_shape] * PARTS + [kept_shape],
             "spectral_forward",
             flops=20 * 10**9,
             nbytes=8 * PARTS * message,
-        )(
-            *held,
-            table,
-            as_table(up),
-            inner_full,
-            bias_rows(inner_bias),
-            outer_full,
-            bias_rows(outer_bias),
-        )
-        return outs[:PARTS], outs[PARTS:]
-
-    def spectral_backward(held, saved):
+        )(*held, table, as_table(up), *forward_mix)
+        return outs[:PARTS], outs[PARTS]
+
+    def spectral_keep(entries):
+        return call(
+            functools.partial(spectral_keep_kernel, height),
+            bin_steps,
+            [kept] + forward_specs,
+            [kept] * 3,
+            [kept_shape] * 3,
+            "spectral_keep",
+            flops=10 * 10**9,
+            nbytes=2 * PARTS * message,
+        )(entries, *forward_mix)
+
+    def spectral_backward(held, slope, damp):
         outs = call(
             functools.partial(spectral_backward_kernel, factor),
             bin_steps,
-            [held_bins] * PARTS + [up_spec, up_spec, mix_spec, mix_spec] + [kept] * 4,
-            [held_bins] * PARTS + [mix_spec, bias_spec, mix_spec, bias_spec],
-            [held_shape] * PARTS + [shape((2, width, width), f32), shape((2, width), f32)] * 2,
+            [held_bins] * PARTS + [up_spec, up_spec, mix_spec, mix_spec] + [kept] * 2,
+            [held_bins] * PARTS + [kept, bias_spec] * 2,
+            [held_shape] * PARTS + [kept_shape, shape((2, width), f32)] * 2,
             "spectral_backward",
             flops=20 * 10**9,
             nbytes=8 * PARTS * message,
-        )(*held, as_table(down), as_table(up), turn(inner_full), turn(outer_full), *saved)
+        )(*held, as_table(down), as_table(up), turn(inner_full), turn(outer_full), slope, damp)
         return outs[:PARTS], outs[PARTS:]
+
+    def filter_grad(*operands):
+        return call(
+            functools.partial(filter_grad_kernel, height),
+            bin_steps,
+            [kept] * 4,
+            [mix_spec] * 2,
+            [shape((2, width, width), f32)] * 2,
+            "filter_grad",
+            flops=10 * 10**9,
+            nbytes=2 * PARTS * message,
+        )(*operands)
 
     slab = chans
     slabs = hidden // slab
@@ -816,13 +916,15 @@
     for q in every:
         got.append(exchange(first_norm(q), *got[-1:]))
     held = [wide_in(v, fine_table(plain), True) for v in got]
-    given, saved = spectral_forward(held)
+    given, entries = spectral_forward(held)
 
     made = [wide_out(v, as_table(doubled.T)) for v in given]
     spatial, backs, later_grads, sums, expand_bias_grad, before = [], [], [], 0.0, 0.0, ()
+    active, slope, damp = spectral_keep(entries)
     for q in range(PARTS + 1):
         if q < PARTS:
-            spatial.append(exchange(made[q], *spatial[-1:], *backs[-1:]))
+            beside = (active, *made[1:2]) if q == 1 else ()
+            spatial.append(exchange(made[q], *spatial[-1:], *backs[-1:], *beside))
         if q > 0:
             result, back, kept_grad, part, bias_part, grads = dense(q - 1, spatial[q - 1], before)
             before = (grads, result)
@@ -839,13 +941,14 @@
     held.append(wide_in(behind(got[-1], held[-1]), as_table(doubled), False))
     grads = scatter(behind(grads, held[-1]), "rows")
 
-    given, filter_grads = spectral_backward(held, saved)
-    inner_grad, inner_bias_grad, outer_grad, outer_bias_grad = filter_grads
+    given, (inner_low, inner_bias_grad, outer_low, outer_bias_grad) = spectral_backward(
+        held, slope, damp
+    )
+    inner_grad, outer_grad = filter_grad(entries, inner_low, active, outer_low)
     filter_parts = (
         gather_blocks(inner_grad), inner_bias_grad, gather_blocks(outer_grad), outer_bias_grad
     )
-    flat = jnp.concatenate([v.reshape(-1) for v in filter_parts])
-    flat = lax.psum(jnp.pad(flat, (0, -flat.shape[0] % 1024)).reshape(-1, 128), "rows").reshape(-1)
+    flat = sum_rows(jnp.concatenate([v.reshape(-1) for v in filter_parts]))
     made = [wide_out(v, as_table(plain.T)) for v in given]
     got, first_sums, states_grad = [], [], None
     for q in range(PARTS + 1):

time: 2100 us -> 1560 us (0.74)
  Pallas kernels: 1100 us -> 635 us
  waiting for transfers between devices: 875 us -> 791 us
    pallas_call x13 -> x16, Pallas kernels: 667 us -> 228 us  [the longest x1 94.3 us: sum_rows(): pl.pallas_call(functools.partial(rows_sum_kernel, ranks), in_specs=[vmem]...]
    all_gather x1, waiting for transfers between devices: 107 us -> 0.01 us  [gather(): return lax.all_gather(v, axis, axis=0, tiled=True)]
    all_to_all x12, waiting for transfers between devices: 769 us -> 791 us  [exchange(): v = lax.all_to_all(v, ('rows', 'cols'), 0, 0, tiled=True)]
  transfers between devices with their start and end apart: 16 -> 15, of which waited for: 12 -> 11; matrix products, arithmetic and copies ran while one was open for 1% -> 1% of each run, Pallas kernels for 47% -> 35%
where the time goes in v4:
time: 1560 us; the launch traced here: 1550 us
  waiting for transfers between devices  791 us (51%)
  Pallas kernels  635 us (41%)
  starting transfers between devices  83.6 us (5%)
  local copies, waits for them, and re-layouts  19.6 us (1%)
    all_to_all x12, waiting for transfers between devices, exchange(): v = lax.all_to_all(v, ('rows', 'cols'), 0, 0, tiled=True)  791 us
    pallas_call x3, Pallas kernels, dense(): call(functools.partial(dense_kernel, steps, slabs, q == 0), dense_steps,...  245 us
    pallas_call x1, Pallas kernels, sum_rows(): pl.pallas_call(functools.partial(rows_sum_kernel, ranks), in_specs=[vmem]...  94.3 us
    all_to_all x12, starting transfers between devices, exchange(): v = lax.all_to_all(v, ('rows', 'cols'), 0, 0, tiled=True)  83.5 us
    pallas_call x6, Pallas kernels, wide_in(): call(functools.partial(wide_in_kernel, cols_here, fine), ranks // at_once...  36.3 us
    pallas_call x1, Pallas kernels, spectral_forward(): call(functools.partial(spectral_forward_kernel, factor), bin_steps, [held...  35 us
    pallas_call x3, Pallas kernels, last_norm(): call(last_kernel, steps, [token_spec(q, same), token_spec(0, same), packe...  35 us
    pallas_call x6, Pallas kernels, wide_out(): call(functools.partial(wide_out_kernel, cols_here, factor), ranks // at_o...  32.7 us
  transfers between devices with their start and end apart: 15, of which 11 were waited for; matrix products, arithmetic and copies ran while one was open for 1% of the time, Pallas kernels for 35%

profile of v4, /device:TPU:15, one launch (start us, length us, event | category | flops | bytes accessed | tf_op | source)
XLA Modules:
  0.0 1547.1 jit_solution(10057470043605351776)
XLA Ops:
  13.5 10.0 first_norm.3
  23.5 6.3 all-to-all-start
  29.8 10.0 first_norm.4
  39.9 85.6 %all-to-all-done = f32[32,88,384]{2,1,0:T(8,128)} async-done(((f32[32,88,384]{2,1,0:T(8,128)}), f32[32,88,384]{2,1,0:T(8,128)}, u32[]{:S(2)}, u32[]{:S(2)}) %all-to-all-start) | async-done | bytes 4325408 | tf_op jit(solution)/shard_map/all_to_all | solution.py:717
  125.4 6.9 all-to-all-start.1
  132.3 10.0 first_norm.5
  142.4 85.5 %all-to-all-done.1 = f32[32,88,384]{2,1,0:T(8,128)} async-done(((f32[32,88,384]{2,1,0:T(8,128)}), f32[32,88,384]{2,1,0:T(8,128)}, u32[]{:S(2)}, u32[]{:S(2)}) %all-to-all-start.1) | async-done | bytes 4325408 | tf_op jit(solution)/shard_map/all_to_all | solution.py:717
  227.9 6.9 all-to-all-start.2
  238.7 6.4 wide_in.6.refs_0_
  245.1 6.4 wide_in.7.refs_1_
  251.4 79.0 %all-to-all-done.2 = f32[32,88,384]{2,1,0:T(8,128)} async-done(((f32[32,88,384]{2,1,0:T(8,128)}), f32[32,88,384]{2,1,0:T(8,128)}, u32[]{:S(2)}, u32[]{:S(2)}) %all-to-all-start.2) | async-done | bytes 4325408 | tf_op jit(solution)/shard_map/all_to_all | solution.py:717
  330.4 6.4 wide_in.8.refs_2_
  336.8 35.0 %spectral_forward.1 = (f32[16,2,96,384]{3,2,1,0:T(8,128)}, f32[16,2,96,384]{3,2,1,0:T(8,128)}, f32[16,2,96,384]{3,2,1,0:T(8,128)}, bf16[18432,192]{1,0:T(8,128)(2,1)}) custom-call(f32[16,2,96,384]{3,2,1,0:T(8,128)} %wide_in.6.refs_0_, f32[16,2,96,384]{3,2,1,0:T(8,128)} %wide_in.7.refs_1_, f32[16,2,96,384]{3,2,1,0:T(8,128)} %wide_in.8.refs_2_, ...), custom_call_target="tpu_custom_call" | custom-call | flops 20000000000 | bytes 103809024 | tf_op jit(solution)/shard_map/spectral_forward/pallas_call | solution.py:782
  377.2 6.9 all-to-all-start.3
  384.1 5.5 wide_out.7
  389.6 25.5 %spectral_keep.1 = (bf16[18432,192]{1,0:T(8,128)(2,1)}, bf16[18432,192]{1,0:T(8,128)(2,1)}, bf16[18432,192]{1,0:T(8,128)(2,1)}) custom-call(bf16[18432,192]{1,0:T(8,128)(2,1)} %get-tuple-element.75.entries, bf16[2,192,192]{2,1,0:T(8,128)(2,1)} %copy.59.refs_5_.inner, f32[2,192]{1,0:T(2,128)} %reshape.315.refs_6_.inner_bias, ...), custom_call_target="tpu_custom_call" | custom-call | flops 10000000000 | bytes 25952256 | tf_op jit(solution)/shard_map/spectral_keep/pallas_call | solution.py:795
  415.1 64.6 %all-to-all-done.3 = f32[32,88,384]{2,1,0:T(8,128)} async-done(((f32[32,88,384]{2,1,0:T(8,128)}), f32[32,88,384]{2,1,0:T(8,128)}, u32[]{:S(2)}, u32[]{:S(2)}) %all-to-all-start.3) | async-done | bytes 4325408 | tf_op jit(solution)/shard_map/all_to_all | solution.py:717
  479.7 7.2 all-to-all-start.4
  494.1 78.0 %dense_both_ways.3 = (bf16[2,264,8,768]{3,2,1,0:T(8,128)(2,1)}, f32[8,4,88,384]{3,2,1,0:T(8,128)}, f32[2,88,8,768]{3,2,1,0:T(8,128)}, f32[8,768]{1,0:T(8,128)}, f32[4,768]{1,0:T(4,128)}, /*index=5*/f32[6144,768]{1,0:T(8,128)}) custom-call(bf16[2,264,8,768]{3,2,1,0:T(8,128)(2,1)} %bitcast.80, bf16[2,264,8,768]{3,2,1,0:T(8,128)(2,1)} %bitcast.103, ...), custom_call_target="tpu_custom_call" | custom-call | flops 39862665216 | bytes 17301504 | tf_op jit(solution)/shard_map/dense_both_ways/pallas_call | solution.py:840
  572.2 10.3 all-to-all-done.4
  582.4 7.3 all-to-all-start.5
  589.7 83.7 %dense_both_ways.4 = (bf16[2,264,8,768]{3,2,1,0:T(8,128)(2,1)}, f32[8,4,88,384]{3,2,1,0:T(8,128)}, f32[2,88,8,768]{3,2,1,0:T(8,128)}, f32[8,768]{1,0:T(8,128)}, f32[4,768]{1,0:T(4,128)}, /*index=5*/f32[6144,768]{1,0:T(8,128)}) custom-call(bf16[2,264,8,768]{3,2,1,0:T(8,128)(2,1)} %bitcast.81, ...), custom_call_target="tpu_custom_call", output_to_operand_aliasing={{0}: (13, {})} | custom-call | flops 39862665216 | bytes 17301504 | tf_op jit(solution)/shard_map/dense_both_ways/pallas_call | solution.py:840
  673.4 11.8 all-to-all-done.5
  685.2 6.9 all-to-all-start.6
  692.2 83.7 %dense_both_ways.5 = (bf16[2,264,8,768]{3,2,1,0:T(8,128)(2,1)}, f32[8,4,88,384]{3,2,1,0:T(8,128)}, f32[2,88,8,768]{3,2,1,0:T(8,128)}, f32[8,768]{1,0:T(8,128)}, f32[4,768]{1,0:T(4,128)}, /*index=5*/f32[6144,768]{1,0:T(8,128)}) custom-call(bf16[2,264,8,768]{3,2,1,0:T(8,128)(2,1)} %bitcast.82, ...), custom_call_target="tpu_custom_call", output_to_operand_aliasing={{0}: (13, {})} | custom-call | flops 39862665216 | bytes 17301504 | tf_op jit(solution)/shard_map/dense_both_ways/pallas_call | solution.py:840
  775.9 11.8 all-to-all-done.6
  787.7 6.9 all-to-all-start.7
  794.6 6.2 wide_in.9.refs_0_
  800.8 89.4 %all-to-all-done.7 = f32[32,88,384]{2,1,0:T(8,128)} async-done(((f32[32,88,384]{2,1,0:T(8,128)}), f32[32,88,384]{2,1,0:T(8,128)}, u32[]{:S(2)}, u32[]{:S(2)}) %all-to-all-start.7) | async-done | bytes 4325408 | tf_op jit(solution)/shard_map/all_to_all | solution.py:717
  890.2 7.3 all-to-all-start.8
  897.6 5.5 wide_in.10.refs_1_
  903.1 90.0 %all-to-all-done.8 = f32[32,88,384]{2,1,0:T(8,128)} async-done(((f32[32,88,384]{2,1,0:T(8,128)}), f32[32,88,384]{2,1,0:T(8,128)}, u32[]{:S(2)}, u32[]{:S(2)}) %all-to-all-start.8) | async-done | bytes 4325408 | tf_op jit(solution)/shard_map/all_to_all | solution.py:717
  993.1 5.6 wide_in.11.refs_2_
  998.7 32.2 %spectral_backward.1 = (f32[16,2,96,384]{3,2,1,0:T(8,128)}, f32[16,2,96,384]{3,2,1,0:T(8,128)}, f32[16,2,96,384]{3,2,1,0:T(8,128)}, bf16[18432,192]{1,0:T(8,128)...) custom-call(f32[16,2,96,384]{3,2,1,0:T(8,128)} %wide_in.9.refs_0_, ...), custom_call_target="tpu_custom_call" | custom-call | flops 20000000000 | bytes 103809024 | tf_op jit(solution)/shard_map/spectral_backward/pallas_call | solution.py:807
  1036.4 7.0 all-to-all-start.9
  1043.4 5.5 wide_out.10
  1048.9 111.3 %all-to-all-done.9 = f32[32,88,384]{2,1,0:T(8,128)} async-done(((f32[32,88,384]{2,1,0:T(8,128)}), f32[32,88,384]{2,1,0:T(8,128)}, u32[]{:S(2)}, u32[]{:S(2)}) %all-to-all-start.9) | async-done | bytes 4325408 | tf_op jit(solution)/shard_map/all_to_all | solution.py:717
  1160.2 6.9 all-to-all-start.10
  1167.1 5.5 wide_out.9
  1172.7 11.7 first_norm_backward.3
  1184.4 151.2 %all-to-all-done.10 = f32[32,88,384]{2,1,0:T(8,128)} async-done(((f32[32,88,384]{2,1,0:T(8,128)}), f32[32,88,384]{2,1,0:T(8,128)}, u32[]{:S(2)}, u32[]{:S(2)}) %all-to-all-start.10) | async-done | bytes 4325408 | tf_op jit(solution)/shard_map/all_to_all | solution.py:717
  1335.6 7.0 all-to-all-start.11
  1342.8 20.6 %filter_grad.1 = (f32[2,192,192]{2,1,0:T(8,128)}, f32[2,192,192]{2,1,0:T(8,128)}) custom-call(bf16[18432,192]{1,0:T(8,128)(2,1)} %get-tuple-element.75.entries, bf16[18432,192]{1,0:T(8,128)(2,1)} %get-tuple-element.119.inner_low, bf16[18432,192]{1,0:T(8,128)(2,1)} %get-tuple-element.76.active, bf16[18432,192]{1,0:T(8,128)(2,1)} %get-tuple-element.120.outer_low), custom_call_target="tpu_custom_call" | custom-call | flops 10000000000 | bytes 25952256 | tf_op jit(solution)/shard_map/filter_grad/pallas_call | solution.py:820
  1365.9 94.3 %filter_sums.1 = f32[640,128]{1,0:T(8,128)} custom-call(f32[640,128]{1,0:T(8,128)} %fusion.own), custom_call_target="tpu_custom_call" | custom-call | tf_op jit(solution)/shard_map/filter_sums/pallas_call | solution.py:682
  1464.9 11.6 first_norm_backward.4
  1476.5 18.5 %split_gradients.1 = (f32[768,3072]{1,0:T(8,128)}, f32[3072,768]{1,0:T(8,128)}) custom-call(f32[6144,768]{1,0:T(8,128)} %all-gather.2.cloned.1.call-done.expand_in.reduce_in, f32[6144,768]{1,0:T(8,128)} %all-gather.2.cloned.1.call-done.expand_in.reduce_in), custom_call_target="tpu_custom_call" | custom-call | bytes 37748736 | tf_op jit(solution)/shard_map/split_gradients/pallas_call | solution.py:695
  1495.0 11.7 first_norm_backward.5
  1508.1 29.3 %small_sums.1 = f32[56,128]{1,0:T(8,128)} custom-call(f32[56,128]{1,0:T(8,128)} %pad.8.own), custom_call_target="tpu_custom_call" | custom-call | tf_op jit(solution)/shard_map/small_sums/pallas_call | solution.py:663
  (94 shorter events, 39.6 us)
Async XLA Ops:
  23.5 101.9 %all-to-all-start = ((f32[32,88,384]{2,1,0:T(8,128)}), f32[32,88,384]{2,1,0:T(8,128)}, u32[]{:S(2)}, u32[]{:S(2)}) async-start(f32[32,88,384]{2,1,0:T(8,128)} %bitcast.89), calls=%async_computation | async-start | bytes 8650752 | tf_op jit(solution)/shard_map/all_to_all | solution.py:717
  125.4 102.5 %all-to-all-start.1 = ((f32[32,88,384]{2,1,0:T(8,128)}), f32[32,88,384]{2,1,0:T(8,128)}, u32[]{:S(2)}, u32[]{:S(2)}) async-start(f32[32,88,384]{2,1,0:T(8,128)} %bitcast.88), calls=%async_computation.1 | async-start | bytes 8650752 | tf_op jit(solution)/shard_map/all_to_all | solution.py:717
  142.4 92.5 %copy-start.13 = (f32[2,2,96]{2,1,0:T(2,128)S(1)}, f32[2,2,96]{2,1,0:T(2,128)}, u32[]{:S(2)}) copy-start(f32[2,2,96]{2,1,0:T(2,128)} %param.38) | copy-start | bytes 4612
  142.4 93.1 %copy-start.14 = (f32[2,2,96]{2,1,0:T(2,128)S(1)}, f32[2,2,96]{2,1,0:T(2,128)}, u32[]{:S(2)}) copy-start(f32[2,2,96]{2,1,0:T(2,128)} %param.40) | copy-start | bytes 4612
  142.4 93.8 %copy-start.2 = (bf16[2,2,96,96]{3,2,1,0:T(8,128)(2,1)S(1)}, bf16[2,2,96,96]{3,2,1,0:T(8,128)(2,1)}, u32[]{:S(2)}) copy-start(bf16[2,2,96,96]{3,2,1,0:T(8,128)(2,1)} %param.37) | copy-start | bytes 221188
  142.4 93.9 %copy-start.3 = (bf16[2,2,96,96]{3,2,1,0:T(8,128)(2,1)S(1)}, bf16[2,2,96,96]{3,2,1,0:T(8,128)(2,1)}, u32[]{:S(2)}) copy-start(bf16[2,2,96,96]{3,2,1,0:T(8,128)(2,1)} %param.39) | copy-start | bytes 221188
  227.9 102.5 %all-to-all-start.2 = ((f32[32,88,384]{2,1,0:T(8,128)}), f32[32,88,384]{2,1,0:T(8,128)}, u32[]{:S(2)}, u32[]{:S(2)}) async-start(f32[32,88,384]{2,1,0:T(8,128)} %bitcast.87), calls=%async_computation.2 | async-start | bytes 8650752 | tf_op jit(solution)/shard_map/all_to_all | solution.py:717
  236.9 8.1 copy-start
  237.9 7.2 copy-start.1
  377.2 102.5 %all-to-all-start.3 = ((f32[32,88,384]{2,1,0:T(8,128)}), f32[32,88,384]{2,1,0:T(8,128)}, u32[]{:S(2)}, u32[]{:S(2)}) async-start(f32[32,88,384]{2,1,0:T(8,128)} %bitcast.94), calls=%async_computation.3 | async-start | bytes 8650752 | tf_op jit(solution)/shard_map/all_to_all | solution.py:717
  415.0 71.9 %copy-start.10 = (f32[768]{0:T(1024)S(1)}, f32[768]{0:T(1024)}, u32[]{:S(2)}) copy-start(f32[768]{0:T(1024)} %param.41) | copy-start | bytes 9220
  415.0 72.5 %copy-start.11 = (f32[768]{0:T(1024)S(1)}, f32[768]{0:T(1024)}, u32[]{:S(2)}) copy-start(f32[768]{0:T(1024)} %param.42) | copy-start | bytes 9220
  415.1 73.1 %copy-start.12 = (f32[768]{0:T(1024)S(1)}, f32[768]{0:T(1024)}, u32[]{:S(2)}) copy-start(f32[768]{0:T(1024)} %param.46) | copy-start | bytes 9220
  479.7 102.7 %all-to-all-start.4 = ((f32[32,88,384]{2,1,0:T(8,128)}), f32[32,88,384]{2,1,0:T(8,128)}, u32[]{:S(2)}, u32[]{:S(2)}) async-start(f32[32,88,384]{2,1,0:T(8,128)} %bitcast.91), calls=%async_computation.4 | async-start | bytes 8650752 | tf_op jit(solution)/shard_map/all_to_all | solution.py:717
  582.4 102.8 %all-to-all-start.5 = ((f32[32,88,384]{2,1,0:T(8,128)}), f32[32,88,384]{2,1,0:T(8,128)}, u32[]{:S(2)}, u32[]{:S(2)}) async-start(f32[32,88,384]{2,1,0:T(8,128)} %bitcast.93), calls=%async_computation.5 | async-start | bytes 8650752 | tf_op jit(solution)/shard_map/all_to_all | solution.py:717
  685.2 102.5 %all-to-all-start.6 = ((f32[32,88,384]{2,1,0:T(8,128)}), f32[32,88,384]{2,1,0:T(8,128)}, u32[]{:S(2)}, u32[]{:S(2)}) async-start(f32[32,88,384]{2,1,0:T(8,128)} %bitcast.97), calls=%async_computation.6 | async-start | bytes 8650752 | tf_op jit(solution)/shard_map/all_to_all | solution.py:717
  692.1 306.6 %reduce-scatter.3.cloned.1.call-start = ((), (), s32[]{:S(2)}) async-start(), calls=%async_computation.14 | async-start | bytes 23592960 | tf_op jit(solution)/shard_map/reduce_scatter | solution.py:654
  787.7 102.5 %all-to-all-start.7 = ((f32[32,88,384]{2,1,0:T(8,128)}), f32[32,88,384]{2,1,0:T(8,128)}, u32[]{:S(2)}, u32[]{:S(2)}) async-start(f32[32,88,384]{2,1,0:T(8,128)} %bitcast.96), calls=%async_computation.7 | async-start | bytes 8650752 | tf_op jit(solution)/shard_map/all_to_all | solution.py:717
  890.2 102.9 %all-to-all-start.8 = ((f32[32,88,384]{2,1,0:T(8,128)}), f32[32,88,384]{2,1,0:T(8,128)}, u32[]{:S(2)}, u32[]{:S(2)}) async-start(f32[32,88,384]{2,1,0:T(8,128)} %bitcast.98), calls=%async_computation.8 | async-start | bytes 8650752 | tf_op jit(solution)/shard_map/all_to_all | solution.py:717
  897.6 262.6 %reduce-scatter.5.cloned.1.call-start = ((), (), s32[]{:S(2)}) async-start(), calls=%async_computation.15 | async-start | bytes 5308416 | tf_op jit(solution)/shard_map/reduce_scatter | solution.py:654
  1036.4 123.8 %all-to-all-start.9 = ((f32[32,88,384]{2,1,0:T(8,128)}), f32[32,88,384]{2,1,0:T(8,128)}, u32[]{:S(2)}, u32[]{:S(2)}) async-start(f32[32,88,384]{2,1,0:T(8,128)} %bitcast.95), calls=%async_computation.9 | async-start | bytes 8650752 | tf_op jit(solution)/shard_map/all_to_all | solution.py:717
  1043.3 433.2 %all-gather.2.cloned.1.call-start = ((), (), s32[]{:S(2)}) async-start(), calls=%async_computation.16 | async-start | bytes 19464192 | tf_op jit(solution)/shard_map/all_gather | solution.py:657
  1160.2 175.4 %all-to-all-start.10 = ((f32[32,88,384]{2,1,0:T(8,128)}), f32[32,88,384]{2,1,0:T(8,128)}, u32[]{:S(2)}, u32[]{:S(2)}) async-start(f32[32,88,384]{2,1,0:T(8,128)} %bitcast.92), calls=%async_computation.10 | async-start | bytes 8650752 | tf_op jit(solution)/shard_map/all_to_all | solution.py:717
  1184.3 158.3 %copy-start.4 = (f32[4,768]{1,0:T(4,128)S(1)}, f32[4,768]{1,0:T(4,128)}, u32[]{:S(2)}) copy-start(f32[4,768]{1,0:T(4,128)} %get-tuple-element.116) | copy-start | bytes 36868
  1184.3 158.4 %copy-start.5 = (f32[4,768]{1,0:T(4,128)S(1)}, f32[4,768]{1,0:T(4,128)}, u32[]{:S(2)}) copy-start(f32[4,768]{1,0:T(4,128)} %get-tuple-element.117) | copy-start | bytes 36868
  1184.3 158.4 %copy-start.6 = (f32[4,768]{1,0:T(4,128)S(1)}, f32[4,768]{1,0:T(4,128)}, u32[]{:S(2)}) copy-start(f32[4,768]{1,0:T(4,128)} %get-tuple-element.118) | copy-start | bytes 36868
  1184.3 158.4 %copy-start.7 = (f32[8,768]{1,0:T(8,128)S(1)}, f32[8,768]{1,0:T(8,128)}, u32[]{:S(2)}) copy-start(f32[8,768]{1,0:T(8,128)} %get-tuple-element.113) | copy-start | bytes 73732
  1184.3 158.4 %copy-start.8 = (f32[8,768]{1,0:T(8,128)S(1)}, f32[8,768]{1,0:T(8,128)}, u32[]{:S(2)}) copy-start(f32[8,768]{1,0:T(8,128)} %get-tuple-element.114) | copy-start | bytes 73732
  1184.4 158.4 %copy-start.9 = (f32[8,768]{1,0:T(8,128)S(1)}, f32[8,768]{1,0:T(8,128)}, u32[]{:S(2)}) copy-start(f32[8,768]{1,0:T(8,128)} %get-tuple-element.115) | copy-start | bytes 73732
  1335.6 159.4 %all-to-all-start.11 = ((f32[32,88,384]{2,1,0:T(8,128)}), f32[32,88,384]{2,1,0:T(8,128)}, u32[]{:S(2)}, u32[]{:S(2)}) async-start(f32[32,88,384]{2,1,0:T(8,128)} %bitcast.90), calls=%async_computation.11 | async-start | bytes 8650752 | tf_op jit(solution)/shard_map/all_to_all | solution.py:717
  1342.8 22.1 %copy-start.16 = (f32[2,192]{1,0:T(2,128)S(1)}, f32[2,192]{1,0:T(2,128)}, u32[]{:S(2)}) copy-start(f32[2,192]{1,0:T(2,128)} %get-tuple-element.122) | copy-start | bytes 4612
  1342.8 22.1 %copy-start.15 = (f32[2,192]{1,0:T(2,128)S(1)}, f32[2,192]{1,0:T(2,128)}, u32[]{:S(2)}) copy-start(f32[2,192]{1,0:T(2,128)} %get-tuple-element.124) | copy-start | bytes 4612
Sparse Core Ops, SparseCore 0:
  787.8 208.2 reduce-scatter.2
  1000.2 144.3 reduce-scatter.4
  1160.3 224.9 all-gather.1

commit v5 on v4

--- a/solution.py
+++ b/solution.py
@@ -953,7 +953,8 @@
     got, first_sums, states_grad = [], [], None
     for q in range(PARTS + 1):
         if q < PARTS:
-            got.append(exchange(made[q], *got[-1:], *first_sums[-1:]))
+            beside = (flat,) if q == PARTS - 1 else ()
+            got.append(exchange(made[q], *got[-1:], *first_sums[-1:], *beside))
         if q == 0:
             grads = gather(behind(grads, got[0], flat, *made[1:2]), ("cols", "rows"))
             expand_sum, reduce_sum = split_grads(grads)

time: 1560 us -> 1530 us (0.981)
  waiting for transfers between devices: 791 us -> 748 us
    all_to_all x12, waiting for transfers between devices: 791 us -> 720 us  [exchange(): v = lax.all_to_all(v, ('rows', 'cols'), 0, 0, tiled=True)]
    all_gather x1, waiting for transfers between devices: 0.01 us -> 28 us  [gather(): return lax.all_gather(v, axis, axis=0, tiled=True)]
    pallas_call x1, Pallas kernels: 94.3 us -> 110 us  [sum_rows(): pl.pallas_call(functools.partial(rows_sum_kernel, ranks), in_specs=[vmem]...]
  transfers between devices with their start and end apart: 15 -> 15, of which waited for: 11 -> 12; matrix products, arithmetic and copies ran while one was open for 1% -> 1% of each run, Pallas kernels for 35% -> 36%
where the time goes in v5:
time: 1530 us; the launch traced here: 1520 us
  waiting for transfers between devices  748 us (49%)
  Pallas kernels  650 us (42%)
  starting transfers between devices  83.5 us (5%)
  local copies, waits for them, and re-layouts  17.9 us (1%)
    all_to_all x12, waiting for transfers between devices, exchange(): v = lax.all_to_all(v, ('rows', 'cols'), 0, 0, tiled=True)  720 us
    pallas_call x3, Pallas kernels, dense(): call(functools.partial(dense_kernel, steps, slabs, q == 0), dense_steps,...  245 us
    pallas_call x1, Pallas kernels, sum_rows(): pl.pallas_call(functools.partial(rows_sum_kernel, ranks), in_specs=[vmem]...  110 us
    all_to_all x12, starting transfers between devices, exchange(): v = lax.all_to_all(v, ('rows', 'cols'), 0, 0, tiled=True)  83.4 us
    pallas_call x6, Pallas kernels, wide_in(): call(functools.partial(wide_in_kernel, cols_here, fine), ranks // at_once...  36.3 us
    pallas_call x1, Pallas kernels, spectral_forward(): call(functools.partial(spectral_forward_kernel, factor), bin_steps, [held...  35.1 us
    pallas_call x3, Pallas kernels, last_norm(): call(last_kernel, steps, [token_spec(q, same), token_spec(0, same), packe...  34.9 us
    pallas_call x6, Pallas kernels, wide_out(): call(functools.partial(wide_out_kernel, cols_here, factor), ranks // at_o...  32.7 us
  transfers between devices with their start and end apart: 15, of which 12 were waited for; matrix products, arithmetic and copies ran while one was open for 1% of the time, Pallas kernels for 36%

profile of v5, /device:TPU:15, one launch (start us, length us, event | category | flops | bytes accessed | tf_op | source)
XLA Modules:
  0.0 1517.6 jit_solution(11832226227378547422)
XLA Ops:
  13.5 10.0 first_norm.3
  23.5 6.3 all-to-all-start
  29.8 10.0 first_norm.4
  39.8 85.6 %all-to-all-done = f32[32,88,384]{2,1,0:T(8,128)} async-done(((f32[32,88,384]{2,1,0:T(8,128)}), f32[32,88,384]{2,1,0:T(8,128)}, u32[]{:S(2)}, u32[]{:S(2)}) %all-to-all-start) | async-done | bytes 4325408 | tf_op jit(solution)/shard_map/all_to_all | solution.py:717
  125.4 6.9 all-to-all-start.1
  132.3 10.0 first_norm.5
  142.3 85.6 %all-to-all-done.1 = f32[32,88,384]{2,1,0:T(8,128)} async-done(((f32[32,88,384]{2,1,0:T(8,128)}), f32[32,88,384]{2,1,0:T(8,128)}, u32[]{:S(2)}, u32[]{:S(2)}) %all-to-all-start.1) | async-done | bytes 4325408 | tf_op jit(solution)/shard_map/all_to_all | solution.py:717
  227.9 6.9 all-to-all-start.2
  238.7 6.4 wide_in.6.refs_0_
  245.0 6.4 wide_in.7.refs_1_
  251.4 79.0 %all-to-all-done.2 = f32[32,88,384]{2,1,0:T(8,128)} async-done(((f32[32,88,384]{2,1,0:T(8,128)}), f32[32,88,384]{2,1,0:T(8,128)}, u32[]{:S(2)}, u32[]{:S(2)}) %all-to-all-start.2) | async-done | bytes 4325408 | tf_op jit(solution)/shard_map/all_to_all | solution.py:717
  330.4 6.4 wide_in.8.refs_2_
  336.8 35.1 %spectral_forward.1 = (f32[16,2,96,384]{3,2,1,0:T(8,128)}, f32[16,2,96,384]{3,2,1,0:T(8,128)}, f32[16,2,96,384]{3,2,1,0:T(8,128)}, bf16[18432,192]{1,0:T(8,128)(2,1)}) custom-call(f32[16,2,96,384]{3,2,1,0:T(8,128)} %wide_in.6.refs_0_, f32[16,2,96,384]{3,2,1,0:T(8,128)} %wide_in.7.refs_1_, f32[16,2,96,384]{3,2,1,0:T(8,128)} %wide_in.8.refs_2_, ...), custom_call_target="tpu_custom_call" | custom-call | flops 20000000000 | bytes 103809024 | tf_op jit(solution)/shard_map/spectral_forward/pallas_call | solution.py:782
  377.2 6.9 all-to-all-start.3
  384.1 5.4 wide_out.7
  389.5 25.5 %spectral_keep.1 = (bf16[18432,192]{1,0:T(8,128)(2,1)}, bf16[18432,192]{1,0:T(8,128)(2,1)}, bf16[18432,192]{1,0:T(8,128)(2,1)}) custom-call(bf16[18432,192]{1,0:T(8,128)(2,1)} %get-tuple-element.75.entries, bf16[2,192,192]{2,1,0:T(8,128)(2,1)} %copy.59.refs_5_.inner, f32[2,192]{1,0:T(2,128)} %reshape.315.refs_6_.inner_bias, ...), custom_call_target="tpu_custom_call" | custom-call | flops 10000000000 | bytes 25952256 | tf_op jit(solution)/shard_map/spectral_keep/pallas_call | solution.py:795
  415.0 64.7 %all-to-all-done.3 = f32[32,88,384]{2,1,0:T(8,128)} async-done(((f32[32,88,384]{2,1,0:T(8,128)}), f32[32,88,384]{2,1,0:T(8,128)}, u32[]{:S(2)}, u32[]{:S(2)}) %all-to-all-start.3) | async-done | bytes 4325408 | tf_op jit(solution)/shard_map/all_to_all | solution.py:717
  479.7 7.2 all-to-all-start.4
  494.1 78.1 %dense_both_ways.3 = (bf16[2,264,8,768]{3,2,1,0:T(8,128)(2,1)}, f32[8,4,88,384]{3,2,1,0:T(8,128)}, f32[2,88,8,768]{3,2,1,0:T(8,128)}, f32[8,768]{1,0:T(8,128)}, f32[4,768]{1,0:T(4,128)}, /*index=5*/f32[6144,768]{1,0:T(8,128)}) custom-call(bf16[2,264,8,768]{3,2,1,0:T(8,128)(2,1)} %bitcast.82, bf16[2,264,8,768]{3,2,1,0:T(8,128)(2,1)} %bitcast.105, ...), custom_call_target="tpu_custom_call" | custom-call | flops 39862665216 | bytes 17301504 | tf_op jit(solution)/shard_map/dense_both_ways/pallas_call | solution.py:840
  572.2 10.3 all-to-all-done.4
  582.4 7.3 all-to-all-start.5
  589.7 83.7 %dense_both_ways.4 = (bf16[2,264,8,768]{3,2,1,0:T(8,128)(2,1)}, f32[8,4,88,384]{3,2,1,0:T(8,128)}, f32[2,88,8,768]{3,2,1,0:T(8,128)}, f32[8,768]{1,0:T(8,128)}, f32[4,768]{1,0:T(4,128)}, /*index=5*/f32[6144,768]{1,0:T(8,128)}) custom-call(bf16[2,264,8,768]{3,2,1,0:T(8,128)(2,1)} %bitcast.83, ...), custom_call_target="tpu_custom_call", output_to_operand_aliasing={{0}: (13, {})} | custom-call | flops 39862665216 | bytes 17301504 | tf_op jit(solution)/shard_map/dense_both_ways/pallas_call | solution.py:840
  673.4 11.8 all-to-all-done.5
  685.2 6.9 all-to-all-start.6
  692.1 83.7 %dense_both_ways.5 = (bf16[2,264,8,768]{3,2,1,0:T(8,128)(2,1)}, f32[8,4,88,384]{3,2,1,0:T(8,128)}, f32[2,88,8,768]{3,2,1,0:T(8,128)}, f32[8,768]{1,0:T(8,128)}, f32[4,768]{1,0:T(4,128)}, /*index=5*/f32[6144,768]{1,0:T(8,128)}) custom-call(bf16[2,264,8,768]{3,2,1,0:T(8,128)(2,1)} %bitcast.84, ...), custom_call_target="tpu_custom_call", output_to_operand_aliasing={{0}: (13, {})} | custom-call | flops 39862665216 | bytes 17301504 | tf_op jit(solution)/shard_map/dense_both_ways/pallas_call | solution.py:840
  775.9 11.8 all-to-all-done.6
  787.7 6.9 all-to-all-start.7
  794.6 6.2 wide_in.9.refs_0_
  800.8 89.4 %all-to-all-done.7 = f32[32,88,384]{2,1,0:T(8,128)} async-done(((f32[32,88,384]{2,1,0:T(8,128)}), f32[32,88,384]{2,1,0:T(8,128)}, u32[]{:S(2)}, u32[]{:S(2)}) %all-to-all-start.7) | async-done | bytes 4325408 | tf_op jit(solution)/shard_map/all_to_all | solution.py:717
  890.2 7.3 all-to-all-start.8
  897.6 5.5 wide_in.10.refs_1_
  903.1 90.0 %all-to-all-done.8 = f32[32,88,384]{2,1,0:T(8,128)} async-done(((f32[32,88,384]{2,1,0:T(8,128)}), f32[32,88,384]{2,1,0:T(8,128)}, u32[]{:S(2)}, u32[]{:S(2)}) %all-to-all-start.8) | async-done | bytes 4325408 | tf_op jit(solution)/shard_map/all_to_all | solution.py:717
  993.1 5.5 wide_in.11.refs_2_
  998.6 32.1 %spectral_backward.1 = (f32[16,2,96,384]{3,2,1,0:T(8,128)}, f32[16,2,96,384]{3,2,1,0:T(8,128)}, f32[16,2,96,384]{3,2,1,0:T(8,128)}, bf16[18432,192]{1,0:T(8,128)...) custom-call(f32[16,2,96,384]{3,2,1,0:T(8,128)} %wide_in.9.refs_0_, ...), custom_call_target="tpu_custom_call" | custom-call | flops 20000000000 | bytes 103809024 | tf_op jit(solution)/shard_map/spectral_backward/pallas_call | solution.py:807
  1036.2 6.9 all-to-all-start.9
  1043.2 20.6 %filter_grad.1 = (f32[2,192,192]{2,1,0:T(8,128)}, f32[2,192,192]{2,1,0:T(8,128)}) custom-call(bf16[18432,192]{1,0:T(8,128)(2,1)} %get-tuple-element.75.entries, bf16[18432,192]{1,0:T(8,128)(2,1)} %get-tuple-element.100.inner_low, bf16[18432,192]{1,0:T(8,128)(2,1)} %get-tuple-element.76.active, bf16[18432,192]{1,0:T(8,128)(2,1)} %get-tuple-element.101.outer_low), custom_call_target="tpu_custom_call" | custom-call | flops 10000000000 | bytes 25952256 | tf_op jit(solution)/shard_map/filter_grad/pallas_call | solution.py:820
  1066.3 110.0 %filter_sums.1 = f32[640,128]{1,0:T(8,128)} custom-call(f32[640,128]{1,0:T(8,128)} %fusion.own), custom_call_target="tpu_custom_call" | custom-call | tf_op jit(solution)/shard_map/filter_sums/pallas_call | solution.py:682
  1181.8 6.9 all-to-all-start.10
  1188.7 5.6 wide_out.9
  1194.3 11.6 first_norm_backward.3
  1206.0 151.2 %all-to-all-done.10 = f32[32,88,384]{2,1,0:T(8,128)} async-done(((f32[32,88,384]{2,1,0:T(8,128)}), f32[32,88,384]{2,1,0:T(8,128)}, u32[]{:S(2)}, u32[]{:S(2)}) %all-to-all-start.10) | async-done | bytes 4325408 | tf_op jit(solution)/shard_map/all_to_all | solution.py:717
  1357.2 7.0 all-to-all-start.11
  1367.3 11.6 first_norm_backward.4
  1378.9 28.0 %all-gather.2.cloned.1.call-done.expand_in.reduce_in = f32[6144,768]{1,0:T(8,128)} async-done(((f32[192,768]{1,0:T(8,128)}), f32[6144,768]{1,0:T(8,128)}) %all-gather.2.cloned.1.call-update) | async-done | bytes 18874384 | tf_op jit(solution)/shard_map/all_gather | solution.py:657
  1406.9 18.4 %split_gradients.1 = (f32[768,3072]{1,0:T(8,128)}, f32[3072,768]{1,0:T(8,128)}) custom-call(f32[6144,768]{1,0:T(8,128)} %all-gather.2.cloned.1.call-done.expand_in.reduce_in, f32[6144,768]{1,0:T(8,128)} %all-gather.2.cloned.1.call-done.expand_in.reduce_in), custom_call_target="tpu_custom_call" | custom-call | bytes 37748736 | tf_op jit(solution)/shard_map/split_gradients/pallas_call | solution.py:695
  1425.3 40.8 %all-to-all-done.11 = f32[32,88,384]{2,1,0:T(8,128)} async-done(((f32[32,88,384]{2,1,0:T(8,128)}), f32[32,88,384]{2,1,0:T(8,128)}, u32[]{:S(2)}, u32[]{:S(2)}) %all-to-all-start.11) | async-done | bytes 4325408 | tf_op jit(solution)/shard_map/all_to_all | solution.py:717
  1466.1 11.6 first_norm_backward.5
  1479.2 28.7 %small_sums.1 = f32[56,128]{1,0:T(8,128)} custom-call(f32[56,128]{1,0:T(8,128)} %pad.9.own), custom_call_target="tpu_custom_call" | custom-call | tf_op jit(solution)/shard_map/small_sums/pallas_call | solution.py:663
  (96 shorter events, 43.3 us)
Async XLA Ops:
  23.5 101.9 %all-to-all-start = ((f32[32,88,384]{2,1,0:T(8,128)}), f32[32,88,384]{2,1,0:T(8,128)}, u32[]{:S(2)}, u32[]{:S(2)}) async-start(f32[32,88,384]{2,1,0:T(8,128)} %bitcast.91), calls=%async_computation | async-start | bytes 8650752 | tf_op jit(solution)/shard_map/all_to_all | solution.py:717
  125.4 102.5 %all-to-all-start.1 = ((f32[32,88,384]{2,1,0:T(8,128)}), f32[32,88,384]{2,1,0:T(8,128)}, u32[]{:S(2)}, u32[]{:S(2)}) async-start(f32[32,88,384]{2,1,0:T(8,128)} %bitcast.90), calls=%async_computation.1 | async-start | bytes 8650752 | tf_op jit(solution)/shard_map/all_to_all | solution.py:717
  142.3 92.5 %copy-start.3 = (bf16[2,2,96,96]{3,2,1,0:T(8,128)(2,1)S(1)}, bf16[2,2,96,96]{3,2,1,0:T(8,128)(2,1)}, u32[]{:S(2)}) copy-start(bf16[2,2,96,96]{3,2,1,0:T(8,128)(2,1)} %param.37) | copy-start | bytes 221188
  142.3 92.6 %copy-start.4 = (bf16[2,2,96,96]{3,2,1,0:T(8,128)(2,1)S(1)}, bf16[2,2,96,96]{3,2,1,0:T(8,128)(2,1)}, u32[]{:S(2)}) copy-start(bf16[2,2,96,96]{3,2,1,0:T(8,128)(2,1)} %param.39) | copy-start | bytes 221188
  227.9 9.5 copy-start.14
  227.9 10.1 copy-start.15
  227.9 102.5 %all-to-all-start.2 = ((f32[32,88,384]{2,1,0:T(8,128)}), f32[32,88,384]{2,1,0:T(8,128)}, u32[]{:S(2)}, u32[]{:S(2)}) async-start(f32[32,88,384]{2,1,0:T(8,128)} %bitcast.89), calls=%async_computation.2 | async-start | bytes 8650752 | tf_op jit(solution)/shard_map/all_to_all | solution.py:717
  235.6 9.5 copy-start.1
  236.5 8.5 copy-start.2
  377.2 102.5 %all-to-all-start.3 = ((f32[32,88,384]{2,1,0:T(8,128)}), f32[32,88,384]{2,1,0:T(8,128)}, u32[]{:S(2)}, u32[]{:S(2)}) async-start(f32[32,88,384]{2,1,0:T(8,128)} %bitcast.97), calls=%async_computation.3 | async-start | bytes 8650752 | tf_op jit(solution)/shard_map/all_to_all | solution.py:717
  415.0 71.9 %copy-start.11 = (f32[768]{0:T(1024)S(1)}, f32[768]{0:T(1024)}, u32[]{:S(2)}) copy-start(f32[768]{0:T(1024)} %param.41) | copy-start | bytes 9220
  415.0 72.5 %copy-start.12 = (f32[768]{0:T(1024)S(1)}, f32[768]{0:T(1024)}, u32[]{:S(2)}) copy-start(f32[768]{0:T(1024)} %param.42) | copy-start | bytes 9220
  415.0 73.1 %copy-start.13 = (f32[768]{0:T(1024)S(1)}, f32[768]{0:T(1024)}, u32[]{:S(2)}) copy-start(f32[768]{0:T(1024)} %param.46) | copy-start | bytes 9220
  479.7 102.7 %all-to-all-start.4 = ((f32[32,88,384]{2,1,0:T(8,128)}), f32[32,88,384]{2,1,0:T(8,128)}, u32[]{:S(2)}, u32[]{:S(2)}) async-start(f32[32,88,384]{2,1,0:T(8,128)} %bitcast.94), calls=%async_computation.4 | async-start | bytes 8650752 | tf_op jit(solution)/shard_map/all_to_all | solution.py:717
  582.4 102.8 %all-to-all-start.5 = ((f32[32,88,384]{2,1,0:T(8,128)}), f32[32,88,384]{2,1,0:T(8,128)}, u32[]{:S(2)}, u32[]{:S(2)}) async-start(f32[32,88,384]{2,1,0:T(8,128)} %bitcast.96), calls=%async_computation.5 | async-start | bytes 8650752 | tf_op jit(solution)/shard_map/all_to_all | solution.py:717
  685.2 102.5 %all-to-all-start.6 = ((f32[32,88,384]{2,1,0:T(8,128)}), f32[32,88,384]{2,1,0:T(8,128)}, u32[]{:S(2)}, u32[]{:S(2)}) async-start(f32[32,88,384]{2,1,0:T(8,128)} %bitcast.99), calls=%async_computation.6 | async-start | bytes 8650752 | tf_op jit(solution)/shard_map/all_to_all | solution.py:717
  692.1 306.5 %reduce-scatter.3.cloned.1.call-start = ((), (), s32[]{:S(2)}) async-start(), calls=%async_computation.14 | async-start | bytes 23592960 | tf_op jit(solution)/shard_map/reduce_scatter | solution.py:654
  787.7 102.5 %all-to-all-start.7 = ((f32[32,88,384]{2,1,0:T(8,128)}), f32[32,88,384]{2,1,0:T(8,128)}, u32[]{:S(2)}, u32[]{:S(2)}) async-start(f32[32,88,384]{2,1,0:T(8,128)} %bitcast.98), calls=%async_computation.7 | async-start | bytes 8650752 | tf_op jit(solution)/shard_map/all_to_all | solution.py:717
  890.2 102.9 %all-to-all-start.8 = ((f32[32,88,384]{2,1,0:T(8,128)}), f32[32,88,384]{2,1,0:T(8,128)}, u32[]{:S(2)}, u32[]{:S(2)}) async-start(f32[32,88,384]{2,1,0:T(8,128)} %bitcast.100), calls=%async_computation.8 | async-start | bytes 8650752 | tf_op jit(solution)/shard_map/all_to_all | solution.py:717
  897.6 284.2 %reduce-scatter.5.cloned.1.call-start = ((), (), s32[]{:S(2)}) async-start(), calls=%async_computation.15 | async-start | bytes 5308416 | tf_op jit(solution)/shard_map/reduce_scatter | solution.py:654
  1036.2 145.5 %all-to-all-start.9 = ((f32[32,88,384]{2,1,0:T(8,128)}), f32[32,88,384]{2,1,0:T(8,128)}, u32[]{:S(2)}, u32[]{:S(2)}) async-start(f32[32,88,384]{2,1,0:T(8,128)} %bitcast.93), calls=%async_computation.9 | async-start | bytes 8650752 | tf_op jit(solution)/shard_map/all_to_all | solution.py:717
  1043.1 363.8 %all-gather.2.cloned.1.call-start = ((), (), s32[]{:S(2)}) async-start(), calls=%async_computation.16 | async-start | bytes 19464192 | tf_op jit(solution)/shard_map/all_gather | solution.py:657
  1043.2 22.2 %copy-start.17 = (f32[2,192]{1,0:T(2,128)S(1)}, f32[2,192]{1,0:T(2,128)}, u32[]{:S(2)}) copy-start(f32[2,192]{1,0:T(2,128)} %get-tuple-element.103) | copy-start | bytes 4612
  1043.2 22.3 %copy-start.16 = (f32[2,192]{1,0:T(2,128)S(1)}, f32[2,192]{1,0:T(2,128)}, u32[]{:S(2)}) copy-start(f32[2,192]{1,0:T(2,128)} %get-tuple-element.105) | copy-start | bytes 4612
  1181.8 175.4 %all-to-all-start.10 = ((f32[32,88,384]{2,1,0:T(8,128)}), f32[32,88,384]{2,1,0:T(8,128)}, u32[]{:S(2)}, u32[]{:S(2)}) async-start(f32[32,88,384]{2,1,0:T(8,128)} %bitcast.95), calls=%async_computation.10 | async-start | bytes 8650752 | tf_op jit(solution)/shard_map/all_to_all | solution.py:717
  1205.9 158.3 %copy-start.5 = (f32[4,768]{1,0:T(4,128)S(1)}, f32[4,768]{1,0:T(4,128)}, u32[]{:S(2)}) copy-start(f32[4,768]{1,0:T(4,128)} %get-tuple-element.122) | copy-start | bytes 36868
  1205.9 158.3 %copy-start.6 = (f32[4,768]{1,0:T(4,128)S(1)}, f32[4,768]{1,0:T(4,128)}, u32[]{:S(2)}) copy-start(f32[4,768]{1,0:T(4,128)} %get-tuple-element.123) | copy-start | bytes 36868
  1205.9 158.3 %copy-start.7 = (f32[4,768]{1,0:T(4,128)S(1)}, f32[4,768]{1,0:T(4,128)}, u32[]{:S(2)}) copy-start(f32[4,768]{1,0:T(4,128)} %get-tuple-element.124) | copy-start | bytes 36868
  1206.0 158.4 %copy-start.8 = (f32[8,768]{1,0:T(8,128)S(1)}, f32[8,768]{1,0:T(8,128)}, u32[]{:S(2)}) copy-start(f32[8,768]{1,0:T(8,128)} %get-tuple-element.119) | copy-start | bytes 73732
  1206.0 158.4 %copy-start.9 = (f32[8,768]{1,0:T(8,128)S(1)}, f32[8,768]{1,0:T(8,128)}, u32[]{:S(2)}) copy-start(f32[8,768]{1,0:T(8,128)} %get-tuple-element.120) | copy-start | bytes 73732
  1206.0 158.4 %copy-start.10 = (f32[8,768]{1,0:T(8,128)S(1)}, f32[8,768]{1,0:T(8,128)}, u32[]{:S(2)}) copy-start(f32[8,768]{1,0:T(8,128)} %get-tuple-element.121) | copy-start | bytes 73732
  1206.0 158.4 %copy-start = (f32[640,128]{1,0:T(8,128)S(1)}, f32[640,128]{1,0:T(8,128)}, u32[]{:S(2)}) copy-start(f32[640,128]{1,0:T(8,128)} %filter_sums.1) | copy-start | bytes 983044
  1357.2 108.9 %all-to-all-start.11 = ((f32[32,88,384]{2,1,0:T(8,128)}), f32[32,88,384]{2,1,0:T(8,128)}, u32[]{:S(2)}, u32[]{:S(2)}) async-start(f32[32,88,384]{2,1,0:T(8,128)} %bitcast.92), calls=%async_computation.11 | async-start | bytes 8650752 | tf_op jit(solution)/shard_map/all_to_all | solution.py:717
Sparse Core Ops, SparseCore 0:
  787.8 208.2 reduce-scatter.2
  1000.2 148.6 reduce-scatter.4
  1181.9 224.9 all-gather.1

commit v6 on v4

--- a/solution.py
+++ b/solution.py
@@ -53,25 +53,52 @@
     return scale * (grad - first - normal * second)
 
 
-def pack(sides, out, width):
+def pack(sides, outs, width, step):
     turned = [jnp.swapaxes(s, 0, 1) for s in sides]
-    for c in range(out.shape[1]):
-        out[:, c] = jnp.concatenate([t[:, :, c * width : (c + 1) * width] for t in turned], axis=2)
-
-
-def unpack(ref, half, width):
-    parts = [ref[:, c, :, half * width : (half + 1) * width] for c in range(ref.shape[1])]
+    cut = width // len(outs)
+
+    def lanes_of(c, g):
+        start = c * width + g * cut
+        return jnp.concatenate([t[:, :, start : start + cut] for t in turned], axis=2)
+
+    for g, out in enumerate(outs):
+        values = [lanes_of(c, g) for c in range(out.shape[1])]
+        if len(outs) == 1:
+            for c, v in enumerate(values):
+                out[:, c] = v
+            continue
+
+        @pl.when(lax.rem(step, 2) == 0)
+        def _():
+            for c, v in enumerate(values):
+                out[:, c] = jnp.concatenate([v, v], axis=2)
+
+        @pl.when(lax.rem(step, 2) == 1)
+        def _():
+            for c, v in enumerate(values):
+                out[:, c] = jnp.concatenate([out[:, c, :, : PAIR * cut], v], axis=2)
+
+
+def unpack(refs, half, width, step):
+    cut = width // len(refs)
+    parts = []
+    for c in range(refs[0].shape[1]):
+        for ref in refs:
+            part = ref[:, c, :, half * cut : (half + 1) * cut]
+            if len(refs) > 1:
+                later = (PAIR + half) * cut
+                part = jnp.where(lax.rem(step, 2) == 1, ref[:, c, :, later : later + cut], part)
+            parts.append(part)
     return jnp.swapaxes(jnp.concatenate(parts, axis=2) if len(parts) > 1 else parts[0], 0, 1)
 
 
-def first_kernel(states, mask, gain, shift, out):
-    width = out.shape[3] // PAIR
+def first_kernel(width, states, mask, gain, shift, *outs):
     sides = []
     for half in range(PAIR):
         inside = mask[half][..., :1]
         normal, _ = standardize(states[half].astype(f32) * inside)
         sides.append(inside * (normal * gain[...] + shift[...]))
-    pack(sides, out, width)
+    pack(sides, outs, width, pl.program_id(0))
 
 
 def table_dot(table, x):
@@ -96,20 +123,72 @@
         held[n, 1] = y[BINS:]
 
 
-def wide_out_kernel(cols_here, factor, held, table, block):
+def wide_out_kernel(cols_here, factor, *refs):
+    held, (table, block) = refs[:-2], refs[-2:]
     groups, rows = block.shape[1], block.shape[2] // cols_here
+    cut = held[0].shape[3] // PAIR
     for n in range(block.shape[0] * rows):
         r, j = divmod(n, rows)
-        x = jnp.concatenate([held[n, 0], held[n, 1]], axis=0).astype(bf16)
-        plane = dot(table[...], x) * factor
+        x = [jnp.concatenate([part[n, 0], part[n, 1]], axis=0) for part in held]
+        if len(x) > 1:
+            x = [part[:, h * cut : (h + 1) * cut] for h in range(PAIR) for part in x]
+            x = jnp.concatenate(x, axis=1)
+        else:
+            x = x[0]
+        plane = dot(table[...], x.astype(bf16)) * factor
         for c in range(groups):
             block[r, c, j * cols_here : (j + 1) * cols_here, :] = plane[
                 c * cols_here : (c + 1) * cols_here, :
             ]
 
 
-def bins_in(held, table, width, fine):
+def wide_in_split_kernel(cols_here, fine, block, table, held, wide, natural):
+    groups, half = block.shape[1], block.shape[3] // 2
+    rows = natural.shape[2] // cols_here
+    for r in range(block.shape[0]):
+        for c in range(groups):
+            for s in range(natural.shape[2] // 8):
+                natural[r, c, s * 8 : s * 8 + 8, :] = block[
+                    r, c, (s // 2) * 8 : (s // 2) * 8 + 8, (s % 2) * half : (s % 2 + 1) * half
+                ]
+        for j in range(rows):
+            n = r * rows + j
+            for c in range(groups):
+                wide[n, c * cols_here : (c + 1) * cols_here, :] = natural[
+                    r, c, j * cols_here : (j + 1) * cols_here, :
+                ]
+            x = wide[n]
+            y = table_dot(table, x) if fine else dot(table[...], x.astype(bf16))
+            held[n, 0] = y[:BINS]
+            held[n, 1] = y[BINS:]
+
+
+def wide_out_split_kernel(cols_here, factor, held, table, block, natural):
+    groups = block.shape[1]
+    rows = natural.shape[2] // cols_here
+    last = natural.shape[2] // 8 - 1
+    for r in range(block.shape[0]):
+        for j in range(rows):
+            n = r * rows + j
+            x = jnp.concatenate([held[n, 0], held[n, 1]], axis=0).astype(bf16)
+            plane = dot(table[...], x) * factor
+            for c in range(groups):
+                natural[r, c, j * cols_here : (j + 1) * cols_here, :] = plane[
+                    c * cols_here : (c + 1) * cols_here, :
+                ]
+        for c in range(groups):
+            for m in range(block.shape[2] // 8):
+                sides = [natural[r, c, at * 8 : at * 8 + 8, :] for at in (2 * m, min(2 * m + 1, last))]
+                block[r, c, m * 8 : m * 8 + 8, :] = jnp.concatenate(sides, axis=1)
+
+
+def bins_in(held, table, width, group, fine):
     kind = f32 if fine else bf16
+
+    def lane(part, h):
+        whole_width = part.shape[-1] // PAIR
+        return h * whole_width + (group * width if whole_width > width else 0)
+
     turned = [
         [jnp.swapaxes(part[:, side], 0, 1).astype(kind) for part in held] for side in range(2)
     ]
@@ -117,7 +196,7 @@
     for k in range(GROUP):
         x = jnp.concatenate(
             [
-                part[k][:, h * width : (h + 1) * width]
+                part[k][:, lane(part, h) : lane(part, h) + width]
                 for side in turned
                 for h in range(PAIR)
                 for part in side
@@ -169,13 +248,13 @@
     return (v * (0.5 * (1.0 + lax.erf(v * math.sqrt(0.5))))).astype(bf16)
 
 
-def spectral_forward_kernel(factor, *refs):
+def spectral_forward_kernel(factor, group, *refs):
     held, refs = refs[:PARTS], refs[PARTS:]
     table_down, table_up, inner, inner_bias, outer, outer_bias = refs[:6]
     given, entries = refs[6 : 6 + PARTS], refs[6 + PARTS]
     width = inner.shape[2]
     tall = table_up.shape[0] // 2
-    spec = bins_in(held, table_down, width, True)
+    spec = bins_in(held, table_down, width, group, True)
     low = jnp.concatenate([(s * factor).astype(bf16) for s in spec], axis=0)
     entries[...] = low
     act = jnp.concatenate([gelu_low(v) for v in activate(low, inner, inner_bias, tall)], axis=0)
@@ -200,7 +279,7 @@
         damp[n * tall : (n + 1) * tall, :] = (t * t).astype(bf16)
 
 
-def spectral_backward_kernel(factor, *refs):
+def spectral_backward_kernel(factor, group, *refs):
     held, refs = refs[:PARTS], refs[PARTS:]
     table_down, table_up, inner_t, outer_t, slope, damp = refs[:6]
     given, refs = refs[6 : 6 + PARTS], refs[6 + PARTS :]
@@ -213,7 +292,7 @@
         for ref in (inner_bias_grad, outer_bias_grad):
             ref[...] = jnp.zeros_like(ref)
 
-    spec = bins_in(held, table_down, width, False)
+    spec = bins_in(held, table_down, width, group, False)
     grads = []
     sums = [0.0, 0.0]
     for k in range(GROUP):
@@ -259,23 +338,24 @@
         grad[1] += dot_tn(before[...], jnp.concatenate(turned, axis=0))
 
 
-def dense_kernel(steps, slabs, first_part, *refs):
+def dense_kernel(steps, slabs, width, first_part, arrays, *refs):
+    spat, refs = refs[:arrays], refs[arrays:]
     (
-        states, cot, spat, mask, first_gain, first_shift, later_gain, later_shift,
+        states, cot, mask, first_gain, first_shift, later_gain, later_shift,
         expand_bias, reduce_bias, expand_hbm, reduce_hbm,
-    ) = refs[:12]
-    refs = refs[12:]
+    ) = refs[:11]
+    refs = refs[11:]
     if not first_part:
         grads_before = refs[0]
         refs = refs[2:]
-    result, back, later_grad, sums, expand_bias_grad, grads_hbm = refs[:6]
+    back, refs = refs[:arrays], refs[arrays:]
+    result, later_grad, sums, expand_bias_grad, grads_hbm = refs[:5]
     (
         expand, reduce, expand_grad, reduce_grad, mixed, normed, low_out, branch, grad_n,
         hidden_all, grad_all, copy_sem,
-    ) = refs[6:]
+    ) = refs[5:]
     step = pl.program_id(0)
     chans = states.shape[3]
-    width = spat.shape[3] // PAIR
     side_tokens = states.shape[1] * states.shape[2]
     slab = expand.shape[2]
     tokens = mixed.shape[0]
@@ -319,7 +399,7 @@
             lower = inside * states[half].astype(f32)
             first, _ = standardize(lower)
             filter_in = first * first_gain[...] + first_shift[...]
-            full = lower + inside * (unpack(spat, half, width) + filter_in)
+            full = lower + inside * (unpack(spat, half, width, step) + filter_in)
             later, _ = standardize(full)
             full = full.reshape(side_tokens, chans)
             mixed[at, :] = full
@@ -380,7 +460,7 @@
             sides.append(inside * g.reshape(square))
             later_grad[half] = sides[-1]
             result[half] = (inside * branch[at, :].reshape(square)).astype(bf16)
-        pack(sides, back, width)
+        pack(sides, back, width, step - steps - slabs)
 
     @pl.when(step == pl.num_programs(0) - 1)
     def _():
@@ -394,9 +474,9 @@
             c.wait()
 
 
-def last_kernel(states, later_grad, spat, mask, gain, *refs):
+def last_kernel(width, arrays, *refs):
+    spat, (states, later_grad, mask, gain) = refs[:arrays], refs[arrays : arrays + 4]
     out, sums = refs[-2:]
-    width = spat.shape[3] // PAIR
     chans = states.shape[3]
 
     @pl.when(pl.program_id(0) == 0)
@@ -407,7 +487,7 @@
         inside = mask[half][..., :1]
         normal, scale = standardize(inside * states[half].astype(f32))
         grad_mixed = later_grad[half]
-        grad = inside * (grad_mixed + unpack(spat, half, width))
+        grad = inside * (grad_mixed + unpack(spat, half, width, pl.program_id(0)))
         flat = (-1, chans)
         sums[0:1, :] += jnp.sum((grad * normal).reshape(flat), axis=0, keepdims=True)
         sums[1:2, :] += jnp.sum(grad.reshape(flat), axis=0, keepdims=True)
@@ -644,6 +724,29 @@
             (ranks, groups, step_pixels, lanes), lambda i: (0, 0, where(i), 0), **buffers
         )
 
+    blocks_here = width // BS
+    split = blocks_here > 1 and steps > 1 and (2 * PAIR * BS) % 128 == 0
+    parties = blocks_here if split else 1
+    cut = width // parties
+    split_rows = 8 * (-(-steps // 2))
+
+    def arrays_of(q):
+        return parties if q == 0 else 1
+
+    def message_specs(q, where):
+        if arrays_of(q) == 1:
+            return [packed_spec(where)]
+        return [
+            pl.BlockSpec(
+                (ranks, groups, step_pixels, 2 * PAIR * cut), lambda i: (0, 0, where(i) // 2, 0)
+            )
+        ] * parties
+
+    def message_shapes(q):
+        if arrays_of(q) == 1:
+            return [packed_shape]
+        return [shape((ranks, groups, split_rows, 2 * PAIR * cut), f32)] * parties
+
     same = lambda i: i
     token_shape = shape((PAIR, pairs * cols_here, frames, chans), bf16)
     packed_shape = shape((ranks, groups, pixels, lanes), f32)
@@ -711,19 +814,20 @@
     def behind(v, *after):
         return lax.optimization_barrier((v,) + after)[0] if after else v
 
-    def exchange(v, *after):
-        v = v.reshape(devices, pixels, lanes)
-        v = behind(v, *after)
-        v = lax.all_to_all(v, ("rows", "cols"), 0, 0, tiled=True)
-        return v.reshape(ranks, groups, pixels, lanes)
+    def exchange(v):
+        sent = v.reshape((devices,) + v.shape[2:])
+        return lax.all_to_all(sent, ("rows", "cols"), 0, 0, tiled=True).reshape(v.shape)
+
+    def tie(*values):
+        return lax.optimization_barrier(values)
 
     def first_norm(q):
         return call(
-            first_kernel,
+            functools.partial(first_kernel, width),
             steps,
             [token_spec(q, same), token_spec(q, same, 128), chan_row, chan_row],
-            packed_spec(same),
-            packed_shape,
+            message_specs(q, same),
+            message_shapes(q),
             "first_norm",
             nbytes=2 * message,
         )(states_in, mask, row(first_gain), row(first_shift))
@@ -736,7 +840,10 @@
         high = t.astype(jnp.bfloat16)
         return jnp.asarray(np.concatenate([high, (t - high.astype(np.float64)).astype(jnp.bfloat16)]))
 
-    inner_full, outer_full = spread(filter_inner), spread(filter_outer)
+    def mixes(weight):
+        return [weight[:, g] for g in range(parties)] if split else [spread(weight)]
+
+    inner_full, outer_full = mixes(filter_inner), mixes(filter_outer)
     turn = lambda t: jnp.swapaxes(t, 1, 2)
     bin_steps = BINS // GROUP
     group_rows = GROUP * 2 * height
@@ -745,53 +852,94 @@
     held_row = pl.BlockSpec((at_once * rows, 2, BINS, lanes), lambda i: (i, 0, 0, 0))
     held_bins = pl.BlockSpec((short, 2, GROUP, lanes), lambda i: (0, 0, i, 0))
     field = pl.BlockSpec((at_once, groups, pixels, lanes), lambda i: (i, 0, 0, 0))
-    kept = pl.BlockSpec((group_rows, width), lambda i: (i, 0))
-    kept_shape = shape((bin_steps * group_rows, width), bf16)
-    mix_spec = whole((2, width, width))
-    bias_spec = whole((2, width))
+    kept = pl.BlockSpec((group_rows, cut), lambda i: (i, 0))
+    kept_shape = shape((bin_steps * group_rows, cut), bf16)
+    mix_spec = whole((2, cut, cut))
+    bias_spec = whole((2, cut))
+
+    def held_of(last, by_row):
+        if by_row:
+            return pl.BlockSpec((at_once * rows, 2, BINS, last), lambda i: (i, 0, 0, 0))
+        return pl.BlockSpec((short, 2, GROUP, last), lambda i: (0, 0, i, 0))
+
+    cut_shape = shape((short, 2, BINS, PAIR * cut), f32)
+    split_field = pl.BlockSpec(
+        (at_once, groups, split_rows, 2 * PAIR * cut), lambda i: (i, 0, 0, 0)
+    )
+    natural = pltpu.VMEM((at_once, groups, pixels, PAIR * cut), f32)
+    cut_in = [held_of(PAIR * cut if split else lanes, False)] + [held_bins] * (PARTS - 1)
+    cut_out = [held_of(PAIR * cut, False)] * PARTS
     up_spec = whole((2 * height, 2 * height))
 
     def wide_in(v, table, fine):
+        divided = v.shape != packed_shape.shape
         return call(
-            functools.partial(wide_in_kernel, cols_here, fine),
+            functools.partial(wide_in_split_kernel if divided else wide_in_kernel, cols_here, fine),
             ranks // at_once,
-            [field, whole(table.shape)],
-            held_row,
-            held_shape,
+            [split_field if divided else field, whole(table.shape)],
+            held_of(PAIR * cut, True) if divided else held_row,
+            cut_shape if divided else held_shape,
             "wide_in",
             nbytes=2 * message,
-            scratch=[pltpu.VMEM((at_once * rows, breadth, lanes), f32)],
+            scratch=[pltpu.VMEM((at_once * rows, breadth, PAIR * cut), f32), natural]
+            if divided
+            else [pltpu.VMEM((at_once * rows, breadth, lanes), f32)],
         )(v, table)
 
-    def wide_out(v, table):
+    def wide_out(parts, table):
         return call(
             functools.partial(wide_out_kernel, cols_here, factor),
             ranks // at_once,
-            [held_row, whole(table.shape)],
+            [held_of(PAIR * cut, True)] * len(parts) + [whole(table.shape)],
             field,
             packed_shape,
             "wide_out",
             nbytes=2 * message,
-        )(v, table)
-
-    forward_mix = (inner_full, bias_rows(inner_bias), outer_full, bias_rows(outer_bias))
+        )(*parts, table)
+
+    def wide_out_split(part, table):
+        return call(
+            functools.partial(wide_out_split_kernel, cols_here, factor),
+            ranks // at_once,
+            [held_of(PAIR * cut, True), whole(table.shape)],
+            split_field,
+            message_shapes(0)[0],
+            "wide_out",
+            nbytes=2 * message,
+            scratch=[natural],
+        )(part, table)
+
+    def first_message(given, table):
+        return wide_out_split(given[0], table) if split else wide_out([given[0]], table)
+
+    def messages_out(given, table, first):
+        first = first + [first_message(v, table) for v in given[len(first) :]]
+        return first + [wide_out([v[q] for v in given], table) for q in range(1, PARTS)]
+
+    def of_group(v, g):
+        return bias_rows(v)[:, g * cut : (g + 1) * cut]
+
+    forward_mix = [
+        (inner_full[g], of_group(inner_bias, g), outer_full[g], of_group(outer_bias, g))
+        for g in range(parties)
+    ]
     forward_specs = [mix_spec, bias_spec, mix_spec, bias_spec]
 
-    def spectral_forward(held):
+    def spectral_forward(g, held):
         table = fine_table(down)
         outs = call(
-            functools.partial(spectral_forward_kernel, factor),
+            functools.partial(spectral_forward_kernel, factor, g),
             bin_steps,
-            [held_bins] * PARTS + [whole(table.shape), up_spec] + forward_specs,
-            [held_bins] * PARTS + [kept],
-            [held_shape] * PARTS + [kept_shape],
+            cut_in + [whole(table.shape), up_spec] + forward_specs,
+            cut_out + [kept],
+            [cut_shape] * PARTS + [kept_shape],
             "spectral_forward",
             flops=20 * 10**9,
-            nbytes=8 * PARTS * message,
-        )(*held, table, as_table(up), *forward_mix)
+            nbytes=8 * PARTS * message // parties,
+        )(*held, table, as_table(up), *forward_mix[g])
         return outs[:PARTS], outs[PARTS]
 
-    def spectral_keep(entries):
+    def spectral_keep(g, entries):
         return call(
             functools.partial(spectral_keep_kernel, height),
             bin_steps,
@@ -800,20 +948,20 @@
             [kept_shape] * 3,
             "spectral_keep",
             flops=10 * 10**9,
-            nbytes=2 * PARTS * message,
-        )(entries, *forward_mix)
-
-    def spectral_backward(held, slope, damp):
+            nbytes=2 * PARTS * message // parties,
+        )(entries, *forward_mix[g])
+
+    def spectral_backward(g, held, slope, damp):
         outs = call(
-            functools.partial(spectral_backward_kernel, factor),
+            functools.partial(spectral_backward_kernel, factor, g),
             bin_steps,
-            [held_bins] * PARTS + [up_spec, up_spec, mix_spec, mix_spec] + [kept] * 2,
-            [held_bins] * PARTS + [kept, bias_spec] * 2,
-            [held_shape] * PARTS + [kept_shape, shape((2, width), f32)] * 2,
+            cut_in + [up_spec, up_spec, mix_spec, mix_spec] + [kept] * 2,
+            cut_out + [kept, bias_spec] * 2,
+            [cut_shape] * PARTS + [kept_shape, shape((2, cut), f32)] * 2,
             "spectral_backward",
             flops=20 * 10**9,
-            nbytes=8 * PARTS * message,
-        )(*held, as_table(down), as_table(up), turn(inner_full), turn(outer_full), slope, damp)
+            nbytes=8 * PARTS * message // parties,
+        )(*held, as_table(down), as_table(up), turn(inner_full[g]), turn(outer_full[g]), slope, damp)
         return outs[:PARTS], outs[PARTS:]
 
     def filter_grad(*operands):
@@ -822,7 +970,7 @@
             bin_steps,
             [kept] * 4,
             [mix_spec] * 2,
-            [shape((2, width, width), f32)] * 2,
+            [shape((2, cut, cut), f32)] * 2,
             "filter_grad",
             flops=10 * 10**9,
             nbytes=2 * PARTS * message,
@@ -838,25 +986,25 @@
     def dense(q, spatial, before):
         grads_before = () if q == 0 else before
         return call(
-            functools.partial(dense_kernel, steps, slabs, q == 0),
+            functools.partial(dense_kernel, steps, slabs, width, q == 0, arrays_of(q)),
             dense_steps,
-            [token_spec(q, enter), token_spec(q, enter), packed_spec(enter)]
-            + [token_spec(q, either, 128)]
+            message_specs(q, enter)
+            + [token_spec(q, enter), token_spec(q, enter), token_spec(q, either, 128)]
             + [chan_row] * 4
             + [pl.BlockSpec((1, slab), lambda i: (0, jnp.clip(i - steps, 0, slabs - 1)))]
             + [chan_row]
             + [anywhere] * (2 + len(grads_before)),
-            [
+            message_specs(q, leave)
+            + [
                 token_spec(q, leave),
-                packed_spec(leave),
                 token_spec(0, leave),
                 whole((8, chans)),
                 whole((slabs, slab)),
                 anywhere,
             ],
-            [
+            message_shapes(q)
+            + [
                 token_shape,
-                packed_shape,
                 shape((PAIR, pixels, frames, chans), f32),
                 shape((8, chans), f32),
                 shape((slabs, slab), f32),
@@ -879,11 +1027,11 @@
                 pltpu.VMEM((tokens, slab), bf16),
                 pltpu.SemaphoreType.DMA((2 * slabs + 2,)),
             ],
-            input_output_aliases={} if q == 0 else {13: 0},
+            input_output_aliases={} if q == 0 else {13: 1},
         )(
+            *spatial,
             states_in,
             cot_in,
-            spatial,
             mask,
             row(first_gain),
             row(first_shift),
@@ -899,9 +1047,10 @@
     def last_norm(q, later_grad, spatial, before):
         given = () if q == 0 else (before,)
         return call(
-            last_kernel,
+            functools.partial(last_kernel, width, arrays_of(q)),
             steps,
-            [token_spec(q, same), token_spec(0, same), packed_spec(same), token_spec(q, same, 128)]
+            message_specs(q, same)
+            + [token_spec(q, same), token_spec(0, same), token_spec(q, same, 128)]
             + [chan_row]
             + [anywhere] * len(given),
             [token_spec(q, same), whole((8, chans))],
@@ -909,59 +1058,114 @@
             "first_norm_backward",
             nbytes=4 * message,
             input_output_aliases={} if q == 0 else {5: 0},
-        )(states_in, later_grad, spatial, mask, row(first_gain), *given)
+        )(*spatial, states_in, later_grad, mask, row(first_gain), *given)
 
     every = range(PARTS)
-    got = []
+
+    def send(made, got):
+        if got:
+            made, got[-1] = tie(made, got[-1])
+        got.append(exchange(made))
+
+    made = [v for q in (*every[1:], 0) for v in first_norm(q)]
+    got, held = [], []
+    for n, v in enumerate(made):
+        if n > 1:
+            v, held[-1] = tie(v, held[-1])
+        send(v, got)
+        if n > 0:
+            held.append(wide_in(got[-2], fine_table(plain), True))
+    held.append(wide_in(got[-1], fine_table(plain), True))
+    rest, first = held[: PARTS - 1], held[PARTS - 1 :]
+    done = [spectral_forward(g, [first[g]] + rest) for g in range(parties)]
+    entries = [v[1] for v in done]
+    made = messages_out([v[0] for v in done], as_table(doubled.T), [])
+    keeps = [list(spectral_keep(g, entries[g])) for g in range(parties)]
+
+    spatial = got[-1:]
+    for n in range(parties):
+        send(made[n], spatial)
+    for keep in keeps:
+        keep[0], made[parties] = tie(keep[0], made[parties])
+    spatial = spatial[1:]
+    backs, later_grads, sums, expand_bias_grad, before = [], [], 0.0, 0.0, ()
     for q in every:
-        got.append(exchange(first_norm(q), *got[-1:]))
-    held = [wide_in(v, fine_table(plain), True) for v in got]
-    given, entries = spectral_forward(held)
-
-    made = [wide_out(v, as_table(doubled.T)) for v in given]
-    spatial, backs, later_grads, sums, expand_bias_grad, before = [], [], [], 0.0, 0.0, ()
-    active, slope, damp = spectral_keep(entries)
-    for q in range(PARTS + 1):
-        if q < PARTS:
-            beside = (active, *made[1:2]) if q == 1 else ()
-            spatial.append(exchange(made[q], *spatial[-1:], *backs[-1:], *beside))
-        if q > 0:
-            result, back, kept_grad, part, bias_part, grads = dense(q - 1, spatial[q - 1], before)
-            before = (grads, result)
-            backs.append(back)
-            later_grads.append(kept_grad)
-            sums, expand_bias_grad = sums + part, expand_bias_grad + bias_part
-    got, held = spatial[-1:], []
+        if q + 1 < PARTS:
+            if backs:
+                made[parties + q], backs[-1][-1] = tie(made[parties + q], backs[-1][-1])
+            send(made[parties + q], spatial)
+        received = spatial[:parties] if q == 0 else spatial[parties + q - 1 : parties + q]
+        if q + 1 == PARTS:
+            backs[-1][-1], spatial[-1] = tie(backs[-1][-1], spatial[-1])
+            got = [exchange(backs[1][0])]
+            received = spatial[-1:]
+        outs = dense(q, received, before)
+        backs.append(list(outs[: arrays_of(q)]))
+        result, kept_grad, part, bias_part, grads = outs[arrays_of(q) :]
+        before = (grads, result)
+        later_grads.append(kept_grad)
+        sums, expand_bias_grad = sums + part, expand_bias_grad + bias_part
+    grads, got[0] = tie(grads, got[0])
+    grads = scatter(grads, "cols")
+    held = []
+    for v in [w for q in (*every[2:], 0) for w in backs[q]]:
+        held.append(wide_in(got[-1], as_table(doubled), False))
+        if len(held) > 1:
+            v, held[-2] = tie(v, held[-2])
+        send(v, got)
+    rest, first, done, ready = held[: PARTS - 1], held[PARTS - 1 :], [], []
+    for g in range(parties):
+        if g + 1 == parties:
+            if done:
+                ready = [first_message(done[0][0], as_table(plain.T))]
+                ready[0], got[-1] = tie(ready[0], got[-1])
+            first.append(wide_in(got[-1], as_table(doubled), False))
+            grads, first[-1] = tie(grads, first[-1])
+            grads = scatter(grads, "rows")
+        given, extras = spectral_backward(g, [first[g]] + rest, keeps[g][1], keeps[g][2])
+        done.append((list(given), extras))
+    made = messages_out([v[0] for v in done], as_table(plain.T), ready)
+    filter_grads = []
+    for g in range(parties):
+        inner_low, _, outer_low, _ = done[g][1]
+        filter_grads.append(filter_grad(entries[g], inner_low, keeps[g][0], outer_low))
+
+    def blocks(n):
+        each = [v[n] for v in filter_grads]
+        return jnp.stack(each, axis=1) if split else gather_blocks(each[0])
+
+    filter_parts = (
+        blocks(0),
+        jnp.concatenate([v[1][1] for v in done], axis=1),
+        blocks(1),
+        jnp.concatenate([v[1][3] for v in done], axis=1),
+    )
+    flat = jnp.concatenate([v.reshape(-1) for v in filter_parts])
+
+    got = got[-1:]
+    for n in range(parties):
+        if n > 0:
+            made[n], made[parties] = tie(made[n], made[parties])
+        send(made[n], got)
+    grads = gather(tie(grads, got[-1])[0], ("cols", "rows"))
+    expand_sum, reduce_sum = split_grads(grads)
+    got = got[1:]
+    first_sums, states_grad = [], None
     for q in every:
-        got.append(exchange(backs[q], got[-1], backs[min(q + 1, PARTS - 1)], *held[-1:]))
+        if q + 1 < PARTS:
+            if q + 2 == PARTS:
+                made[parties + q], flat = tie(made[parties + q], flat)
+            if first_sums:
+                made[parties + q], first_sums[-1] = tie(made[parties + q], first_sums[-1])
+            send(made[parties + q], got)
+        else:
+            states_grad, expand_sum = tie(states_grad, expand_sum)
+        received = got[:parties] if q == 0 else got[parties + q - 1 : parties + q]
+        states_grad, part = last_norm(q, later_grads[q], received, states_grad)
+        first_sums.append(part)
         if q == 0:
-            grads = scatter(behind(grads, got[-1]), "cols")
-        else:
-            held.append(wide_in(got[q], as_table(doubled), False))
-    held.append(wide_in(behind(got[-1], held[-1]), as_table(doubled), False))
-    grads = scatter(behind(grads, held[-1]), "rows")
-
-    given, (inner_low, inner_bias_grad, outer_low, outer_bias_grad) = spectral_backward(
-        held, slope, damp
-    )
-    inner_grad, outer_grad = filter_grad(entries, inner_low, active, outer_low)
-    filter_parts = (
-        gather_blocks(inner_grad), inner_bias_grad, gather_blocks(outer_grad), outer_bias_grad
-    )
-    flat = sum_rows(jnp.concatenate([v.reshape(-1) for v in filter_parts]))
-    made = [wide_out(v, as_table(plain.T)) for v in given]
-    got, first_sums, states_grad = [], [], None
-    for q in range(PARTS + 1):
-        if q < PARTS:
-            got.append(exchange(made[q], *got[-1:], *first_sums[-1:]))
-        if q == 0:
-            grads = gather(behind(grads, got[0], flat, *made[1:2]), ("cols", "rows"))
-            expand_sum, reduce_sum = split_grads(grads)
-        else:
-            if q == PARTS:
-                states_grad = behind(states_grad, expand_sum)
-            states_grad, part = last_norm(q - 1, later_grads[q - 1], got[q - 1], states_grad)
-            first_sums.append(part)
+            flat, first_sums[-1] = tie(flat, first_sums[-1])
+            flat = sum_rows(flat)
     small = sum_small(
         jnp.concatenate([sum(first_sums)[:2], sums[:3], expand_bias_grad.reshape(-1, chans)])
     )

time: 1560 us -> 1550 us (level)
  waiting for transfers between devices: 791 us -> 547 us
  Pallas kernels: 635 us -> 759 us
  blocking collectives: 0 us -> 78.3 us
  starting transfers between devices: 83.6 us -> 105 us
    all_to_all x12 -> x15, waiting for transfers between devices: 791 us -> 547 us  [exchange(): lax.all_to_all(sent, ('rows', 'cols'), 0, 0, tiled=True).reshape(v.shape)]
    all_to_all x0 -> x1, blocking collectives: none -> 78.3 us  [exchange(): lax.all_to_all(sent, ('rows', 'cols'), 0, 0, tiled=True).reshape(v.shape)]
    pallas_call x17 -> x25, Pallas kernels: 414 us -> 487 us  [the longest x3 252 us: dense(): call(functools.partial(dense_kernel, steps, slabs, width, q == 0, arrays_...]
    pallas_call x1, Pallas kernels: 94.3 us -> 142 us  [sum_rows(): pl.pallas_call(functools.partial(rows_sum_kernel, ranks), in_specs=[vmem]...]
    all_to_all x12 -> x15, starting transfers between devices: 83.5 us -> 104 us  [exchange(): lax.all_to_all(sent, ('rows', 'cols'), 0, 0, tiled=True).reshape(v.shape)]
    pallas_call x6 -> x4, Pallas kernels: 32.7 us -> 24.8 us  [wide_out(): call(functools.partial(wide_out_kernel, cols_here, factor), ranks // at_o...]
  transfers between devices with their start and end apart: 15 -> 18, of which waited for: 11 -> 14; matrix products, arithmetic and copies ran while one was open for 1% -> 1% of each run, Pallas kernels for 35% -> 46%
where the time goes in v6:
time: 1550 us; the launch traced here: 1530 us
  Pallas kernels  759 us (49%)
  waiting for transfers between devices  547 us (35%)
  starting transfers between devices  105 us (7%)
  blocking collectives  78.3 us (5%)
  local copies, waits for them, and re-layouts  25.2 us (2%)
    all_to_all x15, waiting for transfers between devices, exchange(): lax.all_to_all(sent, ('rows', 'cols'), 0, 0, tiled=True).reshape(v.shape)  547 us
    pallas_call x3, Pallas kernels, dense(): call(functools.partial(dense_kernel, steps, slabs, width, q == 0, arrays_...  252 us
    pallas_call x1, Pallas kernels, sum_rows(): pl.pallas_call(functools.partial(rows_sum_kernel, ranks), in_specs=[vmem]...  142 us
    all_to_all x15, starting transfers between devices, exchange(): lax.all_to_all(sent, ('rows', 'cols'), 0, 0, tiled=True).reshape(v.shape)  104 us
    all_to_all x1, blocking collectives, exchange(): lax.all_to_all(sent, ('rows', 'cols'), 0, 0, tiled=True).reshape(v.shape)  78.3 us
    pallas_call x2, Pallas kernels, spectral_forward(): call(functools.partial(spectral_forward_kernel, factor, g), bin_steps, cu...  55.1 us
    pallas_call x2, Pallas kernels, spectral_backward(): call(functools.partial(spectral_backward_kernel, factor, g), bin_steps, c...  45.9 us
    pallas_call x8, Pallas kernels, wide_in(): call(functools.partial(wide_in_split_kernel if divided else wide_in_kerne...  44.4 us
  transfers between devices with their start and end apart: 18, of which 14 were waited for; matrix products, arithmetic and copies ran while one was open for 1% of the time, Pallas kernels for 46%

profile of v6, /device:TPU:15, one launch (start us, length us, event | category | flops | bytes accessed | tf_op | source)
XLA Modules:
  0.0 1533.8 jit_solution(4786821711010249169)
XLA Ops:
  13.5 10.0 first_norm.5
  29.8 10.0 first_norm.4
  39.8 85.6 %all-to-all-done = f32[32,88,384]{2,1,0:T(8,128)} async-done(((f32[32,88,384]{2,1,0:T(8,128)}), f32[32,88,384]{2,1,0:T(8,128)}, u32[]{:S(2)}, u32[]{:S(2)}) %all-to-all-start) | async-done | bytes 4325408 | tf_op jit(solution)/shard_map/all_to_all | solution.py:819
  125.4 6.9 all-to-all-start.1
  132.3 12.8 first_norm.3
  151.4 76.5 %all-to-all-done.1 = f32[32,88,384]{2,1,0:T(8,128)} async-done(((f32[32,88,384]{2,1,0:T(8,128)}), f32[32,88,384]{2,1,0:T(8,128)}, u32[]{:S(2)}, u32[]{:S(2)}) %all-to-all-start.1) | async-done | bytes 4325408 | tf_op jit(solution)/shard_map/all_to_all | solution.py:819
  227.9 6.8 all-to-all-start.2
  241.1 45.6 %all-to-all-done.2 = f32[32,48,384]{2,1,0:T(8,128)S(1)} async-done(((f32[32,48,384]{2,1,0:T(8,128)}), f32[32,48,384]{2,1,0:T(8,128)S(1)}, u32[]{:S(2)}, u32[]{:S(2)}) %all-to-all-start.2) | async-done | bytes 2359328 | tf_op jit(solution)/shard_map/all_to_all | solution.py:819
  288.1 6.7 all-to-all-start.3
  301.6 27.4 %spectral_forward.2 = (f32[16,2,96,192]{3,2,1,0:T(8,128)}, f32[16,2,96,192]{3,2,1,0:T(8,128)}, f32[16,2,96,192]{3,2,1,0:T(8,128)}, bf16[18432,96]{1,0:T(8,128)(2,1)}) custom-call(f32[16,2,96,192]{3,2,1,0:T(8,128)} %wide_in.10.refs_0_, f32[16,2,96,384]{3,2,1,0:T(8,128)} %wide_in.8.refs_1_, f32[16,2,96,384]{3,2,1,0:T(8,128)} %wide_in.9.refs_2_, ...), custom_call_target="tpu_custom_call" | custom-call | flops 20000000000 | bytes 51904512 | tf_op jit(solution)/shard_map/spectral_forward/pallas_call | solution.py:930
  333.7 13.1 all-to-all-done.3
  346.8 6.8 all-to-all-start.4
  358.8 27.7 %spectral_forward.3 = (f32[16,2,96,192]{3,2,1,0:T(8,128)}, f32[16,2,96,192]{3,2,1,0:T(8,128)}, f32[16,2,96,192]{3,2,1,0:T(8,128)}, bf16[18432,96]{1,0:T(8,128)(2,1)}) custom-call(f32[16,2,96,192]{3,2,1,0:T(8,128)} %wide_in.11.refs_0_, f32[16,2,96,384]{3,2,1,0:T(8,128)} %wide_in.8.refs_1_, f32[16,2,96,384]{3,2,1,0:T(8,128)} %wide_in.9.refs_2_, ...), custom_call_target="tpu_custom_call" | custom-call | flops 20000000000 | bytes 51904512 | tf_op jit(solution)/shard_map/spectral_forward/pallas_call | solution.py:930
  391.2 14.3 all-to-all-done.4
  405.5 7.1 all-to-all-start.5
  412.6 15.3 %spectral_keep.3 = (bf16[18432,96]{1,0:T(8,128)(2,1)}, bf16[18432,96]{1,0:T(8,128)(2,1)}, bf16[18432,96]{1,0:T(8,128)(2,1)}) custom-call(bf16[18432,96]{1,0:T(8,128)(2,1)} %get-tuple-element.151.entries, bf16[2,96,96]{2,1,0:T(8,128)(2,1)} %get-tuple-element.270.refs_5_.inner, f32[2,96]{1,0:T(2,128)} %get-tuple-element.272.refs_6_.inner_bias, ...), custom_call_target="tpu_custom_call" | custom-call | flops 10000000000 | bytes 12976128 | tf_op jit(solution)/shard_map/spectral_keep/pallas_call | solution.py:943
  434.2 15.3 spectral_keep.2
  449.5 15.0 all-to-all-done.5
  465.9 6.8 all-to-all-start.6
  480.6 85.1 %dense_both_ways.3 = (f32[8,4,48,384]{3,2,1,0:T(8,128)}, f32[8,4,48,384]{3,2,1,0:T(8,128)}, bf16[2,264,8,768]{3,2,1,0:T(8,128)(2,1)}, f32[2,88,8,768]{3,2,1,0:T(...) custom-call(f32[8,4,48,384]{3,2,1,0:T(8,128)} %bitcast.16.refs_0_, f32[8,4,48,384]{3,2,1,0:T(8,128)} %bitcast.122, ...), custom_call_target="tpu_custom_call" | custom-call | flops 39862665216 | bytes 17301504 | tf_op jit(solution)/shard_map/dense_both_ways/pallas_call | solution.py:988
  568.3 7.3 all-to-all-start.7
  575.5 83.3 %dense_both_ways.4 = (f32[8,4,88,384]{3,2,1,0:T(8,128)}, bf16[2,264,8,768]{3,2,1,0:T(8,128)(2,1)}, f32[2,88,8,768]{3,2,1,0:T(8,128)}, f32[8,768]{1,0:T(8,128)}, f32[4,768]{1,0:T(4,128)}, /*index=5*/f32[6144,768]{1,0:T(8,128)}) custom-call(f32[8,4,88,384]{3,2,1,0:T(8,128)} %bitcast.23.refs_0_, ...), custom_call_target="tpu_custom_call", output_to_operand_aliasing={{1}: (13, {})} | custom-call | flops 39862665216 | bytes 17301504 | tf_op jit(solution)/shard_map/dense_both_ways/pallas_call | solution.py:988
  658.8 12.2 all-to-all-done.7
  671.0 6.9 all-to-all-start.8
  678.0 83.2 %dense_both_ways.5 = (f32[8,4,88,384]{3,2,1,0:T(8,128)}, bf16[2,264,8,768]{3,2,1,0:T(8,128)(2,1)}, f32[2,88,8,768]{3,2,1,0:T(8,128)}, f32[8,768]{1,0:T(8,128)}, f32[4,768]{1,0:T(4,128)}, /*index=5*/f32[6144,768]{1,0:T(8,128)}) custom-call(f32[8,4,88,384]{3,2,1,0:T(8,128)} %bitcast.25.refs_0_, ...), custom_call_target="tpu_custom_call", output_to_operand_aliasing={{1}: (13, {})} | custom-call | flops 39862665216 | bytes 17301504 | tf_op jit(solution)/shard_map/dense_both_ways/pallas_call | solution.py:988
  761.2 12.4 all-to-all-done.8
  773.6 6.9 all-to-all-start.9
  786.6 89.4 %all-to-all-done.9 = f32[32,88,384]{2,1,0:T(8,128)} async-done(((f32[32,88,384]{2,1,0:T(8,128)}), f32[32,88,384]{2,1,0:T(8,128)}, u32[]{:S(2)}, u32[]{:S(2)}) %all-to-all-start.9) | async-done | bytes 4325408 | tf_op jit(solution)/shard_map/all_to_all | solution.py:819
  876.1 7.2 all-to-all-start.10
  888.8 46.3 %all-to-all-done.10 = f32[32,48,384]{2,1,0:T(8,128)S(1)} async-done(((f32[32,48,384]{2,1,0:T(8,128)}), f32[32,48,384]{2,1,0:T(8,128)S(1)}, u32[]{:S(2)}, u32[]{:S(2)}) %all-to-all-start.10) | async-done | bytes 2359328 | tf_op jit(solution)/shard_map/all_to_all | solution.py:819
  936.6 6.7 all-to-all-start.11
  949.6 22.7 %spectral_backward.2 = (f32[16,2,96,192]{3,2,1,0:T(8,128)}, f32[16,2,96,192]{3,2,1,0:T(8,128)}, f32[16,2,96,192]{3,2,1,0:T(8,128)}, bf16[18432,96]{1,0:T(8,128)(...) custom-call(f32[16,2,96,192]{3,2,1,0:T(8,128)} %wide_in.13.refs_0_, ...), custom_call_target="tpu_custom_call" | custom-call | flops 20000000000 | bytes 51904512 | tf_op jit(solution)/shard_map/spectral_backward/pallas_call | solution.py:955
  977.0 18.4 %all-to-all-done.11 = f32[32,48,384]{2,1,0:T(8,128)S(1)} async-done(((f32[32,48,384]{2,1,0:T(8,128)}), f32[32,48,384]{2,1,0:T(8,128)S(1)}, u32[]{:S(2)}, u32[]{:S(2)}) %all-to-all-start.11) | async-done | bytes 2359328 | tf_op jit(solution)/shard_map/all_to_all | solution.py:819
  1001.6 6.7 all-to-all-start.12
  1009.8 23.2 %spectral_backward.3 = (f32[16,2,96,192]{3,2,1,0:T(8,128)}, f32[16,2,96,192]{3,2,1,0:T(8,128)}, f32[16,2,96,192]{3,2,1,0:T(8,128)}, bf16[18432,96]{1,0:T(8,128)(...) custom-call(f32[16,2,96,192]{3,2,1,0:T(8,128)} %wide_in.15.refs_0_, ...), custom_call_target="tpu_custom_call" | custom-call | flops 20000000000 | bytes 51904512 | tf_op jit(solution)/shard_map/spectral_backward/pallas_call | solution.py:955
  1043.9 53.6 %all-to-all-done.12 = f32[32,48,384]{2,1,0:T(8,128)S(1)} async-done(((f32[32,48,384]{2,1,0:T(8,128)}), f32[32,48,384]{2,1,0:T(8,128)S(1)}, u32[]{:S(2)}, u32[]{:S(2)}) %all-to-all-start.12) | async-done | bytes 2359328 | tf_op jit(solution)/shard_map/all_to_all | solution.py:819
  1097.6 78.3 %all_to_all.80 = f32[32,48,384]{2,1,0:T(8,128)} all-to-all(f32[32,48,384]{2,1,0:T(8,128)} %bitcast.112), channel_id=1, replica_groups=mesh['rows'=8,'cols'=4] {'rows','cols'}, dimensions={0} | all-to-all | bytes 4718592 | tf_op jit(solution)/shard_map/all_to_all | solution.py:819
  1175.9 6.7 all-to-all-start.14
  1182.6 13.7 filter_grad.2
  1196.3 13.7 filter_grad.3
  1218.8 15.1 first_norm_backward.3
  1234.7 142.4 %filter_sums.1 = f32[640,128]{1,0:T(8,128)} custom-call(f32[640,128]{1,0:T(8,128)} %pad_bitcast_fusion.own), custom_call_target="tpu_custom_call" | custom-call | tf_op jit(solution)/shard_map/filter_sums/pallas_call | solution.py:785
  1378.1 8.6 all-to-all-start.15
  1389.7 11.6 first_norm_backward.4
  1401.3 18.5 %split_gradients.1 = (f32[768,3072]{1,0:T(8,128)}, f32[3072,768]{1,0:T(8,128)}) custom-call(f32[6144,768]{1,0:T(8,128)} %all-gather.2.cloned.1.call-done.expand_in.reduce_in, f32[6144,768]{1,0:T(8,128)} %all-gather.2.cloned.1.call-done.expand_in.reduce_in), custom_call_target="tpu_custom_call" | custom-call | bytes 37748736 | tf_op jit(solution)/shard_map/split_gradients/pallas_call | solution.py:798
  1419.8 62.5 %all-to-all-done.15 = f32[32,88,384]{2,1,0:T(8,128)} async-done(((f32[32,88,384]{2,1,0:T(8,128)}), f32[32,88,384]{2,1,0:T(8,128)}, u32[]{:S(2)}, u32[]{:S(2)}) %all-to-all-start.15) | async-done | bytes 4325408 | tf_op jit(solution)/shard_map/all_to_all | solution.py:819
  1482.3 11.6 first_norm_backward.5
  1495.3 28.7 %small_sums.1 = f32[56,128]{1,0:T(8,128)} custom-call(f32[56,128]{1,0:T(8,128)} %pad.9.own), custom_call_target="tpu_custom_call" | custom-call | tf_op jit(solution)/shard_map/small_sums/pallas_call | solution.py:766
  (134 shorter events, 126.5 us)
Async XLA Ops:
  23.5 101.9 %all-to-all-start = ((f32[32,88,384]{2,1,0:T(8,128)}), f32[32,88,384]{2,1,0:T(8,128)}, u32[]{:S(2)}, u32[]{:S(2)}) async-start(f32[32,88,384]{2,1,0:T(8,128)} %bitcast.102), calls=%async_computation | async-start | bytes 8650752 | tf_op jit(solution)/shard_map/all_to_all | solution.py:819
  125.4 102.5 %all-to-all-start.1 = ((f32[32,88,384]{2,1,0:T(8,128)}), f32[32,88,384]{2,1,0:T(8,128)}, u32[]{:S(2)}, u32[]{:S(2)}) async-start(f32[32,88,384]{2,1,0:T(8,128)} %bitcast.101), calls=%async_computation.1 | async-start | bytes 8650752 | tf_op jit(solution)/shard_map/all_to_all | solution.py:819
  227.9 58.8 %all-to-all-start.2 = ((f32[32,48,384]{2,1,0:T(8,128)}), f32[32,48,384]{2,1,0:T(8,128)S(1)}, u32[]{:S(2)}, u32[]{:S(2)}) async-start(f32[32,48,384]{2,1,0:T(8,128)} %bitcast.123), calls=%async_computation.2 | async-start | bytes 4718592 | tf_op jit(solution)/shard_map/all_to_all | solution.py:819
  241.1 53.7 %copy-start.23 = (f32[2,2,96]{2,1,0:T(2,128)S(1)}, f32[2,2,96]{2,1,0:T(2,128)}, u32[]{:S(2)}) copy-start(f32[2,2,96]{2,1,0:T(2,128)} %param.41) | copy-start | bytes 4612
  241.1 53.8 %copy-start.24 = (f32[2,2,96]{2,1,0:T(2,128)S(1)}, f32[2,2,96]{2,1,0:T(2,128)}, u32[]{:S(2)}) copy-start(f32[2,2,96]{2,1,0:T(2,128)} %param.43) | copy-start | bytes 4612
  241.1 54.6 %copy-start.10 = (bf16[2,2,96,96]{3,2,1,0:T(8,128)(2,1)S(1)}, bf16[2,2,96,96]{3,2,1,0:T(8,128)(2,1)}, u32[]{:S(2)}) copy-start(bf16[2,2,96,96]{3,2,1,0:T(8,128)(2,1)} %param.42) | copy-start | bytes 221188
  241.1 54.6 %copy-start.11 = (bf16[2,2,96,96]{3,2,1,0:T(8,128)(2,1)S(1)}, bf16[2,2,96,96]{3,2,1,0:T(8,128)(2,1)}, u32[]{:S(2)}) copy-start(bf16[2,2,96,96]{3,2,1,0:T(8,128)(2,1)} %param.40) | copy-start | bytes 221188
  286.7 1.4 copy-start.2
  288.1 58.7 %all-to-all-start.3 = ((f32[32,48,384]{2,1,0:T(8,128)}), f32[32,48,384]{2,1,0:T(8,128)S(1)}, u32[]{:S(2)}, u32[]{:S(2)}) async-start(f32[32,48,384]{2,1,0:T(8,128)} %bitcast.121), calls=%async_computation.3 | async-start | bytes 4718592 | tf_op jit(solution)/shard_map/all_to_all | solution.py:819
  346.8 6.8 copy-start.1
  346.8 58.7 %all-to-all-start.4 = ((f32[32,48,384]{2,1,0:T(8,128)}), f32[32,48,384]{2,1,0:T(8,128)}, u32[]{:S(2)}, u32[]{:S(2)}) async-start(f32[32,48,384]{2,1,0:T(8,128)} %bitcast.111), calls=%async_computation.4 | async-start | bytes 4718592 | tf_op jit(solution)/shard_map/all_to_all | solution.py:819
  405.5 59.0 %all-to-all-start.5 = ((f32[32,48,384]{2,1,0:T(8,128)}), f32[32,48,384]{2,1,0:T(8,128)S(1)}, u32[]{:S(2)}, u32[]{:S(2)}) async-start(f32[32,48,384]{2,1,0:T(8,128)} %bitcast.110), calls=%async_computation.5 | async-start | bytes 4718592 | tf_op jit(solution)/shard_map/all_to_all | solution.py:819
  464.5 1.4 copy-start.5
  464.5 8.2 copy-start.20
  464.5 8.8 copy-start.21
  464.5 9.4 copy-start.22
  465.9 102.4 %all-to-all-start.6 = ((f32[32,88,384]{2,1,0:T(8,128)}), f32[32,88,384]{2,1,0:T(8,128)}, u32[]{:S(2)}, u32[]{:S(2)}) async-start(f32[32,88,384]{2,1,0:T(8,128)} %bitcast.105), calls=%async_computation.6 | async-start | bytes 8650752 | tf_op jit(solution)/shard_map/all_to_all | solution.py:819
  568.3 102.8 %all-to-all-start.7 = ((f32[32,88,384]{2,1,0:T(8,128)}), f32[32,88,384]{2,1,0:T(8,128)}, u32[]{:S(2)}, u32[]{:S(2)}) async-start(f32[32,88,384]{2,1,0:T(8,128)} %bitcast.106), calls=%async_computation.7 | async-start | bytes 8650752 | tf_op jit(solution)/shard_map/all_to_all | solution.py:819
  671.0 102.5 %all-to-all-start.8 = ((f32[32,88,384]{2,1,0:T(8,128)}), f32[32,88,384]{2,1,0:T(8,128)}, u32[]{:S(2)}, u32[]{:S(2)}) async-start(f32[32,88,384]{2,1,0:T(8,128)} %bitcast.117), calls=%async_computation.8 | async-start | bytes 8650752 | tf_op jit(solution)/shard_map/all_to_all | solution.py:819
  677.9 323.6 %reduce-scatter.3.cloned.1.call-start = ((), (), s32[]{:S(2)}) async-start(), calls=%async_computation.18 | async-start | bytes 23592960 | tf_op jit(solution)/shard_map/reduce_scatter | solution.py:757
  773.6 102.5 %all-to-all-start.9 = ((f32[32,88,384]{2,1,0:T(8,128)}), f32[32,88,384]{2,1,0:T(8,128)}, u32[]{:S(2)}, u32[]{:S(2)}) async-start(f32[32,88,384]{2,1,0:T(8,128)} %bitcast.118), calls=%async_computation.9 | async-start | bytes 8650752 | tf_op jit(solution)/shard_map/all_to_all | solution.py:819
  876.1 59.1 %all-to-all-start.10 = ((f32[32,48,384]{2,1,0:T(8,128)}), f32[32,48,384]{2,1,0:T(8,128)S(1)}, u32[]{:S(2)}, u32[]{:S(2)}) async-start(f32[32,48,384]{2,1,0:T(8,128)} %bitcast.120), calls=%async_computation.10 | async-start | bytes 4718592 | tf_op jit(solution)/shard_map/all_to_all | solution.py:819
  888.8 54.6 %copy-start.9 = (bf16[2,1,96,96]{3,2,1,0:T(8,128)(2,1)S(1)}, bf16[2,1,96,96]{3,2,1,0:T(8,128)(2,1)}, u32[]{:S(2)}) copy-start(bf16[2,1,96,96]{3,2,1,0:T(8,128)(2,1)} %get-tuple-element.254) | copy-start | bytes 110596
  888.8 55.3 %copy-start.8 = (bf16[2,1,96,96]{3,2,1,0:T(8,128)(2,1)S(1)}, bf16[2,1,96,96]{3,2,1,0:T(8,128)(2,1)}, u32[]{:S(2)}) copy-start(bf16[2,1,96,96]{3,2,1,0:T(8,128)(2,1)} %get-tuple-element.268) | copy-start | bytes 110596
  935.2 1.4 copy-start.4
  936.6 58.7 %all-to-all-start.11 = ((f32[32,48,384]{2,1,0:T(8,128)}), f32[32,48,384]{2,1,0:T(8,128)S(1)}, u32[]{:S(2)}, u32[]{:S(2)}) async-start(f32[32,48,384]{2,1,0:T(8,128)} %bitcast.119), calls=%async_computation.12 | async-start | bytes 4718592 | tf_op jit(solution)/shard_map/all_to_all | solution.py:819
  943.3 232.5 %reduce-scatter.5.cloned.1.call-start = ((), (), s32[]{:S(2)}) async-start(), calls=%async_computation.19 | async-start | bytes 5308416 | tf_op jit(solution)/shard_map/reduce_scatter | solution.py:757
  995.3 1.5 copy-start.3
  1001.6 6.8 copy-start.7
  1001.6 7.6 copy-start.6
  1001.6 96.0 %all-to-all-start.12 = ((f32[32,48,384]{2,1,0:T(8,128)}), f32[32,48,384]{2,1,0:T(8,128)S(1)}, u32[]{:S(2)}, u32[]{:S(2)}) async-start(f32[32,48,384]{2,1,0:T(8,128)} %bitcast.109), calls=%async_computation.13 | async-start | bytes 4718592 | tf_op jit(solution)/shard_map/all_to_all | solution.py:819
  1008.3 393.0 %all-gather.2.cloned.1.call-start = ((), (), s32[]{:S(2)}) async-start(), calls=%async_computation.20 | async-start | bytes 19464192 | tf_op jit(solution)/shard_map/all_gather | solution.py:760
  1097.6 78.4 %copy-start = (f32[32,48,384]{2,1,0:T(8,128)}, f32[32,48,384]{2,1,0:T(8,128)S(1)}, u32[]{:S(2)}) copy-start(f32[32,48,384]{2,1,0:T(8,128)S(1)} %all-to-all-done.12) | copy-start | bytes 7077892
  1175.9 202.1 %all-to-all-start.14 = ((f32[32,88,384]{2,1,0:T(8,128)}), f32[32,88,384]{2,1,0:T(8,128)}, u32[]{:S(2)}, u32[]{:S(2)}) async-start(f32[32,88,384]{2,1,0:T(8,128)} %bitcast.103), calls=%async_computation.15 | async-start | bytes 8650752 | tf_op jit(solution)/shard_map/all_to_all | solution.py:819
  1196.3 13.8 copy-start.13
  1196.3 14.9 copy-start.12
  1196.3 16.0 %copy-start.26 = (f32[2,96]{1,0:T(2,128)S(1)}, f32[2,96]{1,0:T(2,128)}, u32[]{:S(2)}) copy-start(f32[2,96]{1,0:T(2,128)} %get-tuple-element.202) | copy-start | bytes 2308
  1196.3 16.0 %copy-start.28 = (f32[2,96]{1,0:T(2,128)S(1)}, f32[2,96]{1,0:T(2,128)}, u32[]{:S(2)}) copy-start(f32[2,96]{1,0:T(2,128)} %get-tuple-element.203) | copy-start | bytes 2308
  1196.3 16.1 %copy-start.25 = (f32[2,96]{1,0:T(2,128)S(1)}, f32[2,96]{1,0:T(2,128)}, u32[]{:S(2)}) copy-start(f32[2,96]{1,0:T(2,128)} %get-tuple-element.206) | copy-start | bytes 2308
  1196.3 16.1 %copy-start.27 = (f32[2,96]{1,0:T(2,128)S(1)}, f32[2,96]{1,0:T(2,128)}, u32[]{:S(2)}) copy-start(f32[2,96]{1,0:T(2,128)} %get-tuple-element.207) | copy-start | bytes 2308
  1378.1 8.7 copy-start.14
  1378.1 8.7 copy-start.15
  1378.1 8.7 copy-start.16
  1378.1 8.7 copy-start.17
  1378.1 8.7 copy-start.18
  1378.1 8.7 copy-start.19
  1378.1 104.2 %all-to-all-start.15 = ((f32[32,88,384]{2,1,0:T(8,128)}), f32[32,88,384]{2,1,0:T(8,128)}, u32[]{:S(2)}, u32[]{:S(2)}) async-start(f32[32,88,384]{2,1,0:T(8,128)} %bitcast.104), calls=%async_computation.16 | async-start | bytes 8650752 | tf_op jit(solution)/shard_map/all_to_all | solution.py:819
Sparse Core Ops, SparseCore 0:
  773.7 209.4 reduce-scatter.2
  1001.7 169.4 reduce-scatter.4
  1176.0 203.3 all-gather.1

commit v7 on v6

--- a/solution.py
+++ b/solution.py
@@ -279,10 +279,16 @@
         damp[n * tall : (n + 1) * tall, :] = (t * t).astype(bf16)
 
 
-def spectral_backward_kernel(factor, group, *refs):
+def joined(refs):
+    return jnp.concatenate([r[...] for r in refs], axis=1) if len(refs) > 1 else refs[0][...]
+
+
+def spectral_backward_kernel(factor, parties, *refs):
     held, refs = refs[:PARTS], refs[PARTS:]
-    table_down, table_up, inner_t, outer_t, slope, damp = refs[:6]
-    given, refs = refs[6 : 6 + PARTS], refs[6 + PARTS :]
+    table_down, table_up, inner_t, outer_t = refs[:4]
+    slope, damp = joined(refs[4 : 4 + parties]), joined(refs[4 + parties : 4 + 2 * parties])
+    refs = refs[4 + 2 * parties :]
+    given, refs = refs[:PARTS], refs[PARTS:]
     inner_low, inner_bias_grad, outer_low, outer_bias_grad = refs
     width = inner_t.shape[2]
     tall = table_up.shape[0] // 2
@@ -292,14 +298,14 @@
         for ref in (inner_bias_grad, outer_bias_grad):
             ref[...] = jnp.zeros_like(ref)
 
-    spec = bins_in(held, table_down, width, group, False)
+    spec = bins_in(held, table_down, width, 0, False)
     grads = []
     sums = [0.0, 0.0]
     for k in range(GROUP):
         for side in range(2):
             at = (2 * k + side) * tall
             g = spec[k][side * tall : (side + 1) * tall] * factor
-            g = g * damp[at : at + tall, :].astype(f32)
+            g = g * damp[at : at + tall].astype(f32)
             sums[side] = sums[side] + jnp.sum(g, axis=0, keepdims=True)
             grads.append(g.astype(bf16))
     outer_bias_grad[...] += jnp.concatenate(sums, axis=0)
@@ -309,7 +315,7 @@
     grads = []
     sums = [0.0, 0.0]
     for n, part in enumerate(parts):
-        g = part * slope[n * tall : (n + 1) * tall, :].astype(f32)
+        g = part * slope[n * tall : (n + 1) * tall].astype(f32)
         sums[n % 2] = sums[n % 2] + jnp.sum(g, axis=0, keepdims=True)
         grads.append(g.astype(bf16))
     inner_bias_grad[...] += jnp.concatenate(sums, axis=0)
@@ -323,7 +329,10 @@
     bins_out(given, table_up, width, values)
 
 
-def filter_grad_kernel(tall, entries, inner_low, active, outer_low, inner_grad, outer_grad):
+def filter_grad_kernel(tall, parties, *refs):
+    entries, active = refs[:parties], refs[parties : 2 * parties]
+    inner_low, outer_low, inner_grad, outer_grad = refs[2 * parties :]
+
     @pl.when(pl.program_id(0) == 0)
     def _():
         inner_grad[...] = jnp.zeros_like(inner_grad)
@@ -334,8 +343,9 @@
         for k in range(GROUP):
             top, bottom = low[2 * k * tall : (2 * k + 1) * tall], low[(2 * k + 1) * tall : (2 * k + 2) * tall]
             turned += [bottom, -top]
-        grad[0] += dot_tn(before[...], low[...])
-        grad[1] += dot_tn(before[...], jnp.concatenate(turned, axis=0))
+        known = joined(before)
+        grad[0] += dot_tn(known, low[...])
+        grad[1] += dot_tn(known, jnp.concatenate(turned, axis=0))
 
 
 def dense_kernel(steps, slabs, width, first_part, arrays, *refs):
@@ -348,7 +358,7 @@
     if not first_part:
         grads_before = refs[0]
         refs = refs[2:]
-    back, refs = refs[:arrays], refs[arrays:]
+    back, refs = refs[:1], refs[1:]
     result, later_grad, sums, expand_bias_grad, grads_hbm = refs[:5]
     (
         expand, reduce, expand_grad, reduce_grad, mixed, normed, low_out, branch, grad_n,
@@ -495,9 +505,14 @@
         out[half] = (inside * grad).astype(bf16)
 
 
-def sum_kernel(ranks, groups, own, out, got, send_sem, recv_sem):
+def sum_kernel(
+    ranks, groups, own, flat, out, flat_out,
+    got, picked, done, send_sem, recv_sem, pick_send, pick_recv, give_send, give_recv,
+):
     devices = ranks * groups
-    me = lax.axis_index("rows") * groups + lax.axis_index("cols")
+    my_row = lax.axis_index("rows")
+    me = my_row * groups + lax.axis_index("cols")
+    piece = flat.shape[0] // ranks
 
     def place(i):
         other = lax.rem(me + i, devices)
@@ -513,6 +528,19 @@
             device_id_type=pl.DeviceIdType.MESH,
         )
 
+    def along(src, dst, i, send, recv):
+        return pltpu.make_async_remote_copy(
+            src_ref=src,
+            dst_ref=dst,
+            send_sem=send.at[i],
+            recv_sem=recv.at[i],
+            device_id=(lax.rem(my_row + i, ranks), lax.axis_index("cols")),
+            device_id_type=pl.DeviceIdType.MESH,
+        )
+
+    def rows_of(r):
+        return pl.ds(pl.multiple_of(r * piece, piece), piece)
+
     barrier = pltpu.get_barrier_semaphore()
 
     def greet(i, carry):
@@ -531,59 +559,29 @@
 
     lax.fori_loop(1, devices, greet, 0)
     pl.semaphore_wait(barrier, devices - 1)
-    lax.fori_loop(1, devices, start, 0)
-    lax.fori_loop(1, devices, finish, 0)
-    out[...] = lax.fori_loop(1, devices, lambda i, total: total + got[i], own[...])
-
-
-def rows_sum_kernel(ranks, own, out, got, done, pick_send, pick_recv, give_send, give_recv):
-    me = lax.axis_index("rows")
-    piece = own.shape[0] // ranks
-
-    def at(ref, r):
-        return ref.at[pl.ds(pl.multiple_of(r * piece, piece), piece)]
-
-    def copy(src, dst, i, send, recv):
-        return pltpu.make_async_remote_copy(
-            src_ref=src,
-            dst_ref=dst,
-            send_sem=send.at[i],
-            recv_sem=recv.at[i],
-            device_id={"rows": lax.rem(me + i, ranks)},
-            device_id_type=pl.DeviceIdType.MESH,
-        )
-
-    barrier = pltpu.get_barrier_semaphore()
-    for i in range(1, ranks):
-        pl.semaphore_signal(
-            barrier,
-            inc=1,
-            device_id={"rows": lax.rem(me + i, ranks)},
-            device_id_type=pl.DeviceIdType.MESH,
-        )
-    pl.semaphore_wait(barrier, ranks - 1)
     picks = [
-        copy(at(own, lax.rem(me + i, ranks)), got.at[i], i, pick_send, pick_recv)
+        along(flat.at[rows_of(lax.rem(my_row + i, ranks))], picked.at[i], i, pick_send, pick_recv)
         for i in range(1, ranks)
     ]
     for c in picks:
         c.start()
+    lax.fori_loop(1, devices, start, 0)
     for c in picks:
         c.wait()
-    start = pl.ds(pl.multiple_of(me * piece, piece), piece)
-    total = own[start, :]
+    total = flat[rows_of(my_row), :]
     for i in range(1, ranks):
-        total = total + got[i]
+        total = total + picked[i]
     done[0] = total
-    gives = [copy(done.at[0], done.at[i], i, give_send, give_recv) for i in range(1, ranks)]
+    gives = [along(done.at[0], done.at[i], i, give_send, give_recv) for i in range(1, ranks)]
     for c in gives:
         c.start()
+    lax.fori_loop(1, devices, finish, 0)
+    out[...] = lax.fori_loop(1, devices, lambda i, total: total + got[i], own[...])
     for c in gives:
         c.wait()
-    out[start, :] = total
+    flat_out[rows_of(my_row), :] = total
     for i in range(1, ranks):
-        source = lax.rem(me - i + ranks, ranks)
-        out[pl.ds(pl.multiple_of(source * piece, piece), piece), :] = done[i]
+        flat_out[rows_of(lax.rem(my_row - i + ranks, ranks)), :] = done[i]
 
 
 def split_kernel(expand_in, reduce_in, expand_out, reduce_out):
@@ -759,38 +757,26 @@
     def gather(v, axis):
         return lax.all_gather(v, axis, axis=0, tiled=True)
 
-    def sum_small(v):
-        flat = v.reshape(-1, 128)
-        flat = jnp.pad(flat, ((0, -flat.shape[0] % 8), (0, 0)))
+    def sum_small(v, by_rows):
+        def as_rows(v, unit):
+            v = v.reshape(-1)
+            return jnp.pad(v, (0, -v.shape[0] % (unit * 128))).reshape(-1, 128)
+
+        own, flat = as_rows(v, 8), as_rows(by_rows, 8 * ranks)
+        slots = pltpu.VMEM((ranks, flat.shape[0] // ranks, 128), f32)
         vmem = pl.BlockSpec(memory_space=pltpu.VMEM)
-        return pl.pallas_call(
+        out, flat_out = pl.pallas_call(
             functools.partial(sum_kernel, ranks, groups),
-            in_specs=[vmem],
-            out_specs=vmem,
-            out_shape=shape(flat.shape, f32),
-            scratch_shapes=[
-                pltpu.VMEM((devices,) + flat.shape, f32),
-                pltpu.SemaphoreType.DMA((devices,)),
-                pltpu.SemaphoreType.DMA((devices,)),
-            ],
+            in_specs=[vmem, vmem],
+            out_specs=[vmem, vmem],
+            out_shape=[shape(own.shape, f32), shape(flat.shape, f32)],
+            scratch_shapes=[pltpu.VMEM((devices,) + own.shape, f32), slots, slots]
+            + [pltpu.SemaphoreType.DMA((devices,))] * 2
+            + [pltpu.SemaphoreType.DMA((ranks,))] * 4,
             compiler_params=pltpu.CompilerParams(collective_id=0, has_side_effects=True),
             name="small_sums",
-        )(flat).reshape(-1)[: v.size].reshape(v.shape)
-
-    def sum_rows(v):
-        flat = v.reshape(-1)
-        flat = jnp.pad(flat, (0, -flat.shape[0] % (ranks * 1024))).reshape(-1, 128)
-        slots = (ranks, flat.shape[0] // ranks, 128)
-        vmem = pl.BlockSpec(memory_space=pltpu.VMEM)
-        return pl.pallas_call(
-            functools.partial(rows_sum_kernel, ranks),
-            in_specs=[vmem],
-            out_specs=vmem,
-            out_shape=shape(flat.shape, f32),
-            scratch_shapes=[pltpu.VMEM(slots, f32)] * 2 + [pltpu.SemaphoreType.DMA((ranks,))] * 4,
-            compiler_params=pltpu.CompilerParams(collective_id=1, has_side_effects=True),
-            name="filter_sums",
-        )(flat).reshape(-1)[: v.size]
+        )(own, flat)
+        return out.reshape(-1)[: v.size].reshape(v.shape), flat_out.reshape(-1)
 
     def split_grads(v):
         cuts = 4
@@ -890,7 +876,7 @@
         return call(
             functools.partial(wide_out_kernel, cols_here, factor),
             ranks // at_once,
-            [held_of(PAIR * cut, True)] * len(parts) + [whole(table.shape)],
+            [held_of(v.shape[3], True) for v in parts] + [whole(table.shape)],
             field,
             packed_shape,
             "wide_out",
@@ -909,11 +895,8 @@
             scratch=[natural],
         )(part, table)
 
-    def first_message(given, table):
-        return wide_out_split(given[0], table) if split else wide_out([given[0]], table)
-
-    def messages_out(given, table, first):
-        first = first + [first_message(v, table) for v in given[len(first) :]]
+    def messages_out(given, table):
+        first = [wide_out_split(v[0], table) for v in given] if split else [wide_out([given[0][0]], table)]
         return first + [wide_out([v[q] for v in given], table) for q in range(1, PARTS)]
 
     def of_group(v, g):
@@ -951,30 +934,35 @@
             nbytes=2 * PARTS * message // parties,
         )(entries, *forward_mix[g])
 
-    def spectral_backward(g, held, slope, damp):
+    full = pl.BlockSpec((group_rows, width), lambda i: (i, 0))
+    full_shape = shape((bin_steps * group_rows, width), bf16)
+    full_mix, full_bias = whole((2, width, width)), whole((2, width))
+    inner_t, outer_t = turn(spread(filter_inner)), turn(spread(filter_outer))
+
+    def spectral_backward(held, slope, damp):
         outs = call(
-            functools.partial(spectral_backward_kernel, factor, g),
+            functools.partial(spectral_backward_kernel, factor, parties),
             bin_steps,
-            cut_in + [up_spec, up_spec, mix_spec, mix_spec] + [kept] * 2,
-            cut_out + [kept, bias_spec] * 2,
-            [cut_shape] * PARTS + [kept_shape, shape((2, cut), f32)] * 2,
+            [held_bins] * PARTS + [up_spec, up_spec, full_mix, full_mix] + [kept] * (2 * parties),
+            [held_bins] * PARTS + [full, full_bias] * 2,
+            [held_shape] * PARTS + [full_shape, shape((2, width), f32)] * 2,
             "spectral_backward",
             flops=20 * 10**9,
-            nbytes=8 * PARTS * message // parties,
-        )(*held, as_table(down), as_table(up), turn(inner_full[g]), turn(outer_full[g]), slope, damp)
+            nbytes=8 * PARTS * message,
+        )(*held, as_table(down), as_table(up), inner_t, outer_t, *slope, *damp)
         return outs[:PARTS], outs[PARTS:]
 
-    def filter_grad(*operands):
+    def filter_grad(entries, active, inner_low, outer_low):
         return call(
-            functools.partial(filter_grad_kernel, height),
+            functools.partial(filter_grad_kernel, height, parties),
             bin_steps,
-            [kept] * 4,
-            [mix_spec] * 2,
-            [shape((2, cut, cut), f32)] * 2,
+            [kept] * (2 * parties) + [full] * 2,
+            [full_mix] * 2,
+            [shape((2, width, width), f32)] * 2,
             "filter_grad",
             flops=10 * 10**9,
             nbytes=2 * PARTS * message,
-        )(*operands)
+        )(*entries, *active, inner_low, outer_low)
 
     slab = chans
     slabs = hidden // slab
@@ -994,7 +982,7 @@
             + [pl.BlockSpec((1, slab), lambda i: (0, jnp.clip(i - steps, 0, slabs - 1)))]
             + [chan_row]
             + [anywhere] * (2 + len(grads_before)),
-            message_specs(q, leave)
+            [packed_spec(leave)]
             + [
                 token_spec(q, leave),
                 token_spec(0, leave),
@@ -1002,7 +990,7 @@
                 whole((slabs, slab)),
                 anywhere,
             ],
-            message_shapes(q)
+            [packed_shape]
             + [
                 token_shape,
                 shape((PAIR, pixels, frames, chans), f32),
@@ -1047,9 +1035,9 @@
     def last_norm(q, later_grad, spatial, before):
         given = () if q == 0 else (before,)
         return call(
-            functools.partial(last_kernel, width, arrays_of(q)),
+            functools.partial(last_kernel, width, 1),
             steps,
-            message_specs(q, same)
+            [packed_spec(same)]
             + [token_spec(q, same), token_spec(0, same), token_spec(q, same, 128)]
             + [chan_row]
             + [anywhere] * len(given),
@@ -1058,7 +1046,7 @@
             "first_norm_backward",
             nbytes=4 * message,
             input_output_aliases={} if q == 0 else {5: 0},
-        )(*spatial, states_in, later_grad, mask, row(first_gain), *given)
+        )(spatial, states_in, later_grad, mask, row(first_gain), *given)
 
     every = range(PARTS)
 
@@ -1079,7 +1067,7 @@
     rest, first = held[: PARTS - 1], held[PARTS - 1 :]
     done = [spectral_forward(g, [first[g]] + rest) for g in range(parties)]
     entries = [v[1] for v in done]
-    made = messages_out([v[0] for v in done], as_table(doubled.T), [])
+    made = messages_out([v[0] for v in done], as_table(doubled.T))
     keeps = [list(spectral_keep(g, entries[g])) for g in range(parties)]
 
     spatial = got[-1:]
@@ -1092,82 +1080,59 @@
     for q in every:
         if q + 1 < PARTS:
             if backs:
-                made[parties + q], backs[-1][-1] = tie(made[parties + q], backs[-1][-1])
+                made[parties + q], backs[-1] = tie(made[parties + q], backs[-1])
             send(made[parties + q], spatial)
         received = spatial[:parties] if q == 0 else spatial[parties + q - 1 : parties + q]
         if q + 1 == PARTS:
-            backs[-1][-1], spatial[-1] = tie(backs[-1][-1], spatial[-1])
-            got = [exchange(backs[1][0])]
+            backs[-1], spatial[-1] = tie(backs[-1], spatial[-1])
+            got = [exchange(backs[1])]
             received = spatial[-1:]
         outs = dense(q, received, before)
-        backs.append(list(outs[: arrays_of(q)]))
-        result, kept_grad, part, bias_part, grads = outs[arrays_of(q) :]
+        back, result, kept_grad, part, bias_part, grads = outs
+        backs.append(back)
         before = (grads, result)
         later_grads.append(kept_grad)
         sums, expand_bias_grad = sums + part, expand_bias_grad + bias_part
     grads, got[0] = tie(grads, got[0])
     grads = scatter(grads, "cols")
     held = []
-    for v in [w for q in (*every[2:], 0) for w in backs[q]]:
+    for v in [backs[q] for q in (*every[2:], 0)]:
         held.append(wide_in(got[-1], as_table(doubled), False))
         if len(held) > 1:
             v, held[-2] = tie(v, held[-2])
         send(v, got)
-    rest, first, done, ready = held[: PARTS - 1], held[PARTS - 1 :], [], []
-    for g in range(parties):
-        if g + 1 == parties:
-            if done:
-                ready = [first_message(done[0][0], as_table(plain.T))]
-                ready[0], got[-1] = tie(ready[0], got[-1])
-            first.append(wide_in(got[-1], as_table(doubled), False))
-            grads, first[-1] = tie(grads, first[-1])
-            grads = scatter(grads, "rows")
-        given, extras = spectral_backward(g, [first[g]] + rest, keeps[g][1], keeps[g][2])
-        done.append((list(given), extras))
-    made = messages_out([v[0] for v in done], as_table(plain.T), ready)
-    filter_grads = []
-    for g in range(parties):
-        inner_low, _, outer_low, _ = done[g][1]
-        filter_grads.append(filter_grad(entries[g], inner_low, keeps[g][0], outer_low))
-
-    def blocks(n):
-        each = [v[n] for v in filter_grads]
-        return jnp.stack(each, axis=1) if split else gather_blocks(each[0])
-
+    got[-1], held[-1] = tie(got[-1], held[-1])
+    held.append(wide_in(got[-1], as_table(doubled), False))
+    grads, held[-1] = tie(grads, held[-1])
+    grads = scatter(grads, "rows")
+    given, (inner_low, inner_bias_grad, outer_low, outer_bias_grad) = spectral_backward(
+        [held[-1]] + held[:-1], [k[1] for k in keeps], [k[2] for k in keeps]
+    )
+    made = [wide_out([v], as_table(plain.T)) for v in given]
+    inner_grad, outer_grad = filter_grad(entries, [k[0] for k in keeps], inner_low, outer_low)
     filter_parts = (
-        blocks(0),
-        jnp.concatenate([v[1][1] for v in done], axis=1),
-        blocks(1),
-        jnp.concatenate([v[1][3] for v in done], axis=1),
+        gather_blocks(inner_grad), inner_bias_grad, gather_blocks(outer_grad), outer_bias_grad
     )
     flat = jnp.concatenate([v.reshape(-1) for v in filter_parts])
 
-    got = got[-1:]
-    for n in range(parties):
-        if n > 0:
-            made[n], made[parties] = tie(made[n], made[parties])
-        send(made[n], got)
-    grads = gather(tie(grads, got[-1])[0], ("cols", "rows"))
+    got = [exchange(made[0])]
+    send(made[1], got)
+    grads, got[0] = tie(grads, got[0])
+    grads = gather(grads, ("cols", "rows"))
     expand_sum, reduce_sum = split_grads(grads)
-    got = got[1:]
     first_sums, states_grad = [], None
     for q in every:
         if q + 1 < PARTS:
-            if q + 2 == PARTS:
-                made[parties + q], flat = tie(made[parties + q], flat)
-            if first_sums:
-                made[parties + q], first_sums[-1] = tie(made[parties + q], first_sums[-1])
-            send(made[parties + q], got)
+            if q > 0:
+                made[q + 1], first_sums[-1] = tie(made[q + 1], first_sums[-1])
+                send(made[q + 1], got)
         else:
+            flat, states_grad = tie(flat, states_grad)
             states_grad, expand_sum = tie(states_grad, expand_sum)
-        received = got[:parties] if q == 0 else got[parties + q - 1 : parties + q]
-        states_grad, part = last_norm(q, later_grads[q], received, states_grad)
+        states_grad, part = last_norm(q, later_grads[q], got[q], states_grad)
         first_sums.append(part)
-        if q == 0:
-            flat, first_sums[-1] = tie(flat, first_sums[-1])
-            flat = sum_rows(flat)
-    small = sum_small(
-        jnp.concatenate([sum(first_sums)[:2], sums[:3], expand_bias_grad.reshape(-1, chans)])
+    small, flat = sum_small(
+        jnp.concatenate([sum(first_sums)[:2], sums[:3], expand_bias_grad.reshape(-1, chans)]), flat
     )
     sizes = [v.size for v in filter_parts]
     ends = np.cumsum(sizes)

time: 1550 us -> 1520 us (0.981)
  waiting for transfers between devices: 547 us -> 764 us
  Pallas kernels: 759 us -> 598 us
  blocking collectives: 78.3 us -> 0 us
    all_to_all x15 -> x14, waiting for transfers between devices: 547 us -> 759 us  [exchange(): lax.all_to_all(sent, ('rows', 'cols'), 0, 0, tiled=True).reshape(v.shape)]
    pallas_call x8 -> x5, Pallas kernels: 254 us -> 92.8 us  [the longest x1 35.4 us: spectral_backward(): call(functools.partial(spectral_backward_kernel, factor, parties), bin_st...]
    all_to_all x1 -> x0, blocking collectives: 78.3 us -> none  [exchange(): lax.all_to_all(sent, ('rows', 'cols'), 0, 0, tiled=True).reshape(v.shape)]
    all_to_all x15 -> x14, starting transfers between devices: 104 us -> 96.6 us  [exchange(): lax.all_to_all(sent, ('rows', 'cols'), 0, 0, tiled=True).reshape(v.shape)]
    pallas_call x8 -> x7, Pallas kernels: 44.4 us -> 40.4 us  [wide_in(): call(functools.partial(wide_in_split_kernel if divided else wide_in_kerne...]
  transfers between devices with their start and end apart: 18 -> 17, of which waited for: 14 -> 15; matrix products, arithmetic and copies ran while one was open for 1% -> 1% of each run, Pallas kernels for 46% -> 36%
where the time goes in v7:
time: 1520 us; the launch traced here: 1500 us
  waiting for transfers between devices  764 us (50%)
  Pallas kernels  598 us (39%)
  starting transfers between devices  96.7 us (6%)
  local copies, waits for them, and re-layouts  24 us (2%)
    all_to_all x14, waiting for transfers between devices, exchange(): lax.all_to_all(sent, ('rows', 'cols'), 0, 0, tiled=True).reshape(v.shape)  759 us
    pallas_call x3, Pallas kernels, dense(): call(functools.partial(dense_kernel, steps, slabs, width, q == 0, arrays_...  248 us
    all_to_all x14, starting transfers between devices, exchange(): lax.all_to_all(sent, ('rows', 'cols'), 0, 0, tiled=True).reshape(v.shape)  96.6 us
    pallas_call x2, Pallas kernels, spectral_forward(): call(functools.partial(spectral_forward_kernel, factor, g), bin_steps, cu...  55 us
    pallas_call x1, Pallas kernels, sum_small(): pl.pallas_call(functools.partial(sum_kernel, ranks, groups), in_specs=[vm...  41.6 us
    pallas_call x7, Pallas kernels, wide_in(): call(functools.partial(wide_in_split_kernel if divided else wide_in_kerne...  40.4 us
    pallas_call x1, Pallas kernels, spectral_backward(): call(functools.partial(spectral_backward_kernel, factor, parties), bin_st...  35.4 us
    pallas_call x3, Pallas kernels, last_norm(): call(functools.partial(last_kernel, width, 1), steps, [packed_spec(same)]...  34.8 us
  transfers between devices with their start and end apart: 17, of which 15 were waited for; matrix products, arithmetic and copies ran while one was open for 1% of the time, Pallas kernels for 36%

profile of v7, /device:TPU:15, one launch (start us, length us, event | category | flops | bytes accessed | tf_op | source)
XLA Modules:
  0.0 1500.0 jit_solution(9166518468759477772)
XLA Ops:
  13.5 10.0 first_norm.5
  23.5 6.3 all-to-all-start
  29.8 10.0 first_norm.4
  39.8 85.6 %all-to-all-done = f32[32,88,384]{2,1,0:T(8,128)} async-done(((f32[32,88,384]{2,1,0:T(8,128)}), f32[32,88,384]{2,1,0:T(8,128)}, u32[]{:S(2)}, u32[]{:S(2)}) %all-to-all-start) | async-done | bytes 4325408 | tf_op jit(solution)/shard_map/all_to_all | solution.py:805
  125.4 6.9 all-to-all-start.1
  132.3 12.8 first_norm.3
  145.1 6.4 wide_in.7.refs_1_
  151.5 76.4 %all-to-all-done.1 = f32[32,88,384]{2,1,0:T(8,128)} async-done(((f32[32,88,384]{2,1,0:T(8,128)}), f32[32,88,384]{2,1,0:T(8,128)}, u32[]{:S(2)}, u32[]{:S(2)}) %all-to-all-start.1) | async-done | bytes 4325408 | tf_op jit(solution)/shard_map/all_to_all | solution.py:805
  227.9 6.8 all-to-all-start.2
  234.7 6.4 wide_in.8.refs_2_
  241.1 45.6 %all-to-all-done.2 = f32[32,48,384]{2,1,0:T(8,128)S(1)} async-done(((f32[32,48,384]{2,1,0:T(8,128)}), f32[32,48,384]{2,1,0:T(8,128)S(1)}, u32[]{:S(2)}, u32[]{:S(2)}) %all-to-all-start.2) | async-done | bytes 2359328 | tf_op jit(solution)/shard_map/all_to_all | solution.py:805
  288.1 6.7 all-to-all-start.3
  301.5 27.3 %spectral_forward.2 = (f32[16,2,96,192]{3,2,1,0:T(8,128)}, f32[16,2,96,192]{3,2,1,0:T(8,128)}, f32[16,2,96,192]{3,2,1,0:T(8,128)}, bf16[18432,96]{1,0:T(8,128)(2,1)}) custom-call(f32[16,2,96,192]{3,2,1,0:T(8,128)} %wide_in.9.refs_0_, f32[16,2,96,384]{3,2,1,0:T(8,128)} %wide_in.7.refs_1_, f32[16,2,96,384]{3,2,1,0:T(8,128)} %wide_in.8.refs_2_, ...), custom_call_target="tpu_custom_call" | custom-call | flops 20000000000 | bytes 51904512 | tf_op jit(solution)/shard_map/spectral_forward/pallas_call | solution.py:913
  333.5 13.3 all-to-all-done.3
  346.8 6.8 all-to-all-start.4
  358.8 27.7 %spectral_forward.3 = (f32[16,2,96,192]{3,2,1,0:T(8,128)}, f32[16,2,96,192]{3,2,1,0:T(8,128)}, f32[16,2,96,192]{3,2,1,0:T(8,128)}, bf16[18432,96]{1,0:T(8,128)(2,1)}) custom-call(f32[16,2,96,192]{3,2,1,0:T(8,128)} %wide_in.10.refs_0_, f32[16,2,96,384]{3,2,1,0:T(8,128)} %wide_in.7.refs_1_, f32[16,2,96,384]{3,2,1,0:T(8,128)} %wide_in.8.refs_2_, ...), custom_call_target="tpu_custom_call" | custom-call | flops 20000000000 | bytes 51904512 | tf_op jit(solution)/shard_map/spectral_forward/pallas_call | solution.py:913
  391.2 14.3 all-to-all-done.4
  405.5 7.1 all-to-all-start.5
  412.6 15.4 %spectral_keep.3 = (bf16[18432,96]{1,0:T(8,128)(2,1)}, bf16[18432,96]{1,0:T(8,128)(2,1)}, bf16[18432,96]{1,0:T(8,128)(2,1)}) custom-call(bf16[18432,96]{1,0:T(8,128)(2,1)} %get-tuple-element.134.entries.refs_0_, bf16[2,96,96]{2,1,0:T(8,128)(2,1)} %get-tuple-element.237.refs_5_.inner, f32[2,96]{1,0:T(2,128)} %get-tuple-element.239.refs_6_.inner_bias, ...), custom_call_target="tpu_custom_call" | custom-call | flops 10000000000 | bytes 12976128 | tf_op jit(solution)/shard_map/spectral_keep/pallas_call | solution.py:926
  434.2 15.3 %spectral_keep.2 = (bf16[18432,96]{1,0:T(8,128)(2,1)}, bf16[18432,96]{1,0:T(8,128)(2,1)}, bf16[18432,96]{1,0:T(8,128)(2,1)}) custom-call(bf16[18432,96]{1,0:T(8,128)(2,1)} %get-tuple-element.132.entries.refs_1_, bf16[2,96,96]{2,1,0:T(8,128)(2,1)} %get-tuple-element.238.refs_5_.inner, f32[2,96]{1,0:T(2,128)} %get-tuple-element.240.refs_6_.inner_bias, ...), custom_call_target="tpu_custom_call" | custom-call | flops 10000000000 | bytes 12976128 | tf_op jit(solution)/shard_map/spectral_keep/pallas_call | solution.py:926
  449.5 15.0 all-to-all-done.5
  466.0 6.8 all-to-all-start.6
  480.7 81.3 %dense_both_ways.3 = (f32[8,4,88,384]{3,2,1,0:T(8,128)}, bf16[2,264,8,768]{3,2,1,0:T(8,128)(2,1)}, f32[2,88,8,768]{3,2,1,0:T(8,128)}, f32[8,768]{1,0:T(8,128)}, f32[4,768]{1,0:T(4,128)}, /*index=5*/f32[6144,768]{1,0:T(8,128)}) custom-call(f32[8,4,48,384]{3,2,1,0:T(8,128)} %bitcast.16.refs_0_, f32[8,4,48,384]{3,2,1,0:T(8,128)} %bitcast.123, ...), custom_call_target="tpu_custom_call" | custom-call | flops 39862665216 | bytes 17301504 | tf_op jit(solution)/shard_map/dense_both_ways/pallas_call | solution.py:976
  562.0 6.3 all-to-all-done.6
  568.3 7.3 all-to-all-start.7
  575.6 83.3 %dense_both_ways.4 = (f32[8,4,88,384]{3,2,1,0:T(8,128)}, bf16[2,264,8,768]{3,2,1,0:T(8,128)(2,1)}, f32[2,88,8,768]{3,2,1,0:T(8,128)}, f32[8,768]{1,0:T(8,128)}, f32[4,768]{1,0:T(4,128)}, /*index=5*/f32[6144,768]{1,0:T(8,128)}) custom-call(f32[8,4,88,384]{3,2,1,0:T(8,128)} %bitcast.23.refs_0_, ...), custom_call_target="tpu_custom_call", output_to_operand_aliasing={{1}: (13, {})} | custom-call | flops 39862665216 | bytes 17301504 | tf_op jit(solution)/shard_map/dense_both_ways/pallas_call | solution.py:976
  659.0 12.2 all-to-all-done.7
  671.1 6.9 all-to-all-start.8
  678.1 83.2 %dense_both_ways.5 = (f32[8,4,88,384]{3,2,1,0:T(8,128)}, bf16[2,264,8,768]{3,2,1,0:T(8,128)(2,1)}, f32[2,88,8,768]{3,2,1,0:T(8,128)}, f32[8,768]{1,0:T(8,128)}, f32[4,768]{1,0:T(4,128)}, /*index=5*/f32[6144,768]{1,0:T(8,128)}) custom-call(f32[8,4,88,384]{3,2,1,0:T(8,128)} %bitcast.25.refs_0_, ...), custom_call_target="tpu_custom_call", output_to_operand_aliasing={{1}: (13, {})} | custom-call | flops 39862665216 | bytes 17301504 | tf_op jit(solution)/shard_map/dense_both_ways/pallas_call | solution.py:976
  761.3 12.4 all-to-all-done.8
  773.6 6.9 all-to-all-start.9
  780.5 6.3 wide_in.11.refs_1_
  786.8 89.3 %all-to-all-done.9 = f32[32,88,384]{2,1,0:T(8,128)} async-done(((f32[32,88,384]{2,1,0:T(8,128)}), f32[32,88,384]{2,1,0:T(8,128)}, u32[]{:S(2)}, u32[]{:S(2)}) %all-to-all-start.9) | async-done | bytes 4325408 | tf_op jit(solution)/shard_map/all_to_all | solution.py:805
  876.2 7.3 all-to-all-start.10
  891.3 87.8 %all-to-all-done.10 = f32[32,88,384]{2,1,0:T(8,128)} async-done(((f32[32,88,384]{2,1,0:T(8,128)}), f32[32,88,384]{2,1,0:T(8,128)}, u32[]{:S(2)}, u32[]{:S(2)}) %all-to-all-start.10) | async-done | bytes 4325408 | tf_op jit(solution)/shard_map/all_to_all | solution.py:805
  984.6 35.4 %spectral_backward.1 = (f32[16,2,96,384]{3,2,1,0:T(8,128)}, f32[16,2,96,384]{3,2,1,0:T(8,128)}, f32[16,2,96,384]{3,2,1,0:T(8,128)}, bf16[18432,192]{1,0:T(8,128)...) custom-call(f32[16,2,96,384]{3,2,1,0:T(8,128)} %wide_in.13.refs_0_, ...), custom_call_target="tpu_custom_call" | custom-call | flops 20000000000 | bytes 103809024 | tf_op jit(solution)/shard_map/spectral_backward/pallas_call | solution.py:943
  1025.4 6.9 all-to-all-start.11
  1037.8 109.1 %all-to-all-done.11 = f32[32,88,384]{2,1,0:T(8,128)} async-done(((f32[32,88,384]{2,1,0:T(8,128)}), f32[32,88,384]{2,1,0:T(8,128)}, u32[]{:S(2)}, u32[]{:S(2)}) %all-to-all-start.11) | async-done | bytes 4325408 | tf_op jit(solution)/shard_map/all_to_all | solution.py:805
  1146.9 6.9 all-to-all-start.12
  1159.3 11.6 first_norm_backward.3
  1170.9 151.3 %all-to-all-done.12 = f32[32,88,384]{2,1,0:T(8,128)} async-done(((f32[32,88,384]{2,1,0:T(8,128)}), f32[32,88,384]{2,1,0:T(8,128)}, u32[]{:S(2)}, u32[]{:S(2)}) %all-to-all-start.12) | async-done | bytes 4325408 | tf_op jit(solution)/shard_map/all_to_all | solution.py:805
  1322.3 7.1 all-to-all-start.13
  1329.5 22.5 %filter_grad.1 = (f32[2,192,192]{2,1,0:T(8,128)}, f32[2,192,192]{2,1,0:T(8,128)}) custom-call(bf16[18432,96]{1,0:T(8,128)(2,1)} %get-tuple-element.134.entries.refs_0_, bf16[18432,96]{1,0:T(8,128)(2,1)} %get-tuple-element.132.entries.refs_1_, bf16[18432,96]{1,0:T(8,128)(2,1)} %get-tuple-element.183.refs_2_, bf16[18432,96]{1,0:T(8,128)(2,1)} %get-tuple-element.184.refs_3_, ...), custom_call_target="tpu_custom_call" | custom-call | flops 10000000000 | bytes 25952256 | tf_op jit(solution)/shard_map/filter_grad/pallas_call | solution.py:956
  1354.8 11.6 first_norm_backward.4
  1371.9 18.4 %split_gradients.1 = (f32[768,3072]{1,0:T(8,128)}, f32[3072,768]{1,0:T(8,128)}) custom-call(f32[6144,768]{1,0:T(8,128)} %all-gather.2.cloned.1.call-done.expand_in.reduce_in, f32[6144,768]{1,0:T(8,128)} %all-gather.2.cloned.1.call-done.expand_in.reduce_in), custom_call_target="tpu_custom_call" | custom-call | bytes 37748736 | tf_op jit(solution)/shard_map/split_gradients/pallas_call | solution.py:784
  1390.3 40.8 %all-to-all-done.13 = f32[32,88,384]{2,1,0:T(8,128)} async-done(((f32[32,88,384]{2,1,0:T(8,128)}), f32[32,88,384]{2,1,0:T(8,128)}, u32[]{:S(2)}, u32[]{:S(2)}) %all-to-all-start.13) | async-done | bytes 4325408 | tf_op jit(solution)/shard_map/all_to_all | solution.py:805
  1431.2 11.6 first_norm_backward.5
  1444.2 41.6 %small_sums.1 = (f32[56,128]{1,0:T(8,128)}, f32[640,128]{1,0:T(8,128)}) custom-call(f32[56,128]{1,0:T(8,128)} %pad_bitcast_fusion.1.own, f32[640,128]{1,0:T(8,128)} %pad_bitcast_fusion.flat), custom_call_target="tpu_custom_call" | custom-call | tf_op jit(solution)/shard_map/small_sums/pallas_call | solution.py:768
  (109 shorter events, 91.2 us)
Async XLA Ops:
  23.5 101.9 %all-to-all-start = ((f32[32,88,384]{2,1,0:T(8,128)}), f32[32,88,384]{2,1,0:T(8,128)}, u32[]{:S(2)}, u32[]{:S(2)}) async-start(f32[32,88,384]{2,1,0:T(8,128)} %bitcast.110), calls=%async_computation | async-start | bytes 8650752 | tf_op jit(solution)/shard_map/all_to_all | solution.py:805
  125.4 102.5 %all-to-all-start.1 = ((f32[32,88,384]{2,1,0:T(8,128)}), f32[32,88,384]{2,1,0:T(8,128)}, u32[]{:S(2)}, u32[]{:S(2)}) async-start(f32[32,88,384]{2,1,0:T(8,128)} %bitcast.109), calls=%async_computation.1 | async-start | bytes 8650752 | tf_op jit(solution)/shard_map/all_to_all | solution.py:805
  227.9 58.8 %all-to-all-start.2 = ((f32[32,48,384]{2,1,0:T(8,128)}), f32[32,48,384]{2,1,0:T(8,128)S(1)}, u32[]{:S(2)}, u32[]{:S(2)}) async-start(f32[32,48,384]{2,1,0:T(8,128)} %bitcast.125), calls=%async_computation.2 | async-start | bytes 4718592 | tf_op jit(solution)/shard_map/all_to_all | solution.py:805
  241.1 53.7 %copy-start.16 = (f32[2,2,96]{2,1,0:T(2,128)S(1)}, f32[2,2,96]{2,1,0:T(2,128)}, u32[]{:S(2)}) copy-start(f32[2,2,96]{2,1,0:T(2,128)} %param.39) | copy-start | bytes 4612
  241.1 53.8 %copy-start.17 = (f32[2,2,96]{2,1,0:T(2,128)S(1)}, f32[2,2,96]{2,1,0:T(2,128)}, u32[]{:S(2)}) copy-start(f32[2,2,96]{2,1,0:T(2,128)} %param.41) | copy-start | bytes 4612
  241.1 54.6 %copy-start.3 = (bf16[2,2,96,96]{3,2,1,0:T(8,128)(2,1)S(1)}, bf16[2,2,96,96]{3,2,1,0:T(8,128)(2,1)}, u32[]{:S(2)}) copy-start(bf16[2,2,96,96]{3,2,1,0:T(8,128)(2,1)} %param.38) | copy-start | bytes 221188
  241.1 54.6 %copy-start.5 = (bf16[2,2,96,96]{3,2,1,0:T(8,128)(2,1)S(1)}, bf16[2,2,96,96]{3,2,1,0:T(8,128)(2,1)}, u32[]{:S(2)}) copy-start(bf16[2,2,96,96]{3,2,1,0:T(8,128)(2,1)} %param.40) | copy-start | bytes 221188
  286.7 1.4 copy-start.1
  288.1 58.7 %all-to-all-start.3 = ((f32[32,48,384]{2,1,0:T(8,128)}), f32[32,48,384]{2,1,0:T(8,128)S(1)}, u32[]{:S(2)}, u32[]{:S(2)}) async-start(f32[32,48,384]{2,1,0:T(8,128)} %bitcast.124), calls=%async_computation.3 | async-start | bytes 4718592 | tf_op jit(solution)/shard_map/all_to_all | solution.py:805
  346.8 6.8 copy-start
  346.8 58.7 %all-to-all-start.4 = ((f32[32,48,384]{2,1,0:T(8,128)}), f32[32,48,384]{2,1,0:T(8,128)}, u32[]{:S(2)}, u32[]{:S(2)}) async-start(f32[32,48,384]{2,1,0:T(8,128)} %bitcast.117), calls=%async_computation.4 | async-start | bytes 4718592 | tf_op jit(solution)/shard_map/all_to_all | solution.py:805
  405.5 59.0 %all-to-all-start.5 = ((f32[32,48,384]{2,1,0:T(8,128)}), f32[32,48,384]{2,1,0:T(8,128)S(1)}, u32[]{:S(2)}, u32[]{:S(2)}) async-start(f32[32,48,384]{2,1,0:T(8,128)} %bitcast.116), calls=%async_computation.5 | async-start | bytes 4718592 | tf_op jit(solution)/shard_map/all_to_all | solution.py:805
  464.5 1.5 copy-start.2
  464.5 8.3 copy-start.13
  464.5 8.9 copy-start.14
  464.5 9.4 copy-start.15
  466.0 102.4 %all-to-all-start.6 = ((f32[32,88,384]{2,1,0:T(8,128)}), f32[32,88,384]{2,1,0:T(8,128)}, u32[]{:S(2)}, u32[]{:S(2)}) async-start(f32[32,88,384]{2,1,0:T(8,128)} %bitcast.112), calls=%async_computation.6 | async-start | bytes 8650752 | tf_op jit(solution)/shard_map/all_to_all | solution.py:805
  568.3 102.8 %all-to-all-start.7 = ((f32[32,88,384]{2,1,0:T(8,128)}), f32[32,88,384]{2,1,0:T(8,128)}, u32[]{:S(2)}, u32[]{:S(2)}) async-start(f32[32,88,384]{2,1,0:T(8,128)} %bitcast.113), calls=%async_computation.7 | async-start | bytes 8650752 | tf_op jit(solution)/shard_map/all_to_all | solution.py:805
  671.1 102.5 %all-to-all-start.8 = ((f32[32,88,384]{2,1,0:T(8,128)}), f32[32,88,384]{2,1,0:T(8,128)}, u32[]{:S(2)}, u32[]{:S(2)}) async-start(f32[32,88,384]{2,1,0:T(8,128)} %bitcast.121), calls=%async_computation.8 | async-start | bytes 8650752 | tf_op jit(solution)/shard_map/all_to_all | solution.py:805
  678.0 306.5 %reduce-scatter.3.cloned.1.call-start = ((), (), s32[]{:S(2)}) async-start(), calls=%async_computation.16 | async-start | bytes 23592960 | tf_op jit(solution)/shard_map/reduce_scatter | solution.py:755
  773.6 102.5 %all-to-all-start.9 = ((f32[32,88,384]{2,1,0:T(8,128)}), f32[32,88,384]{2,1,0:T(8,128)}, u32[]{:S(2)}, u32[]{:S(2)}) async-start(f32[32,88,384]{2,1,0:T(8,128)} %bitcast.122), calls=%async_computation.10 | async-start | bytes 8650752 | tf_op jit(solution)/shard_map/all_to_all | solution.py:805
  876.2 7.4 copy-start.4
  876.2 7.5 copy-start.6
  876.2 102.9 %all-to-all-start.10 = ((f32[32,88,384]{2,1,0:T(8,128)}), f32[32,88,384]{2,1,0:T(8,128)}, u32[]{:S(2)}, u32[]{:S(2)}) async-start(f32[32,88,384]{2,1,0:T(8,128)} %bitcast.120), calls=%async_computation.11 | async-start | bytes 8650752 | tf_op jit(solution)/shard_map/all_to_all | solution.py:805
  883.5 263.4 %reduce-scatter.5.cloned.1.call-start = ((), (), s32[]{:S(2)}) async-start(), calls=%async_computation.17 | async-start | bytes 5308416 | tf_op jit(solution)/shard_map/reduce_scatter | solution.py:755
  1025.4 121.5 %all-to-all-start.11 = ((f32[32,88,384]{2,1,0:T(8,128)}), f32[32,88,384]{2,1,0:T(8,128)}, u32[]{:S(2)}, u32[]{:S(2)}) async-start(f32[32,88,384]{2,1,0:T(8,128)} %bitcast.115), calls=%async_computation.13 | async-start | bytes 8650752 | tf_op jit(solution)/shard_map/all_to_all | solution.py:805
  1032.3 339.6 %all-gather.2.cloned.1.call-start = ((), (), s32[]{:S(2)}) async-start(), calls=%async_computation.18 | async-start | bytes 19464192 | tf_op jit(solution)/shard_map/all_gather | solution.py:758
  1146.9 175.4 %all-to-all-start.12 = ((f32[32,88,384]{2,1,0:T(8,128)}), f32[32,88,384]{2,1,0:T(8,128)}, u32[]{:S(2)}, u32[]{:S(2)}) async-start(f32[32,88,384]{2,1,0:T(8,128)} %bitcast.114), calls=%async_computation.14 | async-start | bytes 8650752 | tf_op jit(solution)/shard_map/all_to_all | solution.py:805
  1322.3 7.1 copy-start.7
  1322.3 7.1 copy-start.8
  1322.3 7.1 copy-start.9
  1322.3 7.1 copy-start.10
  1322.3 7.1 copy-start.11
  1322.3 7.1 copy-start.12
  1322.3 108.8 %all-to-all-start.13 = ((f32[32,88,384]{2,1,0:T(8,128)}), f32[32,88,384]{2,1,0:T(8,128)}, u32[]{:S(2)}, u32[]{:S(2)}) async-start(f32[32,88,384]{2,1,0:T(8,128)} %bitcast.111), calls=%async_computation.15 | async-start | bytes 8650752 | tf_op jit(solution)/shard_map/all_to_all | solution.py:805
  1329.5 25.1 %copy-start.19 = (f32[2,192]{1,0:T(2,128)S(1)}, f32[2,192]{1,0:T(2,128)}, u32[]{:S(2)}) copy-start(f32[2,192]{1,0:T(2,128)} %get-tuple-element.188) | copy-start | bytes 4612
  1329.5 25.2 %copy-start.18 = (f32[2,192]{1,0:T(2,128)S(1)}, f32[2,192]{1,0:T(2,128)}, u32[]{:S(2)}) copy-start(f32[2,192]{1,0:T(2,128)} %get-tuple-element.190) | copy-start | bytes 4612
Sparse Core Ops, SparseCore 0:
  773.8 208.2 reduce-scatter.2
  986.1 144.4 reduce-scatter.4
  1147.0 224.8 all-gather.1

commit v8 on v7

--- a/solution.py
+++ b/solution.py
@@ -505,14 +505,57 @@
         out[half] = (inside * grad).astype(bf16)
 
 
+def row_copies(ranks, sources, slots, send, recv):
+    my_row = lax.axis_index("rows")
+    return [
+        pltpu.make_async_remote_copy(
+            src_ref=sources(i),
+            dst_ref=slots.at[i],
+            send_sem=send.at[i],
+            recv_sem=recv.at[i],
+            device_id=(lax.rem(my_row + i, ranks), lax.axis_index("cols")),
+            device_id_type=pl.DeviceIdType.MESH,
+        )
+        for i in range(1, ranks)
+    ]
+
+
+def row_piece(r, piece):
+    return pl.ds(pl.multiple_of(r * piece, piece), piece)
+
+
+def pick_kernel(ranks, flat, out, picked, send, recv):
+    my_row = lax.axis_index("rows")
+    piece = out.shape[0]
+    barrier = pltpu.get_barrier_semaphore()
+    for i in range(1, ranks):
+        pl.semaphore_signal(
+            barrier,
+            inc=1,
+            device_id=(lax.rem(my_row + i, ranks), lax.axis_index("cols")),
+            device_id_type=pl.DeviceIdType.MESH,
+        )
+    pl.semaphore_wait(barrier, ranks - 1)
+    copies = row_copies(
+        ranks, lambda i: flat.at[row_piece(lax.rem(my_row + i, ranks), piece)], picked, send, recv
+    )
+    for c in copies:
+        c.start()
+    for c in copies:
+        c.wait()
+    total = flat[row_piece(my_row, piece), :]
+    for i in range(1, ranks):
+        total = total + picked[i]
+    out[...] = total
+
+
 def sum_kernel(
-    ranks, groups, own, flat, out, flat_out,
-    got, picked, done, send_sem, recv_sem, pick_send, pick_recv, give_send, give_recv,
+    ranks, groups, own, mine, out, flat_out, got, done, send_sem, recv_sem, give_send, give_recv
 ):
     devices = ranks * groups
     my_row = lax.axis_index("rows")
     me = my_row * groups + lax.axis_index("cols")
-    piece = flat.shape[0] // ranks
+    piece = mine.shape[0]
 
     def place(i):
         other = lax.rem(me + i, devices)
@@ -528,19 +571,6 @@
             device_id_type=pl.DeviceIdType.MESH,
         )
 
-    def along(src, dst, i, send, recv):
-        return pltpu.make_async_remote_copy(
-            src_ref=src,
-            dst_ref=dst,
-            send_sem=send.at[i],
-            recv_sem=recv.at[i],
-            device_id=(lax.rem(my_row + i, ranks), lax.axis_index("cols")),
-            device_id_type=pl.DeviceIdType.MESH,
-        )
-
-    def rows_of(r):
-        return pl.ds(pl.multiple_of(r * piece, piece), piece)
-
     barrier = pltpu.get_barrier_semaphore()
 
     def greet(i, carry):
@@ -559,29 +589,17 @@
 
     lax.fori_loop(1, devices, greet, 0)
     pl.semaphore_wait(barrier, devices - 1)
-    picks = [
-        along(flat.at[rows_of(lax.rem(my_row + i, ranks))], picked.at[i], i, pick_send, pick_recv)
-        for i in range(1, ranks)
-    ]
-    for c in picks:
+    gives = row_copies(ranks, lambda i: mine, done, give_send, give_recv)
+    for c in gives:
         c.start()
     lax.fori_loop(1, devices, start, 0)
-    for c in picks:
-        c.wait()
-    total = flat[rows_of(my_row), :]
-    for i in range(1, ranks):
-        total = total + picked[i]
-    done[0] = total
-    gives = [along(done.at[0], done.at[i], i, give_send, give_recv) for i in range(1, ranks)]
-    for c in gives:
-        c.start()
+    flat_out[row_piece(my_row, piece), :] = mine[...]
     lax.fori_loop(1, devices, finish, 0)
     out[...] = lax.fori_loop(1, devices, lambda i, total: total + got[i], own[...])
     for c in gives:
         c.wait()
-    flat_out[rows_of(my_row), :] = total
     for i in range(1, ranks):
-        flat_out[rows_of(lax.rem(my_row - i + ranks, ranks)), :] = done[i]
+        flat_out[row_piece(lax.rem(my_row - i + ranks, ranks), piece), :] = done[i]
 
 
 def split_kernel(expand_in, reduce_in, expand_out, reduce_out):
@@ -757,25 +775,42 @@
     def gather(v, axis):
         return lax.all_gather(v, axis, axis=0, tiled=True)
 
-    def sum_small(v, by_rows):
-        def as_rows(v, unit):
-            v = v.reshape(-1)
-            return jnp.pad(v, (0, -v.shape[0] % (unit * 128))).reshape(-1, 128)
-
-        own, flat = as_rows(v, 8), as_rows(by_rows, 8 * ranks)
-        slots = pltpu.VMEM((ranks, flat.shape[0] // ranks, 128), f32)
-        vmem = pl.BlockSpec(memory_space=pltpu.VMEM)
+    vmem = pl.BlockSpec(memory_space=pltpu.VMEM)
+
+    def as_rows(v, unit):
+        v = v.reshape(-1)
+        return jnp.pad(v, (0, -v.shape[0] % (unit * 128))).reshape(-1, 128)
+
+    def pick_sums(v):
+        flat = as_rows(v, 8 * ranks)
+        piece = (flat.shape[0] // ranks, 128)
+        return pl.pallas_call(
+            functools.partial(pick_kernel, ranks),
+            in_specs=[vmem],
+            out_specs=vmem,
+            out_shape=shape(piece, f32),
+            scratch_shapes=[pltpu.VMEM((ranks,) + piece, f32)]
+            + [pltpu.SemaphoreType.DMA((ranks,))] * 2,
+            compiler_params=pltpu.CompilerParams(collective_id=1, has_side_effects=True),
+            name="filter_sums",
+        )(flat)
+
+    def sum_small(v, mine):
+        own = as_rows(v, 8)
         out, flat_out = pl.pallas_call(
             functools.partial(sum_kernel, ranks, groups),
             in_specs=[vmem, vmem],
             out_specs=[vmem, vmem],
-            out_shape=[shape(own.shape, f32), shape(flat.shape, f32)],
-            scratch_shapes=[pltpu.VMEM((devices,) + own.shape, f32), slots, slots]
+            out_shape=[shape(own.shape, f32), shape((ranks * mine.shape[0], 128), f32)],
+            scratch_shapes=[
+                pltpu.VMEM((devices,) + own.shape, f32),
+                pltpu.VMEM((ranks,) + mine.shape, f32),
+            ]
             + [pltpu.SemaphoreType.DMA((devices,))] * 2
-            + [pltpu.SemaphoreType.DMA((ranks,))] * 4,
+            + [pltpu.SemaphoreType.DMA((ranks,))] * 2,
             compiler_params=pltpu.CompilerParams(collective_id=0, has_side_effects=True),
             name="small_sums",
-        )(own, flat)
+        )(own, mine)
         return out.reshape(-1)[: v.size].reshape(v.shape), flat_out.reshape(-1)
 
     def split_grads(v):
@@ -1127,10 +1162,13 @@
                 made[q + 1], first_sums[-1] = tie(made[q + 1], first_sums[-1])
                 send(made[q + 1], got)
         else:
-            flat, states_grad = tie(flat, states_grad)
             states_grad, expand_sum = tie(states_grad, expand_sum)
         states_grad, part = last_norm(q, later_grads[q], got[q], states_grad)
         first_sums.append(part)
+        if q == 0:
+            flat, first_sums[0] = tie(flat, first_sums[0])
+            flat = pick_sums(flat)
+            made[2], flat = tie(made[2], flat)
     small, flat = sum_small(
         jnp.concatenate([sum(first_sums)[:2], sums[:3], expand_bias_grad.reshape(-1, chans)]), flat
     )

time: 1520 us -> 1520 us (level)
  Pallas kernels: 598 us -> 731 us
  waiting for transfers between devices: 764 us -> 633 us
    pallas_call x0 -> x1, Pallas kernels: none -> 139 us  [pick_sums(): pl.pallas_call(functools.partial(pick_kernel, ranks), in_specs=[vmem], ou...]
    all_to_all x14, waiting for transfers between devices: 759 us -> 632 us  [exchange(): lax.all_to_all(sent, ('rows', 'cols'), 0, 0, tiled=True).reshape(v.shape)]
  transfers between devices with their start and end apart: 17 -> 17, of which waited for: 15 -> 13; matrix products, arithmetic and copies ran while one was open for 1% -> 1% of each run, Pallas kernels for 36% -> 45%
where the time goes in v8:
time: 1520 us; the launch traced here: 1500 us
  Pallas kernels  731 us (48%)
  waiting for transfers between devices  633 us (42%)
  starting transfers between devices  98.9 us (7%)
  local copies, waits for them, and re-layouts  23.9 us (2%)
    all_to_all x14, waiting for transfers between devices, exchange(): lax.all_to_all(sent, ('rows', 'cols'), 0, 0, tiled=True).reshape(v.shape)  632 us
    pallas_call x3, Pallas kernels, dense(): call(functools.partial(dense_kernel, steps, slabs, width, q == 0, arrays_...  248 us
    pallas_call x1, Pallas kernels, pick_sums(): pl.pallas_call(functools.partial(pick_kernel, ranks), in_specs=[vmem], ou...  139 us
    all_to_all x14, starting transfers between devices, exchange(): lax.all_to_all(sent, ('rows', 'cols'), 0, 0, tiled=True).reshape(v.shape)  98.8 us
    pallas_call x2, Pallas kernels, spectral_forward(): call(functools.partial(spectral_forward_kernel, factor, g), bin_steps, cu...  55.1 us
    pallas_call x7, Pallas kernels, wide_in(): call(functools.partial(wide_in_split_kernel if divided else wide_in_kerne...  40.3 us
    pallas_call x1, Pallas kernels, sum_small(): pl.pallas_call(functools.partial(sum_kernel, ranks, groups), in_specs=[vm...  36.1 us
    pallas_call x1, Pallas kernels, spectral_backward(): call(functools.partial(spectral_backward_kernel, factor, parties), bin_st...  35.4 us
  transfers between devices with their start and end apart: 17, of which 13 were waited for; matrix products, arithmetic and copies ran while one was open for 1% of the time, Pallas kernels for 45%

profile of v8, /device:TPU:15, one launch (start us, length us, event | category | flops | bytes accessed | tf_op | source)
XLA Modules:
  0.0 1503.7 jit_solution(17700644351574370054)
XLA Ops:
  13.5 10.0 first_norm.5
  23.5 6.3 all-to-all-start
  29.8 10.0 first_norm.4
  39.8 85.6 %all-to-all-done = f32[32,88,384]{2,1,0:T(8,128)} async-done(((f32[32,88,384]{2,1,0:T(8,128)}), f32[32,88,384]{2,1,0:T(8,128)}, u32[]{:S(2)}, u32[]{:S(2)}) %all-to-all-start) | async-done | bytes 4325408 | tf_op jit(solution)/shard_map/all_to_all | solution.py:840
  125.4 6.9 all-to-all-start.1
  132.3 12.8 first_norm.3
  145.1 6.4 wide_in.7.refs_1_
  151.5 76.4 %all-to-all-done.1 = f32[32,88,384]{2,1,0:T(8,128)} async-done(((f32[32,88,384]{2,1,0:T(8,128)}), f32[32,88,384]{2,1,0:T(8,128)}, u32[]{:S(2)}, u32[]{:S(2)}) %all-to-all-start.1) | async-done | bytes 4325408 | tf_op jit(solution)/shard_map/all_to_all | solution.py:840
  227.9 6.8 all-to-all-start.2
  234.7 6.4 wide_in.8.refs_2_
  241.1 45.6 %all-to-all-done.2 = f32[32,48,384]{2,1,0:T(8,128)S(1)} async-done(((f32[32,48,384]{2,1,0:T(8,128)}), f32[32,48,384]{2,1,0:T(8,128)S(1)}, u32[]{:S(2)}, u32[]{:S(2)}) %all-to-all-start.2) | async-done | bytes 2359328 | tf_op jit(solution)/shard_map/all_to_all | solution.py:840
  288.1 6.7 all-to-all-start.3
  301.5 27.4 %spectral_forward.2 = (f32[16,2,96,192]{3,2,1,0:T(8,128)}, f32[16,2,96,192]{3,2,1,0:T(8,128)}, f32[16,2,96,192]{3,2,1,0:T(8,128)}, bf16[18432,96]{1,0:T(8,128)(2,1)}) custom-call(f32[16,2,96,192]{3,2,1,0:T(8,128)} %wide_in.9.refs_0_, f32[16,2,96,384]{3,2,1,0:T(8,128)} %wide_in.7.refs_1_, f32[16,2,96,384]{3,2,1,0:T(8,128)} %wide_in.8.refs_2_, ...), custom_call_target="tpu_custom_call" | custom-call | flops 20000000000 | bytes 51904512 | tf_op jit(solution)/shard_map/spectral_forward/pallas_call | solution.py:948
  333.6 13.2 all-to-all-done.3
  346.8 6.8 all-to-all-start.4
  358.8 27.7 %spectral_forward.3 = (f32[16,2,96,192]{3,2,1,0:T(8,128)}, f32[16,2,96,192]{3,2,1,0:T(8,128)}, f32[16,2,96,192]{3,2,1,0:T(8,128)}, bf16[18432,96]{1,0:T(8,128)(2,1)}) custom-call(f32[16,2,96,192]{3,2,1,0:T(8,128)} %wide_in.10.refs_0_, f32[16,2,96,384]{3,2,1,0:T(8,128)} %wide_in.7.refs_1_, f32[16,2,96,384]{3,2,1,0:T(8,128)} %wide_in.8.refs_2_, ...), custom_call_target="tpu_custom_call" | custom-call | flops 20000000000 | bytes 51904512 | tf_op jit(solution)/shard_map/spectral_forward/pallas_call | solution.py:948
  391.2 14.3 all-to-all-done.4
  405.5 7.1 all-to-all-start.5
  412.6 15.4 %spectral_keep.3 = (bf16[18432,96]{1,0:T(8,128)(2,1)}, bf16[18432,96]{1,0:T(8,128)(2,1)}, bf16[18432,96]{1,0:T(8,128)(2,1)}) custom-call(bf16[18432,96]{1,0:T(8,128)(2,1)} %get-tuple-element.136.entries.refs_0_, bf16[2,96,96]{2,1,0:T(8,128)(2,1)} %get-tuple-element.241.refs_5_.inner, f32[2,96]{1,0:T(2,128)} %get-tuple-element.243.refs_6_.inner_bias, ...), custom_call_target="tpu_custom_call" | custom-call | flops 10000000000 | bytes 12976128 | tf_op jit(solution)/shard_map/spectral_keep/pallas_call | solution.py:961
  434.2 15.3 %spectral_keep.2 = (bf16[18432,96]{1,0:T(8,128)(2,1)}, bf16[18432,96]{1,0:T(8,128)(2,1)}, bf16[18432,96]{1,0:T(8,128)(2,1)}) custom-call(bf16[18432,96]{1,0:T(8,128)(2,1)} %get-tuple-element.134.entries.refs_1_, bf16[2,96,96]{2,1,0:T(8,128)(2,1)} %get-tuple-element.242.refs_5_.inner, f32[2,96]{1,0:T(2,128)} %get-tuple-element.244.refs_6_.inner_bias, ...), custom_call_target="tpu_custom_call" | custom-call | flops 10000000000 | bytes 12976128 | tf_op jit(solution)/shard_map/spectral_keep/pallas_call | solution.py:961
  449.5 15.0 all-to-all-done.5
  465.9 6.8 all-to-all-start.6
  480.6 81.3 %dense_both_ways.3 = (f32[8,4,88,384]{3,2,1,0:T(8,128)}, bf16[2,264,8,768]{3,2,1,0:T(8,128)(2,1)}, f32[2,88,8,768]{3,2,1,0:T(8,128)}, f32[8,768]{1,0:T(8,128)}, f32[4,768]{1,0:T(4,128)}, /*index=5*/f32[6144,768]{1,0:T(8,128)}) custom-call(f32[8,4,48,384]{3,2,1,0:T(8,128)} %bitcast.16.refs_0_, f32[8,4,48,384]{3,2,1,0:T(8,128)} %bitcast.123, ...), custom_call_target="tpu_custom_call" | custom-call | flops 39862665216 | bytes 17301504 | tf_op jit(solution)/shard_map/dense_both_ways/pallas_call | solution.py:1011
  562.0 6.3 all-to-all-done.6
  568.3 7.3 all-to-all-start.7
  575.5 83.3 %dense_both_ways.4 = (f32[8,4,88,384]{3,2,1,0:T(8,128)}, bf16[2,264,8,768]{3,2,1,0:T(8,128)(2,1)}, f32[2,88,8,768]{3,2,1,0:T(8,128)}, f32[8,768]{1,0:T(8,128)}, f32[4,768]{1,0:T(4,128)}, /*index=5*/f32[6144,768]{1,0:T(8,128)}) custom-call(f32[8,4,88,384]{3,2,1,0:T(8,128)} %bitcast.23.refs_0_, ...), custom_call_target="tpu_custom_call", output_to_operand_aliasing={{1}: (13, {})} | custom-call | flops 39862665216 | bytes 17301504 | tf_op jit(solution)/shard_map/dense_both_ways/pallas_call | solution.py:1011
  658.8 12.2 all-to-all-done.7
  671.0 6.9 all-to-all-start.8
  678.0 83.2 %dense_both_ways.5 = (f32[8,4,88,384]{3,2,1,0:T(8,128)}, bf16[2,264,8,768]{3,2,1,0:T(8,128)(2,1)}, f32[2,88,8,768]{3,2,1,0:T(8,128)}, f32[8,768]{1,0:T(8,128)}, f32[4,768]{1,0:T(4,128)}, /*index=5*/f32[6144,768]{1,0:T(8,128)}) custom-call(f32[8,4,88,384]{3,2,1,0:T(8,128)} %bitcast.25.refs_0_, ...), custom_call_target="tpu_custom_call", output_to_operand_aliasing={{1}: (13, {})} | custom-call | flops 39862665216 | bytes 17301504 | tf_op jit(solution)/shard_map/dense_both_ways/pallas_call | solution.py:1011
  761.2 12.3 all-to-all-done.8
  773.6 6.9 all-to-all-start.9
  780.5 6.3 wide_in.11.refs_1_
  786.7 89.4 %all-to-all-done.9 = f32[32,88,384]{2,1,0:T(8,128)} async-done(((f32[32,88,384]{2,1,0:T(8,128)}), f32[32,88,384]{2,1,0:T(8,128)}, u32[]{:S(2)}, u32[]{:S(2)}) %all-to-all-start.9) | async-done | bytes 4325408 | tf_op jit(solution)/shard_map/all_to_all | solution.py:840
  876.1 7.3 all-to-all-start.10
  891.2 87.8 %all-to-all-done.10 = f32[32,88,384]{2,1,0:T(8,128)} async-done(((f32[32,88,384]{2,1,0:T(8,128)}), f32[32,88,384]{2,1,0:T(8,128)}, u32[]{:S(2)}, u32[]{:S(2)}) %all-to-all-start.10) | async-done | bytes 4325408 | tf_op jit(solution)/shard_map/all_to_all | solution.py:840
  984.5 35.4 %spectral_backward.1 = (f32[16,2,96,384]{3,2,1,0:T(8,128)}, f32[16,2,96,384]{3,2,1,0:T(8,128)}, f32[16,2,96,384]{3,2,1,0:T(8,128)}, bf16[18432,192]{1,0:T(8,128)...) custom-call(f32[16,2,96,384]{3,2,1,0:T(8,128)} %wide_in.13.refs_0_, ...), custom_call_target="tpu_custom_call" | custom-call | flops 20000000000 | bytes 103809024 | tf_op jit(solution)/shard_map/spectral_backward/pallas_call | solution.py:978
  1025.3 6.9 all-to-all-start.11
  1037.8 109.0 %all-to-all-done.11 = f32[32,88,384]{2,1,0:T(8,128)} async-done(((f32[32,88,384]{2,1,0:T(8,128)}), f32[32,88,384]{2,1,0:T(8,128)}, u32[]{:S(2)}, u32[]{:S(2)}) %all-to-all-start.11) | async-done | bytes 4325408 | tf_op jit(solution)/shard_map/all_to_all | solution.py:840
  1146.8 6.9 all-to-all-start.12
  1153.7 22.5 %filter_grad.1 = (f32[2,192,192]{2,1,0:T(8,128)}, f32[2,192,192]{2,1,0:T(8,128)}) custom-call(bf16[18432,96]{1,0:T(8,128)(2,1)} %get-tuple-element.136.entries.refs_0_, bf16[18432,96]{1,0:T(8,128)(2,1)} %get-tuple-element.134.entries.refs_1_, bf16[18432,96]{1,0:T(8,128)(2,1)} %get-tuple-element.174.refs_2_, bf16[18432,96]{1,0:T(8,128)(2,1)} %get-tuple-element.175.refs_3_, ...), custom_call_target="tpu_custom_call" | custom-call | flops 10000000000 | bytes 25952256 | tf_op jit(solution)/shard_map/filter_grad/pallas_call | solution.py:991
  1184.5 11.6 first_norm_backward.3
  1196.8 138.6 %filter_sums.1.mine = f32[80,128]{1,0:T(8,128)} custom-call(f32[640,128]{1,0:T(8,128)} %pad_bitcast_fusion.flat), custom_call_target="tpu_custom_call" | custom-call | tf_op jit(solution)/shard_map/filter_sums/pallas_call | solution.py:787
  1335.5 9.2 all-to-all-start.13
  1344.8 11.6 first_norm_backward.4
  1356.4 18.5 %split_gradients.1 = (f32[768,3072]{1,0:T(8,128)}, f32[3072,768]{1,0:T(8,128)}) custom-call(f32[6144,768]{1,0:T(8,128)} %all-gather.2.cloned.1.call-done.expand_in.reduce_in, f32[6144,768]{1,0:T(8,128)} %all-gather.2.cloned.1.call-done.expand_in.reduce_in), custom_call_target="tpu_custom_call" | custom-call | bytes 37748736 | tf_op jit(solution)/shard_map/split_gradients/pallas_call | solution.py:819
  1374.9 65.4 %all-to-all-done.13 = f32[32,88,384]{2,1,0:T(8,128)} async-done(((f32[32,88,384]{2,1,0:T(8,128)}), f32[32,88,384]{2,1,0:T(8,128)}, u32[]{:S(2)}, u32[]{:S(2)}) %all-to-all-start.13) | async-done | bytes 4325408 | tf_op jit(solution)/shard_map/all_to_all | solution.py:840
  1440.3 11.6 first_norm_backward.5
  1453.3 36.1 %small_sums.1 = (f32[56,128]{1,0:T(8,128)}, f32[640,128]{1,0:T(8,128)}) custom-call(f32[56,128]{1,0:T(8,128)} %pad_bitcast_fusion.1.own, f32[80,128]{1,0:T(8,128)} %filter_sums.1.mine), custom_call_target="tpu_custom_call" | custom-call | tf_op jit(solution)/shard_map/small_sums/pallas_call | solution.py:800
  (110 shorter events, 86.4 us)
Async XLA Ops:
  23.5 101.9 %all-to-all-start = ((f32[32,88,384]{2,1,0:T(8,128)}), f32[32,88,384]{2,1,0:T(8,128)}, u32[]{:S(2)}, u32[]{:S(2)}) async-start(f32[32,88,384]{2,1,0:T(8,128)} %bitcast.110), calls=%async_computation | async-start | bytes 8650752 | tf_op jit(solution)/shard_map/all_to_all | solution.py:840
  125.4 102.5 %all-to-all-start.1 = ((f32[32,88,384]{2,1,0:T(8,128)}), f32[32,88,384]{2,1,0:T(8,128)}, u32[]{:S(2)}, u32[]{:S(2)}) async-start(f32[32,88,384]{2,1,0:T(8,128)} %bitcast.109), calls=%async_computation.1 | async-start | bytes 8650752 | tf_op jit(solution)/shard_map/all_to_all | solution.py:840
  227.9 58.8 %all-to-all-start.2 = ((f32[32,48,384]{2,1,0:T(8,128)}), f32[32,48,384]{2,1,0:T(8,128)S(1)}, u32[]{:S(2)}, u32[]{:S(2)}) async-start(f32[32,48,384]{2,1,0:T(8,128)} %bitcast.125), calls=%async_computation.2 | async-start | bytes 4718592 | tf_op jit(solution)/shard_map/all_to_all | solution.py:840
  241.1 53.7 %copy-start.16 = (f32[2,2,96]{2,1,0:T(2,128)S(1)}, f32[2,2,96]{2,1,0:T(2,128)}, u32[]{:S(2)}) copy-start(f32[2,2,96]{2,1,0:T(2,128)} %param.39) | copy-start | bytes 4612
  241.1 53.8 %copy-start.17 = (f32[2,2,96]{2,1,0:T(2,128)S(1)}, f32[2,2,96]{2,1,0:T(2,128)}, u32[]{:S(2)}) copy-start(f32[2,2,96]{2,1,0:T(2,128)} %param.41) | copy-start | bytes 4612
  241.1 54.6 %copy-start.3 = (bf16[2,2,96,96]{3,2,1,0:T(8,128)(2,1)S(1)}, bf16[2,2,96,96]{3,2,1,0:T(8,128)(2,1)}, u32[]{:S(2)}) copy-start(bf16[2,2,96,96]{3,2,1,0:T(8,128)(2,1)} %param.38) | copy-start | bytes 221188
  241.1 54.6 %copy-start.5 = (bf16[2,2,96,96]{3,2,1,0:T(8,128)(2,1)S(1)}, bf16[2,2,96,96]{3,2,1,0:T(8,128)(2,1)}, u32[]{:S(2)}) copy-start(bf16[2,2,96,96]{3,2,1,0:T(8,128)(2,1)} %param.40) | copy-start | bytes 221188
  286.7 1.4 copy-start.1
  288.1 58.7 %all-to-all-start.3 = ((f32[32,48,384]{2,1,0:T(8,128)}), f32[32,48,384]{2,1,0:T(8,128)S(1)}, u32[]{:S(2)}, u32[]{:S(2)}) async-start(f32[32,48,384]{2,1,0:T(8,128)} %bitcast.124), calls=%async_computation.3 | async-start | bytes 4718592 | tf_op jit(solution)/shard_map/all_to_all | solution.py:840
  346.8 6.8 copy-start
  346.8 58.7 %all-to-all-start.4 = ((f32[32,48,384]{2,1,0:T(8,128)}), f32[32,48,384]{2,1,0:T(8,128)}, u32[]{:S(2)}, u32[]{:S(2)}) async-start(f32[32,48,384]{2,1,0:T(8,128)} %bitcast.117), calls=%async_computation.4 | async-start | bytes 4718592 | tf_op jit(solution)/shard_map/all_to_all | solution.py:840
  405.5 59.0 %all-to-all-start.5 = ((f32[32,48,384]{2,1,0:T(8,128)}), f32[32,48,384]{2,1,0:T(8,128)S(1)}, u32[]{:S(2)}, u32[]{:S(2)}) async-start(f32[32,48,384]{2,1,0:T(8,128)} %bitcast.116), calls=%async_computation.5 | async-start | bytes 4718592 | tf_op jit(solution)/shard_map/all_to_all | solution.py:840
  464.5 1.4 copy-start.2
  464.5 8.2 copy-start.13
  464.5 8.8 copy-start.14
  464.5 9.4 copy-start.15
  465.9 102.4 %all-to-all-start.6 = ((f32[32,88,384]{2,1,0:T(8,128)}), f32[32,88,384]{2,1,0:T(8,128)}, u32[]{:S(2)}, u32[]{:S(2)}) async-start(f32[32,88,384]{2,1,0:T(8,128)} %bitcast.113), calls=%async_computation.6 | async-start | bytes 8650752 | tf_op jit(solution)/shard_map/all_to_all | solution.py:840
  568.3 102.8 %all-to-all-start.7 = ((f32[32,88,384]{2,1,0:T(8,128)}), f32[32,88,384]{2,1,0:T(8,128)}, u32[]{:S(2)}, u32[]{:S(2)}) async-start(f32[32,88,384]{2,1,0:T(8,128)} %bitcast.114), calls=%async_computation.7 | async-start | bytes 8650752 | tf_op jit(solution)/shard_map/all_to_all | solution.py:840
  671.0 102.5 %all-to-all-start.8 = ((f32[32,88,384]{2,1,0:T(8,128)}), f32[32,88,384]{2,1,0:T(8,128)}, u32[]{:S(2)}, u32[]{:S(2)}) async-start(f32[32,88,384]{2,1,0:T(8,128)} %bitcast.121), calls=%async_computation.8 | async-start | bytes 8650752 | tf_op jit(solution)/shard_map/all_to_all | solution.py:840
  677.9 306.5 %reduce-scatter.3.cloned.1.call-start = ((), (), s32[]{:S(2)}) async-start(), calls=%async_computation.16 | async-start | bytes 23592960 | tf_op jit(solution)/shard_map/reduce_scatter | solution.py:773
  773.6 102.5 %all-to-all-start.9 = ((f32[32,88,384]{2,1,0:T(8,128)}), f32[32,88,384]{2,1,0:T(8,128)}, u32[]{:S(2)}, u32[]{:S(2)}) async-start(f32[32,88,384]{2,1,0:T(8,128)} %bitcast.122), calls=%async_computation.10 | async-start | bytes 8650752 | tf_op jit(solution)/shard_map/all_to_all | solution.py:840
  876.1 7.4 copy-start.4
  876.1 7.5 copy-start.6
  876.1 102.9 %all-to-all-start.10 = ((f32[32,88,384]{2,1,0:T(8,128)}), f32[32,88,384]{2,1,0:T(8,128)}, u32[]{:S(2)}, u32[]{:S(2)}) async-start(f32[32,88,384]{2,1,0:T(8,128)} %bitcast.120), calls=%async_computation.11 | async-start | bytes 8650752 | tf_op jit(solution)/shard_map/all_to_all | solution.py:840
  883.4 263.4 %reduce-scatter.5.cloned.1.call-start = ((), (), s32[]{:S(2)}) async-start(), calls=%async_computation.17 | async-start | bytes 5308416 | tf_op jit(solution)/shard_map/reduce_scatter | solution.py:773
  1025.3 121.5 %all-to-all-start.11 = ((f32[32,88,384]{2,1,0:T(8,128)}), f32[32,88,384]{2,1,0:T(8,128)}, u32[]{:S(2)}, u32[]{:S(2)}) async-start(f32[32,88,384]{2,1,0:T(8,128)} %bitcast.115), calls=%async_computation.13 | async-start | bytes 8650752 | tf_op jit(solution)/shard_map/all_to_all | solution.py:840
  1032.2 324.2 %all-gather.2.cloned.1.call-start = ((), (), s32[]{:S(2)}) async-start(), calls=%async_computation.18 | async-start | bytes 19464192 | tf_op jit(solution)/shard_map/all_gather | solution.py:776
  1146.8 188.6 %all-to-all-start.12 = ((f32[32,88,384]{2,1,0:T(8,128)}), f32[32,88,384]{2,1,0:T(8,128)}, u32[]{:S(2)}, u32[]{:S(2)}) async-start(f32[32,88,384]{2,1,0:T(8,128)} %bitcast.111), calls=%async_computation.14 | async-start | bytes 8650752 | tf_op jit(solution)/shard_map/all_to_all | solution.py:840
  1153.7 25.1 %copy-start.19 = (f32[2,192]{1,0:T(2,128)S(1)}, f32[2,192]{1,0:T(2,128)}, u32[]{:S(2)}) copy-start(f32[2,192]{1,0:T(2,128)} %get-tuple-element.179) | copy-start | bytes 4612
  1153.7 25.1 %copy-start.18 = (f32[2,192]{1,0:T(2,128)S(1)}, f32[2,192]{1,0:T(2,128)}, u32[]{:S(2)}) copy-start(f32[2,192]{1,0:T(2,128)} %get-tuple-element.181) | copy-start | bytes 4612
  1335.4 9.3 copy-start.7
  1335.4 9.3 copy-start.8
  1335.4 9.3 copy-start.9
  1335.4 9.3 copy-start.10
  1335.4 9.3 copy-start.11
  1335.5 9.3 copy-start.12
  1335.5 104.8 %all-to-all-start.13 = ((f32[32,88,384]{2,1,0:T(8,128)}), f32[32,88,384]{2,1,0:T(8,128)}, u32[]{:S(2)}, u32[]{:S(2)}) async-start(f32[32,88,384]{2,1,0:T(8,128)} %bitcast.112), calls=%async_computation.15 | async-start | bytes 8650752 | tf_op jit(solution)/shard_map/all_to_all | solution.py:840
Sparse Core Ops, SparseCore 0:
  773.7 208.2 reduce-scatter.2
  986.1 144.4 reduce-scatter.4
  1146.9 197.3 all-gather.1

commit v9 on v8

--- a/solution.py
+++ b/solution.py
@@ -266,17 +266,29 @@
     bins_out(given, table_up, width, values)
 
 
-def spectral_keep_kernel(tall, entries, inner, inner_bias, outer, outer_bias, active, slope, damp):
-    acts = []
-    for n, v in enumerate(activate(entries[...], inner, inner_bias, tall)):
-        cdf, der = phi_parts(v)
-        acts.append((v * cdf).astype(bf16))
-        slope[n * tall : (n + 1) * tall, :] = der.astype(bf16)
-    act = jnp.concatenate(acts, axis=0)
-    active[...] = act
-    for n, v in enumerate(activate(act, outer, outer_bias, tall)):
-        t = jnp.tanh(v * (1.0 / shrink_width))
-        damp[n * tall : (n + 1) * tall, :] = (t * t).astype(bf16)
+def spectral_keep_kernel(tall, parties, *refs):
+    entries, refs = refs[:parties], refs[parties:]
+    mixes, (active, slope, damp) = refs[: 4 * parties], refs[4 * parties :]
+
+    def joined_parts(each):
+        return [jnp.concatenate(v, axis=1) if parties > 1 else v[0] for v in zip(*each)]
+
+    acts, slopes, damps = [], [], []
+    for g in range(parties):
+        inner, inner_bias, outer, outer_bias = mixes[4 * g : 4 * g + 4]
+        acts.append([])
+        slopes.append([])
+        damps.append([])
+        for v in activate(entries[g][...], inner, inner_bias, tall):
+            cdf, der = phi_parts(v)
+            acts[g].append((v * cdf).astype(bf16))
+            slopes[g].append(der.astype(bf16))
+        for v in activate(jnp.concatenate(acts[g], axis=0), outer, outer_bias, tall):
+            t = jnp.tanh(v * (1.0 / shrink_width))
+            damps[g].append((t * t).astype(bf16))
+    for ref, each in ((active, acts), (slope, slopes), (damp, damps)):
+        for n, v in enumerate(joined_parts(each)):
+            ref[n * tall : (n + 1) * tall, :] = v
 
 
 def joined(refs):
@@ -330,8 +342,8 @@
 
 
 def filter_grad_kernel(tall, parties, *refs):
-    entries, active = refs[:parties], refs[parties : 2 * parties]
-    inner_low, outer_low, inner_grad, outer_grad = refs[2 * parties :]
+    entries, active = refs[:parties], refs[parties : parties + 1]
+    inner_low, outer_low, inner_grad, outer_grad = refs[parties + 1 :]
 
     @pl.when(pl.program_id(0) == 0)
     def _():
@@ -957,47 +969,47 @@
         )(*held, table, as_table(up), *forward_mix[g])
         return outs[:PARTS], outs[PARTS]
 
-    def spectral_keep(g, entries):
-        return call(
-            functools.partial(spectral_keep_kernel, height),
-            bin_steps,
-            [kept] + forward_specs,
-            [kept] * 3,
-            [kept_shape] * 3,
-            "spectral_keep",
-            flops=10 * 10**9,
-            nbytes=2 * PARTS * message // parties,
-        )(entries, *forward_mix[g])
-
     full = pl.BlockSpec((group_rows, width), lambda i: (i, 0))
     full_shape = shape((bin_steps * group_rows, width), bf16)
     full_mix, full_bias = whole((2, width, width)), whole((2, width))
     inner_t, outer_t = turn(spread(filter_inner)), turn(spread(filter_outer))
 
+    def spectral_keep(entries):
+        return call(
+            functools.partial(spectral_keep_kernel, height, parties),
+            bin_steps,
+            [kept] * parties + forward_specs * parties,
+            [full] * 3,
+            [full_shape] * 3,
+            "spectral_keep",
+            flops=10 * 10**9,
+            nbytes=2 * PARTS * message,
+        )(*entries, *[v for mix in forward_mix for v in mix])
+
     def spectral_backward(held, slope, damp):
         outs = call(
-            functools.partial(spectral_backward_kernel, factor, parties),
+            functools.partial(spectral_backward_kernel, factor, 1),
             bin_steps,
-            [held_bins] * PARTS + [up_spec, up_spec, full_mix, full_mix] + [kept] * (2 * parties),
+            [held_bins] * PARTS + [up_spec, up_spec, full_mix, full_mix] + [full] * 2,
             [held_bins] * PARTS + [full, full_bias] * 2,
             [held_shape] * PARTS + [full_shape, shape((2, width), f32)] * 2,
             "spectral_backward",
             flops=20 * 10**9,
             nbytes=8 * PARTS * message,
-        )(*held, as_table(down), as_table(up), inner_t, outer_t, *slope, *damp)
+        )(*held, as_table(down), as_table(up), inner_t, outer_t, slope, damp)
         return outs[:PARTS], outs[PARTS:]
 
     def filter_grad(entries, active, inner_low, outer_low):
         return call(
             functools.partial(filter_grad_kernel, height, parties),
             bin_steps,
-            [kept] * (2 * parties) + [full] * 2,
+            [kept] * parties + [full] * 3,
             [full_mix] * 2,
             [shape((2, width, width), f32)] * 2,
             "filter_grad",
             flops=10 * 10**9,
             nbytes=2 * PARTS * message,
-        )(*entries, *active, inner_low, outer_low)
+        )(*entries, active, inner_low, outer_low)
 
     slab = chans
     slabs = hidden // slab
@@ -1103,13 +1115,12 @@
     done = [spectral_forward(g, [first[g]] + rest) for g in range(parties)]
     entries = [v[1] for v in done]
     made = messages_out([v[0] for v in done], as_table(doubled.T))
-    keeps = [list(spectral_keep(g, entries[g])) for g in range(parties)]
+    active, slope, damp = spectral_keep(entries)
 
     spatial = got[-1:]
     for n in range(parties):
         send(made[n], spatial)
-    for keep in keeps:
-        keep[0], made[parties] = tie(keep[0], made[parties])
+    active, made[parties] = tie(active, made[parties])
     spatial = spatial[1:]
     backs, later_grads, sums, expand_bias_grad, before = [], [], 0.0, 0.0, ()
     for q in every:
@@ -1141,10 +1152,10 @@
     grads, held[-1] = tie(grads, held[-1])
     grads = scatter(grads, "rows")
     given, (inner_low, inner_bias_grad, outer_low, outer_bias_grad) = spectral_backward(
-        [held[-1]] + held[:-1], [k[1] for k in keeps], [k[2] for k in keeps]
+        [held[-1]] + held[:-1], slope, damp
     )
     made = [wide_out([v], as_table(plain.T)) for v in given]
-    inner_grad, outer_grad = filter_grad(entries, [k[0] for k in keeps], inner_low, outer_low)
+    inner_grad, outer_grad = filter_grad(entries, active, inner_low, outer_low)
     filter_parts = (
         gather_blocks(inner_grad), inner_bias_grad, gather_blocks(outer_grad), outer_bias_grad
     )
@@ -1162,13 +1173,14 @@
                 made[q + 1], first_sums[-1] = tie(made[q + 1], first_sums[-1])
                 send(made[q + 1], got)
         else:
+            flat, expand_sum = tie(flat, expand_sum)
+            flat = pick_sums(flat)
+            states_grad, flat = tie(states_grad, flat)
             states_grad, expand_sum = tie(states_grad, expand_sum)
         states_grad, part = last_norm(q, later_grads[q], got[q], states_grad)
         first_sums.append(part)
         if q == 0:
             flat, first_sums[0] = tie(flat, first_sums[0])
-            flat = pick_sums(flat)
-            made[2], flat = tie(made[2], flat)
     small, flat = sum_small(
         jnp.concatenate([sum(first_sums)[:2], sums[:3], expand_bias_grad.reshape(-1, chans)]), flat
     )

time: 1520 us -> 1510 us (level)
  Pallas kernels: 731 us -> 629 us
  waiting for transfers between devices: 633 us -> 734 us
    pallas_call x1, Pallas kernels: 139 us -> 48.3 us  [pick_sums(): pl.pallas_call(functools.partial(pick_kernel, ranks), in_specs=[vmem], ou...]
    all_to_all x14, waiting for transfers between devices: 632 us -> 703 us  [exchange(): lax.all_to_all(sent, ('rows', 'cols'), 0, 0, tiled=True).reshape(v.shape)]
    all_gather x1, waiting for transfers between devices: 0.01 us -> 30.8 us  [gather(): return lax.all_gather(v, axis, axis=0, tiled=True)]
    pallas_call x3 -> x2, Pallas kernels: 66.1 us -> 57.3 us  [the longest x1 33.4 us: spectral_backward(): call(functools.partial(spectral_backward_kernel, factor, 1), bin_steps, [...]
  transfers between devices with their start and end apart: 17 -> 17, of which waited for: 13 -> 14; matrix products, arithmetic and copies ran while one was open for 1% -> 1% of each run, Pallas kernels for 45% -> 38%
where the time goes in v9:
time: 1510 us; the launch traced here: 1500 us
  waiting for transfers between devices  734 us (49%)
  Pallas kernels  629 us (42%)
  starting transfers between devices  96.7 us (6%)
  local copies, waits for them, and re-layouts  24 us (2%)
    all_to_all x14, waiting for transfers between devices, exchange(): lax.all_to_all(sent, ('rows', 'cols'), 0, 0, tiled=True).reshape(v.shape)  703 us
    pallas_call x3, Pallas kernels, dense(): call(functools.partial(dense_kernel, steps, slabs, width, q == 0, arrays_...  248 us
    all_to_all x14, starting transfers between devices, exchange(): lax.all_to_all(sent, ('rows', 'cols'), 0, 0, tiled=True).reshape(v.shape)  96.6 us
    pallas_call x2, Pallas kernels, spectral_forward(): call(functools.partial(spectral_forward_kernel, factor, g), bin_steps, cu...  55 us
    pallas_call x1, Pallas kernels, pick_sums(): pl.pallas_call(functools.partial(pick_kernel, ranks), in_specs=[vmem], ou...  48.3 us
    pallas_call x7, Pallas kernels, wide_in(): call(functools.partial(wide_in_split_kernel if divided else wide_in_kerne...  40.3 us
    pallas_call x1, Pallas kernels, sum_small(): pl.pallas_call(functools.partial(sum_kernel, ranks, groups), in_specs=[vm...  35.7 us
    pallas_call x3, Pallas kernels, last_norm(): call(functools.partial(last_kernel, width, 1), steps, [packed_spec(same)]...  34.9 us
  transfers between devices with their start and end apart: 17, of which 14 were waited for; matrix products, arithmetic and copies ran while one was open for 1% of the time, Pallas kernels for 38%

profile of v9, /device:TPU:15, one launch (start us, length us, event | category | flops | bytes accessed | tf_op | source)
XLA Modules:
  0.0 1501.3 jit_solution(5102681593012557496)
XLA Ops:
  13.5 10.0 first_norm.5
  23.5 6.3 all-to-all-start
  29.8 10.0 first_norm.4
  39.9 85.6 %all-to-all-done = f32[32,88,384]{2,1,0:T(8,128)} async-done(((f32[32,88,384]{2,1,0:T(8,128)}), f32[32,88,384]{2,1,0:T(8,128)}, u32[]{:S(2)}, u32[]{:S(2)}) %all-to-all-start) | async-done | bytes 4325408 | tf_op jit(solution)/shard_map/all_to_all | solution.py:852
  125.4 6.9 all-to-all-start.1
  132.3 12.8 first_norm.3
  145.1 6.3 wide_in.7.refs_1_
  151.5 76.5 %all-to-all-done.1 = f32[32,88,384]{2,1,0:T(8,128)} async-done(((f32[32,88,384]{2,1,0:T(8,128)}), f32[32,88,384]{2,1,0:T(8,128)}, u32[]{:S(2)}, u32[]{:S(2)}) %all-to-all-start.1) | async-done | bytes 4325408 | tf_op jit(solution)/shard_map/all_to_all | solution.py:852
  227.9 6.8 all-to-all-start.2
  234.8 6.4 wide_in.8.refs_2_
  241.2 45.6 %all-to-all-done.2 = f32[32,48,384]{2,1,0:T(8,128)S(1)} async-done(((f32[32,48,384]{2,1,0:T(8,128)}), f32[32,48,384]{2,1,0:T(8,128)S(1)}, u32[]{:S(2)}, u32[]{:S(2)}) %all-to-all-start.2) | async-done | bytes 2359328 | tf_op jit(solution)/shard_map/all_to_all | solution.py:852
  288.1 6.7 all-to-all-start.3
  301.6 27.3 %spectral_forward.2 = (f32[16,2,96,192]{3,2,1,0:T(8,128)}, f32[16,2,96,192]{3,2,1,0:T(8,128)}, f32[16,2,96,192]{3,2,1,0:T(8,128)}, bf16[18432,96]{1,0:T(8,128)(2,1)}) custom-call(f32[16,2,96,192]{3,2,1,0:T(8,128)} %wide_in.9.refs_0_, f32[16,2,96,384]{3,2,1,0:T(8,128)} %wide_in.7.refs_1_, f32[16,2,96,384]{3,2,1,0:T(8,128)} %wide_in.8.refs_2_, ...), custom_call_target="tpu_custom_call" | custom-call | flops 20000000000 | bytes 51904512 | tf_op jit(solution)/shard_map/spectral_forward/pallas_call | solution.py:960
  333.5 13.3 all-to-all-done.3
  346.8 6.8 all-to-all-start.4
  358.8 27.7 %spectral_forward.3 = (f32[16,2,96,192]{3,2,1,0:T(8,128)}, f32[16,2,96,192]{3,2,1,0:T(8,128)}, f32[16,2,96,192]{3,2,1,0:T(8,128)}, bf16[18432,96]{1,0:T(8,128)(2,1)}) custom-call(f32[16,2,96,192]{3,2,1,0:T(8,128)} %wide_in.10.refs_0_, f32[16,2,96,384]{3,2,1,0:T(8,128)} %wide_in.7.refs_1_, f32[16,2,96,384]{3,2,1,0:T(8,128)} %wide_in.8.refs_2_, ...), custom_call_target="tpu_custom_call" | custom-call | flops 20000000000 | bytes 51904512 | tf_op jit(solution)/shard_map/spectral_forward/pallas_call | solution.py:960
  391.2 14.3 all-to-all-done.4
  405.5 7.1 all-to-all-start.5
  412.7 6.3 wide_out.10
  419.0 24.0 %spectral_keep.1 = (bf16[18432,192]{1,0:T(8,128)(2,1)}, bf16[18432,192]{1,0:T(8,128)(2,1)}, bf16[18432,192]{1,0:T(8,128)(2,1)}) custom-call(bf16[18432,96]{1,0:T(8,128)(2,1)} %get-tuple-element.131.refs_0_, bf16[18432,96]{1,0:T(8,128)(2,1)} %get-tuple-element.132.refs_1_, bf16[2,96,96]{2,1,0:T(8,128)(2,1)} %get-tuple-element.235.refs_5_.refs_2_, ...), custom_call_target="tpu_custom_call" | custom-call | flops 10000000000 | bytes 25952256 | tf_op jit(solution)/shard_map/spectral_keep/pallas_call | solution.py:978
  442.9 21.6 %all-to-all-done.5 = f32[32,48,384]{2,1,0:T(8,128)S(1)} async-done(((f32[32,48,384]{2,1,0:T(8,128)}), f32[32,48,384]{2,1,0:T(8,128)S(1)}, u32[]{:S(2)}, u32[]{:S(2)}) %all-to-all-start.5) | async-done | bytes 2359328 | tf_op jit(solution)/shard_map/all_to_all | solution.py:852
  465.9 6.8 all-to-all-start.6
  480.7 81.2 %dense_both_ways.3 = (f32[8,4,88,384]{3,2,1,0:T(8,128)}, bf16[2,264,8,768]{3,2,1,0:T(8,128)(2,1)}, f32[2,88,8,768]{3,2,1,0:T(8,128)}, f32[8,768]{1,0:T(8,128)}, f32[4,768]{1,0:T(4,128)}, /*index=5*/f32[6144,768]{1,0:T(8,128)}) custom-call(f32[8,4,48,384]{3,2,1,0:T(8,128)} %bitcast.16.refs_0_, f32[8,4,48,384]{3,2,1,0:T(8,128)} %bitcast.124, ...), custom_call_target="tpu_custom_call" | custom-call | flops 39862665216 | bytes 17301504 | tf_op jit(solution)/shard_map/dense_both_ways/pallas_call | solution.py:1023
  561.9 6.4 all-to-all-done.6
  568.3 7.3 all-to-all-start.7
  575.6 83.3 %dense_both_ways.4 = (f32[8,4,88,384]{3,2,1,0:T(8,128)}, bf16[2,264,8,768]{3,2,1,0:T(8,128)(2,1)}, f32[2,88,8,768]{3,2,1,0:T(8,128)}, f32[8,768]{1,0:T(8,128)}, f32[4,768]{1,0:T(4,128)}, /*index=5*/f32[6144,768]{1,0:T(8,128)}) custom-call(f32[8,4,88,384]{3,2,1,0:T(8,128)} %bitcast.23.refs_0_, ...), custom_call_target="tpu_custom_call", output_to_operand_aliasing={{1}: (13, {})} | custom-call | flops 39862665216 | bytes 17301504 | tf_op jit(solution)/shard_map/dense_both_ways/pallas_call | solution.py:1023
  659.0 12.1 all-to-all-done.7
  671.1 6.9 all-to-all-start.8
  678.0 83.2 %dense_both_ways.5 = (f32[8,4,88,384]{3,2,1,0:T(8,128)}, bf16[2,264,8,768]{3,2,1,0:T(8,128)(2,1)}, f32[2,88,8,768]{3,2,1,0:T(8,128)}, f32[8,768]{1,0:T(8,128)}, f32[4,768]{1,0:T(4,128)}, /*index=5*/f32[6144,768]{1,0:T(8,128)}) custom-call(f32[8,4,88,384]{3,2,1,0:T(8,128)} %bitcast.25.refs_0_, ...), custom_call_target="tpu_custom_call", output_to_operand_aliasing={{1}: (13, {})} | custom-call | flops 39862665216 | bytes 17301504 | tf_op jit(solution)/shard_map/dense_both_ways/pallas_call | solution.py:1023
  761.2 12.4 all-to-all-done.8
  773.6 6.9 all-to-all-start.9
  786.7 89.4 %all-to-all-done.9 = f32[32,88,384]{2,1,0:T(8,128)} async-done(((f32[32,88,384]{2,1,0:T(8,128)}), f32[32,88,384]{2,1,0:T(8,128)}, u32[]{:S(2)}, u32[]{:S(2)}) %all-to-all-start.9) | async-done | bytes 4325408 | tf_op jit(solution)/shard_map/all_to_all | solution.py:852
  876.1 7.3 all-to-all-start.10
  891.3 87.7 %all-to-all-done.10 = f32[32,88,384]{2,1,0:T(8,128)} async-done(((f32[32,88,384]{2,1,0:T(8,128)}), f32[32,88,384]{2,1,0:T(8,128)}, u32[]{:S(2)}, u32[]{:S(2)}) %all-to-all-start.10) | async-done | bytes 4325408 | tf_op jit(solution)/shard_map/all_to_all | solution.py:852
  984.6 33.4 %spectral_backward.1 = (f32[16,2,96,384]{3,2,1,0:T(8,128)}, f32[16,2,96,384]{3,2,1,0:T(8,128)}, f32[16,2,96,384]{3,2,1,0:T(8,128)}, bf16[18432,192]{1,0:T(8,128)...) custom-call(f32[16,2,96,384]{3,2,1,0:T(8,128)} %wide_in.13.refs_0_, ...), custom_call_target="tpu_custom_call" | custom-call | flops 20000000000 | bytes 103809024 | tf_op jit(solution)/shard_map/spectral_backward/pallas_call | solution.py:990
  1023.4 6.9 all-to-all-start.11
  1035.8 109.9 %all-to-all-done.11 = f32[32,88,384]{2,1,0:T(8,128)} async-done(((f32[32,88,384]{2,1,0:T(8,128)}), f32[32,88,384]{2,1,0:T(8,128)}, u32[]{:S(2)}, u32[]{:S(2)}) %all-to-all-start.11) | async-done | bytes 4325408 | tf_op jit(solution)/shard_map/all_to_all | solution.py:852
  1145.8 6.8 all-to-all-start.12
  1152.6 20.7 %filter_grad.1 = (f32[2,192,192]{2,1,0:T(8,128)}, f32[2,192,192]{2,1,0:T(8,128)}) custom-call(bf16[18432,96]{1,0:T(8,128)(2,1)} %get-tuple-element.131.refs_0_, bf16[18432,96]{1,0:T(8,128)(2,1)} %get-tuple-element.132.refs_1_, bf16[18432,192]{1,0:T(8,128)(2,1)} %get-tuple-element.167.refs_2_, bf16[18432,192]{1,0:T(8,128)(2,1)} %get-tuple-element.168.refs_3_, ...), custom_call_target="tpu_custom_call" | custom-call | flops 10000000000 | bytes 25952256 | tf_op jit(solution)/shard_map/filter_grad/pallas_call | solution.py:1003
  1181.5 11.6 first_norm_backward.3
  1193.1 128.0 %all-to-all-done.12 = f32[32,88,384]{2,1,0:T(8,128)} async-done(((f32[32,88,384]{2,1,0:T(8,128)}), f32[32,88,384]{2,1,0:T(8,128)}, u32[]{:S(2)}, u32[]{:S(2)}) %all-to-all-start.12) | async-done | bytes 4325408 | tf_op jit(solution)/shard_map/all_to_all | solution.py:852
  1321.1 7.1 all-to-all-start.13
  1328.2 11.7 first_norm_backward.4
  1339.9 30.8 %all-gather.2.cloned.1.call-done.expand_in.reduce_in = f32[6144,768]{1,0:T(8,128)} async-done(((f32[192,768]{1,0:T(8,128)}), f32[6144,768]{1,0:T(8,128)}) %all-gather.2.cloned.1.call-update) | async-done | bytes 18874384 | tf_op jit(solution)/shard_map/all_gather | solution.py:788
  1370.7 18.4 %split_gradients.1 = (f32[768,3072]{1,0:T(8,128)}, f32[3072,768]{1,0:T(8,128)}) custom-call(f32[6144,768]{1,0:T(8,128)} %all-gather.2.cloned.1.call-done.expand_in.reduce_in, f32[6144,768]{1,0:T(8,128)} %all-gather.2.cloned.1.call-done.expand_in.reduce_in), custom_call_target="tpu_custom_call" | custom-call | bytes 37748736 | tf_op jit(solution)/shard_map/split_gradients/pallas_call | solution.py:831
  1390.0 48.3 %filter_sums.1.mine = f32[80,128]{1,0:T(8,128)} custom-call(f32[640,128]{1,0:T(8,128)} %pad_bitcast_fusion.flat), custom_call_target="tpu_custom_call" | custom-call | tf_op jit(solution)/shard_map/filter_sums/pallas_call | solution.py:799
  1438.2 11.6 first_norm_backward.5
  1451.3 35.7 %small_sums.1 = (f32[56,128]{1,0:T(8,128)}, f32[640,128]{1,0:T(8,128)}) custom-call(f32[56,128]{1,0:T(8,128)} %pad_bitcast_fusion.1.own, f32[80,128]{1,0:T(8,128)} %filter_sums.1.mine), custom_call_target="tpu_custom_call" | custom-call | tf_op jit(solution)/shard_map/small_sums/pallas_call | solution.py:812
  (109 shorter events, 86.4 us)
Async XLA Ops:
  23.5 101.9 %all-to-all-start = ((f32[32,88,384]{2,1,0:T(8,128)}), f32[32,88,384]{2,1,0:T(8,128)}, u32[]{:S(2)}, u32[]{:S(2)}) async-start(f32[32,88,384]{2,1,0:T(8,128)} %bitcast.110), calls=%async_computation | async-start | bytes 8650752 | tf_op jit(solution)/shard_map/all_to_all | solution.py:852
  125.4 102.5 %all-to-all-start.1 = ((f32[32,88,384]{2,1,0:T(8,128)}), f32[32,88,384]{2,1,0:T(8,128)}, u32[]{:S(2)}, u32[]{:S(2)}) async-start(f32[32,88,384]{2,1,0:T(8,128)} %bitcast.109), calls=%async_computation.1 | async-start | bytes 8650752 | tf_op jit(solution)/shard_map/all_to_all | solution.py:852
  227.9 58.8 %all-to-all-start.2 = ((f32[32,48,384]{2,1,0:T(8,128)}), f32[32,48,384]{2,1,0:T(8,128)S(1)}, u32[]{:S(2)}, u32[]{:S(2)}) async-start(f32[32,48,384]{2,1,0:T(8,128)} %bitcast.125), calls=%async_computation.2 | async-start | bytes 4718592 | tf_op jit(solution)/shard_map/all_to_all | solution.py:852
  241.1 53.7 %copy-start.16 = (f32[2,2,96]{2,1,0:T(2,128)S(1)}, f32[2,2,96]{2,1,0:T(2,128)}, u32[]{:S(2)}) copy-start(f32[2,2,96]{2,1,0:T(2,128)} %param.39) | copy-start | bytes 4612
  241.1 53.8 %copy-start.17 = (f32[2,2,96]{2,1,0:T(2,128)S(1)}, f32[2,2,96]{2,1,0:T(2,128)}, u32[]{:S(2)}) copy-start(f32[2,2,96]{2,1,0:T(2,128)} %param.41) | copy-start | bytes 4612
  241.1 54.6 %copy-start.3 = (bf16[2,2,96,96]{3,2,1,0:T(8,128)(2,1)S(1)}, bf16[2,2,96,96]{3,2,1,0:T(8,128)(2,1)}, u32[]{:S(2)}) copy-start(bf16[2,2,96,96]{3,2,1,0:T(8,128)(2,1)} %param.38) | copy-start | bytes 221188
  241.1 54.6 %copy-start.5 = (bf16[2,2,96,96]{3,2,1,0:T(8,128)(2,1)S(1)}, bf16[2,2,96,96]{3,2,1,0:T(8,128)(2,1)}, u32[]{:S(2)}) copy-start(bf16[2,2,96,96]{3,2,1,0:T(8,128)(2,1)} %param.40) | copy-start | bytes 221188
  286.7 1.4 copy-start.1
  288.1 58.7 %all-to-all-start.3 = ((f32[32,48,384]{2,1,0:T(8,128)}), f32[32,48,384]{2,1,0:T(8,128)S(1)}, u32[]{:S(2)}, u32[]{:S(2)}) async-start(f32[32,48,384]{2,1,0:T(8,128)} %bitcast.123), calls=%async_computation.3 | async-start | bytes 4718592 | tf_op jit(solution)/shard_map/all_to_all | solution.py:852
  346.8 6.8 copy-start
  346.8 58.7 %all-to-all-start.4 = ((f32[32,48,384]{2,1,0:T(8,128)}), f32[32,48,384]{2,1,0:T(8,128)}, u32[]{:S(2)}, u32[]{:S(2)}) async-start(f32[32,48,384]{2,1,0:T(8,128)} %bitcast.116), calls=%async_computation.4 | async-start | bytes 4718592 | tf_op jit(solution)/shard_map/all_to_all | solution.py:852
  405.5 59.0 %all-to-all-start.5 = ((f32[32,48,384]{2,1,0:T(8,128)}), f32[32,48,384]{2,1,0:T(8,128)S(1)}, u32[]{:S(2)}, u32[]{:S(2)}) async-start(f32[32,48,384]{2,1,0:T(8,128)} %bitcast.117), calls=%async_computation.5 | async-start | bytes 4718592 | tf_op jit(solution)/shard_map/all_to_all | solution.py:852
  464.5 1.4 copy-start.2
  464.5 8.2 copy-start.13
  464.5 8.8 copy-start.14
  464.5 9.4 copy-start.15
  465.9 102.4 %all-to-all-start.6 = ((f32[32,88,384]{2,1,0:T(8,128)}), f32[32,88,384]{2,1,0:T(8,128)}, u32[]{:S(2)}, u32[]{:S(2)}) async-start(f32[32,88,384]{2,1,0:T(8,128)} %bitcast.113), calls=%async_computation.6 | async-start | bytes 8650752 | tf_op jit(solution)/shard_map/all_to_all | solution.py:852
  568.3 102.8 %all-to-all-start.7 = ((f32[32,88,384]{2,1,0:T(8,128)}), f32[32,88,384]{2,1,0:T(8,128)}, u32[]{:S(2)}, u32[]{:S(2)}) async-start(f32[32,88,384]{2,1,0:T(8,128)} %bitcast.114), calls=%async_computation.7 | async-start | bytes 8650752 | tf_op jit(solution)/shard_map/all_to_all | solution.py:852
  671.1 102.5 %all-to-all-start.8 = ((f32[32,88,384]{2,1,0:T(8,128)}), f32[32,88,384]{2,1,0:T(8,128)}, u32[]{:S(2)}, u32[]{:S(2)}) async-start(f32[32,88,384]{2,1,0:T(8,128)} %bitcast.121), calls=%async_computation.8 | async-start | bytes 8650752 | tf_op jit(solution)/shard_map/all_to_all | solution.py:852
  678.0 306.5 %reduce-scatter.3.cloned.1.call-start = ((), (), s32[]{:S(2)}) async-start(), calls=%async_computation.16 | async-start | bytes 23592960 | tf_op jit(solution)/shard_map/reduce_scatter | solution.py:785
  773.6 102.5 %all-to-all-start.9 = ((f32[32,88,384]{2,1,0:T(8,128)}), f32[32,88,384]{2,1,0:T(8,128)}, u32[]{:S(2)}, u32[]{:S(2)}) async-start(f32[32,88,384]{2,1,0:T(8,128)} %bitcast.122), calls=%async_computation.10 | async-start | bytes 8650752 | tf_op jit(solution)/shard_map/all_to_all | solution.py:852
  876.1 7.4 copy-start.4
  876.1 7.5 copy-start.6
  876.1 102.9 %all-to-all-start.10 = ((f32[32,88,384]{2,1,0:T(8,128)}), f32[32,88,384]{2,1,0:T(8,128)}, u32[]{:S(2)}, u32[]{:S(2)}) async-start(f32[32,88,384]{2,1,0:T(8,128)} %bitcast.120), calls=%async_computation.11 | async-start | bytes 8650752 | tf_op jit(solution)/shard_map/all_to_all | solution.py:852
  883.5 262.3 %reduce-scatter.5.cloned.1.call-start = ((), (), s32[]{:S(2)}) async-start(), calls=%async_computation.17 | async-start | bytes 5308416 | tf_op jit(solution)/shard_map/reduce_scatter | solution.py:785
  1023.4 122.4 %all-to-all-start.11 = ((f32[32,88,384]{2,1,0:T(8,128)}), f32[32,88,384]{2,1,0:T(8,128)}, u32[]{:S(2)}, u32[]{:S(2)}) async-start(f32[32,88,384]{2,1,0:T(8,128)} %bitcast.115), calls=%async_computation.13 | async-start | bytes 8650752 | tf_op jit(solution)/shard_map/all_to_all | solution.py:852
  1030.3 340.5 %all-gather.2.cloned.1.call-start = ((), (), s32[]{:S(2)}) async-start(), calls=%async_computation.18 | async-start | bytes 19464192 | tf_op jit(solution)/shard_map/all_gather | solution.py:788
  1145.8 175.3 %all-to-all-start.12 = ((f32[32,88,384]{2,1,0:T(8,128)}), f32[32,88,384]{2,1,0:T(8,128)}, u32[]{:S(2)}, u32[]{:S(2)}) async-start(f32[32,88,384]{2,1,0:T(8,128)} %bitcast.111), calls=%async_computation.14 | async-start | bytes 8650752 | tf_op jit(solution)/shard_map/all_to_all | solution.py:852
  1152.6 23.2 %copy-start.19 = (f32[2,192]{1,0:T(2,128)S(1)}, f32[2,192]{1,0:T(2,128)}, u32[]{:S(2)}) copy-start(f32[2,192]{1,0:T(2,128)} %get-tuple-element.171) | copy-start | bytes 4612
  1152.6 23.3 %copy-start.18 = (f32[2,192]{1,0:T(2,128)S(1)}, f32[2,192]{1,0:T(2,128)}, u32[]{:S(2)}) copy-start(f32[2,192]{1,0:T(2,128)} %get-tuple-element.173) | copy-start | bytes 4612
  1321.1 7.1 copy-start.7
  1321.1 7.1 copy-start.8
  1321.1 7.1 copy-start.9
  1321.1 7.1 copy-start.10
  1321.1 7.1 copy-start.11
  1321.1 7.1 copy-start.12
  1321.1 117.1 %all-to-all-start.13 = ((f32[32,88,384]{2,1,0:T(8,128)}), f32[32,88,384]{2,1,0:T(8,128)}, u32[]{:S(2)}, u32[]{:S(2)}) async-start(f32[32,88,384]{2,1,0:T(8,128)} %bitcast.112), calls=%async_computation.15 | async-start | bytes 8650752 | tf_op jit(solution)/shard_map/all_to_all | solution.py:852
Sparse Core Ops, SparseCore 0:
  773.7 208.2 reduce-scatter.2
  986.1 144.3 reduce-scatter.4
  1145.9 224.8 all-gather.1

commit v10 on v9

--- a/solution.py
+++ b/solution.py
@@ -1165,7 +1165,6 @@
     send(made[1], got)
     grads, got[0] = tie(grads, got[0])
     grads = gather(grads, ("cols", "rows"))
-    expand_sum, reduce_sum = split_grads(grads)
     first_sums, states_grad = [], None
     for q in every:
         if q + 1 < PARTS:
@@ -1173,9 +1172,10 @@
                 made[q + 1], first_sums[-1] = tie(made[q + 1], first_sums[-1])
                 send(made[q + 1], got)
         else:
-            flat, expand_sum = tie(flat, expand_sum)
+            flat, first_sums[-1] = tie(flat, first_sums[-1])
             flat = pick_sums(flat)
-            states_grad, flat = tie(states_grad, flat)
+            grads, flat = tie(grads, flat)
+            expand_sum, reduce_sum = split_grads(grads)
             states_grad, expand_sum = tie(states_grad, expand_sum)
         states_grad, part = last_norm(q, later_grads[q], got[q], states_grad)
         first_sums.append(part)

time: 1510 us -> 1530 us (1.013)
  Pallas kernels: 629 us -> 679 us
  waiting for transfers between devices: 734 us -> 703 us
    pallas_call x1, Pallas kernels: 48.3 us -> 97.6 us  [pick_sums(): pl.pallas_call(functools.partial(pick_kernel, ranks), in_specs=[vmem], ou...]
    all_gather x1, waiting for transfers between devices: 30.8 us -> 0.02 us  [gather(): return lax.all_gather(v, axis, axis=0, tiled=True)]
  transfers between devices with their start and end apart: 17 -> 17, of which waited for: 14 -> 13; matrix products, arithmetic and copies ran while one was open for 1% -> 1% of each run, Pallas kernels for 38% -> 41%
where the time goes in v10:
time: 1530 us; the launch traced here: 1520 us
  waiting for transfers between devices  703 us (46%)
  Pallas kernels  679 us (44%)
  starting transfers between devices  96.7 us (6%)
  local copies, waits for them, and re-layouts  24 us (2%)
    all_to_all x14, waiting for transfers between devices, exchange(): lax.all_to_all(sent, ('rows', 'cols'), 0, 0, tiled=True).reshape(v.shape)  703 us
    pallas_call x3, Pallas kernels, dense(): call(functools.partial(dense_kernel, steps, slabs, width, q == 0, arrays_...  248 us
    pallas_call x1, Pallas kernels, pick_sums(): pl.pallas_call(functools.partial(pick_kernel, ranks), in_specs=[vmem], ou...  97.6 us
    all_to_all x14, starting transfers between devices, exchange(): lax.all_to_all(sent, ('rows', 'cols'), 0, 0, tiled=True).reshape(v.shape)  96.6 us
    pallas_call x2, Pallas kernels, spectral_forward(): call(functools.partial(spectral_forward_kernel, factor, g), bin_steps, cu...  55 us
    pallas_call x7, Pallas kernels, wide_in(): call(functools.partial(wide_in_split_kernel if divided else wide_in_kerne...  40.3 us
    pallas_call x1, Pallas kernels, sum_small(): pl.pallas_call(functools.partial(sum_kernel, ranks, groups), in_specs=[vm...  35.7 us
    pallas_call x3, Pallas kernels, last_norm(): call(functools.partial(last_kernel, width, 1), steps, [packed_spec(same)]...  34.9 us
  transfers between devices with their start and end apart: 17, of which 13 were waited for; matrix products, arithmetic and copies ran while one was open for 1% of the time, Pallas kernels for 41%

profile of v10, /device:TPU:15, one launch (start us, length us, event | category | flops | bytes accessed | tf_op | source)
XLA Modules:
  0.0 1519.8 jit_solution(14789810528544166319)
XLA Ops:
  13.5 10.0 first_norm.5
  23.5 6.3 all-to-all-start
  29.8 10.0 first_norm.4
  39.9 85.6 %all-to-all-done = f32[32,88,384]{2,1,0:T(8,128)} async-done(((f32[32,88,384]{2,1,0:T(8,128)}), f32[32,88,384]{2,1,0:T(8,128)}, u32[]{:S(2)}, u32[]{:S(2)}) %all-to-all-start) | async-done | bytes 4325408 | tf_op jit(solution)/shard_map/all_to_all | solution.py:852
  125.4 6.9 all-to-all-start.1
  132.3 12.8 first_norm.3
  145.2 6.3 wide_in.7.refs_1_
  151.5 76.4 %all-to-all-done.1 = f32[32,88,384]{2,1,0:T(8,128)} async-done(((f32[32,88,384]{2,1,0:T(8,128)}), f32[32,88,384]{2,1,0:T(8,128)}, u32[]{:S(2)}, u32[]{:S(2)}) %all-to-all-start.1) | async-done | bytes 4325408 | tf_op jit(solution)/shard_map/all_to_all | solution.py:852
  227.9 6.8 all-to-all-start.2
  234.8 6.4 wide_in.8.refs_2_
  241.2 45.6 %all-to-all-done.2 = f32[32,48,384]{2,1,0:T(8,128)S(1)} async-done(((f32[32,48,384]{2,1,0:T(8,128)}), f32[32,48,384]{2,1,0:T(8,128)S(1)}, u32[]{:S(2)}, u32[]{:S(2)}) %all-to-all-start.2) | async-done | bytes 2359328 | tf_op jit(solution)/shard_map/all_to_all | solution.py:852
  288.1 6.7 all-to-all-start.3
  301.6 27.3 %spectral_forward.2 = (f32[16,2,96,192]{3,2,1,0:T(8,128)}, f32[16,2,96,192]{3,2,1,0:T(8,128)}, f32[16,2,96,192]{3,2,1,0:T(8,128)}, bf16[18432,96]{1,0:T(8,128)(2,1)}) custom-call(f32[16,2,96,192]{3,2,1,0:T(8,128)} %wide_in.9.refs_0_, f32[16,2,96,384]{3,2,1,0:T(8,128)} %wide_in.7.refs_1_, f32[16,2,96,384]{3,2,1,0:T(8,128)} %wide_in.8.refs_2_, ...), custom_call_target="tpu_custom_call" | custom-call | flops 20000000000 | bytes 51904512 | tf_op jit(solution)/shard_map/spectral_forward/pallas_call | solution.py:960
  333.6 13.3 all-to-all-done.3
  346.8 6.8 all-to-all-start.4
  358.8 27.7 %spectral_forward.3 = (f32[16,2,96,192]{3,2,1,0:T(8,128)}, f32[16,2,96,192]{3,2,1,0:T(8,128)}, f32[16,2,96,192]{3,2,1,0:T(8,128)}, bf16[18432,96]{1,0:T(8,128)(2,1)}) custom-call(f32[16,2,96,192]{3,2,1,0:T(8,128)} %wide_in.10.refs_0_, f32[16,2,96,384]{3,2,1,0:T(8,128)} %wide_in.7.refs_1_, f32[16,2,96,384]{3,2,1,0:T(8,128)} %wide_in.8.refs_2_, ...), custom_call_target="tpu_custom_call" | custom-call | flops 20000000000 | bytes 51904512 | tf_op jit(solution)/shard_map/spectral_forward/pallas_call | solution.py:960
  391.2 14.3 all-to-all-done.4
  405.5 7.1 all-to-all-start.5
  418.8 23.9 %spectral_keep.1 = (bf16[18432,192]{1,0:T(8,128)(2,1)}, bf16[18432,192]{1,0:T(8,128)(2,1)}, bf16[18432,192]{1,0:T(8,128)(2,1)}) custom-call(bf16[18432,96]{1,0:T(8,128)(2,1)} %get-tuple-element.131.refs_0_, bf16[18432,96]{1,0:T(8,128)(2,1)} %get-tuple-element.132.refs_1_, bf16[2,96,96]{2,1,0:T(8,128)(2,1)} %get-tuple-element.235.refs_5_.refs_2_, ...), custom_call_target="tpu_custom_call" | custom-call | flops 10000000000 | bytes 25952256 | tf_op jit(solution)/shard_map/spectral_keep/pallas_call | solution.py:978
  442.8 21.7 %all-to-all-done.5 = f32[32,48,384]{2,1,0:T(8,128)S(1)} async-done(((f32[32,48,384]{2,1,0:T(8,128)}), f32[32,48,384]{2,1,0:T(8,128)S(1)}, u32[]{:S(2)}, u32[]{:S(2)}) %all-to-all-start.5) | async-done | bytes 2359328 | tf_op jit(solution)/shard_map/all_to_all | solution.py:852
  466.0 6.8 all-to-all-start.6
  474.5 6.2 wide_out.7
  480.7 81.4 %dense_both_ways.3 = (f32[8,4,88,384]{3,2,1,0:T(8,128)}, bf16[2,264,8,768]{3,2,1,0:T(8,128)(2,1)}, f32[2,88,8,768]{3,2,1,0:T(8,128)}, f32[8,768]{1,0:T(8,128)}, f32[4,768]{1,0:T(4,128)}, /*index=5*/f32[6144,768]{1,0:T(8,128)}) custom-call(f32[8,4,48,384]{3,2,1,0:T(8,128)} %bitcast.16.refs_0_, f32[8,4,48,384]{3,2,1,0:T(8,128)} %bitcast.124, ...), custom_call_target="tpu_custom_call" | custom-call | flops 39862665216 | bytes 17301504 | tf_op jit(solution)/shard_map/dense_both_ways/pallas_call | solution.py:1023
  562.1 6.3 all-to-all-done.6
  568.3 7.3 all-to-all-start.7
  575.6 83.2 %dense_both_ways.4 = (f32[8,4,88,384]{3,2,1,0:T(8,128)}, bf16[2,264,8,768]{3,2,1,0:T(8,128)(2,1)}, f32[2,88,8,768]{3,2,1,0:T(8,128)}, f32[8,768]{1,0:T(8,128)}, f32[4,768]{1,0:T(4,128)}, /*index=5*/f32[6144,768]{1,0:T(8,128)}) custom-call(f32[8,4,88,384]{3,2,1,0:T(8,128)} %bitcast.23.refs_0_, ...), custom_call_target="tpu_custom_call", output_to_operand_aliasing={{1}: (13, {})} | custom-call | flops 39862665216 | bytes 17301504 | tf_op jit(solution)/shard_map/dense_both_ways/pallas_call | solution.py:1023
  658.9 12.3 all-to-all-done.7
  671.1 6.9 all-to-all-start.8
  678.1 83.2 %dense_both_ways.5 = (f32[8,4,88,384]{3,2,1,0:T(8,128)}, bf16[2,264,8,768]{3,2,1,0:T(8,128)(2,1)}, f32[2,88,8,768]{3,2,1,0:T(8,128)}, f32[8,768]{1,0:T(8,128)}, f32[4,768]{1,0:T(4,128)}, /*index=5*/f32[6144,768]{1,0:T(8,128)}) custom-call(f32[8,4,88,384]{3,2,1,0:T(8,128)} %bitcast.25.refs_0_, ...), custom_call_target="tpu_custom_call", output_to_operand_aliasing={{1}: (13, {})} | custom-call | flops 39862665216 | bytes 17301504 | tf_op jit(solution)/shard_map/dense_both_ways/pallas_call | solution.py:1023
  761.3 12.3 all-to-all-done.8
  773.6 6.9 all-to-all-start.9
  780.5 6.2 wide_in.11.refs_1_
  786.7 89.4 %all-to-all-done.9 = f32[32,88,384]{2,1,0:T(8,128)} async-done(((f32[32,88,384]{2,1,0:T(8,128)}), f32[32,88,384]{2,1,0:T(8,128)}, u32[]{:S(2)}, u32[]{:S(2)}) %all-to-all-start.9) | async-done | bytes 4325408 | tf_op jit(solution)/shard_map/all_to_all | solution.py:852
  876.2 7.3 all-to-all-start.10
  891.4 87.7 %all-to-all-done.10 = f32[32,88,384]{2,1,0:T(8,128)} async-done(((f32[32,88,384]{2,1,0:T(8,128)}), f32[32,88,384]{2,1,0:T(8,128)}, u32[]{:S(2)}, u32[]{:S(2)}) %all-to-all-start.10) | async-done | bytes 4325408 | tf_op jit(solution)/shard_map/all_to_all | solution.py:852
  984.6 33.4 %spectral_backward.1 = (f32[16,2,96,384]{3,2,1,0:T(8,128)}, f32[16,2,96,384]{3,2,1,0:T(8,128)}, f32[16,2,96,384]{3,2,1,0:T(8,128)}, bf16[18432,192]{1,0:T(8,128)...) custom-call(f32[16,2,96,384]{3,2,1,0:T(8,128)} %wide_in.13.refs_0_, ...), custom_call_target="tpu_custom_call" | custom-call | flops 20000000000 | bytes 103809024 | tf_op jit(solution)/shard_map/spectral_backward/pallas_call | solution.py:990
  1023.4 6.9 all-to-all-start.11
  1035.9 109.9 %all-to-all-done.11 = f32[32,88,384]{2,1,0:T(8,128)} async-done(((f32[32,88,384]{2,1,0:T(8,128)}), f32[32,88,384]{2,1,0:T(8,128)}, u32[]{:S(2)}, u32[]{:S(2)}) %all-to-all-start.11) | async-done | bytes 4325408 | tf_op jit(solution)/shard_map/all_to_all | solution.py:852
  1145.8 6.8 all-to-all-start.12
  1152.6 20.7 %filter_grad.1 = (f32[2,192,192]{2,1,0:T(8,128)}, f32[2,192,192]{2,1,0:T(8,128)}) custom-call(bf16[18432,96]{1,0:T(8,128)(2,1)} %get-tuple-element.131.refs_0_, bf16[18432,96]{1,0:T(8,128)(2,1)} %get-tuple-element.132.refs_1_, bf16[18432,192]{1,0:T(8,128)(2,1)} %get-tuple-element.167.refs_2_, bf16[18432,192]{1,0:T(8,128)(2,1)} %get-tuple-element.168.refs_3_, ...), custom_call_target="tpu_custom_call" | custom-call | flops 10000000000 | bytes 25952256 | tf_op jit(solution)/shard_map/filter_grad/pallas_call | solution.py:1003
  1181.5 11.6 first_norm_backward.3
  1193.1 128.0 %all-to-all-done.12 = f32[32,88,384]{2,1,0:T(8,128)} async-done(((f32[32,88,384]{2,1,0:T(8,128)}), f32[32,88,384]{2,1,0:T(8,128)}, u32[]{:S(2)}, u32[]{:S(2)}) %all-to-all-start.12) | async-done | bytes 4325408 | tf_op jit(solution)/shard_map/all_to_all | solution.py:852
  1321.1 7.1 all-to-all-start.13
  1328.3 11.7 first_norm_backward.4
  1340.7 97.6 %filter_sums.1.mine = f32[80,128]{1,0:T(8,128)} custom-call(f32[640,128]{1,0:T(8,128)} %pad_bitcast_fusion.flat), custom_call_target="tpu_custom_call" | custom-call | tf_op jit(solution)/shard_map/filter_sums/pallas_call | solution.py:799
  1438.3 18.5 %split_gradients.1 = (f32[768,3072]{1,0:T(8,128)}, f32[3072,768]{1,0:T(8,128)}) custom-call(f32[6144,768]{1,0:T(8,128)} %all-gather.2.cloned.1.call-done.expand_in.reduce_in, f32[6144,768]{1,0:T(8,128)} %all-gather.2.cloned.1.call-done.expand_in.reduce_in), custom_call_target="tpu_custom_call" | custom-call | bytes 37748736 | tf_op jit(solution)/shard_map/split_gradients/pallas_call | solution.py:831
  1456.8 11.6 first_norm_backward.5
  1469.8 35.7 %small_sums.1 = (f32[56,128]{1,0:T(8,128)}, f32[640,128]{1,0:T(8,128)}) custom-call(f32[56,128]{1,0:T(8,128)} %pad_bitcast_fusion.1.own, f32[80,128]{1,0:T(8,128)} %filter_sums.1.mine), custom_call_target="tpu_custom_call" | custom-call | tf_op jit(solution)/shard_map/small_sums/pallas_call | solution.py:812
  (109 shorter events, 80.3 us)
Async XLA Ops:
  23.5 101.9 %all-to-all-start = ((f32[32,88,384]{2,1,0:T(8,128)}), f32[32,88,384]{2,1,0:T(8,128)}, u32[]{:S(2)}, u32[]{:S(2)}) async-start(f32[32,88,384]{2,1,0:T(8,128)} %bitcast.110), calls=%async_computation | async-start | bytes 8650752 | tf_op jit(solution)/shard_map/all_to_all | solution.py:852
  125.4 102.5 %all-to-all-start.1 = ((f32[32,88,384]{2,1,0:T(8,128)}), f32[32,88,384]{2,1,0:T(8,128)}, u32[]{:S(2)}, u32[]{:S(2)}) async-start(f32[32,88,384]{2,1,0:T(8,128)} %bitcast.109), calls=%async_computation.1 | async-start | bytes 8650752 | tf_op jit(solution)/shard_map/all_to_all | solution.py:852
  227.9 58.8 %all-to-all-start.2 = ((f32[32,48,384]{2,1,0:T(8,128)}), f32[32,48,384]{2,1,0:T(8,128)S(1)}, u32[]{:S(2)}, u32[]{:S(2)}) async-start(f32[32,48,384]{2,1,0:T(8,128)} %bitcast.125), calls=%async_computation.2 | async-start | bytes 4718592 | tf_op jit(solution)/shard_map/all_to_all | solution.py:852
  241.1 53.7 %copy-start.16 = (f32[2,2,96]{2,1,0:T(2,128)S(1)}, f32[2,2,96]{2,1,0:T(2,128)}, u32[]{:S(2)}) copy-start(f32[2,2,96]{2,1,0:T(2,128)} %param.39) | copy-start | bytes 4612
  241.1 53.8 %copy-start.17 = (f32[2,2,96]{2,1,0:T(2,128)S(1)}, f32[2,2,96]{2,1,0:T(2,128)}, u32[]{:S(2)}) copy-start(f32[2,2,96]{2,1,0:T(2,128)} %param.41) | copy-start | bytes 4612
  241.1 54.6 %copy-start.3 = (bf16[2,2,96,96]{3,2,1,0:T(8,128)(2,1)S(1)}, bf16[2,2,96,96]{3,2,1,0:T(8,128)(2,1)}, u32[]{:S(2)}) copy-start(bf16[2,2,96,96]{3,2,1,0:T(8,128)(2,1)} %param.38) | copy-start | bytes 221188
  241.1 54.6 %copy-start.5 = (bf16[2,2,96,96]{3,2,1,0:T(8,128)(2,1)S(1)}, bf16[2,2,96,96]{3,2,1,0:T(8,128)(2,1)}, u32[]{:S(2)}) copy-start(bf16[2,2,96,96]{3,2,1,0:T(8,128)(2,1)} %param.40) | copy-start | bytes 221188
  286.7 1.4 copy-start.1
  288.1 58.7 %all-to-all-start.3 = ((f32[32,48,384]{2,1,0:T(8,128)}), f32[32,48,384]{2,1,0:T(8,128)S(1)}, u32[]{:S(2)}, u32[]{:S(2)}) async-start(f32[32,48,384]{2,1,0:T(8,128)} %bitcast.123), calls=%async_computation.3 | async-start | bytes 4718592 | tf_op jit(solution)/shard_map/all_to_all | solution.py:852
  346.8 6.8 copy-start
  346.8 58.7 %all-to-all-start.4 = ((f32[32,48,384]{2,1,0:T(8,128)}), f32[32,48,384]{2,1,0:T(8,128)}, u32[]{:S(2)}, u32[]{:S(2)}) async-start(f32[32,48,384]{2,1,0:T(8,128)} %bitcast.116), calls=%async_computation.4 | async-start | bytes 4718592 | tf_op jit(solution)/shard_map/all_to_all | solution.py:852
  405.5 59.0 %all-to-all-start.5 = ((f32[32,48,384]{2,1,0:T(8,128)}), f32[32,48,384]{2,1,0:T(8,128)S(1)}, u32[]{:S(2)}, u32[]{:S(2)}) async-start(f32[32,48,384]{2,1,0:T(8,128)} %bitcast.117), calls=%async_computation.5 | async-start | bytes 4718592 | tf_op jit(solution)/shard_map/all_to_all | solution.py:852
  464.5 1.4 copy-start.2
  464.5 8.2 copy-start.13
  464.5 8.8 copy-start.14
  464.5 9.4 copy-start.15
  466.0 102.4 %all-to-all-start.6 = ((f32[32,88,384]{2,1,0:T(8,128)}), f32[32,88,384]{2,1,0:T(8,128)}, u32[]{:S(2)}, u32[]{:S(2)}) async-start(f32[32,88,384]{2,1,0:T(8,128)} %bitcast.113), calls=%async_computation.6 | async-start | bytes 8650752 | tf_op jit(solution)/shard_map/all_to_all | solution.py:852
  568.3 102.8 %all-to-all-start.7 = ((f32[32,88,384]{2,1,0:T(8,128)}), f32[32,88,384]{2,1,0:T(8,128)}, u32[]{:S(2)}, u32[]{:S(2)}) async-start(f32[32,88,384]{2,1,0:T(8,128)} %bitcast.114), calls=%async_computation.7 | async-start | bytes 8650752 | tf_op jit(solution)/shard_map/all_to_all | solution.py:852
  671.1 102.5 %all-to-all-start.8 = ((f32[32,88,384]{2,1,0:T(8,128)}), f32[32,88,384]{2,1,0:T(8,128)}, u32[]{:S(2)}, u32[]{:S(2)}) async-start(f32[32,88,384]{2,1,0:T(8,128)} %bitcast.121), calls=%async_computation.8 | async-start | bytes 8650752 | tf_op jit(solution)/shard_map/all_to_all | solution.py:852
  678.0 306.5 %reduce-scatter.3.cloned.1.call-start = ((), (), s32[]{:S(2)}) async-start(), calls=%async_computation.16 | async-start | bytes 23592960 | tf_op jit(solution)/shard_map/reduce_scatter | solution.py:785
  773.6 102.5 %all-to-all-start.9 = ((f32[32,88,384]{2,1,0:T(8,128)}), f32[32,88,384]{2,1,0:T(8,128)}, u32[]{:S(2)}, u32[]{:S(2)}) async-start(f32[32,88,384]{2,1,0:T(8,128)} %bitcast.122), calls=%async_computation.10 | async-start | bytes 8650752 | tf_op jit(solution)/shard_map/all_to_all | solution.py:852
  876.1 7.4 copy-start.4
  876.2 7.5 copy-start.6
  876.2 102.9 %all-to-all-start.10 = ((f32[32,88,384]{2,1,0:T(8,128)}), f32[32,88,384]{2,1,0:T(8,128)}, u32[]{:S(2)}, u32[]{:S(2)}) async-start(f32[32,88,384]{2,1,0:T(8,128)} %bitcast.120), calls=%async_computation.11 | async-start | bytes 8650752 | tf_op jit(solution)/shard_map/all_to_all | solution.py:852
  883.5 262.3 %reduce-scatter.5.cloned.1.call-start = ((), (), s32[]{:S(2)}) async-start(), calls=%async_computation.17 | async-start | bytes 5308416 | tf_op jit(solution)/shard_map/reduce_scatter | solution.py:785
  1023.4 122.4 %all-to-all-start.11 = ((f32[32,88,384]{2,1,0:T(8,128)}), f32[32,88,384]{2,1,0:T(8,128)}, u32[]{:S(2)}, u32[]{:S(2)}) async-start(f32[32,88,384]{2,1,0:T(8,128)} %bitcast.115), calls=%async_computation.13 | async-start | bytes 8650752 | tf_op jit(solution)/shard_map/all_to_all | solution.py:852
  1030.3 408.0 %all-gather.2.cloned.1.call-start = ((), (), s32[]{:S(2)}) async-start(), calls=%async_computation.18 | async-start | bytes 19464192 | tf_op jit(solution)/shard_map/all_gather | solution.py:788
  1145.8 175.3 %all-to-all-start.12 = ((f32[32,88,384]{2,1,0:T(8,128)}), f32[32,88,384]{2,1,0:T(8,128)}, u32[]{:S(2)}, u32[]{:S(2)}) async-start(f32[32,88,384]{2,1,0:T(8,128)} %bitcast.111), calls=%async_computation.14 | async-start | bytes 8650752 | tf_op jit(solution)/shard_map/all_to_all | solution.py:852
  1152.6 23.2 %copy-start.19 = (f32[2,192]{1,0:T(2,128)S(1)}, f32[2,192]{1,0:T(2,128)}, u32[]{:S(2)}) copy-start(f32[2,192]{1,0:T(2,128)} %get-tuple-element.171) | copy-start | bytes 4612
  1152.6 23.3 %copy-start.18 = (f32[2,192]{1,0:T(2,128)S(1)}, f32[2,192]{1,0:T(2,128)}, u32[]{:S(2)}) copy-start(f32[2,192]{1,0:T(2,128)} %get-tuple-element.173) | copy-start | bytes 4612
  1321.1 7.1 copy-start.7
  1321.1 7.1 copy-start.8
  1321.1 7.1 copy-start.9
  1321.1 7.1 copy-start.10
  1321.1 7.1 copy-start.11
  1321.1 7.1 copy-start.12
  1321.1 135.7 %all-to-all-start.13 = ((f32[32,88,384]{2,1,0:T(8,128)}), f32[32,88,384]{2,1,0:T(8,128)}, u32[]{:S(2)}, u32[]{:S(2)}) async-start(f32[32,88,384]{2,1,0:T(8,128)} %bitcast.112), calls=%async_computation.15 | async-start | bytes 8650752 | tf_op jit(solution)/shard_map/all_to_all | solution.py:852
Sparse Core Ops, SparseCore 0:
  773.8 208.2 reduce-scatter.2
  986.1 144.3 reduce-scatter.4
  1145.9 224.8 all-gather.1

commit v11 on v9

--- a/solution.py
+++ b/solution.py
@@ -881,7 +881,7 @@
     bin_steps = BINS // GROUP
     group_rows = GROUP * 2 * height
     held_shape = shape((short, 2, BINS, lanes), f32)
-    at_once = 2
+    at_once = 4
     held_row = pl.BlockSpec((at_once * rows, 2, BINS, lanes), lambda i: (i, 0, 0, 0))
     held_bins = pl.BlockSpec((short, 2, GROUP, lanes), lambda i: (0, 0, i, 0))
     field = pl.BlockSpec((at_once, groups, pixels, lanes), lambda i: (i, 0, 0, 0))

time: 1510 us -> 1520 us (level)
  transfers between devices with their start and end apart: 17 -> 17, of which waited for: 14 -> 14; matrix products, arithmetic and copies ran while one was open for 1% -> 1% of each run, Pallas kernels for 38% -> 37%
where the time goes in v11:
time: 1520 us; the launch traced here: 1500 us
  waiting for transfers between devices  748 us (49%)
  Pallas kernels  616 us (41%)
  starting transfers between devices  96.7 us (6%)
  local copies, waits for them, and re-layouts  24 us (2%)
    all_to_all x14, waiting for transfers between devices, exchange(): lax.all_to_all(sent, ('rows', 'cols'), 0, 0, tiled=True).reshape(v.shape)  717 us
    pallas_call x3, Pallas kernels, dense(): call(functools.partial(dense_kernel, steps, slabs, width, q == 0, arrays_...  248 us
    all_to_all x14, starting transfers between devices, exchange(): lax.all_to_all(sent, ('rows', 'cols'), 0, 0, tiled=True).reshape(v.shape)  96.6 us
    pallas_call x2, Pallas kernels, spectral_forward(): call(functools.partial(spectral_forward_kernel, factor, g), bin_steps, cu...  55 us
    pallas_call x1, Pallas kernels, pick_sums(): pl.pallas_call(functools.partial(pick_kernel, ranks), in_specs=[vmem], ou...  48.3 us
    pallas_call x1, Pallas kernels, sum_small(): pl.pallas_call(functools.partial(sum_kernel, ranks, groups), in_specs=[vm...  35.7 us
    pallas_call x3, Pallas kernels, last_norm(): call(functools.partial(last_kernel, width, 1), steps, [packed_spec(same)]...  34.9 us
    pallas_call x7, Pallas kernels, wide_in(): call(functools.partial(wide_in_split_kernel if divided else wide_in_kerne...  34.7 us
  transfers between devices with their start and end apart: 17, of which 14 were waited for; matrix products, arithmetic and copies ran while one was open for 1% of the time, Pallas kernels for 37%

profile of v11, /device:TPU:15, one launch (start us, length us, event | category | flops | bytes accessed | tf_op | source)
XLA Modules:
  0.0 1501.5 jit_solution(10623061961216826543)
XLA Ops:
  13.5 10.0 first_norm.5
  23.5 6.3 all-to-all-start
  29.8 10.0 first_norm.4
  39.9 85.6 %all-to-all-done = f32[32,88,384]{2,1,0:T(8,128)} async-done(((f32[32,88,384]{2,1,0:T(8,128)}), f32[32,88,384]{2,1,0:T(8,128)}, u32[]{:S(2)}, u32[]{:S(2)}) %all-to-all-start) | async-done | bytes 4325408 | tf_op jit(solution)/shard_map/all_to_all | solution.py:852
  125.4 6.9 all-to-all-start.1
  132.3 12.8 first_norm.3
  145.1 5.8 wide_in.7.refs_1_
  150.9 77.0 %all-to-all-done.1 = f32[32,88,384]{2,1,0:T(8,128)} async-done(((f32[32,88,384]{2,1,0:T(8,128)}), f32[32,88,384]{2,1,0:T(8,128)}, u32[]{:S(2)}, u32[]{:S(2)}) %all-to-all-start.1) | async-done | bytes 4325408 | tf_op jit(solution)/shard_map/all_to_all | solution.py:852
  227.9 6.8 all-to-all-start.2
  234.8 5.8 wide_in.8.refs_2_
  240.6 46.1 %all-to-all-done.2 = f32[32,48,384]{2,1,0:T(8,128)S(1)} async-done(((f32[32,48,384]{2,1,0:T(8,128)}), f32[32,48,384]{2,1,0:T(8,128)S(1)}, u32[]{:S(2)}, u32[]{:S(2)}) %all-to-all-start.2) | async-done | bytes 2359328 | tf_op jit(solution)/shard_map/all_to_all | solution.py:852
  288.1 6.7 all-to-all-start.3
  300.7 27.3 %spectral_forward.2 = (f32[16,2,96,192]{3,2,1,0:T(8,128)}, f32[16,2,96,192]{3,2,1,0:T(8,128)}, f32[16,2,96,192]{3,2,1,0:T(8,128)}, bf16[18432,96]{1,0:T(8,128)(2,1)}) custom-call(f32[16,2,96,192]{3,2,1,0:T(8,128)} %wide_in.9.refs_0_, f32[16,2,96,384]{3,2,1,0:T(8,128)} %wide_in.7.refs_1_, f32[16,2,96,384]{3,2,1,0:T(8,128)} %wide_in.8.refs_2_, ...), custom_call_target="tpu_custom_call" | custom-call | flops 20000000000 | bytes 51904512 | tf_op jit(solution)/shard_map/spectral_forward/pallas_call | solution.py:960
  331.4 15.5 %all-to-all-done.3 = f32[32,48,384]{2,1,0:T(8,128)S(1)} async-done(((f32[32,48,384]{2,1,0:T(8,128)}), f32[32,48,384]{2,1,0:T(8,128)S(1)}, u32[]{:S(2)}, u32[]{:S(2)}) %all-to-all-start.3) | async-done | bytes 2359328 | tf_op jit(solution)/shard_map/all_to_all | solution.py:852
  346.8 6.8 all-to-all-start.4
  358.0 27.7 %spectral_forward.3 = (f32[16,2,96,192]{3,2,1,0:T(8,128)}, f32[16,2,96,192]{3,2,1,0:T(8,128)}, f32[16,2,96,192]{3,2,1,0:T(8,128)}, bf16[18432,96]{1,0:T(8,128)(2,1)}) custom-call(f32[16,2,96,192]{3,2,1,0:T(8,128)} %wide_in.10.refs_0_, f32[16,2,96,384]{3,2,1,0:T(8,128)} %wide_in.7.refs_1_, f32[16,2,96,384]{3,2,1,0:T(8,128)} %wide_in.8.refs_2_, ...), custom_call_target="tpu_custom_call" | custom-call | flops 20000000000 | bytes 51904512 | tf_op jit(solution)/shard_map/spectral_forward/pallas_call | solution.py:960
  389.1 16.5 %all-to-all-done.4 = f32[32,48,384]{2,1,0:T(8,128)} async-done(((f32[32,48,384]{2,1,0:T(8,128)}), f32[32,48,384]{2,1,0:T(8,128)}, u32[]{:S(2)}, u32[]{:S(2)}) %all-to-all-start.4) | async-done | bytes 2359328 | tf_op jit(solution)/shard_map/all_to_all | solution.py:852
  405.5 7.1 all-to-all-start.5
  417.9 24.0 %spectral_keep.1 = (bf16[18432,192]{1,0:T(8,128)(2,1)}, bf16[18432,192]{1,0:T(8,128)(2,1)}, bf16[18432,192]{1,0:T(8,128)(2,1)}) custom-call(bf16[18432,96]{1,0:T(8,128)(2,1)} %get-tuple-element.131.refs_0_, bf16[18432,96]{1,0:T(8,128)(2,1)} %get-tuple-element.132.refs_1_, bf16[2,96,96]{2,1,0:T(8,128)(2,1)} %get-tuple-element.235.refs_5_.refs_2_, ...), custom_call_target="tpu_custom_call" | custom-call | flops 10000000000 | bytes 25952256 | tf_op jit(solution)/shard_map/spectral_keep/pallas_call | solution.py:978
  441.8 22.7 %all-to-all-done.5 = f32[32,48,384]{2,1,0:T(8,128)S(1)} async-done(((f32[32,48,384]{2,1,0:T(8,128)}), f32[32,48,384]{2,1,0:T(8,128)S(1)}, u32[]{:S(2)}, u32[]{:S(2)}) %all-to-all-start.5) | async-done | bytes 2359328 | tf_op jit(solution)/shard_map/all_to_all | solution.py:852
  465.9 6.8 all-to-all-start.6
  479.6 81.2 %dense_both_ways.3 = (f32[8,4,88,384]{3,2,1,0:T(8,128)}, bf16[2,264,8,768]{3,2,1,0:T(8,128)(2,1)}, f32[2,88,8,768]{3,2,1,0:T(8,128)}, f32[8,768]{1,0:T(8,128)}, f32[4,768]{1,0:T(4,128)}, /*index=5*/f32[6144,768]{1,0:T(8,128)}) custom-call(f32[8,4,48,384]{3,2,1,0:T(8,128)} %bitcast.16.refs_0_, f32[8,4,48,384]{3,2,1,0:T(8,128)} %bitcast.124, ...), custom_call_target="tpu_custom_call" | custom-call | flops 39862665216 | bytes 17301504 | tf_op jit(solution)/shard_map/dense_both_ways/pallas_call | solution.py:1023
  560.9 7.5 all-to-all-done.6
  568.3 7.3 all-to-all-start.7
  575.6 83.3 %dense_both_ways.4 = (f32[8,4,88,384]{3,2,1,0:T(8,128)}, bf16[2,264,8,768]{3,2,1,0:T(8,128)(2,1)}, f32[2,88,8,768]{3,2,1,0:T(8,128)}, f32[8,768]{1,0:T(8,128)}, f32[4,768]{1,0:T(4,128)}, /*index=5*/f32[6144,768]{1,0:T(8,128)}) custom-call(f32[8,4,88,384]{3,2,1,0:T(8,128)} %bitcast.23.refs_0_, ...), custom_call_target="tpu_custom_call", output_to_operand_aliasing={{1}: (13, {})} | custom-call | flops 39862665216 | bytes 17301504 | tf_op jit(solution)/shard_map/dense_both_ways/pallas_call | solution.py:1023
  659.0 12.1 all-to-all-done.7
  671.1 6.9 all-to-all-start.8
  678.0 83.2 %dense_both_ways.5 = (f32[8,4,88,384]{3,2,1,0:T(8,128)}, bf16[2,264,8,768]{3,2,1,0:T(8,128)(2,1)}, f32[2,88,8,768]{3,2,1,0:T(8,128)}, f32[8,768]{1,0:T(8,128)}, f32[4,768]{1,0:T(4,128)}, /*index=5*/f32[6144,768]{1,0:T(8,128)}) custom-call(f32[8,4,88,384]{3,2,1,0:T(8,128)} %bitcast.25.refs_0_, ...), custom_call_target="tpu_custom_call", output_to_operand_aliasing={{1}: (13, {})} | custom-call | flops 39862665216 | bytes 17301504 | tf_op jit(solution)/shard_map/dense_both_ways/pallas_call | solution.py:1023
  761.2 12.4 all-to-all-done.8
  773.6 7.3 all-to-all-start.9
  780.9 5.7 wide_in.11.refs_1_
  786.6 89.8 %all-to-all-done.9 = f32[32,88,384]{2,1,0:T(8,128)} async-done(((f32[32,88,384]{2,1,0:T(8,128)}), f32[32,88,384]{2,1,0:T(8,128)}, u32[]{:S(2)}, u32[]{:S(2)}) %all-to-all-start.9) | async-done | bytes 4325408 | tf_op jit(solution)/shard_map/all_to_all | solution.py:852
  876.4 6.9 all-to-all-start.10
  890.0 89.1 %all-to-all-done.10 = f32[32,88,384]{2,1,0:T(8,128)} async-done(((f32[32,88,384]{2,1,0:T(8,128)}), f32[32,88,384]{2,1,0:T(8,128)}, u32[]{:S(2)}, u32[]{:S(2)}) %all-to-all-start.10) | async-done | bytes 4325408 | tf_op jit(solution)/shard_map/all_to_all | solution.py:852
  983.4 33.4 %spectral_backward.1 = (f32[16,2,96,384]{3,2,1,0:T(8,128)}, f32[16,2,96,384]{3,2,1,0:T(8,128)}, f32[16,2,96,384]{3,2,1,0:T(8,128)}, bf16[18432,192]{1,0:T(8,128)...) custom-call(f32[16,2,96,384]{3,2,1,0:T(8,128)} %wide_in.13.refs_0_, ...), custom_call_target="tpu_custom_call" | custom-call | flops 20000000000 | bytes 103809024 | tf_op jit(solution)/shard_map/spectral_backward/pallas_call | solution.py:990
  1021.2 6.8 all-to-all-start.11
  1032.3 113.6 %all-to-all-done.11 = f32[32,88,384]{2,1,0:T(8,128)} async-done(((f32[32,88,384]{2,1,0:T(8,128)}), f32[32,88,384]{2,1,0:T(8,128)}, u32[]{:S(2)}, u32[]{:S(2)}) %all-to-all-start.11) | async-done | bytes 4325408 | tf_op jit(solution)/shard_map/all_to_all | solution.py:852
  1145.9 6.9 all-to-all-start.12
  1152.9 20.7 %filter_grad.1 = (f32[2,192,192]{2,1,0:T(8,128)}, f32[2,192,192]{2,1,0:T(8,128)}) custom-call(bf16[18432,96]{1,0:T(8,128)(2,1)} %get-tuple-element.131.refs_0_, bf16[18432,96]{1,0:T(8,128)(2,1)} %get-tuple-element.132.refs_1_, bf16[18432,192]{1,0:T(8,128)(2,1)} %get-tuple-element.167.refs_2_, bf16[18432,192]{1,0:T(8,128)(2,1)} %get-tuple-element.168.refs_3_, ...), custom_call_target="tpu_custom_call" | custom-call | flops 10000000000 | bytes 25952256 | tf_op jit(solution)/shard_map/filter_grad/pallas_call | solution.py:1003
  1180.6 11.6 first_norm_backward.3
  1192.2 129.1 %all-to-all-done.12 = f32[32,88,384]{2,1,0:T(8,128)} async-done(((f32[32,88,384]{2,1,0:T(8,128)}), f32[32,88,384]{2,1,0:T(8,128)}, u32[]{:S(2)}, u32[]{:S(2)}) %all-to-all-start.12) | async-done | bytes 4325408 | tf_op jit(solution)/shard_map/all_to_all | solution.py:852
  1321.3 7.1 all-to-all-start.13
  1328.5 11.7 first_norm_backward.4
  1340.2 30.8 %all-gather.2.cloned.1.call-done.expand_in.reduce_in = f32[6144,768]{1,0:T(8,128)} async-done(((f32[192,768]{1,0:T(8,128)}), f32[6144,768]{1,0:T(8,128)}) %all-gather.2.cloned.1.call-update) | async-done | bytes 18874384 | tf_op jit(solution)/shard_map/all_gather | solution.py:788
  1371.0 18.4 %split_gradients.1 = (f32[768,3072]{1,0:T(8,128)}, f32[3072,768]{1,0:T(8,128)}) custom-call(f32[6144,768]{1,0:T(8,128)} %all-gather.2.cloned.1.call-done.expand_in.reduce_in, f32[6144,768]{1,0:T(8,128)} %all-gather.2.cloned.1.call-done.expand_in.reduce_in), custom_call_target="tpu_custom_call" | custom-call | bytes 37748736 | tf_op jit(solution)/shard_map/split_gradients/pallas_call | solution.py:831
  1390.2 48.3 %filter_sums.1.mine = f32[80,128]{1,0:T(8,128)} custom-call(f32[640,128]{1,0:T(8,128)} %pad_bitcast_fusion.flat), custom_call_target="tpu_custom_call" | custom-call | tf_op jit(solution)/shard_map/filter_sums/pallas_call | solution.py:799
  1438.5 11.6 first_norm_backward.5
  1451.6 35.7 %small_sums.1 = (f32[56,128]{1,0:T(8,128)}, f32[640,128]{1,0:T(8,128)}) custom-call(f32[56,128]{1,0:T(8,128)} %pad_bitcast_fusion.1.own, f32[80,128]{1,0:T(8,128)} %filter_sums.1.mine), custom_call_target="tpu_custom_call" | custom-call | tf_op jit(solution)/shard_map/small_sums/pallas_call | solution.py:812
  (109 shorter events, 74.4 us)
Async XLA Ops:
  23.5 101.9 %all-to-all-start = ((f32[32,88,384]{2,1,0:T(8,128)}), f32[32,88,384]{2,1,0:T(8,128)}, u32[]{:S(2)}, u32[]{:S(2)}) async-start(f32[32,88,384]{2,1,0:T(8,128)} %bitcast.110), calls=%async_computation | async-start | bytes 8650752 | tf_op jit(solution)/shard_map/all_to_all | solution.py:852
  125.4 102.5 %all-to-all-start.1 = ((f32[32,88,384]{2,1,0:T(8,128)}), f32[32,88,384]{2,1,0:T(8,128)}, u32[]{:S(2)}, u32[]{:S(2)}) async-start(f32[32,88,384]{2,1,0:T(8,128)} %bitcast.109), calls=%async_computation.1 | async-start | bytes 8650752 | tf_op jit(solution)/shard_map/all_to_all | solution.py:852
  227.9 58.8 %all-to-all-start.2 = ((f32[32,48,384]{2,1,0:T(8,128)}), f32[32,48,384]{2,1,0:T(8,128)S(1)}, u32[]{:S(2)}, u32[]{:S(2)}) async-start(f32[32,48,384]{2,1,0:T(8,128)} %bitcast.125), calls=%async_computation.2 | async-start | bytes 4718592 | tf_op jit(solution)/shard_map/all_to_all | solution.py:852
  240.6 54.3 %copy-start.16 = (f32[2,2,96]{2,1,0:T(2,128)S(1)}, f32[2,2,96]{2,1,0:T(2,128)}, u32[]{:S(2)}) copy-start(f32[2,2,96]{2,1,0:T(2,128)} %param.39) | copy-start | bytes 4612
  240.6 54.4 %copy-start.17 = (f32[2,2,96]{2,1,0:T(2,128)S(1)}, f32[2,2,96]{2,1,0:T(2,128)}, u32[]{:S(2)}) copy-start(f32[2,2,96]{2,1,0:T(2,128)} %param.41) | copy-start | bytes 4612
  240.6 55.1 %copy-start.3 = (bf16[2,2,96,96]{3,2,1,0:T(8,128)(2,1)S(1)}, bf16[2,2,96,96]{3,2,1,0:T(8,128)(2,1)}, u32[]{:S(2)}) copy-start(bf16[2,2,96,96]{3,2,1,0:T(8,128)(2,1)} %param.38) | copy-start | bytes 221188
  240.6 55.1 %copy-start.5 = (bf16[2,2,96,96]{3,2,1,0:T(8,128)(2,1)S(1)}, bf16[2,2,96,96]{3,2,1,0:T(8,128)(2,1)}, u32[]{:S(2)}) copy-start(bf16[2,2,96,96]{3,2,1,0:T(8,128)(2,1)} %param.40) | copy-start | bytes 221188
  286.7 1.4 copy-start.1
  288.1 58.7 %all-to-all-start.3 = ((f32[32,48,384]{2,1,0:T(8,128)}), f32[32,48,384]{2,1,0:T(8,128)S(1)}, u32[]{:S(2)}, u32[]{:S(2)}) async-start(f32[32,48,384]{2,1,0:T(8,128)} %bitcast.123), calls=%async_computation.3 | async-start | bytes 4718592 | tf_op jit(solution)/shard_map/all_to_all | solution.py:852
  346.8 6.8 copy-start
  346.8 58.7 %all-to-all-start.4 = ((f32[32,48,384]{2,1,0:T(8,128)}), f32[32,48,384]{2,1,0:T(8,128)}, u32[]{:S(2)}, u32[]{:S(2)}) async-start(f32[32,48,384]{2,1,0:T(8,128)} %bitcast.116), calls=%async_computation.4 | async-start | bytes 4718592 | tf_op jit(solution)/shard_map/all_to_all | solution.py:852
  405.5 59.0 %all-to-all-start.5 = ((f32[32,48,384]{2,1,0:T(8,128)}), f32[32,48,384]{2,1,0:T(8,128)S(1)}, u32[]{:S(2)}, u32[]{:S(2)}) async-start(f32[32,48,384]{2,1,0:T(8,128)} %bitcast.117), calls=%async_computation.5 | async-start | bytes 4718592 | tf_op jit(solution)/shard_map/all_to_all | solution.py:852
  464.5 1.4 copy-start.2
  464.5 8.2 copy-start.13
  464.5 8.8 copy-start.14
  464.5 9.4 copy-start.15
  465.9 102.4 %all-to-all-start.6 = ((f32[32,88,384]{2,1,0:T(8,128)}), f32[32,88,384]{2,1,0:T(8,128)}, u32[]{:S(2)}, u32[]{:S(2)}) async-start(f32[32,88,384]{2,1,0:T(8,128)} %bitcast.113), calls=%async_computation.6 | async-start | bytes 8650752 | tf_op jit(solution)/shard_map/all_to_all | solution.py:852
  568.3 102.8 %all-to-all-start.7 = ((f32[32,88,384]{2,1,0:T(8,128)}), f32[32,88,384]{2,1,0:T(8,128)}, u32[]{:S(2)}, u32[]{:S(2)}) async-start(f32[32,88,384]{2,1,0:T(8,128)} %bitcast.114), calls=%async_computation.7 | async-start | bytes 8650752 | tf_op jit(solution)/shard_map/all_to_all | solution.py:852
  671.1 102.5 %all-to-all-start.8 = ((f32[32,88,384]{2,1,0:T(8,128)}), f32[32,88,384]{2,1,0:T(8,128)}, u32[]{:S(2)}, u32[]{:S(2)}) async-start(f32[32,88,384]{2,1,0:T(8,128)} %bitcast.121), calls=%async_computation.8 | async-start | bytes 8650752 | tf_op jit(solution)/shard_map/all_to_all | solution.py:852
  678.0 305.4 %reduce-scatter.3.cloned.1.call-start = ((), (), s32[]{:S(2)}) async-start(), calls=%async_computation.16 | async-start | bytes 23592960 | tf_op jit(solution)/shard_map/reduce_scatter | solution.py:785
  773.6 102.8 %all-to-all-start.9 = ((f32[32,88,384]{2,1,0:T(8,128)}), f32[32,88,384]{2,1,0:T(8,128)}, u32[]{:S(2)}, u32[]{:S(2)}) async-start(f32[32,88,384]{2,1,0:T(8,128)} %bitcast.122), calls=%async_computation.10 | async-start | bytes 8650752 | tf_op jit(solution)/shard_map/all_to_all | solution.py:852
  876.4 6.9 copy-start.4
  876.4 7.1 copy-start.6
  876.4 102.6 %all-to-all-start.10 = ((f32[32,88,384]{2,1,0:T(8,128)}), f32[32,88,384]{2,1,0:T(8,128)}, u32[]{:S(2)}, u32[]{:S(2)}) async-start(f32[32,88,384]{2,1,0:T(8,128)} %bitcast.120), calls=%async_computation.11 | async-start | bytes 8650752 | tf_op jit(solution)/shard_map/all_to_all | solution.py:852
  883.3 262.6 %reduce-scatter.5.cloned.1.call-start = ((), (), s32[]{:S(2)}) async-start(), calls=%async_computation.17 | async-start | bytes 5308416 | tf_op jit(solution)/shard_map/reduce_scatter | solution.py:785
  1021.2 124.7 %all-to-all-start.11 = ((f32[32,88,384]{2,1,0:T(8,128)}), f32[32,88,384]{2,1,0:T(8,128)}, u32[]{:S(2)}, u32[]{:S(2)}) async-start(f32[32,88,384]{2,1,0:T(8,128)} %bitcast.115), calls=%async_computation.13 | async-start | bytes 8650752 | tf_op jit(solution)/shard_map/all_to_all | solution.py:852
  1028.0 343.0 %all-gather.2.cloned.1.call-start = ((), (), s32[]{:S(2)}) async-start(), calls=%async_computation.18 | async-start | bytes 19464192 | tf_op jit(solution)/shard_map/all_gather | solution.py:788
  1145.9 175.4 %all-to-all-start.12 = ((f32[32,88,384]{2,1,0:T(8,128)}), f32[32,88,384]{2,1,0:T(8,128)}, u32[]{:S(2)}, u32[]{:S(2)}) async-start(f32[32,88,384]{2,1,0:T(8,128)} %bitcast.111), calls=%async_computation.14 | async-start | bytes 8650752 | tf_op jit(solution)/shard_map/all_to_all | solution.py:852
  1152.9 23.2 %copy-start.19 = (f32[2,192]{1,0:T(2,128)S(1)}, f32[2,192]{1,0:T(2,128)}, u32[]{:S(2)}) copy-start(f32[2,192]{1,0:T(2,128)} %get-tuple-element.171) | copy-start | bytes 4612
  1152.9 23.3 %copy-start.18 = (f32[2,192]{1,0:T(2,128)S(1)}, f32[2,192]{1,0:T(2,128)}, u32[]{:S(2)}) copy-start(f32[2,192]{1,0:T(2,128)} %get-tuple-element.173) | copy-start | bytes 4612
  1321.3 7.1 copy-start.7
  1321.3 7.1 copy-start.8
  1321.3 7.1 copy-start.9
  1321.3 7.1 copy-start.10
  1321.3 7.1 copy-start.11
  1321.3 7.1 copy-start.12
  1321.3 117.1 %all-to-all-start.13 = ((f32[32,88,384]{2,1,0:T(8,128)}), f32[32,88,384]{2,1,0:T(8,128)}, u32[]{:S(2)}, u32[]{:S(2)}) async-start(f32[32,88,384]{2,1,0:T(8,128)} %bitcast.112), calls=%async_computation.15 | async-start | bytes 8650752 | tf_op jit(solution)/shard_map/all_to_all | solution.py:852
Sparse Core Ops, SparseCore 0:
  773.7 208.4 reduce-scatter.2
  986.3 143.5 reduce-scatter.4
  1146.1 224.8 all-gather.1
